TPU v7x, 32 devices: a whole 2x2x4 slice. The times are simulated.
32 devices in a mesh: tok: 4 (over y, x), feat: 8 (over z, core).
Axes of the slice: x: 2, y: 2, z: 4, core: 2. Of those that a mesh axis runs over, the one named last changes fastest.
Arguments:
- resid: bfloat16 [1024, 8192], P(None, ('tok', 'feat')), may hold values from -6 to 6
- resid_grad: bfloat16 [1024, 8192], P(None, ('tok', 'feat')), may hold values from -6 to 6
- active: int32 [8, 20], P('tok'), may hold values from 0 to 39, all different within a row
- w_enc: bfloat16 [8192, 5120], P(None, 'feat'), may hold values from -0.0625 to 0.0625
- b_enc: float32 [5120], P('feat'), may hold values from -3 to 3
- w_dec: bfloat16 [5120, 8192], P('feat'), may hold values from -0.25 to 0.25
- b_dec: float32 [8192], P('feat'), may hold values from -3 to 3
Outputs:
- feature_attr: float32 [1024, 5120], P('tok', 'feat')
- error: float32 [1024, 8192], P('tok', 'feat')
- error_attr: float32 [1024], P('tok')
Inputs may be any that keep to these rules, and one draw needn't show every extreme that they name: `active`: each row lists 20 different feature blocks; every block is listed by some tile.
All inputs are finite; a program needn't handle non-finite values.
Results may differ from a plain program's by a relative error of at most 0.012.
Values may be sent and summed in bfloat16 or wider, within the bound.
No kernel may reach another device: no remote copies, remote signals or barrier semaphores. Data moves between devices by JAX's collectives and lax.ppermute only.
A program may use at most 128 MiB of HBM per device.

v0:
```python
import jax
import jax.numpy as jnp
from jax import lax
from jax.sharding import PartitionSpec as P

BLOCK = 128
TILE = 128


def per_device(resid, resid_grad, active, w_enc, b_enc, w_dec, b_dec):
    n_tok = lax.axis_size("tok")
    n_feat = lax.axis_size("feat")
    width = resid.shape[1]
    part_x, part_g = (
        lax.all_to_all(resid, "tok", split_axis=0, concat_axis=1, tiled=True),
        lax.all_to_all(resid_grad, "tok", split_axis=0, concat_axis=1, tiled=True),
    )
    tok_rows = part_x.shape[0]
    part_x = part_x.reshape(tok_rows, n_tok, 1, width)
    part_g = part_g.reshape(tok_rows, n_tok, 1, width)
    rows_x, rows_g = (
        lax.all_gather(part_x, "feat", axis=2, tiled=True),
        lax.all_gather(part_g, "feat", axis=2, tiled=True),
    )
    rows_x = rows_x.reshape(tok_rows, n_tok * n_feat * width)
    rows_g = rows_g.reshape(tok_rows, n_tok * n_feat * width)
    tok_rows = rows_x.shape[0]
    feat_dev = w_enc.shape[1]
    blocks = feat_dev // BLOCK
    tiles_dev = active.shape[0]
    block_ids = lax.axis_index("feat") * blocks + jnp.arange(blocks, dtype=jnp.int32)
    hits = jnp.any(active[:, :, None] == block_ids[None, None, :], axis=1).astype(jnp.float32)
    pre = jnp.dot(rows_x, w_enc, preferred_element_type=jnp.float32) + b_enc
    shaped = jnp.maximum(pre, 0.0).reshape(tiles_dev, TILE, blocks, BLOCK) * hits[:, None, :, None]
    acts = shaped.reshape(tok_rows, feat_dev).astype(jnp.bfloat16)
    partial_recon = jnp.dot(acts, w_dec, preferred_element_type=jnp.float32)
    recon_share = lax.psum_scatter(
        partial_recon.astype(jnp.bfloat16), "feat", scatter_dimension=1, tiled=True
    ).astype(jnp.float32)
    share = recon_share.shape[1]
    start = lax.axis_index("feat") * share
    own_x = lax.dynamic_slice_in_dim(rows_x, start, share, 1)
    own_g = lax.dynamic_slice_in_dim(rows_g, start, share, 1)
    recon = recon_share + b_dec
    error = own_x.astype(jnp.float32) - recon
    local_terms = jnp.sum(error * own_g.astype(jnp.float32), axis=1)
    error_attr = lax.psum(local_terms, "feat")
    proj = lax.dot_general(
        rows_g, w_dec, (((1,), (1,)), ((), ())), preferred_element_type=jnp.float32
    )
    feature_attr = acts.astype(jnp.float32) * proj
    return (feature_attr, error, error_attr)


def solution(mesh):
    placed = (
        P(None, ("tok", "feat")),
        P(None, ("tok", "feat")),
        P("tok", None),
        P(None, "feat"),
        P("feat"),
        P("feat", None),
        P("feat"),
    )
    return jax.shard_map(
        per_device,
        mesh=mesh,
        in_specs=placed,
        out_specs=(P("tok", "feat"), P("tok", "feat"), P("tok")),
        check_vma=False,
    )
```

profile of v0, /device:TPU:0, one launch (start us, length us, event | category | flops | bytes accessed | tf_op | source)
XLA Modules:
  0.0 191.0 jit_solution(815981625661044178)
XLA Ops:
  7.2 0.0 all-gather.5.cloned.1.call-start
  7.2 14.3 %all_to_all.32 = bf16[4,256,256]{2,1,0:T(8,128)(2,1)} all-to-all(bf16[4,256,256]{2,1,0:T(8,128)(2,1)} %bitcast.31), channel_id=1, replica_groups=mesh['tok'=4,'feat'=8] {'tok'}, dimensions={0} | all-to-all | bytes 1048576 | tf_op jit(solution)/shard_map/all_to_all | solution.py:15
  21.5 0.0 all-gather.5.cloned.1.call-update
  21.5 0.0 all-gather.7.cloned.1.call-start
  21.6 12.0 %all_to_all.33 = bf16[4,256,256]{2,1,0:T(8,128)(2,1)} all-to-all(bf16[4,256,256]{2,1,0:T(8,128)(2,1)} %bitcast.32), channel_id=1, replica_groups=mesh['tok'=4,'feat'=8] {'tok'}, dimensions={0} | all-to-all | bytes 1048576 | tf_op jit(solution)/shard_map/all_to_all | solution.py:16
  33.6 0.0 all-gather.7.cloned.1.call-update
  33.6 0.0 reduce-scatter.2.cloned.1.call-start
  33.7 0.9 compare_reduce_fusion
  34.5 0.1 copy.19
  34.6 0.2 mul.24
  34.9 0.2 copy.20
  35.2 34.2 %all-gather.5.cloned.1.call-done = bf16[256,4,2048]{2,0,1:T(8,128)(2,1)} async-done(((bf16[256,4,256]{2,0,1:T(8,128)(2,1)}), bf16[256,4,2048]{2,0,1:T(8,128)(2,1)}) %all-gather.5.cloned.1.call-update) | async-done | bytes 4194320 | tf_op jit(solution)/shard_map/all_gather | solution.py:22
  69.4 0.0 copy-start.3
  69.4 2.7 %copy.22 = bf16[4,32,8,2048]{3,2,0,1:T(8,128)(2,1)S(1)} copy(bf16[4,32,8,2048]{3,2,1,0:T(8,128)(2,1)} %bitcast.26) | data formatting | bytes 8388608 | tf_op jit(solution)/shard_map/reshape | solution.py:25
  72.1 0.0 copy-start
  72.1 2.0 %copy-done = bf16[4,32,8,2048]{3,2,0,1:T(8,128)(2,1)} copy-done((bf16[4,32,8,2048]{3,2,0,1:T(8,128)(2,1)}, bf16[4,32,8,2048]{3,2,0,1:T(8,128)(2,1)S(1)}, u32[]{:S(2)}) %copy-start) | copy-done | bytes 4194328
  74.0 0.0 copy-done.3
  74.0 6.7 %fusion.2 = bf16[256,640]{1,0:T(8,128)(2,1)S(1)} fusion(f32[256,640]{1,0:T(8,128)S(1)} %copy.20, bf16[256,8192]{1,0:T(8,128)(2,1)S(1)} %bitcast.21, bf16[8192,640]{1,0:T(8,128)(2,1)} %param.10, f32[640]{0:T(1024)S(1)} %copy-done.3), kind=kOutput, calls=%fused_computation.5 | convolution fusion | flops 2685009920 | bytes 15665664 | tf_op jit(solution)/shard_map/dot_general | solution.py:33
  80.8 0.0 slice-done
  80.8 0.0 slice-done.1
  80.8 0.0 slice-done.2
  80.8 5.1 %convolution_convert_fusion = bf16[256,8192]{1,0:T(8,128)(2,1)} fusion(bf16[256,640]{1,0:T(8,128)(2,1)S(1)} %fusion.2, bf16[640,8192]{1,0:T(8,128)(2,1)S(1)} %bitcast.34), kind=kOutput, calls=%fused_computation | convolution fusion | flops 2686451712 | bytes 15007744 | tf_op jit(solution)/shard_map/dot_general | solution.py:36
  85.9 0.0 reduce-scatter.2.cloned.1.call-update
  85.9 31.1 %all-gather.7.cloned.1.call-done = bf16[256,4,2048]{2,0,1:T(8,128)(2,1)} async-done(((bf16[256,4,256]{2,0,1:T(8,128)(2,1)}), bf16[256,4,2048]{2,0,1:T(8,128)(2,1)}) %all-gather.7.cloned.1.call-update) | async-done | bytes 4194320 | tf_op jit(solution)/shard_map/all_gather | solution.py:23
  117.0 2.5 %copy.23 = bf16[4,32,8,2048]{3,2,0,1:T(8,128)(2,1)S(1)} copy(bf16[4,32,8,2048]{3,2,1,0:T(8,128)(2,1)} %bitcast.25) | data formatting | bytes 8388608 | tf_op jit(solution)/shard_map/reshape | solution.py:26
  119.5 0.0 copy-start.1
  119.6 1.9 %copy-done.1 = bf16[4,32,8,2048]{3,2,0,1:T(8,128)(2,1)} copy-done((bf16[4,32,8,2048]{3,2,0,1:T(8,128)(2,1)}, bf16[4,32,8,2048]{3,2,0,1:T(8,128)(2,1)S(1)}, u32[]{:S(2)}) %copy-start.1) | copy-done | bytes 4194328
  121.5 7.4 %convolution_multiply_fusion = f32[256,640]{1,0:T(8,128)} fusion(bf16[256,8192]{1,0:T(8,128)(2,1)S(1)} %bitcast.23, bf16[640,8192]{1,0:T(8,128)(2,1)} %param.12, bf16[256,640]{1,0:T(8,128)(2,1)S(1)} %fusion.2), kind=kOutput, calls=%fused_computation.1 | convolution fusion | flops 2684682240 | bytes 15663104 | tf_op jit(solution)/shard_map/dot_general | solution.py:48
  128.9 38.7 %reduce-scatter.2.cloned.1.call-done = bf16[256,1024]{1,0:T(8,128)(2,1)} async-done(((bf16[256,8192]{1,0:T(8,128)(2,1)}), bf16[256,1024]{1,0:T(8,128)(2,1)}) %reduce-scatter.2.cloned.1.call-update) | async-done | bytes 524304 | tf_op jit(solution)/shard_map/reduce_scatter | solution.py:37
  167.6 0.0 copy-done.2
  167.6 2.6 %multiply_reduce_fusion = (f32[256]{0:T(256)S(1)}, f32[256,1024]{1,0:T(8,128)}) fusion(bf16[256,8192]{1,0:T(8,128)(2,1)} %bitcast.24, s32[]{:T(128)S(6)} %select_n.4, f32[1024]{0:T(1024)S(1)} %copy-done.2, bf16[256,1024]{1,0:T(8,128)(2,1)} %reduce-scatter.2.cloned.1.call-done, bf16[256,8192]{1,0:T(8,128)(2,1)} %bitcast.22), kind=kLoop, calls=%fused_computation.6 | loop fusion | flops 1834752 | bytes 2626564 | tf_op jit(solution)/shard_map/reduce_sum | solution.py:46
  170.2 14.3 %psum.7 = f32[256]{0:T(256)} all-reduce(f32[256]{0:T(256)S(1)} %get-tuple-element.3), channel_id=1, replica_groups=mesh['tok'=4,'feat'=8] {'feat'}, use_global_device_ids=true, to_apply=%region_3.0 | all-reduce | flops 256 | bytes 2048 | tf_op jit(solution)/shard_map/psum | solution.py:47
  (8 shorter events, 0.1 us)
Async XLA Ops:
  7.2 62.2 %all-gather.5.cloned.1.call-start = ((), (), s32[]{:S(2)}) async-start(), calls=%async_computation.4 | async-start | bytes 4718592 | tf_op jit(solution)/shard_map/all_gather | solution.py:22
  21.5 95.5 %all-gather.7.cloned.1.call-start = ((), (), s32[]{:S(2)}) async-start(), calls=%async_computation.5 | async-start | bytes 4718592 | tf_op jit(solution)/shard_map/all_gather | solution.py:23
  33.6 134.0 %reduce-scatter.2.cloned.1.call-start = ((), (), s32[]{:S(2)}) async-start(), calls=%async_computation.3 | async-start | bytes 4718592 | tf_op jit(solution)/shard_map/reduce_scatter | solution.py:37
  69.4 4.6 %copy-start.3 = (f32[640]{0:T(1024)S(1)}, f32[640]{0:T(1024)}, u32[]{:S(2)}) copy-start(f32[640]{0:T(1024)} %param.11) | copy-start | bytes 7684
  69.4 11.4 %slice-start = ((s8[10485760]{0:T(1024)(128)(4,1)}), s8[4194304]{0:T(1024)(128)(4,1)S(1)}, s32[]{:S(2)}) async-start(s8[10485760]{0:T(1024)(128)(4,1)} %bitcast.33), calls=%async_computation.6 | async-start | bytes 8388608
  72.1 2.0 %copy-start = (bf16[4,32,8,2048]{3,2,0,1:T(8,128)(2,1)}, bf16[4,32,8,2048]{3,2,0,1:T(8,128)(2,1)S(1)}, u32[]{:S(2)}) copy-start(bf16[4,32,8,2048]{3,2,0,1:T(8,128)(2,1)S(1)} %copy.22) | copy-start | bytes 12582916
  74.0 6.7 %slice-start.1 = ((s8[10485760]{0:T(1024)(128)(4,1)}), s8[4194304]{0:T(1024)(128)(4,1)S(1)}, s32[]{:S(2)}) async-start(s8[10485760]{0:T(1024)(128)(4,1)} %bitcast.33), calls=%async_computation.7 | async-start | bytes 8388608
  74.0 6.8 %slice-start.2 = ((s8[10485760]{0:T(1024)(128)(4,1)}), s8[2097152]{0:T(1024)(128)(4,1)S(1)}, s32[]{:S(2)}) async-start(s8[10485760]{0:T(1024)(128)(4,1)} %bitcast.33), calls=%async_computation.8 | async-start | bytes 4194304
  119.5 1.9 %copy-start.1 = (bf16[4,32,8,2048]{3,2,0,1:T(8,128)(2,1)}, bf16[4,32,8,2048]{3,2,0,1:T(8,128)(2,1)S(1)}, u32[]{:S(2)}) copy-start(bf16[4,32,8,2048]{3,2,0,1:T(8,128)(2,1)S(1)} %copy.23) | copy-start | bytes 12582916
  121.5 46.1 %copy-start.2 = (f32[1024]{0:T(1024)S(1)}, f32[1024]{0:T(1024)}, u32[]{:S(2)}) copy-start(f32[1024]{0:T(1024)} %param.13) | copy-start | bytes 12292
Sparse Core Ops, SparseCore 0:
  21.6 47.7 all-gather.4
  71.0 46.0 all-gather.6
  119.3 48.2 reduce-scatter.1
where the time goes:
time: 191 us
  waiting for transfers between devices  104 us (54%)
  blocking collectives  40.6 us (21%)
  matrix products  19.2 us (10%)
  between operations  13.9 us (7%)
  local copies, waits for them, and re-layouts  9.68 us (5%)
  other arithmetic  3.44 us (2%)
    reduce_scatter x1, waiting for transfers between devices, per_device(): lax.psum_scatter(partial_recon.astype(jnp.bfloat16), 'feat', scatter_dime...  38.7 us
    all_gather x1, waiting for transfers between devices, per_device(): lax.all_gather(part_x, 'feat', axis=2, tiled=True)  34.2 us
    all_gather x1, waiting for transfers between devices, per_device(): lax.all_gather(part_g, 'feat', axis=2, tiled=True)  31.1 us
    psum x1, blocking collectives, per_device(): error_attr = lax.psum(local_terms, 'feat')  14.3 us
    all_to_all x1, blocking collectives, per_device(): lax.all_to_all(resid, 'tok', split_axis=0, concat_axis=1, tiled=True)  14.3 us
    all_to_all x1, blocking collectives, per_device(): lax.all_to_all(resid_grad, 'tok', split_axis=0, concat_axis=1, tiled=True)  12 us
    dot_general x1, matrix products, per_device(): lax.dot_general(rows_g, w_dec, (((1,), (1,)), ((), ())), preferred_elemen...  7.4 us
    dot_general x1, matrix products, per_device(): pre = jnp.dot(rows_x, w_enc, preferred_element_type=jnp.float32) + b_enc  6.73 us
  transfers between devices with their start and end apart: 3, of which 3 were waited for; matrix products, arithmetic and copies ran while one was open for 14% of the time, Pallas kernels for 0%

commit v1 on v0

v1 whole, which is shorter than its diff:
```python
import functools

import jax
import jax.numpy as jnp
from jax import lax
from jax.experimental import pallas as pl
from jax.experimental.pallas import tpu as pltpu
from jax.sharding import PartitionSpec as P

BLOCK = 128
TILE = 128
STREAMS = ((0, 1), (2, 3))
PARAMS = pltpu.CompilerParams(vmem_limit_bytes=40 << 20)
F32 = jnp.float32
BF16 = jnp.bfloat16


def whole(shape):
    zeros = (0,) * len(shape)
    return pl.BlockSpec(shape, lambda *_: zeros)


def cost(flops, moved):
    return pl.CostEstimate(flops=flops, bytes_accessed=moved, transcendentals=0)


def pieces(refs, streams):
    return [refs[a].at[b] for a, stream in enumerate(streams) for b in range(len(stream))]


def enc_body(streams, first, last, table, *refs):
    count = len(streams)
    near, far = pieces(refs[:count], streams), pieces(refs[count:2 * count], streams)
    refs = refs[2 * count:]
    w_ref, bias_ref, hit_ref = refs[:3]
    refs = refs[3:]
    if not first:
        acc_ref, refs = refs[0], refs[2:]
    out_ref, own_ref = refs[:2]
    core = pl.program_id(0)
    for side, blocks in ((0, near), (1, far)):

        @pl.when(core == side)
        def _():
            total = None
            for s, x in enumerate(blocks):
                term = jnp.dot(x[...], w_ref[table[0] ^ s, 0], preferred_element_type=F32)
                total = term if total is None else total + term

                @pl.when(table[1] == s)
                def _():
                    own_ref[0] = x[...]

            if side == 0:
                target = refs[2] if last else out_ref
                target[...] = total if first else total + acc_ref[...]
            elif last:
                pre = refs[2][...] + total + bias_ref[...]
                tiles = hit_ref.shape[0]
                shaped = jnp.maximum(pre, 0.0).reshape(tiles, TILE, -1) * hit_ref[...][:, None, :]
                out_ref[...] = shaped.reshape(pre.shape).astype(BF16)
            else:
                out_ref[...] += total


def encode(table, near, far, w4, bias, hit, carry, streams, first, last):
    n_tok, n_feat, width, feats = w4.shape
    rows = near[0].shape[1]
    specs = [whole(a.shape) for a in near] + [whole(a.shape) for a in far]
    specs += [
        pl.BlockSpec((n_tok, 1, width, feats), lambda c, t: (0, t[2 + c], 0, 0)),
        whole(bias.shape),
        whole(hit.shape),
    ]
    args = [*near, *far, w4, bias, hit]
    aliases = {}
    if not first:
        acc, own = carry
        specs += [whole(acc.shape), pl.BlockSpec(memory_space=pl.ANY)]
        args += [acc, own]
        aliases = {len(args): 1}
    scratch = [pltpu.VMEM((rows, feats), F32)] if last else []
    return pl.pallas_call(
        functools.partial(enc_body, streams, first, last),
        grid_spec=pltpu.PrefetchScalarGridSpec(
            num_scalar_prefetch=1,
            grid=(2,),
            in_specs=specs,
            out_specs=[
                whole((rows, feats)),
                pl.BlockSpec((1, rows, width), lambda c, t: (t[2 + c], 0, 0)),
            ],
            scratch_shapes=scratch,
        ),
        out_shape=[
            jax.ShapeDtypeStruct((rows, feats), BF16 if last else F32),
            jax.ShapeDtypeStruct((n_feat, rows, width), BF16),
        ],
        input_output_aliases=aliases,
        compiler_params=PARAMS,
        cost_estimate=cost(4 * rows * n_tok * width * feats, 4 * n_tok * width * (feats + rows)),
        name="encode",
    )(table, *args)


def proj_body(streams, first, last, n_tok, table, *refs):
    count = len(streams)
    near, far = pieces(refs[:count], streams), pieces(refs[count:2 * count], streams)
    refs = refs[2 * count:]
    w_refs, acts_ref = refs[:n_tok], refs[n_tok]
    refs = refs[n_tok + 1:]
    if not first:
        acc_ref, refs = refs[0], refs[2:]
    out_ref, own_ref = refs[:2]
    core = pl.program_id(0)
    for side, blocks in ((0, near), (1, far)):

        @pl.when(core == side)
        def _():
            total = None
            for s, x in enumerate(blocks):
                term = lax.dot_general(
                    x[...], w_refs[s][...], (((1,), (1,)), ((), ())), preferred_element_type=F32
                )
                total = term if total is None else total + term

                @pl.when(table[1] == s)
                def _():
                    own_ref[0] = x[...]

            if side == 0:
                out_ref[...] = total if first else total + acc_ref[...]
            elif last:
                attr = acts_ref[...].astype(F32) * (out_ref[...] + total)
                out_ref[...] = attr
                refs[2][...] = jnp.sum(attr, axis=1, keepdims=True)
            else:
                out_ref[...] += total


def project(table, near, far, w_dec, acts, carry, streams, first, last, n_feat):
    rows, width = near[0].shape[1:]
    feats = w_dec.shape[0]
    n_tok = sum(len(s) for s in streams)
    specs = [whole(a.shape) for a in near] + [whole(a.shape) for a in far]
    for s in range(n_tok):
        specs.append(
            pl.BlockSpec(
                (feats, width), lambda c, t, s=s: (0, (t[0] ^ s) * n_feat + t[2 + c])
            )
        )
    args = [*near, *far] + [w_dec] * n_tok
    specs.append(whole(acts.shape))
    args.append(acts)
    aliases = {}
    if not first:
        acc, own = carry
        specs += [whole(acc.shape), pl.BlockSpec(memory_space=pl.ANY)]
        args += [acc, own]
        aliases = {len(args): 1}
    out_specs = [
        whole((rows, feats)),
        pl.BlockSpec((1, rows, width), lambda c, t: (t[2 + c], 0, 0)),
    ]
    out_shape = [
        jax.ShapeDtypeStruct((rows, feats), F32),
        jax.ShapeDtypeStruct((n_feat, rows, width), BF16),
    ]
    if last:
        out_specs.append(whole((rows, 1)))
        out_shape.append(jax.ShapeDtypeStruct((rows, 1), F32))
    return pl.pallas_call(
        functools.partial(proj_body, streams, first, last, n_tok),
        grid_spec=pltpu.PrefetchScalarGridSpec(
            num_scalar_prefetch=1, grid=(2,), in_specs=specs, out_specs=out_specs
        ),
        out_shape=out_shape,
        input_output_aliases=aliases,
        compiler_params=PARAMS,
        cost_estimate=cost(4 * rows * n_tok * width * feats, 4 * n_tok * width * (feats + rows)),
        name="project",
    )(table, *args)


def dec_body(table, acts_ref, w_ref, far_ref, near_ref):
    for side, out_ref in ((0, far_ref), (1, near_ref)):

        @pl.when(pl.program_id(0) == side)
        def _():
            out_ref[...] = jnp.dot(
                acts_ref[...], w_ref[...], preferred_element_type=F32
            ).astype(BF16)


def decode(table, acts, w_dec, share):
    rows, feats = acts.shape
    out = jax.ShapeDtypeStruct((rows, share), BF16)
    return pl.pallas_call(
        dec_body,
        grid_spec=pltpu.PrefetchScalarGridSpec(
            num_scalar_prefetch=1,
            grid=(2,),
            in_specs=[whole(acts.shape), pl.BlockSpec((feats, share), lambda c, t: (0, t[c]))],
            out_specs=[whole(out.shape), whole(out.shape)],
        ),
        out_shape=[out, out],
        compiler_params=PARAMS,
        cost_estimate=cost(4 * rows * feats * share, 4 * share * (feats + rows)),
        name="decode",
    )(table, acts, w_dec)


def local_body(table, x_ref, g_ref, bias_ref, fa_ref, out_ref):
    term = (x_ref[0].astype(F32) - bias_ref[...]) * g_ref[0].astype(F32)
    term = jnp.sum(term, axis=1, keepdims=True)
    step = pl.program_id(0)

    @pl.when(step == 0)
    def _():
        out_ref[...] = term - fa_ref[...]

    @pl.when(step > 0)
    def _():
        out_ref[...] += term


def local_terms(table, own_x, own_g, bias, fa_sum):
    _, rows, width = own_x.shape
    picked = pl.BlockSpec((1, rows, width), lambda r, t: (t[0] + r, 0, 0))
    return pl.pallas_call(
        local_body,
        grid_spec=pltpu.PrefetchScalarGridSpec(
            num_scalar_prefetch=1,
            grid=(bias.shape[1] // width,),
            in_specs=[picked, picked, pl.BlockSpec((1, width), lambda r, t: (0, r)), whole((rows, 1))],
            out_specs=whole((rows, 1)),
        ),
        out_shape=jax.ShapeDtypeStruct((rows, 1), F32),
        compiler_params=PARAMS,
        name="local_terms",
    )(table, own_x, own_g, bias, fa_sum)


def error_body(table, x_ref, near_ref, far_ref, come_ref, bias_ref, out_ref):
    recon = near_ref[...].astype(F32) + far_ref[...].astype(F32)
    recon = recon + come_ref[...].astype(F32) + bias_ref[...]
    out_ref[...] = x_ref[0].astype(F32) - recon


def final_error(table, own_x, near, far, come, bias):
    _, rows, width = own_x.shape
    share = bias.shape[1]
    part = pl.BlockSpec((rows, width), lambda r, t: (0, r))
    return pl.pallas_call(
        error_body,
        grid_spec=pltpu.PrefetchScalarGridSpec(
            num_scalar_prefetch=1,
            grid=(share // width,),
            in_specs=[
                pl.BlockSpec((1, rows, width), lambda r, t: (t[0] + r, 0, 0)),
                part,
                part,
                part,
                pl.BlockSpec((1, width), lambda r, t: (0, r)),
            ],
            out_specs=part,
        ),
        out_shape=jax.ShapeDtypeStruct((rows, share), F32),
        compiler_params=PARAMS,
        name="final_error",
    )(table, own_x, near, far, come, bias)


def ring_program(resid, resid_grad, active, w_enc, b_enc, w_dec, b_dec):
    n_tok, n_feat = lax.axis_size("tok"), lax.axis_size("feat")
    i, j = lax.axis_index("tok"), lax.axis_index("feat")
    chips = n_feat // 2
    chip, core = j // 2, j % 2
    width = resid.shape[1]
    rows = resid.shape[0] // n_tok
    feats = w_enc.shape[1]
    share = n_tok * width
    streams = STREAMS

    def exchange(array):
        def block(s):
            mine = lax.dynamic_slice_in_dim(array, (i ^ s) * rows, rows, 0)
            if s == 0:
                return mine
            return lax.ppermute(mine, "tok", [(a, a ^ s) for a in range(n_tok)])

        blocks = [block(s) for s in range(n_tok)]
        return [jnp.stack([blocks[s] for s in stream]) for stream in streams]

    ring = [(a, (a + 2) % n_feat) for a in range(n_feat)]
    swap = [(a, a ^ 1) for a in range(n_feat)]

    def gather(shards, after=None):
        near, far = [list(shards)], []
        for k in range(1, chips):
            step = []
            for n, held in enumerate(near[-1]):
                if k == 1 and after is not None:
                    held, _ = lax.optimization_barrier((held, after[n]))
                step.append(lax.ppermute(held, "feat", ring))
            near.append(step)
        for step in near:
            far.append([lax.ppermute(held, "feat", swap) for held in step])
        return near, far

    near_x, far_x = gather(exchange(resid))
    near_g, far_g = gather(exchange(resid_grad), after=near_x[-1])

    blocks = feats // BLOCK
    block_ids = j * blocks + jnp.arange(blocks, dtype=jnp.int32)
    hits = jnp.any(active[:, :, None] == block_ids[None, None, :], axis=1).astype(F32)
    hit = jnp.repeat(hits, BLOCK, axis=1)
    bias = b_enc.reshape(1, feats)
    b_row = b_dec.reshape(1, share)
    ratio = n_feat // n_tok
    own_sub = i ^ (j // ratio)
    own_start = ((j % ratio) * n_tok).astype(jnp.int32).reshape(1)

    def table(k):
        source = 2 * ((chip + chips - k) % chips)
        return jnp.stack([i, own_sub, source + core, source + 1 - core]).astype(jnp.int32)

    tables = [table(k) for k in range(chips)]
    w4 = w_enc.reshape(n_tok, n_feat, width, feats)
    carry = None
    for k in range(chips):
        carry = encode(
            tables[k], near_x[k], far_x[k], w4, bias, hit, carry, streams, k == 0, k == chips - 1
        )
    acts, own_x = carry

    come = None
    for k in range(chips - 1, -1, -1):
        dest = 2 * ((chip + k) % chips)
        far_out, near_out = decode(
            jnp.stack([dest + 1 - core, dest + core]).astype(jnp.int32), acts, w_dec, share
        )
        far_in = lax.ppermute(far_out, "feat", swap)
        if k == 0:
            break
        total = near_out.astype(F32) + far_in.astype(F32)
        if come is not None:
            total = total + come.astype(F32)
        come = lax.ppermute(total.astype(BF16), "feat", ring)

    carry = None
    for k in range(chips):
        carry = project(
            tables[k], near_g[k], far_g[k], w_dec, acts, carry, streams, k == 0, k == chips - 1, n_feat
        )
    feature_attr, own_g, fa_sum = carry

    attr = local_terms(own_start, own_x, own_g, b_row, fa_sum).reshape(-1, TILE)
    reach = 1
    while reach < n_feat:
        attr = attr + lax.ppermute(attr, "feat", [(a, a ^ reach) for a in range(n_feat)])
        reach *= 2

    error = final_error(own_start, own_x, near_out, far_in, come, b_row)
    return feature_attr, error, attr.reshape(rows)


def gathered_program(resid, resid_grad, active, w_enc, b_enc, w_dec, b_dec):
    n_tok = lax.axis_size("tok")
    n_feat = lax.axis_size("feat")
    width = resid.shape[1]

    def rows_of(array):
        part = lax.all_to_all(array, "tok", split_axis=0, concat_axis=1, tiled=True)
        part = part.reshape(part.shape[0], n_tok, 1, width)
        part = lax.all_gather(part, "feat", axis=2, tiled=True)
        return part.reshape(part.shape[0], n_tok * n_feat * width)

    rows_x, rows_g = rows_of(resid), rows_of(resid_grad)
    tok_rows = rows_x.shape[0]
    feat_dev = w_enc.shape[1]
    blocks = feat_dev // BLOCK
    tiles_dev = active.shape[0]
    block_ids = lax.axis_index("feat") * blocks + jnp.arange(blocks, dtype=jnp.int32)
    hits = jnp.any(active[:, :, None] == block_ids[None, None, :], axis=1).astype(F32)
    pre = jnp.dot(rows_x, w_enc, preferred_element_type=F32) + b_enc
    shaped = jnp.maximum(pre, 0.0).reshape(tiles_dev, TILE, blocks, BLOCK) * hits[:, None, :, None]
    acts = shaped.reshape(tok_rows, feat_dev).astype(BF16)
    partial_recon = jnp.dot(acts, w_dec, preferred_element_type=F32)
    recon_share = lax.psum_scatter(
        partial_recon.astype(BF16), "feat", scatter_dimension=1, tiled=True
    ).astype(F32)
    share = recon_share.shape[1]
    start = lax.axis_index("feat") * share
    own_x = lax.dynamic_slice_in_dim(rows_x, start, share, 1)
    own_g = lax.dynamic_slice_in_dim(rows_g, start, share, 1)
    recon = recon_share + b_dec
    error = own_x.astype(F32) - recon
    local_sums = jnp.sum(error * own_g.astype(F32), axis=1)
    error_attr = lax.psum(local_sums, "feat")
    proj = lax.dot_general(rows_g, w_dec, (((1,), (1,)), ((), ())), preferred_element_type=F32)
    return acts.astype(F32) * proj, error, error_attr


def per_device(resid, *rest):
    n_tok, n_feat = lax.axis_size("tok"), lax.axis_size("feat")
    fits = resid.shape[1] % 128 == 0 and n_tok == 4 and n_feat % n_tok == 0
    return (ring_program if fits else gathered_program)(resid, *rest)


def solution(mesh):
    placed = (
        P(None, ("tok", "feat")),
        P(None, ("tok", "feat")),
        P("tok", None),
        P(None, "feat"),
        P("feat"),
        P("feat", None),
        P("feat"),
    )
    return jax.shard_map(
        per_device,
        mesh=mesh,
        in_specs=placed,
        out_specs=(P("tok", "feat"), P("tok", "feat"), P("tok")),
        check_vma=False,
    )
```

time: 191 us -> 214 us (1.12)
  Pallas kernels: 0 us -> 43.9 us
  blocking collectives: 40.6 us -> 0 us
  local copies, waits for them, and re-layouts: 9.68 us -> 48.2 us
  starting transfers between devices: 0.12 us -> 21.7 us
  matrix products: 19.2 us -> 0 us
  waiting for transfers between devices: 104 us -> 89.7 us
  between operations: 13.9 us -> 1.2 us
  other arithmetic: 3.44 us -> 8.35 us
    ppermute x0 -> x44, waiting for transfers between devices: none -> 89.7 us  [the longest x12 64.5 us: gather(): step.append(lax.ppermute(held, 'feat', ring))]
    all_gather x2 -> x0, waiting for transfers between devices: 65.4 us -> none  [the longest x1 34.2 us: per_device(): lax.all_gather(part_x, 'feat', axis=2, tiled=True)]
    pallas_call x0 -> x14, Pallas kernels: none -> 43.9 us  [the longest x4 16.1 us: project(): pl.pallas_call(functools.partial(proj_body, streams, first, last, n_tok),...]
    unnamed x15 -> x128, local copies, waits for them, and re-layouts: 3.96 us -> 46.4 us
    reduce_scatter x1 -> x0, waiting for transfers between devices: 38.7 us -> none  [per_device(): lax.psum_scatter(partial_recon.astype(jnp.bfloat16), 'feat', scatter_dime...]
    all_to_all x2 -> x0, blocking collectives: 26.3 us -> none  [the longest x1 14.3 us: per_device(): lax.all_to_all(resid, 'tok', split_axis=0, concat_axis=1, tiled=True)]
    ppermute x0 -> x44, starting transfers between devices: none -> 21.7 us  [the longest x6 8.13 us: block(): return lax.ppermute(mine, 'tok', [(a, a ^ s) for a in range(n_tok)])]
    dot_general x3 -> x0, matrix products: 19.2 us -> none  [the longest x1 7.4 us: per_device(): lax.dot_general(rows_g, w_dec, (((1,), (1,)), ((), ())), preferred_elemen...]
  transfers between devices with their start and end apart: 3 -> 44, of which waited for: 3 -> 19; matrix products, arithmetic and copies ran while one was open for 14% -> 4% of each run, Pallas kernels for 0% -> 16%
where the time goes in v1:
time: 214 us; the launch traced here: 213 us
  waiting for transfers between devices  89.7 us (42%)
  local copies, waits for them, and re-layouts  48.2 us (23%)
  Pallas kernels  43.9 us (21%)
  starting transfers between devices  21.7 us (10%)
  other arithmetic  8.35 us (4%)
    ppermute x12, waiting for transfers between devices, gather(): step.append(lax.ppermute(held, 'feat', ring))  64.5 us
    unnamed x128, local copies, waits for them, and re-layouts  46.4 us
    pallas_call x4, Pallas kernels, project(): pl.pallas_call(functools.partial(proj_body, streams, first, last, n_tok),...  16.1 us
    pallas_call x4, Pallas kernels, encode(): pl.pallas_call(functools.partial(enc_body, streams, first, last), grid_sp...  14.6 us
    ppermute x3, waiting for transfers between devices, ring_program(): lax.ppermute(attr, 'feat', [(a, a ^ reach) for a in range(n_feat)])  13.6 us
    ppermute x6, waiting for transfers between devices, block(): return lax.ppermute(mine, 'tok', [(a, a ^ s) for a in range(n_tok)])  11.6 us
    pallas_call x4, Pallas kernels, decode(): pl.pallas_call(dec_body, grid_spec=pltpu.PrefetchScalarGridSpec(num_scala...  9.28 us
    ppermute x6, starting transfers between devices, block(): return lax.ppermute(mine, 'tok', [(a, a ^ s) for a in range(n_tok)])  8.13 us
  transfers between devices with their start and end apart: 44, of which 19 were waited for; matrix products, arithmetic and copies ran while one was open for 4% of the time, Pallas kernels for 16%

profile of v1, /device:TPU:0, one launch (start us, length us, event | category | flops | bytes accessed | tf_op | source)
XLA Modules:
  0.0 213.1 jit_solution(9563102437907789082)
XLA Ops:
  1.8 3.0 %collective-permute-start.10 = (bf16[256,256]{1,0:T(8,128)(2,1)S(1)}, bf16[256,256]{1,0:T(8,128)(2,1)S(1)}, u32[]{:S(2)}, u32[]{:S(2)}) collective-permute-start(bf16[256,256]{1,0:T(8,128)(2,1)S(1)} %get-tuple-element.59), channel_id=1, source_target_pairs={{0,16},{8,24},{16,0},{24,8},{1,17},{9,25},{17,1},{25,9},{2,18},{10... | collective-permute-start | bytes 393224 | tf_op jit(solution)/shard_map/ppermute | solution.py:290
  6.4 4.0 %collective-permute-done.10 = bf16[256,256]{1,0:T(8,128)(2,1)S(1)} collective-permute-done((bf16[256,256]{1,0:T(8,128)(2,1)S(1)}, bf16[256,256]{1,0:T(8,128)(2,1)S(1)}, u32[]{:S(2)}, u32[]{:S(2)}) %collective-permute-start.10) | collective-permute-done | bytes 131104 | tf_op jit(solution)/shard_map/ppermute | solution.py:290
  15.5 7.8 %collective-permute-done.12.refs_1_ = bf16[2,256,256]{2,1,0:T(8,128)(2,1)S(1)} collective-permute-done((bf16[2,256,256]{2,1,0:T(8,128)(2,1)S(1)}, bf16[2,256,256]{2,1,0:T(8,128)(2,1)S(1)}, u32[]{:S(2)}, u32[]{:S(2)}) %collective-permute-start.12) | collective-permute-done | bytes 262176 | tf_op jit(solution)/shard_map/ppermute | solution.py:305
  23.3 5.6 %collective-permute-done.2.refs_0_ = bf16[2,256,256]{2,1,0:T(8,128)(2,1)S(1)} collective-permute-done((bf16[2,256,256]{2,1,0:T(8,128)(2,1)S(1)}, bf16[2,256,256]{2,1,0:T(8,128)(2,1)S(1)}, u32[]{:S(2)}, u32[]{:S(2)}) %collective-permute-start.2) | collective-permute-done | bytes 262176 | tf_op jit(solution)/shard_map/ppermute | solution.py:305
  30.5 2.9 %collective-permute-done.13.refs_1_ = bf16[2,256,256]{2,1,0:T(8,128)(2,1)S(1)} collective-permute-done((bf16[2,256,256]{2,1,0:T(8,128)(2,1)S(1)}, bf16[2,256,256]{2,1,0:T(8,128)(2,1)S(1)}, u32[]{:S(2)}, u32[]{:S(2)}) %collective-permute-start.13) | collective-permute-done | bytes 262176 | tf_op jit(solution)/shard_map/ppermute | solution.py:305
  33.4 5.1 %collective-permute-done.3.refs_0_ = bf16[2,256,256]{2,1,0:T(8,128)(2,1)} collective-permute-done((bf16[2,256,256]{2,1,0:T(8,128)(2,1)S(1)}, bf16[2,256,256]{2,1,0:T(8,128)(2,1)}, u32[]{:S(2)}, u32[]{:S(2)}) %collective-permute-start.3) | collective-permute-done | bytes 262176 | tf_op jit(solution)/shard_map/ppermute | solution.py:305
  41.8 2.7 %collective-permute-done.14.refs_1_ = bf16[2,256,256]{2,1,0:T(8,128)(2,1)} collective-permute-done((bf16[2,256,256]{2,1,0:T(8,128)(2,1)S(1)}, bf16[2,256,256]{2,1,0:T(8,128)(2,1)}, u32[]{:S(2)}, u32[]{:S(2)}) %collective-permute-start.14) | collective-permute-done | bytes 262176 | tf_op jit(solution)/shard_map/ppermute | solution.py:305
  44.6 3.8 %collective-permute-done.4.refs_0_ = bf16[2,256,256]{2,1,0:T(8,128)(2,1)} collective-permute-done((bf16[2,256,256]{2,1,0:T(8,128)(2,1)}, bf16[2,256,256]{2,1,0:T(8,128)(2,1)}, u32[]{:S(2)}, u32[]{:S(2)}) %collective-permute-start.4) | collective-permute-done | bytes 262176 | tf_op jit(solution)/shard_map/ppermute | solution.py:305
  49.0 4.0 %copy-done.3 = bf16[8192,640]{1,0:T(8,128)(2,1)S(1)} copy-done((bf16[8192,640]{1,0:T(8,128)(2,1)S(1)}, bf16[8192,640]{1,0:T(8,128)(2,1)}, u32[]{:S(2)}) %copy-start.3) | copy-done | bytes 10485784
  54.6 2.9 %encode.4 = (f32[256,640]{1,0:T(8,128)S(1)}, bf16[8,256,256]{2,1,0:T(8,128)(2,1)S(1)}) custom-call(s32[4]{0:T(128)S(1)} %copy-done.50, bf16[2,256,256]{2,1,0:T(8,128)(2,1)S(1)} %pad_maximum_fusion.1.refs_0_, bf16[2,256,256]{2,1,0:T(8,128)(2,1)S(1)} %pad_maximum_fusion.3.refs_1_, bf16[2,256,256]{2,1,0:T(8,128)(2,1)S(1)} %copy-done.42, ...), custom_call_target="tpu_custom_call" | custom-call | flops 671088640 | bytes 3670016 | tf_op jit(solution)/shard_map/encode/pallas_call | solution.py:83
  63.7 3.0 %encode.5 = (f32[256,640]{1,0:T(8,128)S(1)}, bf16[8,256,256]{2,1,0:T(8,128)(2,1)S(1)}) custom-call(s32[4]{0:T(128)S(1)} %copy-done.48, bf16[2,256,256]{2,1,0:T(8,128)(2,1)S(1)} %collective-permute-done.2.refs_0_, bf16[2,256,256]{2,1,0:T(8,128)(2,1)S(1)} %collective-permute-done.12.refs_1_, ...), custom_call_target="tpu_custom_call", output_to_operand_aliasing={{1}: (9, {})} | custom-call | flops 671088640 | bytes 3670016 | tf_op jit(solution)/shard_map/encode/pallas_call | solution.py:83
  69.5 4.3 %encode.6 = (f32[256,640]{1,0:T(8,128)S(1)}, bf16[8,256,256]{2,1,0:T(8,128)(2,1)S(1)}) custom-call(s32[4]{0:T(128)S(1)} %copy-done.46, bf16[2,256,256]{2,1,0:T(8,128)(2,1)} %collective-permute-done.3.refs_0_, bf16[2,256,256]{2,1,0:T(8,128)(2,1)S(1)} %collective-permute-done.13.refs_1_, ...), custom_call_target="tpu_custom_call", output_to_operand_aliasing={{1}: (9, {})} | custom-call | flops 671088640 | bytes 3670016 | tf_op jit(solution)/shard_map/encode/pallas_call | solution.py:83
  75.8 4.4 %encode.7 = (bf16[256,640]{1,0:T(8,128)(2,1)S(1)}, bf16[8,256,256]{2,1,0:T(8,128)(2,1)S(1)}) custom-call(s32[4]{0:T(128)S(1)} %get-tuple-element.69.table, bf16[2,256,256]{2,1,0:T(8,128)(2,1)} %collective-permute-done.4.refs_0_, bf16[2,256,256]{2,1,0:T(8,128)(2,1)} %collective-permute-done.14.refs_1_, ...), custom_call_target="tpu_custom_call", output_to_operand_aliasing={{1}: (9, {})} | custom-call | flops 671088640 | bytes 3670016 | tf_op jit(solution)/shard_map/encode/pallas_call | solution.py:83
  87.3 4.4 %collective-permute-done.8 = bf16[256,256]{1,0:T(8,128)(2,1)S(1)} collective-permute-done((bf16[256,256]{1,0:T(8,128)(2,1)S(1)}, bf16[256,256]{1,0:T(8,128)(2,1)S(1)}, u32[]{:S(2)}, u32[]{:S(2)}) %collective-permute-start.8) | collective-permute-done | bytes 131104 | tf_op jit(solution)/shard_map/ppermute | solution.py:290
  93.9 2.7 %decode.6 = (bf16[256,1024]{1,0:T(8,128)(2,1)}, bf16[256,1024]{1,0:T(8,128)(2,1)S(1)}) custom-call(s32[2]{0:T(128)S(1)} %copy-done.52, bf16[256,640]{1,0:T(8,128)(2,1)S(1)} %get-tuple-element.38.refs_8_.acts_ref, bf16[640,8192]{1,0:T(8,128)(2,1)S(1)} %bitcast.37), custom_call_target="tpu_custom_call" | custom-call | flops 671088640 | bytes 3670016 | tf_op jit(solution)/shard_map/decode/pallas_call | solution.py:198
  99.4 5.1 %collective-permute-done.15.refs_1_ = bf16[2,256,256]{2,1,0:T(8,128)(2,1)S(1)} collective-permute-done((bf16[2,256,256]{2,1,0:T(8,128)(2,1)S(1)}, bf16[2,256,256]{2,1,0:T(8,128)(2,1)S(1)}, u32[]{:S(2)}, u32[]{:S(2)}) %collective-permute-start.15) | collective-permute-done | bytes 262176 | tf_op jit(solution)/shard_map/ppermute | solution.py:305
  104.4 5.6 %collective-permute-done.5.refs_0_ = bf16[2,256,256]{2,1,0:T(8,128)(2,1)S(1)} collective-permute-done((bf16[2,256,256]{2,1,0:T(8,128)(2,1)S(1)}, bf16[2,256,256]{2,1,0:T(8,128)(2,1)S(1)}, u32[]{:S(2)}, u32[]{:S(2)}) %collective-permute-start.5) | collective-permute-done | bytes 262176 | tf_op jit(solution)/shard_map/ppermute | solution.py:305
  110.1 4.0 %copy-done = bf16[640,8192]{1,0:T(8,128)(2,1)S(1)} copy-done((bf16[640,8192]{1,0:T(8,128)(2,1)S(1)}, bf16[640,8192]{1,0:T(8,128)(2,1)}, u32[]{:S(2)}) %copy-start) | copy-done | bytes 10485784
  114.1 2.7 %decode.5 = (bf16[256,1024]{1,0:T(8,128)(2,1)}, bf16[256,1024]{1,0:T(8,128)(2,1)S(1)}) custom-call(s32[2]{0:T(128)S(1)} %get-tuple-element.71.table, bf16[256,640]{1,0:T(8,128)(2,1)S(1)} %get-tuple-element.38.refs_8_.acts_ref, bf16[640,8192]{1,0:T(8,128)(2,1)S(1)} %copy-done), custom_call_target="tpu_custom_call" | custom-call | flops 671088640 | bytes 3670016 | tf_op jit(solution)/shard_map/decode/pallas_call | solution.py:198
  117.0 9.9 %collective-permute-done.16.refs_1_ = bf16[2,256,256]{2,1,0:T(8,128)(2,1)S(1)} collective-permute-done((bf16[2,256,256]{2,1,0:T(8,128)(2,1)S(1)}, bf16[2,256,256]{2,1,0:T(8,128)(2,1)S(1)}, u32[]{:S(2)}, u32[]{:S(2)}) %collective-permute-start.16) | collective-permute-done | bytes 262176 | tf_op jit(solution)/shard_map/ppermute | solution.py:305
  126.9 4.5 %collective-permute-done.6.refs_0_ = bf16[2,256,256]{2,1,0:T(8,128)(2,1)} collective-permute-done((bf16[2,256,256]{2,1,0:T(8,128)(2,1)S(1)}, bf16[2,256,256]{2,1,0:T(8,128)(2,1)}, u32[]{:S(2)}, u32[]{:S(2)}) %collective-permute-start.6) | collective-permute-done | bytes 262176 | tf_op jit(solution)/shard_map/ppermute | solution.py:305
  136.6 5.8 %collective-permute-done.17.refs_1_ = bf16[2,256,256]{2,1,0:T(8,128)(2,1)} collective-permute-done((bf16[2,256,256]{2,1,0:T(8,128)(2,1)S(1)}, bf16[2,256,256]{2,1,0:T(8,128)(2,1)}, u32[]{:S(2)}, u32[]{:S(2)}) %collective-permute-start.17) | collective-permute-done | bytes 262176 | tf_op jit(solution)/shard_map/ppermute | solution.py:305
  142.4 5.6 %collective-permute-done.7.refs_0_ = bf16[2,256,256]{2,1,0:T(8,128)(2,1)} collective-permute-done((bf16[2,256,256]{2,1,0:T(8,128)(2,1)}, bf16[2,256,256]{2,1,0:T(8,128)(2,1)}, u32[]{:S(2)}, u32[]{:S(2)}) %collective-permute-start.7) | collective-permute-done | bytes 262176 | tf_op jit(solution)/shard_map/ppermute | solution.py:305
  148.0 4.0 %copy-done.1 = bf16[640,8192]{1,0:T(8,128)(2,1)S(1)} copy-done((bf16[640,8192]{1,0:T(8,128)(2,1)S(1)}, bf16[640,8192]{1,0:T(8,128)(2,1)}, u32[]{:S(2)}) %copy-start.1) | copy-done | bytes 10485784
  155.6 4.0 %copy-done.2 = bf16[640,8192]{1,0:T(8,128)(2,1)S(1)} copy-done((bf16[640,8192]{1,0:T(8,128)(2,1)S(1)}, bf16[640,8192]{1,0:T(8,128)(2,1)}, u32[]{:S(2)}) %copy-start.2) | copy-done | bytes 10485784
  160.5 3.2 %project.4 = (f32[256,640]{1,0:T(8,128)S(1)}, bf16[8,256,256]{2,1,0:T(8,128)(2,1)S(1)}) custom-call(s32[4]{0:T(128)S(1)} %copy-done.51, bf16[2,256,256]{2,1,0:T(8,128)(2,1)S(1)} %copy-done.20, bf16[2,256,256]{2,1,0:T(8,128)(2,1)S(1)} %copy-done.18, bf16[2,256,256]{2,1,0:T(8,128)(2,1)S(1)} %copy-done.32, ...), custom_call_target="tpu_custom_call" | custom-call | flops 671088640 | bytes 3670016 | tf_op jit(solution)/shard_map/project/pallas_call | solution.py:172
  170.7 3.4 %project.5 = (f32[256,640]{1,0:T(8,128)S(1)}, bf16[8,256,256]{2,1,0:T(8,128)(2,1)S(1)}) custom-call(s32[4]{0:T(128)S(1)} %copy-done.49, bf16[2,256,256]{2,1,0:T(8,128)(2,1)S(1)} %copy-done.28, bf16[2,256,256]{2,1,0:T(8,128)(2,1)S(1)} %collective-permute-done.15.refs_1_, bf16[2,256,256]{2,1,0:T(8,128)(2,1)S(1)} %copy-done.38, ...), custom_call_target="tpu_custom_call", output_to_operand_aliasing={{1}: (11, {})} | custom-call | flops 671088640 | bytes 3670016 | tf_op jit(solution)/shard_map/project/pallas_call | solution.py:172
  176.8 4.2 %project.6 = (f32[256,640]{1,0:T(8,128)S(1)}, bf16[8,256,256]{2,1,0:T(8,128)(2,1)S(1)}) custom-call(s32[4]{0:T(128)S(1)} %copy-done.47, bf16[2,256,256]{2,1,0:T(8,128)(2,1)} %collective-permute-done.6.refs_0_, bf16[2,256,256]{2,1,0:T(8,128)(2,1)S(1)} %copy-done.30, ...), custom_call_target="tpu_custom_call", output_to_operand_aliasing={{1}: (11, {})} | custom-call | flops 671088640 | bytes 3670016 | tf_op jit(solution)/shard_map/project/pallas_call | solution.py:172
  181.0 5.3 %project.7 = (f32[256,640]{1,0:T(8,128)}, bf16[8,256,256]{2,1,0:T(8,128)(2,1)S(1)}, f32[256,1]{1,0:T(8,128)S(1)}) custom-call(s32[4]{0:T(128)S(1)} %get-tuple-element.69.table, bf16[2,256,256]{2,1,0:T(8,128)(2,1)} %collective-permute-done.7.refs_0_, bf16[2,256,256]{2,1,0:T(8,128)(2,1)} %collective-permute-done.17.refs_1_, ...), custom_call_target="tpu_custom_call", output_to_operand_aliasing={{1}: (11, {})} | custom-call | flops 671088640 | bytes 3670016 | tf_op jit(solution)/shard_map/project/pallas_call | solution.py:172
  188.7 12.0 %collective-permute-done.42 = f32[2,128]{1,0:T(2,128)S(1)} collective-permute-done((f32[2,128]{1,0:T(2,128)S(1)}, f32[2,128]{1,0:T(2,128)S(1)}, u32[]{:S(2)}, u32[]{:S(2)}) %collective-permute-start.42) | collective-permute-done | bytes 1056 | tf_op jit(solution)/shard_map/ppermute | solution.py:361
  200.8 4.5 %collective-permute-start.43 = (f32[2,128]{1,0:T(2,128)S(1)}, f32[2,128]{1,0:T(2,128)S(1)}, u32[]{:S(2)}, u32[]{:S(2)}) collective-permute-start(f32[2,128]{1,0:T(2,128)S(1)} %fusion), channel_id=1, source_target_pairs={{0,4},{1,5},{2,6},{3,7},{4,0},{5,1},{6,2},{7,3},{8,12},{9,13},{10,... | collective-permute-start | bytes 3080 | tf_op jit(solution)/shard_map/ppermute | solution.py:361
  209.7 3.4 %final_error.1 = f32[256,1024]{1,0:T(8,128)} custom-call(s32[1]{0:T(128)} %bitcast.19.table, bf16[8,256,256]{2,1,0:T(8,128)(2,1)S(1)} %copy-done.12, bf16[256,1024]{1,0:T(8,128)(2,1)S(1)} %copy-done.26, bf16[256,1024]{1,0:T(8,128)(2,1)} %collective-permute-done.34.far_ref, bf16[256,1024]{1,0:T(8,128)(2,1)S(1)} %collective-permute-done.40.come_ref, ...), custom_call_target="tpu_custom_call" | custom-call | tf_op jit(solution)/shard_map/final_error/pallas_call | solution.py:254
  (221 shorter events, 64.0 us)
Async XLA Ops:
  12.2 11.1 %collective-permute-start.12 = (bf16[2,256,256]{2,1,0:T(8,128)(2,1)S(1)}, bf16[2,256,256]{2,1,0:T(8,128)(2,1)S(1)}, u32[]{:S(2)}, u32[]{:S(2)}) collective-permute-start(bf16[2,256,256]{2,1,0:T(8,128)(2,1)S(1)} %pad_maximum_fusion.3.refs_1_), channel_id=1, source_target_pairs={{0,2},{1,3},{2,4},{3,5},{4,6},{5,7},{6,0},{7,1},{8,10},{9,11},{10,... | collective-permute-start | bytes 786440 | tf_op jit(solution)/shard_map/ppermute | solution.py:305
  13.8 15.1 %collective-permute-start.2 = (bf16[2,256,256]{2,1,0:T(8,128)(2,1)S(1)}, bf16[2,256,256]{2,1,0:T(8,128)(2,1)S(1)}, u32[]{:S(2)}, u32[]{:S(2)}) collective-permute-start(bf16[2,256,256]{2,1,0:T(8,128)(2,1)S(1)} %pad_maximum_fusion.1.refs_0_), channel_id=1, source_target_pairs={{0,2},{1,3},{2,4},{3,5},{4,6},{5,7},{6,0},{7,1},{8,10},{9,11},{10,... | collective-permute-start | bytes 786440 | tf_op jit(solution)/shard_map/ppermute | solution.py:305
  23.3 10.1 %collective-permute-start.13 = (bf16[2,256,256]{2,1,0:T(8,128)(2,1)S(1)}, bf16[2,256,256]{2,1,0:T(8,128)(2,1)S(1)}, u32[]{:S(2)}, u32[]{:S(2)}) collective-permute-start(bf16[2,256,256]{2,1,0:T(8,128)(2,1)S(1)} %collective-permute-done.12.refs_1_), channel_id=1, source_target_pairs={{0,2},{1,3},{2,4},{3,5},{4,6},{5,7},{6,0},{7,1},{8,10},{9,11},{10,... | collective-permute-start | bytes 786440 | tf_op jit(solution)/shard_map/ppermute | solution.py:305
  28.9 9.7 %collective-permute-start.3 = (bf16[2,256,256]{2,1,0:T(8,128)(2,1)S(1)}, bf16[2,256,256]{2,1,0:T(8,128)(2,1)}, u32[]{:S(2)}, u32[]{:S(2)}) collective-permute-start(bf16[2,256,256]{2,1,0:T(8,128)(2,1)S(1)} %collective-permute-done.2.refs_0_), channel_id=1, source_target_pairs={{0,2},{1,3},{2,4},{3,5},{4,6},{5,7},{6,0},{7,1},{8,10},{9,11},{10,... | collective-permute-start | bytes 786440 | tf_op jit(solution)/shard_map/ppermute | solution.py:305
  29.8 9.4 %collective-permute-start.27 = (bf16[2,256,256]{2,1,0:T(8,128)(2,1)S(1)}, bf16[2,256,256]{2,1,0:T(8,128)(2,1)S(1)}, u32[]{:S(2)}, u32[]{:S(2)}) collective-permute-start(bf16[2,256,256]{2,1,0:T(8,128)(2,1)S(1)} %pad_maximum_fusion.3.refs_1_), channel_id=1, source_target_pairs={{0,1},{1,0},{2,3},{3,2},{4,5},{5,4},{6,7},{7,6},{8,9},{9,8},{10,11... | collective-permute-start | bytes 786440 | tf_op jit(solution)/shard_map/ppermute | solution.py:308
  30.4 10.0 %collective-permute-start.25 = (bf16[2,256,256]{2,1,0:T(8,128)(2,1)S(1)}, bf16[2,256,256]{2,1,0:T(8,128)(2,1)S(1)}, u32[]{:S(2)}, u32[]{:S(2)}) collective-permute-start(bf16[2,256,256]{2,1,0:T(8,128)(2,1)S(1)} %collective-permute-done.12.refs_1_), channel_id=1, source_target_pairs={{0,1},{1,0},{2,3},{3,2},{4,5},{5,4},{6,7},{7,6},{8,9},{9,8},{10,11... | collective-permute-start | bytes 786440 | tf_op jit(solution)/shard_map/ppermute | solution.py:308
  33.4 11.1 %collective-permute-start.14 = (bf16[2,256,256]{2,1,0:T(8,128)(2,1)S(1)}, bf16[2,256,256]{2,1,0:T(8,128)(2,1)}, u32[]{:S(2)}, u32[]{:S(2)}) collective-permute-start(bf16[2,256,256]{2,1,0:T(8,128)(2,1)S(1)} %collective-permute-done.13.refs_1_), channel_id=1, source_target_pairs={{0,2},{1,3},{2,4},{3,5},{4,6},{5,7},{6,0},{7,1},{8,10},{9,11},{10,... | collective-permute-start | bytes 786440 | tf_op jit(solution)/shard_map/ppermute | solution.py:305
  38.5 9.9 %collective-permute-start.4 = (bf16[2,256,256]{2,1,0:T(8,128)(2,1)}, bf16[2,256,256]{2,1,0:T(8,128)(2,1)}, u32[]{:S(2)}, u32[]{:S(2)}) collective-permute-start(bf16[2,256,256]{2,1,0:T(8,128)(2,1)} %collective-permute-done.3.refs_0_), channel_id=1, source_target_pairs={{0,2},{1,3},{2,4},{3,5},{4,6},{5,7},{6,0},{7,1},{8,10},{9,11},{10,... | collective-permute-start | bytes 786440 | tf_op jit(solution)/shard_map/ppermute | solution.py:305
  39.2 19.3 %collective-permute-start.24 = (bf16[2,256,256]{2,1,0:T(8,128)(2,1)S(1)}, bf16[2,256,256]{2,1,0:T(8,128)(2,1)S(1)}, u32[]{:S(2)}, u32[]{:S(2)}) collective-permute-start(bf16[2,256,256]{2,1,0:T(8,128)(2,1)S(1)} %collective-permute-done.2.refs_0_), channel_id=1, source_target_pairs={{0,1},{1,0},{2,3},{3,2},{4,5},{5,4},{6,7},{7,6},{8,9},{9,8},{10,11... | collective-permute-start | bytes 786440 | tf_op jit(solution)/shard_map/ppermute | solution.py:308
  39.9 27.7 %collective-permute-start.23 = (bf16[2,256,256]{2,1,0:T(8,128)(2,1)S(1)}, bf16[2,256,256]{2,1,0:T(8,128)(2,1)}, u32[]{:S(2)}, u32[]{:S(2)}) collective-permute-start(bf16[2,256,256]{2,1,0:T(8,128)(2,1)S(1)} %collective-permute-done.13.refs_1_), channel_id=1, source_target_pairs={{0,1},{1,0},{2,3},{3,2},{4,5},{5,4},{6,7},{7,6},{8,9},{9,8},{10,11... | collective-permute-start | bytes 786440 | tf_op jit(solution)/shard_map/ppermute | solution.py:308
  40.4 27.2 %collective-permute-start.22 = (bf16[2,256,256]{2,1,0:T(8,128)(2,1)}, bf16[2,256,256]{2,1,0:T(8,128)(2,1)}, u32[]{:S(2)}, u32[]{:S(2)}) collective-permute-start(bf16[2,256,256]{2,1,0:T(8,128)(2,1)} %collective-permute-done.3.refs_0_), channel_id=1, source_target_pairs={{0,1},{1,0},{2,3},{3,2},{4,5},{5,4},{6,7},{7,6},{8,9},{9,8},{10,11... | collective-permute-start | bytes 786440 | tf_op jit(solution)/shard_map/ppermute | solution.py:308
  44.6 30.1 %collective-permute-start.21 = (bf16[2,256,256]{2,1,0:T(8,128)(2,1)}, bf16[2,256,256]{2,1,0:T(8,128)(2,1)}, u32[]{:S(2)}, u32[]{:S(2)}) collective-permute-start(bf16[2,256,256]{2,1,0:T(8,128)(2,1)} %collective-permute-done.14.refs_1_), channel_id=1, source_target_pairs={{0,1},{1,0},{2,3},{3,2},{4,5},{5,4},{6,7},{7,6},{8,9},{9,8},{10,11... | collective-permute-start | bytes 786440 | tf_op jit(solution)/shard_map/ppermute | solution.py:308
  48.4 26.3 %collective-permute-start.20 = (bf16[2,256,256]{2,1,0:T(8,128)(2,1)}, bf16[2,256,256]{2,1,0:T(8,128)(2,1)}, u32[]{:S(2)}, u32[]{:S(2)}) collective-permute-start(bf16[2,256,256]{2,1,0:T(8,128)(2,1)} %collective-permute-done.4.refs_0_), channel_id=1, source_target_pairs={{0,1},{1,0},{2,3},{3,2},{4,5},{5,4},{6,7},{7,6},{8,9},{9,8},{10,11... | collective-permute-start | bytes 786440 | tf_op jit(solution)/shard_map/ppermute | solution.py:308
  83.2 13.5 %collective-permute-start.37 = (bf16[256,1024]{1,0:T(8,128)(2,1)S(1)}, bf16[256,1024]{1,0:T(8,128)(2,1)S(1)}, u32[]{:S(2)}, u32[]{:S(2)}) collective-permute-start(bf16[256,1024]{1,0:T(8,128)(2,1)S(1)} %get-tuple-element.54), channel_id=1, source_target_pairs={{0,1},{1,0},{2,3},{3,2},{4,5},{5,4},{6,7},{7,6},{8,9},{9,8},{10,11... | collective-permute-start | bytes 1572872 | tf_op jit(solution)/shard_map/ppermute | solution.py:343
  93.4 11.1 %collective-permute-start.15 = (bf16[2,256,256]{2,1,0:T(8,128)(2,1)S(1)}, bf16[2,256,256]{2,1,0:T(8,128)(2,1)S(1)}, u32[]{:S(2)}, u32[]{:S(2)}) collective-permute-start(bf16[2,256,256]{2,1,0:T(8,128)(2,1)S(1)} %pad_maximum_fusion.2.refs_1_), channel_id=1, source_target_pairs={{0,2},{1,3},{2,4},{3,5},{4,6},{5,7},{6,0},{7,1},{8,10},{9,11},{10,... | collective-permute-start | bytes 786440 | tf_op jit(solution)/shard_map/ppermute | solution.py:305
  93.4 16.6 %collective-permute-start.5 = (bf16[2,256,256]{2,1,0:T(8,128)(2,1)S(1)}, bf16[2,256,256]{2,1,0:T(8,128)(2,1)S(1)}, u32[]{:S(2)}, u32[]{:S(2)}) collective-permute-start(bf16[2,256,256]{2,1,0:T(8,128)(2,1)S(1)} %pad_maximum_fusion.refs_0_), channel_id=1, source_target_pairs={{0,2},{1,3},{2,4},{3,5},{4,6},{5,7},{6,0},{7,1},{8,10},{9,11},{10,... | collective-permute-start | bytes 786440 | tf_op jit(solution)/shard_map/ppermute | solution.py:305
  96.6 34.7 %collective-permute-start.36 = (bf16[256,1024]{1,0:T(8,128)(2,1)}, bf16[256,1024]{1,0:T(8,128)(2,1)}, u32[]{:S(2)}, u32[]{:S(2)}) collective-permute-start(bf16[256,1024]{1,0:T(8,128)(2,1)} %get-tuple-element.52), channel_id=1, source_target_pairs={{0,1},{1,0},{2,3},{3,2},{4,5},{5,4},{6,7},{7,6},{8,9},{9,8},{10,11... | collective-permute-start | bytes 1572872 | tf_op jit(solution)/shard_map/ppermute | solution.py:343
  97.6 33.8 %collective-permute-start.38 = (bf16[256,1024]{1,0:T(8,128)(2,1)}, bf16[256,1024]{1,0:T(8,128)(2,1)}, u32[]{:S(2)}, u32[]{:S(2)}) collective-permute-start(bf16[256,1024]{1,0:T(8,128)(2,1)} %add_convert_fusion.2), channel_id=1, source_target_pairs={{0,2},{1,3},{2,4},{3,5},{4,6},{5,7},{6,0},{7,1},{8,10},{9,11},{10,... | collective-permute-start | bytes 1572872 | tf_op jit(solution)/shard_map/ppermute | solution.py:349
  99.2 17.7 %collective-permute-start.32 = (bf16[2,256,256]{2,1,0:T(8,128)(2,1)S(1)}, bf16[2,256,256]{2,1,0:T(8,128)(2,1)S(1)}, u32[]{:S(2)}, u32[]{:S(2)}) collective-permute-start(bf16[2,256,256]{2,1,0:T(8,128)(2,1)S(1)} %pad_maximum_fusion.refs_0_), channel_id=1, source_target_pairs={{0,1},{1,0},{2,3},{3,2},{4,5},{5,4},{6,7},{7,6},{8,9},{9,8},{10,11... | collective-permute-start | bytes 786440 | tf_op jit(solution)/shard_map/ppermute | solution.py:308
  104.4 22.5 %collective-permute-start.16 = (bf16[2,256,256]{2,1,0:T(8,128)(2,1)S(1)}, bf16[2,256,256]{2,1,0:T(8,128)(2,1)S(1)}, u32[]{:S(2)}, u32[]{:S(2)}) collective-permute-start(bf16[2,256,256]{2,1,0:T(8,128)(2,1)S(1)} %collective-permute-done.15.refs_1_), channel_id=1, source_target_pairs={{0,2},{1,3},{2,4},{3,5},{4,6},{5,7},{6,0},{7,1},{8,10},{9,11},{10,... | collective-permute-start | bytes 786440 | tf_op jit(solution)/shard_map/ppermute | solution.py:305
  110.1 21.3 %collective-permute-start.6 = (bf16[2,256,256]{2,1,0:T(8,128)(2,1)S(1)}, bf16[2,256,256]{2,1,0:T(8,128)(2,1)}, u32[]{:S(2)}, u32[]{:S(2)}) collective-permute-start(bf16[2,256,256]{2,1,0:T(8,128)(2,1)S(1)} %collective-permute-done.5.refs_0_), channel_id=1, source_target_pairs={{0,2},{1,3},{2,4},{3,5},{4,6},{5,7},{6,0},{7,1},{8,10},{9,11},{10,... | collective-permute-start | bytes 786440 | tf_op jit(solution)/shard_map/ppermute | solution.py:305
  116.9 16.9 %collective-permute-start.31 = (bf16[2,256,256]{2,1,0:T(8,128)(2,1)S(1)}, bf16[2,256,256]{2,1,0:T(8,128)(2,1)S(1)}, u32[]{:S(2)}, u32[]{:S(2)}) collective-permute-start(bf16[2,256,256]{2,1,0:T(8,128)(2,1)S(1)} %collective-permute-done.15.refs_1_), channel_id=1, source_target_pairs={{0,1},{1,0},{2,3},{3,2},{4,5},{5,4},{6,7},{7,6},{8,9},{9,8},{10,11... | collective-permute-start | bytes 786440 | tf_op jit(solution)/shard_map/ppermute | solution.py:308
  131.4 11.0 %collective-permute-start.17 = (bf16[2,256,256]{2,1,0:T(8,128)(2,1)S(1)}, bf16[2,256,256]{2,1,0:T(8,128)(2,1)}, u32[]{:S(2)}, u32[]{:S(2)}) collective-permute-start(bf16[2,256,256]{2,1,0:T(8,128)(2,1)S(1)} %collective-permute-done.16.refs_1_), channel_id=1, source_target_pairs={{0,2},{1,3},{2,4},{3,5},{4,6},{5,7},{6,0},{7,1},{8,10},{9,11},{10,... | collective-permute-start | bytes 786440 | tf_op jit(solution)/shard_map/ppermute | solution.py:305
  131.4 16.6 %collective-permute-start.7 = (bf16[2,256,256]{2,1,0:T(8,128)(2,1)}, bf16[2,256,256]{2,1,0:T(8,128)(2,1)}, u32[]{:S(2)}, u32[]{:S(2)}) collective-permute-start(bf16[2,256,256]{2,1,0:T(8,128)(2,1)} %collective-permute-done.6.refs_0_), channel_id=1, source_target_pairs={{0,2},{1,3},{2,4},{3,5},{4,6},{5,7},{6,0},{7,1},{8,10},{9,11},{10,... | collective-permute-start | bytes 786440 | tf_op jit(solution)/shard_map/ppermute | solution.py:305
  134.5 52.6 %collective-permute-start.35 = (bf16[256,1024]{1,0:T(8,128)(2,1)}, bf16[256,1024]{1,0:T(8,128)(2,1)}, u32[]{:S(2)}, u32[]{:S(2)}) collective-permute-start(bf16[256,1024]{1,0:T(8,128)(2,1)} %get-tuple-element.50), channel_id=1, source_target_pairs={{0,1},{1,0},{2,3},{3,2},{4,5},{5,4},{6,7},{7,6},{8,9},{9,8},{10,11... | collective-permute-start | bytes 1572872 | tf_op jit(solution)/shard_map/ppermute | solution.py:343
  135.7 51.4 %collective-permute-start.39 = (bf16[256,1024]{1,0:T(8,128)(2,1)}, bf16[256,1024]{1,0:T(8,128)(2,1)}, u32[]{:S(2)}, u32[]{:S(2)}) collective-permute-start(bf16[256,1024]{1,0:T(8,128)(2,1)} %add_convert_fusion.1), channel_id=1, source_target_pairs={{0,2},{1,3},{2,4},{3,5},{4,6},{5,7},{6,0},{7,1},{8,10},{9,11},{10,... | collective-permute-start | bytes 1572872 | tf_op jit(solution)/shard_map/ppermute | solution.py:349
  136.4 38.7 %collective-permute-start.28 = (bf16[2,256,256]{2,1,0:T(8,128)(2,1)}, bf16[2,256,256]{2,1,0:T(8,128)(2,1)}, u32[]{:S(2)}, u32[]{:S(2)}) collective-permute-start(bf16[2,256,256]{2,1,0:T(8,128)(2,1)} %collective-permute-done.6.refs_0_), channel_id=1, source_target_pairs={{0,1},{1,0},{2,3},{3,2},{4,5},{5,4},{6,7},{7,6},{8,9},{9,8},{10,11... | collective-permute-start | bytes 786440 | tf_op jit(solution)/shard_map/ppermute | solution.py:308
  142.4 38.6 %collective-permute-start.19 = (bf16[2,256,256]{2,1,0:T(8,128)(2,1)}, bf16[2,256,256]{2,1,0:T(8,128)(2,1)}, u32[]{:S(2)}, u32[]{:S(2)}) collective-permute-start(bf16[2,256,256]{2,1,0:T(8,128)(2,1)} %collective-permute-done.17.refs_1_), channel_id=1, source_target_pairs={{0,1},{1,0},{2,3},{3,2},{4,5},{5,4},{6,7},{7,6},{8,9},{9,8},{10,11... | collective-permute-start | bytes 786440 | tf_op jit(solution)/shard_map/ppermute | solution.py:308
  148.0 33.0 %collective-permute-start.18 = (bf16[2,256,256]{2,1,0:T(8,128)(2,1)}, bf16[2,256,256]{2,1,0:T(8,128)(2,1)}, u32[]{:S(2)}, u32[]{:S(2)}) collective-permute-start(bf16[2,256,256]{2,1,0:T(8,128)(2,1)} %collective-permute-done.7.refs_0_), channel_id=1, source_target_pairs={{0,1},{1,0},{2,3},{3,2},{4,5},{5,4},{6,7},{7,6},{8,9},{9,8},{10,11... | collective-permute-start | bytes 786440 | tf_op jit(solution)/shard_map/ppermute | solution.py:308
  175.1 32.4 %collective-permute-start.34 = (bf16[256,1024]{1,0:T(8,128)(2,1)S(1)}, bf16[256,1024]{1,0:T(8,128)(2,1)}, u32[]{:S(2)}, u32[]{:S(2)}) collective-permute-start(bf16[256,1024]{1,0:T(8,128)(2,1)S(1)} %copy-done.55), channel_id=1, source_target_pairs={{0,1},{1,0},{2,3},{3,2},{4,5},{5,4},{6,7},{7,6},{8,9},{9,8},{10,11... | collective-permute-start | bytes 1572872 | tf_op jit(solution)/shard_map/ppermute | solution.py:343
  188.6 18.9 %collective-permute-start.40 = (bf16[256,1024]{1,0:T(8,128)(2,1)S(1)}, bf16[256,1024]{1,0:T(8,128)(2,1)S(1)}, u32[]{:S(2)}, u32[]{:S(2)}) collective-permute-start(bf16[256,1024]{1,0:T(8,128)(2,1)S(1)} %add_convert_fusion), channel_id=1, source_target_pairs={{0,2},{1,3},{2,4},{3,5},{4,6},{5,7},{6,0},{7,1},{8,10},{9,11},{10,... | collective-permute-start | bytes 1572872 | tf_op jit(solution)/shard_map/ppermute | solution.py:349
  188.7 12.1 %collective-permute-start.42 = (f32[2,128]{1,0:T(2,128)S(1)}, f32[2,128]{1,0:T(2,128)S(1)}, u32[]{:S(2)}, u32[]{:S(2)}) collective-permute-start(f32[2,128]{1,0:T(2,128)S(1)} %bitcast_add_fusion), channel_id=1, source_target_pairs={{0,2},{1,3},{2,0},{3,1},{4,6},{5,7},{6,4},{7,5},{8,10},{9,11},{10,... | collective-permute-start | bytes 3080 | tf_op jit(solution)/shard_map/ppermute | solution.py:361
  (75 other events, 466.2 us)

commit v2 on v0

v2 whole, which is shorter than its diff:
```python
import functools

import jax
import jax.numpy as jnp
from jax import lax
from jax.experimental import pallas as pl
from jax.experimental.pallas import tpu as pltpu
from jax.sharding import PartitionSpec as P

BLOCK = 128
TILE = 128
X_STREAMS = ((0,), (1, 2, 3))
G_STREAMS = ((0, 1, 2, 3),)
PARAMS = pltpu.CompilerParams(vmem_limit_bytes=56 << 20)
F32 = jnp.float32
BF16 = jnp.bfloat16
LIGHT = pl.CostEstimate(flops=1, bytes_accessed=1, transcendentals=0)


def whole(shape):
    zeros = (0,) * len(shape)
    return pl.BlockSpec(shape, lambda *_: zeros)


def after(value, *others):
    return lax.optimization_barrier((value, others))[0]


def pieces(refs, streams):
    return [refs[a].at[b] for a, stream in enumerate(streams) for b in range(len(stream))]


def enc_body(streams, count, first, last, table, *refs):
    size = len(streams)
    slots = [pieces(refs[q * size:(q + 1) * size], streams) for q in range(count)]
    refs = refs[count * size:]
    n_tok = len(slots[0])
    w_refs = refs[:n_tok]
    bias_ref, hit_ref = refs[n_tok:n_tok + 2]
    refs = refs[n_tok + 2:]
    carry_ref = None
    if not first:
        carry_ref, refs = refs[0], refs[2:]
    out_ref, own_ref = refs[:2]
    total_ref = refs[2] if last else out_ref
    step = pl.program_id(0)
    for q, blocks in enumerate(slots):

        @pl.when(step == q)
        def _():
            total = None
            for x, w_ref in zip(blocks, w_refs):
                term = jnp.dot(x[...], w_ref[0, 0], preferred_element_type=F32)
                total = term if total is None else total + term
            if q > 0:
                total = total + total_ref[...]
            elif not first:
                total = total + carry_ref[...]
            if last and q == count - 1:
                pre = total + bias_ref[...]
                tiles = hit_ref.shape[0]
                shaped = jnp.maximum(pre, 0.0).reshape(tiles, TILE, -1) * hit_ref[...][:, None, :]
                out_ref[...] = shaped.reshape(pre.shape).astype(BF16)
            else:
                total_ref[...] = total
            for s, x in enumerate(blocks):

                @pl.when(table[1] == s)
                def _():
                    own_ref[0] = x[...]


def encode(table, slots, w4, bias, hit, carry, streams, last):
    n_tok, n_feat, width, feats = w4.shape
    rows = slots[0][0].shape[1]
    first = carry is None
    flat = [a for slot in slots for a in slot]
    specs = [whole(a.shape) for a in flat]
    for s in range(n_tok):
        specs.append(
            pl.BlockSpec((1, 1, width, feats), lambda q, t, s=s: (t[0] ^ s, t[2 + q], 0, 0))
        )
    specs += [whole(bias.shape), whole(hit.shape)]
    args = [*flat] + [w4] * n_tok + [bias, hit]
    aliases = {}
    if not first:
        specs += [whole(carry[0].shape), pl.BlockSpec(memory_space=pl.ANY)]
        args += carry
        aliases = {len(args): 1}
    count = len(slots)
    return pl.pallas_call(
        functools.partial(enc_body, streams, count, first, last),
        grid_spec=pltpu.PrefetchScalarGridSpec(
            num_scalar_prefetch=1,
            grid=(count,),
            in_specs=specs,
            out_specs=[
                whole((rows, feats)),
                pl.BlockSpec((1, rows, width), lambda q, t: (t[2 + q], 0, 0)),
            ],
            scratch_shapes=[pltpu.VMEM((rows, feats), F32)] if last else [],
        ),
        out_shape=[
            jax.ShapeDtypeStruct((rows, feats), BF16 if last else F32),
            jax.ShapeDtypeStruct((n_feat, rows, width), BF16),
        ],
        input_output_aliases=aliases,
        compiler_params=PARAMS,
        cost_estimate=LIGHT,
        name="encode",
    )(table, *args)


def dec_body(table, acts_ref, w_ref, *out_refs):
    for q, out_ref in enumerate(out_refs):

        @pl.when(pl.program_id(0) == q)
        def _():
            out_ref[...] = jnp.dot(
                acts_ref[...], w_ref[...], preferred_element_type=F32
            ).astype(BF16)


def decode(table, acts, w_dec, share, count):
    rows, feats = acts.shape
    outs = [jax.ShapeDtypeStruct((rows, share), BF16)] * count
    return pl.pallas_call(
        dec_body,
        grid_spec=pltpu.PrefetchScalarGridSpec(
            num_scalar_prefetch=1,
            grid=(count,),
            in_specs=[whole(acts.shape), pl.BlockSpec((feats, share), lambda q, t: (0, t[q]))],
            out_specs=[whole(out.shape) for out in outs],
        ),
        out_shape=outs,
        compiler_params=PARAMS,
        cost_estimate=LIGHT,
        name="decode",
    )(table, acts, w_dec)


def proj_body(n_tok, table, g_ref, *refs):
    w_refs, (acts_ref, x_ref, bias_ref, out_ref, sum_ref) = refs[:n_tok], refs[n_tok:]
    step, steps = pl.program_id(0), pl.num_programs(0)
    total = None
    for s, w_ref in enumerate(w_refs):
        term = lax.dot_general(
            g_ref[0, s], w_ref[...], (((1,), (1,)), ((), ())), preferred_element_type=F32
        )
        total = term if total is None else total + term

    @pl.when(step == 0)
    def _():
        out_ref[...] = total
        sum_ref[...] = jnp.zeros_like(sum_ref)

    @pl.when((step > 0) & (step < steps - 1))
    def _():
        out_ref[...] += total

    @pl.when(step // n_tok == table[2])
    def _():
        term = (x_ref[0].astype(F32) - bias_ref[...]) * g_ref[0, table[1]].astype(F32)
        sum_ref[...] += jnp.sum(term, axis=1, keepdims=True)

    @pl.when(step == steps - 1)
    def _():
        attr = acts_ref[...].astype(F32) * (out_ref[...] + total)
        out_ref[...] = attr
        sum_ref[...] -= jnp.sum(attr, axis=1, keepdims=True)


def project(table, rows_g, w_dec, acts, own_x, bias):
    n_feat, n_tok, rows, width = rows_g.shape
    feats = w_dec.shape[0]
    specs = [pl.BlockSpec((1, n_tok, rows, width), lambda q, t: (q, 0, 0, 0))]
    for s in range(n_tok):
        specs.append(pl.BlockSpec((feats, width), lambda q, t, s=s: (0, (t[0] ^ s) * n_feat + q)))
    specs += [
        whole(acts.shape),
        pl.BlockSpec((1, rows, width), lambda q, t: (t[2] * n_tok + q % n_tok, 0, 0)),
        pl.BlockSpec((1, width), lambda q, t: (0, q % n_tok)),
    ]
    return pl.pallas_call(
        functools.partial(proj_body, n_tok),
        grid_spec=pltpu.PrefetchScalarGridSpec(
            num_scalar_prefetch=1,
            grid=(n_feat,),
            in_specs=specs,
            out_specs=[whole((rows, feats)), whole((rows, 1))],
        ),
        out_shape=[
            jax.ShapeDtypeStruct((rows, feats), F32),
            jax.ShapeDtypeStruct((rows, 1), F32),
        ],
        compiler_params=PARAMS,
        cost_estimate=LIGHT,
        name="project",
    )(table, rows_g, *[w_dec] * n_tok, acts, own_x, bias)


def error_body(table, x_ref, bias_ref, *refs):
    terms, out_ref = refs[:-1], refs[-1]
    recon = bias_ref[...]
    for term in terms:
        recon = recon + term[...].astype(F32)
    width = x_ref.shape[2]
    for r in range(x_ref.shape[0]):
        cols = slice(r * width, (r + 1) * width)
        out_ref[:, cols] = x_ref[r].astype(F32) - recon[:, cols]


def final_error(table, own_x, bias, terms):
    _, rows, width = own_x.shape
    share = bias.shape[1]
    part = pl.BlockSpec((rows, share // 2), lambda r, t: (0, r))
    return pl.pallas_call(
        error_body,
        grid_spec=pltpu.PrefetchScalarGridSpec(
            num_scalar_prefetch=1,
            grid=(2,),
            in_specs=[
                pl.BlockSpec(
                    (share // width // 2, rows, width), lambda r, t: (2 * t[2] + r, 0, 0)
                ),
                pl.BlockSpec((1, share // 2), lambda r, t: (0, r)),
            ]
            + [part] * len(terms),
            out_specs=part,
        ),
        out_shape=jax.ShapeDtypeStruct((rows, share), F32),
        compiler_params=PARAMS,
        cost_estimate=LIGHT,
        name="final_error",
    )(table, own_x, bias, *terms)


def line_program(resid, resid_grad, active, w_enc, b_enc, w_dec, b_dec):
    n_tok, n_feat = lax.axis_size("tok"), lax.axis_size("feat")
    i, j = lax.axis_index("tok"), lax.axis_index("feat")
    chips = n_feat // 2
    chip, core = j // 2, j % 2
    width = resid.shape[1]
    rows = resid.shape[0] // n_tok
    feats = w_enc.shape[1]
    share = n_tok * width

    def along(pairs):
        return [(2 * a + c, 2 * b + c) for a, b in pairs for c in range(2)]

    def send(array, pairs):
        return lax.ppermute(array, "feat", along(pairs))

    def cross(array):
        return lax.ppermute(array, "feat", [(a, a ^ 1) for a in range(n_feat)])

    def exchange(array, streams):
        def block(s):
            mine = lax.dynamic_slice_in_dim(array, (i ^ s) * rows, rows, 0)
            if s == 0:
                return mine
            return lax.ppermute(mine, "tok", [(a, a ^ s) for a in range(n_tok)])

        blocks = [block(s) for s in range(n_tok)]
        return [jnp.stack([blocks[s] for s in stream]) for stream in streams]

    own_sub = i ^ (j // (n_feat // n_tok))

    def numbers(*values):
        return jnp.stack([jnp.asarray(v).astype(jnp.int32) for v in values])

    def table(*steps):
        sources = [2 * ((chip + chips - k) % chips) + (core ^ side) for k in steps for side in (0, 1)]
        return numbers(i, own_sub, *sources)

    own_table = numbers(i, own_sub, j % (n_feat // n_tok))
    blocks = feats // BLOCK
    block_ids = j * blocks + jnp.arange(blocks, dtype=jnp.int32)
    hits = jnp.any(active[:, :, None] == block_ids[None, None, :], axis=1).astype(F32)
    hit = jnp.repeat(hits, BLOCK, axis=1)
    bias = b_enc.reshape(1, feats)
    b_row = b_dec.reshape(1, share)
    w4 = w_enc.reshape(n_tok, n_feat, width, feats)

    shard_x = exchange(resid, X_STREAMS)
    shard_g = exchange(resid_grad, G_STREAMS)

    ring = [(a, (a + 1) % chips) for a in range(chips)]
    near_x = [shard_x]
    far_x = [[cross(a) for a in shard_x]]
    carry = None
    for k in range(1, chips):
        first, rest = near_x[-1]
        first = send(first, ring)
        rest = after(rest, first)
        if k == 2:
            rest = after(rest, *shard_g)
        if k == 3:
            slots = [near_x[0], far_x[0], near_x[1], far_x[1]]
            carry = encode(table(0, 1), slots, w4, bias, hit, None, X_STREAMS, False)
            rest = after(rest, carry)
        near_x.append([first, send(rest, ring)])
        far_x.append([cross(a) for a in near_x[-1]])
    slots = [near_x[2], far_x[2], near_x[3], far_x[3]]
    acts, own_x = encode(table(2, 3), slots, w4, bias, hit, carry, X_STREAMS, True)

    shard_g = after(shard_g[0], near_x[-1])
    rows_g = lax.all_gather(shard_g, "feat", axis=0)

    order = (3, 2, 1, 0)
    dests = [2 * (chip ^ k) + (1 - core if side == 0 else core) for k in order for side in (0, 1)]
    outs = decode(numbers(*dests), acts, w_dec, share, len(dests))
    parts = {k: (outs[2 * n + 1], cross(outs[2 * n])) for n, k in enumerate(order)}

    def pair_sum(k):
        return parts[k][0].astype(F32) + parts[k][1].astype(F32)

    up_pairs = [(a, a + 1) for a in range(chips - 1)]
    down_pairs = [(a + 1, a) for a in range(chips - 1)]
    sum_3, sum_1 = pair_sum(3), pair_sum(1)
    come = send(sum_3.astype(BF16), [(0, 1), (3, 2)])
    going = (pair_sum(2) + come.astype(F32)).astype(BF16)
    up = send(going, up_pairs[:2])
    down = send(going, down_pairs[1:])
    going_up = (jnp.where(chip == 1, sum_3, sum_1) + up.astype(F32)).astype(BF16)
    going_down = (jnp.where(chip == 2, sum_3, sum_1) + down.astype(F32)).astype(BF16)
    up = send(going_up, up_pairs)
    down = send(going_down, down_pairs)

    feature_attr, attr = project(own_table, rows_g, w_dec, acts, own_x, b_row)
    attr = attr.reshape(-1, TILE)
    reach = 1
    while reach < n_feat:
        attr = attr + lax.ppermute(attr, "feat", [(a, a ^ reach) for a in range(n_feat)])
        reach *= 2

    error = final_error(own_table, own_x, b_row, [*parts[0], up, down])
    return feature_attr, error, attr.reshape(rows)


def gathered_program(resid, resid_grad, active, w_enc, b_enc, w_dec, b_dec):
    n_tok = lax.axis_size("tok")
    n_feat = lax.axis_size("feat")
    width = resid.shape[1]

    def rows_of(array):
        part = lax.all_to_all(array, "tok", split_axis=0, concat_axis=1, tiled=True)
        part = part.reshape(part.shape[0], n_tok, 1, width)
        part = lax.all_gather(part, "feat", axis=2, tiled=True)
        return part.reshape(part.shape[0], n_tok * n_feat * width)

    rows_x, rows_g = rows_of(resid), rows_of(resid_grad)
    tok_rows = rows_x.shape[0]
    feat_dev = w_enc.shape[1]
    blocks = feat_dev // BLOCK
    tiles_dev = active.shape[0]
    block_ids = lax.axis_index("feat") * blocks + jnp.arange(blocks, dtype=jnp.int32)
    hits = jnp.any(active[:, :, None] == block_ids[None, None, :], axis=1).astype(F32)
    pre = jnp.dot(rows_x, w_enc, preferred_element_type=F32) + b_enc
    shaped = jnp.maximum(pre, 0.0).reshape(tiles_dev, TILE, blocks, BLOCK) * hits[:, None, :, None]
    acts = shaped.reshape(tok_rows, feat_dev).astype(BF16)
    partial_recon = jnp.dot(acts, w_dec, preferred_element_type=F32)
    recon_share = lax.psum_scatter(
        partial_recon.astype(BF16), "feat", scatter_dimension=1, tiled=True
    ).astype(F32)
    share = recon_share.shape[1]
    start = lax.axis_index("feat") * share
    own_x = lax.dynamic_slice_in_dim(rows_x, start, share, 1)
    own_g = lax.dynamic_slice_in_dim(rows_g, start, share, 1)
    recon = recon_share + b_dec
    error = own_x.astype(F32) - recon
    local_sums = jnp.sum(error * own_g.astype(F32), axis=1)
    error_attr = lax.psum(local_sums, "feat")
    proj = lax.dot_general(rows_g, w_dec, (((1,), (1,)), ((), ())), preferred_element_type=F32)
    return acts.astype(F32) * proj, error, error_attr


def per_device(resid, *rest):
    fits = resid.shape[1] % 128 == 0 and lax.axis_size("tok") == 4 and lax.axis_size("feat") == 8
    return (line_program if fits else gathered_program)(resid, *rest)


def solution(mesh):
    placed = (
        P(None, ("tok", "feat")),
        P(None, ("tok", "feat")),
        P("tok", None),
        P(None, "feat"),
        P("feat"),
        P("feat", None),
        P("feat"),
    )
    return jax.shard_map(
        per_device,
        mesh=mesh,
        in_specs=placed,
        out_specs=(P("tok", "feat"), P("tok", "feat"), P("tok")),
        check_vma=False,
    )
```

time: 191 us -> 180 us (0.942)
  Pallas kernels: 0 us -> 41.4 us
  blocking collectives: 40.6 us -> 0 us
  waiting for transfers between devices: 104 us -> 68.6 us
  starting transfers between devices: 0.12 us -> 35.3 us
  matrix products: 19.2 us -> 0 us
  other arithmetic: 3.44 us -> 8.57 us
    ppermute x0 -> x32, waiting for transfers between devices: none -> 68.5 us  [the longest x11 55.8 us: send(): return lax.ppermute(array, 'feat', along(pairs))]
    all_gather x2 -> x1, waiting for transfers between devices: 65.4 us -> 0.01 us  [line_program(): rows_g = lax.all_gather(shard_g, 'feat', axis=0)]
    pallas_call x0 -> x5, Pallas kernels: none -> 41.4 us  [the longest x2 14.5 us: encode(): pl.pallas_call(functools.partial(enc_body, streams, count, first, last),...]
    reduce_scatter x1 -> x0, waiting for transfers between devices: 38.7 us -> none  [per_device(): lax.psum_scatter(partial_recon.astype(jnp.bfloat16), 'feat', scatter_dime...]
    ppermute x0 -> x32, starting transfers between devices: none -> 35.2 us  [the longest x11 21.2 us: send(): return lax.ppermute(array, 'feat', along(pairs))]
    all_to_all x2 -> x0, blocking collectives: 26.3 us -> none  [the longest x1 14.3 us: per_device(): lax.all_to_all(resid, 'tok', split_axis=0, concat_axis=1, tiled=True)]
    dot_general x3 -> x0, matrix products: 19.2 us -> none  [the longest x1 7.4 us: per_device(): lax.dot_general(rows_g, w_dec, (((1,), (1,)), ((), ())), preferred_elemen...]
    psum x1 -> x0, blocking collectives: 14.3 us -> none  [per_device(): error_attr = lax.psum(local_terms, 'feat')]
  transfers between devices with their start and end apart: 3 -> 33, of which waited for: 3 -> 16; matrix products, arithmetic and copies ran while one was open for 14% -> 7% of each run, Pallas kernels for 0% -> 19%
where the time goes in v2:
time: 180 us; the launch traced here: 179 us
  waiting for transfers between devices  68.6 us (38%)
  Pallas kernels  41.4 us (23%)
  starting transfers between devices  35.3 us (20%)
  between operations  14.4 us (8%)
  local copies, waits for them, and re-layouts  10.6 us (6%)
  other arithmetic  8.57 us (5%)
    ppermute x11, waiting for transfers between devices, send(): return lax.ppermute(array, 'feat', along(pairs))  55.8 us
    ppermute x11, starting transfers between devices, send(): return lax.ppermute(array, 'feat', along(pairs))  21.2 us
    pallas_call x2, Pallas kernels, encode(): pl.pallas_call(functools.partial(enc_body, streams, count, first, last),...  14.5 us
    pallas_call x1, Pallas kernels, project(): pl.pallas_call(functools.partial(proj_body, n_tok), grid_spec=pltpu.Prefe...  12.1 us
    pallas_call x1, Pallas kernels, decode(): pl.pallas_call(dec_body, grid_spec=pltpu.PrefetchScalarGridSpec(num_scala...  11.5 us
    ppermute x6, starting transfers between devices, block(): return lax.ppermute(mine, 'tok', [(a, a ^ s) for a in range(n_tok)])  8.15 us
    ppermute x6, waiting for transfers between devices, block(): return lax.ppermute(mine, 'tok', [(a, a ^ s) for a in range(n_tok)])  8.14 us
    unnamed x42, local copies, waits for them, and re-layouts  5.08 us
  transfers between devices with their start and end apart: 33, of which 16 were waited for; matrix products, arithmetic and copies ran while one was open for 7% of the time, Pallas kernels for 19%

profile of v2, /device:TPU:0, one launch (start us, length us, event | category | flops | bytes accessed | tf_op | source)
XLA Modules:
  0.0 178.8 jit_solution(5951771245832368115)
XLA Ops:
  8.4 4.0 %collective-permute-start.8 = (bf16[256,256]{1,0:T(8,128)(2,1)S(1)}, bf16[256,256]{1,0:T(8,128)(2,1)S(1)}, u32[]{:S(2)}, u32[]{:S(2)}) collective-permute-start(bf16[256,256]{1,0:T(8,128)(2,1)S(1)} %get-tuple-element.47), channel_id=1, source_target_pairs={{0,24},{8,16},{16,8},{24,0},{1,25},{9,17},{17,9},{25,1},{2,26},{10... | collective-permute-start | bytes 393224 | tf_op jit(solution)/shard_map/ppermute | solution.py:262
  13.0 2.0 %collective-permute-start.3 = (bf16[1,256,256]{2,1,0:T(8,128)(2,1)S(1)}, bf16[1,256,256]{2,1,0:T(8,128)(2,1)S(1)}, u32[]{:S(2)}, u32[]{:S(2)}) collective-permute-start(bf16[1,256,256]{2,1,0:T(8,128)(2,1)S(1)} %get-tuple-element.46.refs_0_), channel_id=1, source_target_pairs={{0,2},{1,3},{2,4},{3,5},{4,6},{5,7},{6,0},{7,1},{8,10},{9,11},{10,... | collective-permute-start | bytes 393224 | tf_op jit(solution)/shard_map/ppermute | solution.py:252
  15.0 1.7 collective-permute-done.8
  16.7 2.2 %collective-permute-done.6 = bf16[256,256]{1,0:T(8,128)(2,1)S(1)} collective-permute-done((bf16[256,256]{1,0:T(8,128)(2,1)S(1)}, bf16[256,256]{1,0:T(8,128)(2,1)S(1)}, u32[]{:S(2)}, u32[]{:S(2)}) %collective-permute-start.6) | collective-permute-done | bytes 131104 | tf_op jit(solution)/shard_map/ppermute | solution.py:262
  21.7 1.6 collective-permute-start
  23.3 1.5 collective-permute-start.1
  25.3 1.6 collective-permute-start.4
  27.5 3.6 %collective-permute-done.1 = bf16[256,256]{1,0:T(8,128)(2,1)S(1)} collective-permute-done((bf16[256,256]{1,0:T(8,128)(2,1)S(1)}, bf16[256,256]{1,0:T(8,128)(2,1)S(1)}, u32[]{:S(2)}, u32[]{:S(2)}) %collective-permute-start.1) | collective-permute-done | bytes 131104 | tf_op jit(solution)/shard_map/ppermute | solution.py:262
  31.9 2.0 %collective-permute-done.4.refs_0_ = bf16[1,256,256]{2,1,0:T(8,128)(2,1)S(1)} collective-permute-done((bf16[1,256,256]{2,1,0:T(8,128)(2,1)S(1)}, bf16[1,256,256]{2,1,0:T(8,128)(2,1)S(1)}, u32[]{:S(2)}, u32[]{:S(2)}) %collective-permute-start.4) | collective-permute-done | bytes 131104 | tf_op jit(solution)/shard_map/ppermute | solution.py:252
  34.0 1.3 collective-permute-start.10
  36.1 6.0 %collective-permute-done.5.refs_4_ = bf16[1,256,256]{2,1,0:T(8,128)(2,1)S(1)} collective-permute-done((bf16[1,256,256]{2,1,0:T(8,128)(2,1)S(1)}, bf16[1,256,256]{2,1,0:T(8,128)(2,1)S(1)}, u32[]{:S(2)}, u32[]{:S(2)}) %collective-permute-start.5) | collective-permute-done | bytes 131104 | tf_op jit(solution)/shard_map/ppermute | solution.py:252
  42.8 1.3 reshape.30.refs_12_
  44.8 3.3 %collective-permute-done.10.refs_1_ = bf16[3,256,256]{2,1,0:T(8,128)(2,1)S(1)} collective-permute-done((bf16[3,256,256]{2,1,0:T(8,128)(2,1)S(1)}, bf16[3,256,256]{2,1,0:T(8,128)(2,1)S(1)}, u32[]{:S(2)}, u32[]{:S(2)}) %collective-permute-start.10) | collective-permute-done | bytes 393248 | tf_op jit(solution)/shard_map/ppermute | solution.py:252
  49.1 7.0 %encode.2 = (f32[256,640]{1,0:T(8,128)}, bf16[8,256,256]{2,1,0:T(8,128)(2,1)}) custom-call(s32[6]{0:T(128)} %stack.121.table, bf16[1,256,256]{2,1,0:T(8,128)(2,1)} %copy-done.1, bf16[3,256,256]{2,1,0:T(8,128)(2,1)} %copy-done, bf16[1,256,256]{2,1,0:T(8,128)(2,1)} %copy-done.16, bf16[3,256,256]{2,1,0:T(8,128)(2,1)} %copy-done.8, ...), custom_call_target="tpu_custom_call" | custom-call | flops 1 | bytes 1 | tf_op jit(solution)/shard_map/encode/pallas_call | solution.py:91
  56.1 10.4 %collective-permute-done.15.refs_5_ = bf16[3,256,256]{2,1,0:T(8,128)(2,1)S(1)} collective-permute-done((bf16[3,256,256]{2,1,0:T(8,128)(2,1)S(1)}, bf16[3,256,256]{2,1,0:T(8,128)(2,1)S(1)}, u32[]{:S(2)}, u32[]{:S(2)}) %collective-permute-start.15) | collective-permute-done | bytes 393248 | tf_op jit(solution)/shard_map/ppermute | solution.py:252
  70.8 7.5 %encode.3 = (bf16[256,640]{1,0:T(8,128)(2,1)}, bf16[8,256,256]{2,1,0:T(8,128)(2,1)}) custom-call(s32[6]{0:T(128)} %stack.126.table, bf16[1,256,256]{2,1,0:T(8,128)(2,1)} %copy-done.13, bf16[3,256,256]{2,1,0:T(8,128)(2,1)} %copy-done.6, bf16[1,256,256]{2,1,0:T(8,128)(2,1)} %copy-done.17, ...), custom_call_target="tpu_custom_call", output_to_operand_aliasing={{1}: (16, {})} | custom-call | flops 1 | bytes 1 | tf_op jit(solution)/shard_map/encode/pallas_call | solution.py:91
  78.4 11.5 %decode.1 = (bf16[256,1024]{1,0:T(8,128)(2,1)}, bf16[256,1024]{1,0:T(8,128)(2,1)}, bf16[256,1024]{1,0:T(8,128)(2,1)}, bf16[256,1024]{1,0:T(8,128)(2,1)}, bf16[25...) custom-call(s32[8]{0:T(128)} %stack.135.table, ...), custom_call_target="tpu_custom_call" | custom-call | flops 1 | bytes 1 | tf_op jit(solution)/shard_map/decode/pallas_call | solution.py:127
  90.4 1.6 collective-permute-done.21
  92.0 1.2 fusion
  93.2 1.5 collective-permute-start.24
  94.8 23.1 %collective-permute-done.24 = bf16[256,1024]{1,0:T(8,128)(2,1)S(1)} collective-permute-done((bf16[256,1024]{1,0:T(8,128)(2,1)S(1)}, bf16[256,1024]{1,0:T(8,128)(2,1)S(1)}, u32[]{:S(2)}, u32[]{:S(2)}) %collective-permute-start.24) | collective-permute-done | bytes 524320 | tf_op jit(solution)/shard_map/ppermute | solution.py:252
  118.0 1.3 add_convert_fusion.2
  119.3 4.4 %collective-permute-start.25 = (bf16[256,1024]{1,0:T(8,128)(2,1)S(1)}, bf16[256,1024]{1,0:T(8,128)(2,1)S(1)}, u32[]{:S(2)}, u32[]{:S(2)}) collective-permute-start(bf16[256,1024]{1,0:T(8,128)(2,1)S(1)} %add_convert_fusion.2), channel_id=1, source_target_pairs={{0,2},{1,3},{2,4},{3,5},{8,10},{9,11},{10,12},{11,13},{16,18},{17,... | collective-permute-start | bytes 1572872 | tf_op jit(solution)/shard_map/ppermute | solution.py:252
  124.5 10.0 %collective-permute-done.25 = bf16[256,1024]{1,0:T(8,128)(2,1)S(1)} collective-permute-done((bf16[256,1024]{1,0:T(8,128)(2,1)S(1)}, bf16[256,1024]{1,0:T(8,128)(2,1)S(1)}, u32[]{:S(2)}, u32[]{:S(2)}) %collective-permute-start.25) | collective-permute-done | bytes 524320 | tf_op jit(solution)/shard_map/ppermute | solution.py:252
  135.3 2.0 %add_convert_fusion = (bf16[256,1024]{1,0:T(8,128)(2,1)S(1)}, bf16[256,1024]{1,0:T(8,128)(2,1)S(1)}) fusion(bf16[256,1024]{1,0:T(8,128)(2,1)} %copy-done.5, bf16[256,1024]{1,0:T(8,128)(2,1)S(1)} %collective-permute-done.22, bf16[256,1024]{1,0:T(8,128)(2,1)} %get-tuple-element.38, bf16[256,1024]{1,0:T(8,128)(2,1)S(1)} %collective-permute-done.21, ...), kind=kLoop, calls=%fused_computation | loop fusion | flops 3670016 | bytes 4194306 | tf_op jit(solution)/shard_map/convert_element_type | solution.py:326
  137.3 7.7 %collective-permute-start.26 = (bf16[256,1024]{1,0:T(8,128)(2,1)S(1)}, bf16[256,1024]{1,0:T(8,128)(2,1)S(1)}, u32[]{:S(2)}, u32[]{:S(2)}) collective-permute-start(bf16[256,1024]{1,0:T(8,128)(2,1)S(1)} %get-tuple-element.44), channel_id=1, source_target_pairs={{0,2},{1,3},{2,4},{3,5},{4,6},{5,7},{8,10},{9,11},{10,12},{11,13},... | collective-permute-start | bytes 1572872 | tf_op jit(solution)/shard_map/ppermute | solution.py:252
  144.9 1.3 collective-permute-start.28
  146.9 12.1 %project.1 = (f32[256,640]{1,0:T(8,128)}, f32[256,1]{1,0:T(8,128)}) custom-call(s32[3]{0:T(128)} %pad_add_fusion.table, bf16[8,4,256,256]{3,2,1,0:T(8,128)(2,1)} %bitcast.51, bf16[640,8192]{1,0:T(8,128)(2,1)} %w_ref.1, bf16[640,8192]{1,0:T(8,128)(2,1)} %w_ref.1, bf16[640,8192]{1,0:T(8,128)(2,1)} %w_ref.1, bf16[640,8192]{1,0:T(8,128)(2,1)} %w_ref.1, ...), custom_call_target="tpu_custom_call" | custom-call | flops 1 | bytes 1 | tf_op jit(solution)/shard_map/project/pallas_call | solution.py:184
  161.2 2.6 %collective-permute-start.30 = (f32[2,128]{1,0:T(2,128)S(1)}, f32[2,128]{1,0:T(2,128)S(1)}, u32[]{:S(2)}, u32[]{:S(2)}) collective-permute-start(f32[2,128]{1,0:T(2,128)S(1)} %bitcast_add_fusion), channel_id=1, source_target_pairs={{0,2},{1,3},{2,0},{3,1},{4,6},{5,7},{6,4},{7,5},{8,10},{9,11},{10,... | collective-permute-start | bytes 3080 | tf_op jit(solution)/shard_map/ppermute | solution.py:334
  163.8 1.5 collective-permute-done.30
  165.4 1.4 collective-permute-start.31
  168.0 3.3 %final_error.1 = f32[256,1024]{1,0:T(8,128)} custom-call(s32[3]{0:T(128)} %pad_add_fusion.table, bf16[8,256,256]{2,1,0:T(8,128)(2,1)} %get-tuple-element.32.refs_5_.x_ref, f32[1,1024]{1,0:T(1,128)} %bitcast.61, bf16[256,1024]{1,0:T(8,128)(2,1)} %get-tuple-element.34.refs_0_, bf16[256,1024]{1,0:T(8,128)(2,1)} %copy-done.2, bf16[256,1024]{1,0:T(8,128)(2,1)} %copy-done.3, ...), custom_call_target="tpu_custom_call" | custom-call | flops 1 | bytes 1 | tf_op jit(solution)/shard_map/final_error/pallas_call | solution.py:217
  (101 shorter events, 20.9 us)
Async XLA Ops:
  7.2 139.7 %all-gather.3.cloned.1.call-start = ((), (), s32[]{:S(2)}) async-start(), calls=%async_computation | async-start | bytes 4718592 | tf_op jit(solution)/shard_map/all_gather | solution.py:308
  8.4 8.3 %collective-permute-start.8 = (bf16[256,256]{1,0:T(8,128)(2,1)S(1)}, bf16[256,256]{1,0:T(8,128)(2,1)S(1)}, u32[]{:S(2)}, u32[]{:S(2)}) collective-permute-start(bf16[256,256]{1,0:T(8,128)(2,1)S(1)} %get-tuple-element.47), channel_id=1, source_target_pairs={{0,24},{8,16},{16,8},{24,0},{1,25},{9,17},{17,9},{25,1},{2,26},{10... | collective-permute-start | bytes 393224 | tf_op jit(solution)/shard_map/ppermute | solution.py:262
  12.3 6.6 %collective-permute-start.6 = (bf16[256,256]{1,0:T(8,128)(2,1)S(1)}, bf16[256,256]{1,0:T(8,128)(2,1)S(1)}, u32[]{:S(2)}, u32[]{:S(2)}) collective-permute-start(bf16[256,256]{1,0:T(8,128)(2,1)S(1)} %get-tuple-element.45), channel_id=1, source_target_pairs={{0,8},{8,0},{16,24},{24,16},{1,9},{9,1},{17,25},{25,17},{2,10},{10... | collective-permute-start | bytes 393224 | tf_op jit(solution)/shard_map/ppermute | solution.py:262
  12.9 6.0 %collective-permute-start.7 = (bf16[256,256]{1,0:T(8,128)(2,1)S(1)}, bf16[256,256]{1,0:T(8,128)(2,1)S(1)}, u32[]{:S(2)}, u32[]{:S(2)}) collective-permute-start(bf16[256,256]{1,0:T(8,128)(2,1)S(1)} %get-tuple-element.48), channel_id=1, source_target_pairs={{0,16},{8,24},{16,0},{24,8},{1,17},{9,25},{17,1},{25,9},{2,18},{10... | collective-permute-start | bytes 393224 | tf_op jit(solution)/shard_map/ppermute | solution.py:262
  13.0 6.9 %collective-permute-start.3 = (bf16[1,256,256]{2,1,0:T(8,128)(2,1)S(1)}, bf16[1,256,256]{2,1,0:T(8,128)(2,1)S(1)}, u32[]{:S(2)}, u32[]{:S(2)}) collective-permute-start(bf16[1,256,256]{2,1,0:T(8,128)(2,1)S(1)} %get-tuple-element.46.refs_0_), channel_id=1, source_target_pairs={{0,2},{1,3},{2,4},{3,5},{4,6},{5,7},{6,0},{7,1},{8,10},{9,11},{10,... | collective-permute-start | bytes 393224 | tf_op jit(solution)/shard_map/ppermute | solution.py:252
  19.9 14.0 %collective-permute-start.9 = (bf16[3,256,256]{2,1,0:T(8,128)(2,1)S(1)}, bf16[3,256,256]{2,1,0:T(8,128)(2,1)S(1)}, u32[]{:S(2)}, u32[]{:S(2)}) collective-permute-start(bf16[3,256,256]{2,1,0:T(8,128)(2,1)S(1)} %pad_maximum_fusion.1.refs_1_), channel_id=1, source_target_pairs={{0,2},{1,3},{2,4},{3,5},{4,6},{5,7},{6,0},{7,1},{8,10},{9,11},{10,... | collective-permute-start | bytes 1179656 | tf_op jit(solution)/shard_map/ppermute | solution.py:252
  21.7 5.8 %collective-permute-start = (bf16[256,256]{1,0:T(8,128)(2,1)S(1)}, bf16[256,256]{1,0:T(8,128)(2,1)S(1)}, u32[]{:S(2)}, u32[]{:S(2)}) collective-permute-start(bf16[256,256]{1,0:T(8,128)(2,1)S(1)} %get-tuple-element.50), channel_id=1, source_target_pairs={{0,8},{8,0},{16,24},{24,16},{1,9},{9,1},{17,25},{25,17},{2,10},{10... | collective-permute-start | bytes 393224 | tf_op jit(solution)/shard_map/ppermute | solution.py:262
  23.3 7.8 %collective-permute-start.1 = (bf16[256,256]{1,0:T(8,128)(2,1)S(1)}, bf16[256,256]{1,0:T(8,128)(2,1)S(1)}, u32[]{:S(2)}, u32[]{:S(2)}) collective-permute-start(bf16[256,256]{1,0:T(8,128)(2,1)S(1)} %get-tuple-element.52), channel_id=1, source_target_pairs={{0,16},{8,24},{16,0},{24,8},{1,17},{9,25},{17,1},{25,9},{2,18},{10... | collective-permute-start | bytes 393224 | tf_op jit(solution)/shard_map/ppermute | solution.py:262
  24.8 6.3 %collective-permute-start.2 = (bf16[256,256]{1,0:T(8,128)(2,1)S(1)}, bf16[256,256]{1,0:T(8,128)(2,1)S(1)}, u32[]{:S(2)}, u32[]{:S(2)}) collective-permute-start(bf16[256,256]{1,0:T(8,128)(2,1)S(1)} %get-tuple-element.51), channel_id=1, source_target_pairs={{0,24},{8,16},{16,8},{24,0},{1,25},{9,17},{17,9},{25,1},{2,26},{10... | collective-permute-start | bytes 393224 | tf_op jit(solution)/shard_map/ppermute | solution.py:262
  25.3 8.6 %collective-permute-start.4 = (bf16[1,256,256]{2,1,0:T(8,128)(2,1)S(1)}, bf16[1,256,256]{2,1,0:T(8,128)(2,1)S(1)}, u32[]{:S(2)}, u32[]{:S(2)}) collective-permute-start(bf16[1,256,256]{2,1,0:T(8,128)(2,1)S(1)} %collective-permute-done.3.refs_4_), channel_id=1, source_target_pairs={{0,2},{1,3},{2,4},{3,5},{4,6},{5,7},{6,0},{7,1},{8,10},{9,11},{10,... | collective-permute-start | bytes 393224 | tf_op jit(solution)/shard_map/ppermute | solution.py:252
  27.5 20.6 %collective-permute-start.11 = (bf16[1,256,256]{2,1,0:T(8,128)(2,1)S(1)}, bf16[1,256,256]{2,1,0:T(8,128)(2,1)S(1)}, u32[]{:S(2)}, u32[]{:S(2)}) collective-permute-start(bf16[1,256,256]{2,1,0:T(8,128)(2,1)S(1)} %get-tuple-element.46.refs_0_), channel_id=1, source_target_pairs={{0,1},{1,0},{2,3},{3,2},{4,5},{5,4},{6,7},{7,6},{8,9},{9,8},{10,11... | collective-permute-start | bytes 393224 | tf_op jit(solution)/shard_map/ppermute | solution.py:255
  31.1 17.0 %collective-permute-start.12 = (bf16[3,256,256]{2,1,0:T(8,128)(2,1)S(1)}, bf16[3,256,256]{2,1,0:T(8,128)(2,1)S(1)}, u32[]{:S(2)}, u32[]{:S(2)}) collective-permute-start(bf16[3,256,256]{2,1,0:T(8,128)(2,1)S(1)} %pad_maximum_fusion.1.refs_1_), channel_id=1, source_target_pairs={{0,1},{1,0},{2,3},{3,2},{4,5},{5,4},{6,7},{7,6},{8,9},{9,8},{10,11... | collective-permute-start | bytes 1179656 | tf_op jit(solution)/shard_map/ppermute | solution.py:255
  33.9 8.2 %collective-permute-start.5 = (bf16[1,256,256]{2,1,0:T(8,128)(2,1)S(1)}, bf16[1,256,256]{2,1,0:T(8,128)(2,1)S(1)}, u32[]{:S(2)}, u32[]{:S(2)}) collective-permute-start(bf16[1,256,256]{2,1,0:T(8,128)(2,1)S(1)} %collective-permute-done.4.refs_0_), channel_id=1, source_target_pairs={{0,2},{1,3},{2,4},{3,5},{4,6},{5,7},{6,0},{7,1},{8,10},{9,11},{10,... | collective-permute-start | bytes 393224 | tf_op jit(solution)/shard_map/ppermute | solution.py:252
  34.0 14.1 %collective-permute-start.10 = (bf16[3,256,256]{2,1,0:T(8,128)(2,1)S(1)}, bf16[3,256,256]{2,1,0:T(8,128)(2,1)S(1)}, u32[]{:S(2)}, u32[]{:S(2)}) collective-permute-start(bf16[3,256,256]{2,1,0:T(8,128)(2,1)S(1)} %collective-permute-done.9.refs_5_), channel_id=1, source_target_pairs={{0,2},{1,3},{2,4},{3,5},{4,6},{5,7},{6,0},{7,1},{8,10},{9,11},{10,... | collective-permute-start | bytes 1179656 | tf_op jit(solution)/shard_map/ppermute | solution.py:252
  35.3 12.9 %collective-permute-start.14 = (bf16[3,256,256]{2,1,0:T(8,128)(2,1)S(1)}, bf16[3,256,256]{2,1,0:T(8,128)(2,1)S(1)}, u32[]{:S(2)}, u32[]{:S(2)}) collective-permute-start(bf16[3,256,256]{2,1,0:T(8,128)(2,1)S(1)} %collective-permute-done.9.refs_5_), channel_id=1, source_target_pairs={{0,1},{1,0},{2,3},{3,2},{4,5},{5,4},{6,7},{7,6},{8,9},{9,8},{10,11... | collective-permute-start | bytes 1179656 | tf_op jit(solution)/shard_map/ppermute | solution.py:255
  42.2 5.9 %collective-permute-start.13 = (bf16[1,256,256]{2,1,0:T(8,128)(2,1)S(1)}, bf16[1,256,256]{2,1,0:T(8,128)(2,1)S(1)}, u32[]{:S(2)}, u32[]{:S(2)}) collective-permute-start(bf16[1,256,256]{2,1,0:T(8,128)(2,1)S(1)} %collective-permute-done.3.refs_4_), channel_id=1, source_target_pairs={{0,1},{1,0},{2,3},{3,2},{4,5},{5,4},{6,7},{7,6},{8,9},{9,8},{10,11... | collective-permute-start | bytes 393224 | tf_op jit(solution)/shard_map/ppermute | solution.py:255
  56.1 10.5 %collective-permute-start.15 = (bf16[3,256,256]{2,1,0:T(8,128)(2,1)S(1)}, bf16[3,256,256]{2,1,0:T(8,128)(2,1)S(1)}, u32[]{:S(2)}, u32[]{:S(2)}) collective-permute-start(bf16[3,256,256]{2,1,0:T(8,128)(2,1)S(1)} %collective-permute-done.10.refs_1_), channel_id=1, source_target_pairs={{0,2},{1,3},{2,4},{3,5},{4,6},{5,7},{6,0},{7,1},{8,10},{9,11},{10,... | collective-permute-start | bytes 1179656 | tf_op jit(solution)/shard_map/ppermute | solution.py:252
  66.6 2.7 %collective-permute-start.17 = (bf16[3,256,256]{2,1,0:T(8,128)(2,1)S(1)}, bf16[3,256,256]{2,1,0:T(8,128)(2,1)S(1)}, u32[]{:S(2)}, u32[]{:S(2)}) collective-permute-start(bf16[3,256,256]{2,1,0:T(8,128)(2,1)S(1)} %collective-permute-done.10.refs_1_), channel_id=1, source_target_pairs={{0,1},{1,0},{2,3},{3,2},{4,5},{5,4},{6,7},{7,6},{8,9},{9,8},{10,11... | collective-permute-start | bytes 1179656 | tf_op jit(solution)/shard_map/ppermute | solution.py:255
  66.7 2.7 %collective-permute-start.19 = (bf16[3,256,256]{2,1,0:T(8,128)(2,1)S(1)}, bf16[3,256,256]{2,1,0:T(8,128)(2,1)S(1)}, u32[]{:S(2)}, u32[]{:S(2)}) collective-permute-start(bf16[3,256,256]{2,1,0:T(8,128)(2,1)S(1)} %collective-permute-done.15.refs_5_), channel_id=1, source_target_pairs={{0,1},{1,0},{2,3},{3,2},{4,5},{5,4},{6,7},{7,6},{8,9},{9,8},{10,11... | collective-permute-start | bytes 1179656 | tf_op jit(solution)/shard_map/ppermute | solution.py:255
  67.2 2.0 %collective-permute-start.16 = (bf16[1,256,256]{2,1,0:T(8,128)(2,1)S(1)}, bf16[1,256,256]{2,1,0:T(8,128)(2,1)S(1)}, u32[]{:S(2)}, u32[]{:S(2)}) collective-permute-start(bf16[1,256,256]{2,1,0:T(8,128)(2,1)S(1)} %collective-permute-done.4.refs_0_), channel_id=1, source_target_pairs={{0,1},{1,0},{2,3},{3,2},{4,5},{5,4},{6,7},{7,6},{8,9},{9,8},{10,11... | collective-permute-start | bytes 393224 | tf_op jit(solution)/shard_map/ppermute | solution.py:255
  67.2 2.1 %collective-permute-start.18 = (bf16[1,256,256]{2,1,0:T(8,128)(2,1)S(1)}, bf16[1,256,256]{2,1,0:T(8,128)(2,1)S(1)}, u32[]{:S(2)}, u32[]{:S(2)}) collective-permute-start(bf16[1,256,256]{2,1,0:T(8,128)(2,1)S(1)} %collective-permute-done.5.refs_4_), channel_id=1, source_target_pairs={{0,1},{1,0},{2,3},{3,2},{4,5},{5,4},{6,7},{7,6},{8,9},{9,8},{10,11... | collective-permute-start | bytes 393224 | tf_op jit(solution)/shard_map/ppermute | solution.py:255
  89.8 2.1 %collective-permute-start.21 = (bf16[256,1024]{1,0:T(8,128)(2,1)}, bf16[256,1024]{1,0:T(8,128)(2,1)S(1)}, u32[]{:S(2)}, u32[]{:S(2)}) collective-permute-start(bf16[256,1024]{1,0:T(8,128)(2,1)} %get-tuple-element.37), channel_id=1, source_target_pairs={{0,1},{1,0},{2,3},{3,2},{4,5},{5,4},{6,7},{7,6},{8,9},{9,8},{10,11... | collective-permute-start | bytes 1572872 | tf_op jit(solution)/shard_map/ppermute | solution.py:255
  89.8 5.0 %collective-permute-start.23 = (bf16[256,1024]{1,0:T(8,128)(2,1)}, bf16[256,1024]{1,0:T(8,128)(2,1)S(1)}, u32[]{:S(2)}, u32[]{:S(2)}) collective-permute-start(bf16[256,1024]{1,0:T(8,128)(2,1)} %get-tuple-element.41), channel_id=1, source_target_pairs={{0,1},{1,0},{2,3},{3,2},{4,5},{5,4},{6,7},{7,6},{8,9},{9,8},{10,11... | collective-permute-start | bytes 1572872 | tf_op jit(solution)/shard_map/ppermute | solution.py:255
  93.2 24.7 %collective-permute-start.24 = (bf16[256,1024]{1,0:T(8,128)(2,1)S(1)}, bf16[256,1024]{1,0:T(8,128)(2,1)S(1)}, u32[]{:S(2)}, u32[]{:S(2)}) collective-permute-start(bf16[256,1024]{1,0:T(8,128)(2,1)S(1)} %fusion), channel_id=1, source_target_pairs={{0,2},{1,3},{6,4},{7,5},{8,10},{9,11},{14,12},{15,13},{16,18},{17,... | collective-permute-start | bytes 1572872 | tf_op jit(solution)/shard_map/ppermute | solution.py:252
  94.7 29.7 %collective-permute-start.22 = (bf16[256,1024]{1,0:T(8,128)(2,1)}, bf16[256,1024]{1,0:T(8,128)(2,1)S(1)}, u32[]{:S(2)}, u32[]{:S(2)}) collective-permute-start(bf16[256,1024]{1,0:T(8,128)(2,1)} %get-tuple-element.39), channel_id=1, source_target_pairs={{0,1},{1,0},{2,3},{3,2},{4,5},{5,4},{6,7},{7,6},{8,9},{9,8},{10,11... | collective-permute-start | bytes 1572872 | tf_op jit(solution)/shard_map/ppermute | solution.py:255
  119.3 15.2 %collective-permute-start.25 = (bf16[256,1024]{1,0:T(8,128)(2,1)S(1)}, bf16[256,1024]{1,0:T(8,128)(2,1)S(1)}, u32[]{:S(2)}, u32[]{:S(2)}) collective-permute-start(bf16[256,1024]{1,0:T(8,128)(2,1)S(1)} %add_convert_fusion.2), channel_id=1, source_target_pairs={{0,2},{1,3},{2,4},{3,5},{8,10},{9,11},{10,12},{11,13},{16,18},{17,... | collective-permute-start | bytes 1572872 | tf_op jit(solution)/shard_map/ppermute | solution.py:252
  123.7 10.8 %collective-permute-start.27 = (bf16[256,1024]{1,0:T(8,128)(2,1)S(1)}, bf16[256,1024]{1,0:T(8,128)(2,1)S(1)}, u32[]{:S(2)}, u32[]{:S(2)}) collective-permute-start(bf16[256,1024]{1,0:T(8,128)(2,1)S(1)} %add_convert_fusion.2), channel_id=1, source_target_pairs={{4,2},{5,3},{6,4},{7,5},{12,10},{13,11},{14,12},{15,13},{20,18},{2... | collective-permute-start | bytes 1572872 | tf_op jit(solution)/shard_map/ppermute | solution.py:252
  124.4 42.4 %collective-permute-start.20 = (bf16[256,1024]{1,0:T(8,128)(2,1)}, bf16[256,1024]{1,0:T(8,128)(2,1)S(1)}, u32[]{:S(2)}, u32[]{:S(2)}) collective-permute-start(bf16[256,1024]{1,0:T(8,128)(2,1)} %get-tuple-element.35), channel_id=1, source_target_pairs={{0,1},{1,0},{2,3},{3,2},{4,5},{5,4},{6,7},{7,6},{8,9},{9,8},{10,11... | collective-permute-start | bytes 1572872 | tf_op jit(solution)/shard_map/ppermute | solution.py:255
  137.3 29.6 %collective-permute-start.26 = (bf16[256,1024]{1,0:T(8,128)(2,1)S(1)}, bf16[256,1024]{1,0:T(8,128)(2,1)S(1)}, u32[]{:S(2)}, u32[]{:S(2)}) collective-permute-start(bf16[256,1024]{1,0:T(8,128)(2,1)S(1)} %get-tuple-element.44), channel_id=1, source_target_pairs={{0,2},{1,3},{2,4},{3,5},{4,6},{5,7},{8,10},{9,11},{10,12},{11,13},... | collective-permute-start | bytes 1572872 | tf_op jit(solution)/shard_map/ppermute | solution.py:252
  144.9 21.9 %collective-permute-start.28 = (bf16[256,1024]{1,0:T(8,128)(2,1)S(1)}, bf16[256,1024]{1,0:T(8,128)(2,1)S(1)}, u32[]{:S(2)}, u32[]{:S(2)}) collective-permute-start(bf16[256,1024]{1,0:T(8,128)(2,1)S(1)} %get-tuple-element.43), channel_id=1, source_target_pairs={{2,0},{3,1},{4,2},{5,3},{6,4},{7,5},{10,8},{11,9},{12,10},{13,11},... | collective-permute-start | bytes 1572872 | tf_op jit(solution)/shard_map/ppermute | solution.py:252
  161.2 4.2 %collective-permute-start.30 = (f32[2,128]{1,0:T(2,128)S(1)}, f32[2,128]{1,0:T(2,128)S(1)}, u32[]{:S(2)}, u32[]{:S(2)}) collective-permute-start(f32[2,128]{1,0:T(2,128)S(1)} %bitcast_add_fusion), channel_id=1, source_target_pairs={{0,2},{1,3},{2,0},{3,1},{4,6},{5,7},{6,4},{7,5},{8,10},{9,11},{10,... | collective-permute-start | bytes 3080 | tf_op jit(solution)/shard_map/ppermute | solution.py:334
  165.4 6.0 %collective-permute-start.31 = (f32[2,128]{1,0:T(2,128)S(1)}, f32[2,128]{1,0:T(2,128)S(1)}, u32[]{:S(2)}, u32[]{:S(2)}) collective-permute-start(f32[2,128]{1,0:T(2,128)S(1)} %fusion.1), channel_id=1, source_target_pairs={{0,4},{1,5},{2,6},{3,7},{4,0},{5,1},{6,2},{7,3},{8,12},{9,13},{10,... | collective-permute-start | bytes 3080 | tf_op jit(solution)/shard_map/ppermute | solution.py:334
  (21 other events, 204.2 us)
Sparse Core Ops, SparseCore 0:
  66.7 52.0 all-gather.2

commit v3 on v2

--- a/solution.py
+++ b/solution.py
@@ -9,7 +9,7 @@
 
 BLOCK = 128
 TILE = 128
-X_STREAMS = ((0,), (1, 2, 3))
+X_STREAMS = ((0,), (1, 2), (3,))
 G_STREAMS = ((0, 1, 2, 3),)
 PARAMS = pltpu.CompilerParams(vmem_limit_bytes=56 << 20)
 F32 = jnp.float32
@@ -30,44 +30,52 @@
     return [refs[a].at[b] for a, stream in enumerate(streams) for b in range(len(stream))]
 
 
+def cost(rows, depth, feats):
+    return pl.CostEstimate(
+        flops=2 * rows * depth * feats, bytes_accessed=2 * depth * (rows + feats), transcendentals=0
+    )
+
+
 def enc_body(streams, count, first, last, table, *refs):
     size = len(streams)
     slots = [pieces(refs[q * size:(q + 1) * size], streams) for q in range(count)]
-    refs = refs[count * size:]
-    n_tok = len(slots[0])
-    w_refs = refs[:n_tok]
-    bias_ref, hit_ref = refs[n_tok:n_tok + 2]
-    refs = refs[n_tok + 2:]
+    w_ref, bias_ref, hit_ref = refs[count * size:count * size + 3]
+    refs = refs[count * size + 3:]
     carry_ref = None
     if not first:
         carry_ref, refs = refs[0], refs[2:]
-    out_ref, own_ref = refs[:2]
-    total_ref = refs[2] if last else out_ref
+    out_ref, own_ref, x_ref = refs[:3]
+    total_ref = refs[3] if last else out_ref
     step = pl.program_id(0)
+    n_tok, _, width, feats = w_ref.shape
     for q, blocks in enumerate(slots):
 
         @pl.when(step == q)
         def _():
-            total = None
-            for x, w_ref in zip(blocks, w_refs):
-                term = jnp.dot(x[...], w_ref[0, 0], preferred_element_type=F32)
-                total = term if total is None else total + term
-            if q > 0:
-                total = total + total_ref[...]
-            elif not first:
-                total = total + carry_ref[...]
-            if last and q == count - 1:
-                pre = total + bias_ref[...]
-                tiles = hit_ref.shape[0]
-                shaped = jnp.maximum(pre, 0.0).reshape(tiles, TILE, -1) * hit_ref[...][:, None, :]
-                out_ref[...] = shaped.reshape(pre.shape).astype(BF16)
-            else:
-                total_ref[...] = total
             for s, x in enumerate(blocks):
-
-                @pl.when(table[1] == s)
-                def _():
-                    own_ref[0] = x[...]
+                x_ref[:, pl.ds(pl.multiple_of((table[0] ^ s) * width, width), width)] = x[...]
+
+    total = jnp.dot(
+        x_ref[...], w_ref[...].reshape(n_tok * width, feats), preferred_element_type=F32
+    )
+
+    @pl.when(step == 0)
+    def _():
+        total_ref[...] = total if first else total + carry_ref[...]
+
+    @pl.when(step > 0)
+    def _():
+        total_ref[...] += total
+
+    own_ref[0] = x_ref[:, pl.ds(pl.multiple_of(table[1] * width, width), width)]
+    if last:
+
+        @pl.when(step == count - 1)
+        def _():
+            pre = total_ref[...] + bias_ref[...]
+            tiles = hit_ref.shape[0]
+            shaped = jnp.maximum(pre, 0.0).reshape(tiles, TILE, -1) * hit_ref[...][:, None, :]
+            out_ref[...] = shaped.reshape(pre.shape).astype(BF16)
 
 
 def encode(table, slots, w4, bias, hit, carry, streams, last):
@@ -76,18 +84,19 @@
     first = carry is None
     flat = [a for slot in slots for a in slot]
     specs = [whole(a.shape) for a in flat]
-    for s in range(n_tok):
-        specs.append(
-            pl.BlockSpec((1, 1, width, feats), lambda q, t, s=s: (t[0] ^ s, t[2 + q], 0, 0))
-        )
-    specs += [whole(bias.shape), whole(hit.shape)]
-    args = [*flat] + [w4] * n_tok + [bias, hit]
+    specs += [
+        pl.BlockSpec((n_tok, 1, width, feats), lambda q, t: (0, t[2 + q], 0, 0)),
+        whole(bias.shape),
+        whole(hit.shape),
+    ]
+    args = [*flat, w4, bias, hit]
     aliases = {}
     if not first:
         specs += [whole(carry[0].shape), pl.BlockSpec(memory_space=pl.ANY)]
         args += carry
         aliases = {len(args): 1}
     count = len(slots)
+    scratch = [pltpu.VMEM((rows, n_tok * width), BF16)]
     return pl.pallas_call(
         functools.partial(enc_body, streams, count, first, last),
         grid_spec=pltpu.PrefetchScalarGridSpec(
@@ -98,7 +107,7 @@
                 whole((rows, feats)),
                 pl.BlockSpec((1, rows, width), lambda q, t: (t[2 + q], 0, 0)),
             ],
-            scratch_shapes=[pltpu.VMEM((rows, feats), F32)] if last else [],
+            scratch_shapes=scratch + ([pltpu.VMEM((rows, feats), F32)] if last else []),
         ),
         out_shape=[
             jax.ShapeDtypeStruct((rows, feats), BF16 if last else F32),
@@ -106,7 +115,7 @@
         ],
         input_output_aliases=aliases,
         compiler_params=PARAMS,
-        cost_estimate=LIGHT,
+        cost_estimate=LIGHT if last else cost(rows, count * n_tok * width, feats),
         name="encode",
     )(table, *args)
 
@@ -139,64 +148,106 @@
     )(table, acts, w_dec)
 
 
-def proj_body(n_tok, table, g_ref, *refs):
-    w_refs, (acts_ref, x_ref, bias_ref, out_ref, sum_ref) = refs[:n_tok], refs[n_tok:]
-    step, steps = pl.program_id(0), pl.num_programs(0)
-    total = None
-    for s, w_ref in enumerate(w_refs):
-        term = lax.dot_general(
-            g_ref[0, s], w_ref[...], (((1,), (1,)), ((), ())), preferred_element_type=F32
+def proj_body(count, n_tok, first, last, table, *refs):
+    slots, w_refs, acts_ref = refs[:count], refs[count:count + n_tok], refs[count + n_tok]
+    refs = refs[count + n_tok + 1:]
+    carry_ref = None
+    if not first:
+        carry_ref, refs = refs[0], refs[2:]
+    out_ref, own_ref = refs[:2]
+    step = pl.program_id(0)
+    for q, g_ref in enumerate(slots):
+
+        @pl.when((step == q) & (table[3 + 2 * q] == 1))
+        def _():
+            total = lax.dot_general(
+                jnp.concatenate([g_ref[s] for s in range(n_tok)], axis=1),
+                jnp.concatenate([w_ref[...] for w_ref in w_refs], axis=1),
+                (((1,), (1,)), ((), ())),
+                preferred_element_type=F32,
+            )
+            if q > 0:
+                total = total + out_ref[...]
+            elif not first:
+                total = total + carry_ref[...]
+            out_ref[...] = total
+            own_ref[0] = g_ref[table[1]]
+
+    if last:
+
+        @pl.when(step == count - 1)
+        def _():
+            attr = acts_ref[...].astype(F32) * out_ref[...]
+            out_ref[...] = attr
+            refs[2][...] = jnp.sum(attr, axis=1, keepdims=True)
+
+
+def project(table, slots, w_dec, acts, carry, last, n_feat):
+    n_tok, rows, width = slots[0].shape
+    feats = w_dec.shape[0]
+    first = carry is None
+    specs = [whole(a.shape) for a in slots]
+    for s in range(n_tok):
+        specs.append(
+            pl.BlockSpec((feats, width), lambda q, t, s=s: (0, (t[0] ^ s) * n_feat + t[2 + 2 * q]))
         )
-        total = term if total is None else total + term
-
-    @pl.when(step == 0)
-    def _():
-        out_ref[...] = total
-        sum_ref[...] = jnp.zeros_like(sum_ref)
-
-    @pl.when((step > 0) & (step < steps - 1))
-    def _():
-        out_ref[...] += total
-
-    @pl.when(step // n_tok == table[2])
-    def _():
-        term = (x_ref[0].astype(F32) - bias_ref[...]) * g_ref[0, table[1]].astype(F32)
-        sum_ref[...] += jnp.sum(term, axis=1, keepdims=True)
-
-    @pl.when(step == steps - 1)
-    def _():
-        attr = acts_ref[...].astype(F32) * (out_ref[...] + total)
-        out_ref[...] = attr
-        sum_ref[...] -= jnp.sum(attr, axis=1, keepdims=True)
-
-
-def project(table, rows_g, w_dec, acts, own_x, bias):
-    n_feat, n_tok, rows, width = rows_g.shape
-    feats = w_dec.shape[0]
-    specs = [pl.BlockSpec((1, n_tok, rows, width), lambda q, t: (q, 0, 0, 0))]
-    for s in range(n_tok):
-        specs.append(pl.BlockSpec((feats, width), lambda q, t, s=s: (0, (t[0] ^ s) * n_feat + q)))
-    specs += [
-        whole(acts.shape),
-        pl.BlockSpec((1, rows, width), lambda q, t: (t[2] * n_tok + q % n_tok, 0, 0)),
-        pl.BlockSpec((1, width), lambda q, t: (0, q % n_tok)),
+    specs.append(whole(acts.shape))
+    args = [*slots] + [w_dec] * n_tok + [acts]
+    aliases = {}
+    if not first:
+        specs += [whole(carry[0].shape), pl.BlockSpec(memory_space=pl.ANY)]
+        args += carry
+        aliases = {len(args): 1}
+    out_specs = [
+        whole((rows, feats)),
+        pl.BlockSpec((1, rows, width), lambda q, t: (t[2 + 2 * q], 0, 0)),
     ]
+    out_shape = [
+        jax.ShapeDtypeStruct((rows, feats), F32),
+        jax.ShapeDtypeStruct((n_feat, rows, width), BF16),
+    ]
+    if last:
+        out_specs.append(whole((rows, 1)))
+        out_shape.append(jax.ShapeDtypeStruct((rows, 1), F32))
+    count = len(slots)
     return pl.pallas_call(
-        functools.partial(proj_body, n_tok),
+        functools.partial(proj_body, count, n_tok, first, last),
+        grid_spec=pltpu.PrefetchScalarGridSpec(
+            num_scalar_prefetch=1, grid=(count,), in_specs=specs, out_specs=out_specs
+        ),
+        out_shape=out_shape,
+        input_output_aliases=aliases,
+        compiler_params=PARAMS,
+        cost_estimate=LIGHT if last else cost(rows, count * n_tok * width, feats),
+        name="project",
+    )(table, *args)
+
+
+def local_body(table, x_ref, g_ref, bias_ref, fa_ref, out_ref):
+    total = -fa_ref[...]
+    width = x_ref.shape[2]
+    for r in range(x_ref.shape[0]):
+        term = x_ref[r].astype(F32) - bias_ref[:, r * width:(r + 1) * width]
+        total += jnp.sum(term * g_ref[r].astype(F32), axis=1, keepdims=True)
+    out_ref[...] = total
+
+
+def local_terms(table, own_x, own_g, bias, fa_sum):
+    _, rows, width = own_x.shape
+    picked = pl.BlockSpec((bias.shape[1] // width, rows, width), lambda r, t: (t[0], 0, 0))
+    return pl.pallas_call(
+        local_body,
         grid_spec=pltpu.PrefetchScalarGridSpec(
             num_scalar_prefetch=1,
-            grid=(n_feat,),
-            in_specs=specs,
-            out_specs=[whole((rows, feats)), whole((rows, 1))],
+            grid=(1,),
+            in_specs=[picked, picked, whole(bias.shape), whole((rows, 1))],
+            out_specs=whole((rows, 1)),
         ),
-        out_shape=[
-            jax.ShapeDtypeStruct((rows, feats), F32),
-            jax.ShapeDtypeStruct((rows, 1), F32),
-        ],
+        out_shape=jax.ShapeDtypeStruct((rows, 1), F32),
         compiler_params=PARAMS,
         cost_estimate=LIGHT,
-        name="project",
-    )(table, rows_g, *[w_dec] * n_tok, acts, own_x, bias)
+        name="local_terms",
+    )(table, own_x, own_g, bias, fa_sum)
 
 
 def error_body(table, x_ref, bias_ref, *refs):
@@ -221,7 +272,7 @@
             grid=(2,),
             in_specs=[
                 pl.BlockSpec(
-                    (share // width // 2, rows, width), lambda r, t: (2 * t[2] + r, 0, 0)
+                    (share // width // 2, rows, width), lambda r, t: (2 * t[0] + r, 0, 0)
                 ),
                 pl.BlockSpec((1, share // 2), lambda r, t: (0, r)),
             ]
@@ -264,16 +315,24 @@
         blocks = [block(s) for s in range(n_tok)]
         return [jnp.stack([blocks[s] for s in stream]) for stream in streams]
 
-    own_sub = i ^ (j // (n_feat // n_tok))
+    own_tok = j // (n_feat // n_tok)
 
     def numbers(*values):
         return jnp.stack([jnp.asarray(v).astype(jnp.int32) for v in values])
 
     def table(*steps):
         sources = [2 * ((chip + chips - k) % chips) + (core ^ side) for k in steps for side in (0, 1)]
-        return numbers(i, own_sub, *sources)
-
-    own_table = numbers(i, own_sub, j % (n_feat // n_tok))
+        return numbers(i, own_tok, *sources)
+
+    def line_table(*sources):
+        values, seen = [i, i ^ own_tok], 0
+        for place, valid in sources:
+            seen = jnp.where(valid, place, seen)
+            for side in (0, 1):
+                values += [2 * seen + (core ^ side), valid]
+        return numbers(*values)
+
+    own_start = numbers(j % (n_feat // n_tok))
     blocks = feats // BLOCK
     block_ids = j * blocks + jnp.arange(blocks, dtype=jnp.int32)
     hits = jnp.any(active[:, :, None] == block_ids[None, None, :], axis=1).astype(F32)
@@ -283,58 +342,82 @@
     w4 = w_enc.reshape(n_tok, n_feat, width, feats)
 
     shard_x = exchange(resid, X_STREAMS)
-    shard_g = exchange(resid_grad, G_STREAMS)
 
     ring = [(a, (a + 1) % chips) for a in range(chips)]
     near_x = [shard_x]
     far_x = [[cross(a) for a in shard_x]]
-    carry = None
     for k in range(1, chips):
-        first, rest = near_x[-1]
-        first = send(first, ring)
-        rest = after(rest, first)
-        if k == 2:
-            rest = after(rest, *shard_g)
+        held = near_x[-1]
         if k == 3:
             slots = [near_x[0], far_x[0], near_x[1], far_x[1]]
             carry = encode(table(0, 1), slots, w4, bias, hit, None, X_STREAMS, False)
-            rest = after(rest, carry)
-        near_x.append([first, send(rest, ring)])
+            held = [*held[:-1], after(held[-1], shard_g, carry)]
+        near_x.append([send(a, ring) for a in held])
         far_x.append([cross(a) for a in near_x[-1]])
+        if k == 2:
+            shard_g, = exchange(after(resid_grad, near_x[2][0]), G_STREAMS)
+
+    up_pairs = [(a, a + 1) for a in range(chips - 1)]
+    down_pairs = [(a + 1, a) for a in range(chips - 1)]
+    shard_g = after(shard_g, near_x[-1])
+    up_1, down_1 = send(shard_g, up_pairs), send(shard_g, down_pairs)
+
     slots = [near_x[2], far_x[2], near_x[3], far_x[3]]
     acts, own_x = encode(table(2, 3), slots, w4, bias, hit, carry, X_STREAMS, True)
 
-    shard_g = after(shard_g[0], near_x[-1])
-    rows_g = lax.all_gather(shard_g, "feat", axis=0)
-
-    order = (3, 2, 1, 0)
-    dests = [2 * (chip ^ k) + (1 - core if side == 0 else core) for k in order for side in (0, 1)]
-    outs = decode(numbers(*dests), acts, w_dec, share, len(dests))
-    parts = {k: (outs[2 * n + 1], cross(outs[2 * n])) for n, k in enumerate(order)}
+    parts = {}
+    far_3, near_3 = decode(
+        numbers(2 * (chip ^ 3) + 1 - core, 2 * (chip ^ 3) + core), acts, w_dec, share, 2
+    )
+    up_1, down_1 = after((up_1, down_1), far_3)
+    parts[3] = (near_3, cross(far_3))
+    acts = after(acts, far_3)
+    for k in (2, 1, 0):
+        far_out, near_out = [
+            jnp.dot(
+                acts,
+                lax.dynamic_slice_in_dim(w_dec, (2 * (chip ^ k) + place) * share, share, 1),
+                preferred_element_type=F32,
+            ).astype(BF16)
+            for place in (1 - core, core)
+        ]
+        parts[k] = (near_out, cross(far_out))
 
     def pair_sum(k):
         return parts[k][0].astype(F32) + parts[k][1].astype(F32)
 
-    up_pairs = [(a, a + 1) for a in range(chips - 1)]
-    down_pairs = [(a + 1, a) for a in range(chips - 1)]
     sum_3, sum_1 = pair_sum(3), pair_sum(1)
     come = send(sum_3.astype(BF16), [(0, 1), (3, 2)])
+    up_2, down_2 = send(up_1, up_pairs[1:]), send(down_1, down_pairs[:-1])
+    two_g = up_2 + down_2
+    three_g = send(two_g, [(2, 3), (1, 0)])
+
     going = (pair_sum(2) + come.astype(F32)).astype(BF16)
     up = send(going, up_pairs[:2])
     down = send(going, down_pairs[1:])
+
+    slots = [shard_g, cross(shard_g), up_1, cross(up_1), down_1, cross(down_1)]
+    sources = line_table((chip, True), (chip - 1, chip >= 1), (chip + 1, chip <= chips - 2))
+    acts = after(acts, going)
+    carry = project(sources, slots, w_dec, acts, None, False, n_feat)
+
     going_up = (jnp.where(chip == 1, sum_3, sum_1) + up.astype(F32)).astype(BF16)
     going_down = (jnp.where(chip == 2, sum_3, sum_1) + down.astype(F32)).astype(BF16)
+    going_up, going_down = after((going_up, going_down), carry, parts[0])
     up = send(going_up, up_pairs)
     down = send(going_down, down_pairs)
 
-    feature_attr, attr = project(own_table, rows_g, w_dec, acts, own_x, b_row)
-    attr = attr.reshape(-1, TILE)
-    reach = 1
-    while reach < n_feat:
-        attr = attr + lax.ppermute(attr, "feat", [(a, a ^ reach) for a in range(n_feat)])
-        reach *= 2
-
-    error = final_error(own_table, own_x, b_row, [*parts[0], up, down])
+    slots = [two_g, cross(two_g), three_g, cross(three_g)]
+    sources = line_table((chip ^ 2, True), (chip ^ 3, (chip == 0) | (chip == chips - 1)))
+    acts = after(acts, going_up, going_down)
+    feature_attr, own_g, fa_sum = project(sources, slots, w_dec, acts, carry, True, n_feat)
+    attr = local_terms(own_start, own_x, own_g, b_row, fa_sum).reshape(-1, TILE)
+    attr = attr + cross(attr)
+    others = [send(attr, [(a, a ^ k) for a in range(chips)]) for k in range(1, chips)]
+    for other in others:
+        attr = attr + other
+
+    error = final_error(own_start, own_x, b_row, [*parts[0], up, down])
     return feature_attr, error, attr.reshape(rows)
 
 

time: 180 us -> 159 us (0.88)
  waiting for transfers between devices: 68.6 us -> 32.2 us
  starting transfers between devices: 35.3 us -> 53.2 us
  between operations: 14.4 us -> 1.42 us
  matrix products: 0 us -> 12.2 us
    ppermute x11 -> x22, waiting for transfers between devices: 55.8 us -> 22.1 us  [send(): return lax.ppermute(array, 'feat', along(pairs))]
    ppermute x11 -> x22, starting transfers between devices: 21.2 us -> 39.7 us  [send(): return lax.ppermute(array, 'feat', along(pairs))]
    dot_general x0 -> x6, matrix products: none -> 12.2 us  [line_program(): jnp.dot(acts, lax.dynamic_slice_in_dim(w_dec, (2 * (chip ^ k) + place) *...]
    pallas_call x1, Pallas kernels: 11.5 us -> 4.35 us  [decode(): pl.pallas_call(dec_body, grid_spec=pltpu.PrefetchScalarGridSpec(num_scala...]
    pallas_call x1 -> x3, Pallas kernels: 12.1 us -> 18.6 us  [the longest x2 16.5 us: project(): pl.pallas_call(functools.partial(proj_body, count, n_tok, first, last), g...]
    ppermute x3 -> x0, starting transfers between devices: 4.16 us -> none  [line_program(): lax.ppermute(attr, 'feat', [(a, a ^ reach) for a in range(n_feat)])]
    ppermute x3 -> x0, waiting for transfers between devices: 2.67 us -> none  [line_program(): lax.ppermute(attr, 'feat', [(a, a ^ reach) for a in range(n_feat)])]
    ppermute x12 -> x22, starting transfers between devices: 1.74 us -> 3.92 us  [cross(): return lax.ppermute(array, 'feat', [(a, a ^ 1) for a in range(n_feat)])]
  transfers between devices with their start and end apart: 33 -> 50, of which waited for: 16 -> 14; matrix products, arithmetic and copies ran while one was open for 7% -> 17% of each run, Pallas kernels for 19% -> 24%
where the time goes in v3:
time: 159 us; the launch traced here: 158 us
  starting transfers between devices  53.2 us (33%)
  Pallas kernels  40.3 us (25%)
  waiting for transfers between devices  32.2 us (20%)
  matrix products  12.2 us (8%)
  local copies, waits for them, and re-layouts  10.5 us (7%)
  other arithmetic  8.25 us (5%)
    ppermute x22, starting transfers between devices, send(): return lax.ppermute(array, 'feat', along(pairs))  39.7 us
    ppermute x22, waiting for transfers between devices, send(): return lax.ppermute(array, 'feat', along(pairs))  22.1 us
    pallas_call x2, Pallas kernels, project(): pl.pallas_call(functools.partial(proj_body, count, n_tok, first, last), g...  16.5 us
    pallas_call x2, Pallas kernels, encode(): pl.pallas_call(functools.partial(enc_body, streams, count, first, last),...  14.6 us
    dot_general x6, matrix products, line_program(): jnp.dot(acts, lax.dynamic_slice_in_dim(w_dec, (2 * (chip ^ k) + place) *...  12.2 us
    ppermute x6, starting transfers between devices, block(): return lax.ppermute(mine, 'tok', [(a, a ^ s) for a in range(n_tok)])  9.61 us
    ppermute x6, waiting for transfers between devices, block(): return lax.ppermute(mine, 'tok', [(a, a ^ s) for a in range(n_tok)])  8.95 us
    pallas_call x1, Pallas kernels, decode(): pl.pallas_call(dec_body, grid_spec=pltpu.PrefetchScalarGridSpec(num_scala...  4.35 us
  transfers between devices with their start and end apart: 50, of which 14 were waited for; matrix products, arithmetic and copies ran while one was open for 17% of the time, Pallas kernels for 24%

profile of v3, /device:TPU:0, one launch (start us, length us, event | category | flops | bytes accessed | tf_op | source)
XLA Modules:
  0.0 158.0 jit_solution(8134539929409320432)
XLA Ops:
  1.8 3.0 %collective-permute-start.6 = (bf16[256,256]{1,0:T(8,128)(2,1)S(1)}, bf16[256,256]{1,0:T(8,128)(2,1)S(1)}, u32[]{:S(2)}, u32[]{:S(2)}) collective-permute-start(bf16[256,256]{1,0:T(8,128)(2,1)S(1)} %get-tuple-element.48), channel_id=1, source_target_pairs={{0,8},{8,0},{16,24},{24,16},{1,9},{9,1},{17,25},{25,17},{2,10},{10... | collective-permute-start | bytes 393224 | tf_op jit(solution)/shard_map/ppermute | solution.py:313
  6.3 1.6 collective-permute-start
  9.8 1.6 %collective-permute-start.8 = (bf16[2,256,256]{2,1,0:T(8,128)(2,1)S(1)}, bf16[2,256,256]{2,1,0:T(8,128)(2,1)S(1)}, u32[]{:S(2)}, u32[]{:S(2)}) collective-permute-start(bf16[2,256,256]{2,1,0:T(8,128)(2,1)S(1)} %pad_maximum_fusion.1.refs_1_), channel_id=1, source_target_pairs={{0,2},{1,3},{2,4},{3,5},{4,6},{5,7},{6,0},{7,1},{8,10},{9,11},{10,... | collective-permute-start | bytes 786440 | tf_op jit(solution)/shard_map/ppermute | solution.py:303
  14.5 2.8 %collective-permute-done.11 = bf16[256,256]{1,0:T(8,128)(2,1)S(1)} collective-permute-done((bf16[256,256]{1,0:T(8,128)(2,1)S(1)}, bf16[256,256]{1,0:T(8,128)(2,1)S(1)}, u32[]{:S(2)}, u32[]{:S(2)}) %collective-permute-start.11) | collective-permute-done | bytes 131104 | tf_op jit(solution)/shard_map/ppermute | solution.py:313
  18.9 4.0 %collective-permute-done.1.refs_0_ = bf16[1,256,256]{2,1,0:T(8,128)(2,1)S(1)} collective-permute-done((bf16[1,256,256]{2,1,0:T(8,128)(2,1)S(1)}, bf16[1,256,256]{2,1,0:T(8,128)(2,1)S(1)}, u32[]{:S(2)}, u32[]{:S(2)}) %collective-permute-start.1) | collective-permute-done | bytes 131104 | tf_op jit(solution)/shard_map/ppermute | solution.py:303
  27.0 1.9 %collective-permute-start.2 = (bf16[256,256]{1,0:T(8,128)(2,1)S(1)}, bf16[256,256]{1,0:T(8,128)(2,1)S(1)}, u32[]{:S(2)}, u32[]{:S(2)}) collective-permute-start(bf16[256,256]{1,0:T(8,128)(2,1)S(1)} %get-tuple-element.54), channel_id=1, source_target_pairs={{0,8},{8,0},{16,24},{24,16},{1,9},{9,1},{17,25},{25,17},{2,10},{10... | collective-permute-start | bytes 393224 | tf_op jit(solution)/shard_map/ppermute | solution.py:313
  28.8 4.2 %collective-permute-done.3 = bf16[256,256]{1,0:T(8,128)(2,1)} collective-permute-done((bf16[256,256]{1,0:T(8,128)(2,1)S(1)}, bf16[256,256]{1,0:T(8,128)(2,1)}, u32[]{:S(2)}, u32[]{:S(2)}) %collective-permute-start.3) | collective-permute-done | bytes 131104 | tf_op jit(solution)/shard_map/ppermute | solution.py:313
  37.2 1.6 collective-permute-start.13
  39.9 2.0 %collective-permute-start.5 = (bf16[1,256,256]{2,1,0:T(8,128)(2,1)S(1)}, bf16[1,256,256]{2,1,0:T(8,128)(2,1)S(1)}, u32[]{:S(2)}, u32[]{:S(2)}) collective-permute-start(bf16[1,256,256]{2,1,0:T(8,128)(2,1)S(1)} %collective-permute-done.1.refs_0_), channel_id=1, source_target_pairs={{0,2},{1,3},{2,4},{3,5},{4,6},{5,7},{6,0},{7,1},{8,10},{9,11},{10,... | collective-permute-start | bytes 393224 | tf_op jit(solution)/shard_map/ppermute | solution.py:303
  42.7 7.2 %encode.2 = (f32[256,640]{1,0:T(8,128)}, bf16[8,256,256]{2,1,0:T(8,128)(2,1)}) custom-call(s32[6]{0:T(128)} %stack.167.table, bf16[1,256,256]{2,1,0:T(8,128)(2,1)} %copy-done.12, bf16[2,256,256]{2,1,0:T(8,128)(2,1)} %copy-done.4, bf16[1,256,256]{2,1,0:T(8,128)(2,1)} %bitcast.60, bf16[1,256,256]{2,1,0:T(8,128)(2,1)} %copy-done.24, ...), custom_call_target="tpu_custom_call" | custom-call | flops 1342177280 | bytes 7340032 | tf_op jit(solution)/shard_map/encode/pallas_call | solution.py:100
  51.6 6.0 %collective-permute-done.20.refs_8_ = bf16[1,256,256]{2,1,0:T(8,128)(2,1)S(1)} collective-permute-done((bf16[1,256,256]{2,1,0:T(8,128)(2,1)S(1)}, bf16[1,256,256]{2,1,0:T(8,128)(2,1)S(1)}, u32[]{:S(2)}, u32[]{:S(2)}) %collective-permute-start.20) | collective-permute-done | bytes 131104 | tf_op jit(solution)/shard_map/ppermute | solution.py:303
  63.1 7.4 %encode.3 = (bf16[256,640]{1,0:T(8,128)(2,1)}, bf16[8,256,256]{2,1,0:T(8,128)(2,1)}) custom-call(s32[6]{0:T(128)} %stack.175.table, bf16[1,256,256]{2,1,0:T(8,128)(2,1)} %copy-done.21, bf16[2,256,256]{2,1,0:T(8,128)(2,1)} %copy-done.14, bf16[1,256,256]{2,1,0:T(8,128)(2,1)} %copy-done.28, ...), custom_call_target="tpu_custom_call", output_to_operand_aliasing={{1}: (17, {})} | custom-call | flops 1 | bytes 1 | tf_op jit(solution)/shard_map/encode/pallas_call | solution.py:100
  70.5 4.4 %decode.1 = (bf16[256,1024]{1,0:T(8,128)(2,1)}, bf16[256,1024]{1,0:T(8,128)(2,1)}) custom-call(s32[2]{0:T(128)} %pad_add_fusion.table, bf16[256,640]{1,0:T(8,128)(2,1)} %get-tuple-element.40.acts_ref.refs_10_.refs_8_, bf16[640,8192]{1,0:T(8,128)(2,1)} %refs_7_.3), custom_call_target="tpu_custom_call" | custom-call | flops 1 | bytes 1 | tf_op jit(solution)/shard_map/decode/pallas_call | solution.py:136
  76.1 1.9 %fusion.18 = bf16[256,1024]{1,0:T(8,128)(2,1)S(1)} fusion(bf16[256,640]{1,0:T(8,128)(2,1)S(1)} %copy-done, bf16[640,8192]{1,0:T(8,128)(2,1)} %refs_7_.3, s32[]{:T(128)S(6)} %select_n.110), kind=kOutput, calls=%fused_computation.14 | convolution fusion | flops 335806464 | bytes 2162692 | tf_op jit(solution)/shard_map/dot_general | solution.py:377
  81.8 6.2 %collective-permute-start.36 = (bf16[256,1024]{1,0:T(8,128)(2,1)S(1)}, bf16[256,1024]{1,0:T(8,128)(2,1)S(1)}, u32[]{:S(2)}, u32[]{:S(2)}) collective-permute-start(bf16[256,1024]{1,0:T(8,128)(2,1)S(1)} %fusion.36), channel_id=1, source_target_pairs={{0,2},{1,3},{6,4},{7,5},{8,10},{9,11},{14,12},{15,13},{16,18},{17,... | collective-permute-start | bytes 1572872 | tf_op jit(solution)/shard_map/ppermute | solution.py:303
  88.0 1.9 %fusion.27 = bf16[256,1024]{1,0:T(8,128)(2,1)S(1)} fusion(bf16[256,640]{1,0:T(8,128)(2,1)S(1)} %copy-done, bf16[640,8192]{1,0:T(8,128)(2,1)} %refs_7_.3, s32[]{:T(128)S(6)} %select_n.113), kind=kOutput, calls=%fused_computation.17 | convolution fusion | flops 335806464 | bytes 2162692 | tf_op jit(solution)/shard_map/dot_general | solution.py:377
  89.9 1.9 %fusion.15 = f32[256,1024]{1,0:T(8,128)S(1)} fusion(bf16[256,640]{1,0:T(8,128)(2,1)S(1)} %copy-done, bf16[640,8192]{1,0:T(8,128)(2,1)} %refs_7_.3, s32[]{:T(128)S(6)} %select_n.109), kind=kOutput, calls=%fused_computation.13 | convolution fusion | flops 336068608 | bytes 2686980 | tf_op jit(solution)/shard_map/dot_general | solution.py:377
  91.9 1.9 %fusion.33 = bf16[256,1024]{1,0:T(8,128)(2,1)S(1)} fusion(bf16[256,640]{1,0:T(8,128)(2,1)S(1)} %copy-done, bf16[640,8192]{1,0:T(8,128)(2,1)} %refs_7_.3, s32[]{:T(128)S(6)} %select_n.120), kind=kOutput, calls=%fused_computation.19 | convolution fusion | flops 335806464 | bytes 2162692 | tf_op jit(solution)/shard_map/dot_general | solution.py:377
  93.8 3.3 %collective-permute-done.30 = bf16[4,256,256]{2,1,0:T(8,128)(2,1)S(1)} collective-permute-done((bf16[4,256,256]{2,1,0:T(8,128)(2,1)S(1)}, bf16[4,256,256]{2,1,0:T(8,128)(2,1)S(1)}, u32[]{:S(2)}, u32[]{:S(2)}) %collective-permute-start.30) | collective-permute-done | bytes 524320 | tf_op jit(solution)/shard_map/ppermute | solution.py:303
  97.8 1.7 %collective-permute-done.36 = bf16[256,1024]{1,0:T(8,128)(2,1)S(1)} collective-permute-done((bf16[256,1024]{1,0:T(8,128)(2,1)S(1)}, bf16[256,1024]{1,0:T(8,128)(2,1)S(1)}, u32[]{:S(2)}, u32[]{:S(2)}) %collective-permute-start.36) | collective-permute-done | bytes 524320 | tf_op jit(solution)/shard_map/ppermute | solution.py:303
  101.8 4.6 %collective-permute-start.38 = (bf16[256,1024]{1,0:T(8,128)(2,1)}, bf16[256,1024]{1,0:T(8,128)(2,1)S(1)}, u32[]{:S(2)}, u32[]{:S(2)}) collective-permute-start(bf16[256,1024]{1,0:T(8,128)(2,1)} %add_convert_fusion.2), channel_id=1, source_target_pairs={{0,2},{1,3},{2,4},{3,5},{8,10},{9,11},{10,12},{11,13},{16,18},{17,... | collective-permute-start | bytes 1572872 | tf_op jit(solution)/shard_map/ppermute | solution.py:303
  107.9 2.7 %fusion.30.refs_0_ = bf16[256,1024]{1,0:T(8,128)(2,1)} fusion(bf16[256,640]{1,0:T(8,128)(2,1)S(1)} %copy-done, bf16[640,8192]{1,0:T(8,128)(2,1)} %refs_7_.3, s32[]{:T(128)S(6)} %select_n.119), kind=kOutput, calls=%fused_computation.18 | convolution fusion | flops 335806464 | bytes 2162692 | tf_op jit(solution)/shard_map/dot_general | solution.py:377
  110.6 1.9 %fusion.24 = f32[256,1024]{1,0:T(8,128)S(1)} fusion(bf16[256,640]{1,0:T(8,128)(2,1)S(1)} %copy-done, bf16[640,8192]{1,0:T(8,128)(2,1)} %refs_7_.3, s32[]{:T(128)S(6)} %select_n.112), kind=kOutput, calls=%fused_computation.16 | convolution fusion | flops 336068608 | bytes 2686980 | tf_op jit(solution)/shard_map/dot_general | solution.py:377
  114.7 8.9 %project.2 = (f32[256,640]{1,0:T(8,128)}, bf16[8,256,256]{2,1,0:T(8,128)(2,1)}) custom-call(s32[14]{0:T(128)} %stack.186.table, bf16[4,256,256]{2,1,0:T(8,128)(2,1)} %copy-done.2, bf16[4,256,256]{2,1,0:T(8,128)(2,1)} %copy-done.8, bf16[4,256,256]{2,1,0:T(8,128)(2,1)} %copy-done.5, bf16[4,256,256]{2,1,0:T(8,128)(2,1)} %copy-done.10, ...), custom_call_target="tpu_custom_call" | custom-call | flops 2013265920 | bytes 11010048 | tf_op jit(solution)/shard_map/project/pallas_call | solution.py:213
  123.7 1.6 %add_convert_fusion = (bf16[256,1024]{1,0:T(8,128)(2,1)S(1)}, bf16[256,1024]{1,0:T(8,128)(2,1)S(1)}) fusion(bf16[256,1024]{1,0:T(8,128)(2,1)} %collective-permute-done.39, bf16[256,1024]{1,0:T(8,128)(2,1)S(1)} %collective-permute-done.35, bf16[256,1024]{1,0:T(8,128)(2,1)S(1)} %copy-done.3, f32[256,1024]{1,0:T(8,128)S(1)} %fusion.24, ...), kind=kLoop, calls=%fused_computation.20 | loop fusion | flops 3407872 | bytes 4718594 | tf_op jit(solution)/shard_map/convert_element_type | solution.py:405
  125.4 3.1 %collective-permute-start.44 = (bf16[256,1024]{1,0:T(8,128)(2,1)S(1)}, bf16[256,1024]{1,0:T(8,128)(2,1)S(1)}, u32[]{:S(2)}, u32[]{:S(2)}) collective-permute-start(bf16[256,1024]{1,0:T(8,128)(2,1)S(1)} %get-tuple-element.38), channel_id=1, source_target_pairs={{0,2},{1,3},{2,4},{3,5},{4,6},{5,7},{8,10},{9,11},{10,12},{11,13},... | collective-permute-start | bytes 1572872 | tf_op jit(solution)/shard_map/ppermute | solution.py:303
  131.3 7.6 %project.3 = (f32[256,640]{1,0:T(8,128)}, bf16[8,256,256]{2,1,0:T(8,128)(2,1)}, f32[256,1]{1,0:T(8,128)}) custom-call(s32[10]{0:T(128)} %stack.151.table, bf16[4,256,256]{2,1,0:T(8,128)(2,1)} %copy-done.1, bf16[4,256,256]{2,1,0:T(8,128)(2,1)} %copy-done.9, bf16[4,256,256]{2,1,0:T(8,128)(2,1)} %copy-done.7, ...), custom_call_target="tpu_custom_call", output_to_operand_aliasing={{1}: (11, {})} | custom-call | flops 1 | bytes 1 | tf_op jit(solution)/shard_map/project/pallas_call | solution.py:213
  138.8 2.1 %local_terms.1 = f32[256,1]{1,0:T(8,128)} custom-call(s32[1]{0:T(128)} %bitcast.35.table, bf16[8,256,256]{2,1,0:T(8,128)(2,1)} %get-tuple-element.42.x_ref, bf16[8,256,256]{2,1,0:T(8,128)(2,1)} %get-tuple-element.43.g_ref, f32[1,1024]{1,0:T(1,128)} %bitcast.66, f32[256,1]{1,0:T(8,128)} %get-tuple-element.44.fa_ref), custom_call_target="tpu_custom_call" | custom-call | flops 1 | bytes 1 | tf_op jit(solution)/shard_map/local_terms/pallas_call | solution.py:238
  143.2 2.6 %collective-permute-start.47 = (f32[2,128]{1,0:T(2,128)S(1)}, f32[2,128]{1,0:T(2,128)S(1)}, u32[]{:S(2)}, u32[]{:S(2)}) collective-permute-start(f32[2,128]{1,0:T(2,128)S(1)} %bitcast_add_fusion), channel_id=1, source_target_pairs={{0,2},{1,3},{2,0},{3,1},{4,6},{5,7},{6,4},{7,5},{8,10},{9,11},{10,... | collective-permute-start | bytes 3080 | tf_op jit(solution)/shard_map/ppermute | solution.py:303
  145.8 2.8 %collective-permute-start.48 = (f32[2,128]{1,0:T(2,128)S(1)}, f32[2,128]{1,0:T(2,128)S(1)}, u32[]{:S(2)}, u32[]{:S(2)}) collective-permute-start(f32[2,128]{1,0:T(2,128)S(1)} %bitcast_add_fusion), channel_id=1, source_target_pairs={{0,4},{1,5},{2,6},{3,7},{4,0},{5,1},{6,2},{7,3},{8,12},{9,13},{10,... | collective-permute-start | bytes 3080 | tf_op jit(solution)/shard_map/ppermute | solution.py:303
  150.3 3.7 %collective-permute-done.49 = f32[2,128]{1,0:T(2,128)S(1)} collective-permute-done((f32[2,128]{1,0:T(2,128)S(1)}, f32[2,128]{1,0:T(2,128)S(1)}, u32[]{:S(2)}, u32[]{:S(2)}) %collective-permute-start.49) | collective-permute-done | bytes 1056 | tf_op jit(solution)/shard_map/ppermute | solution.py:303
  155.3 2.7 %final_error.1 = f32[256,1024]{1,0:T(8,128)} custom-call(s32[1]{0:T(128)} %bitcast.35.table, bf16[8,256,256]{2,1,0:T(8,128)(2,1)} %get-tuple-element.42.x_ref, f32[1,1024]{1,0:T(1,128)} %bitcast.67, bf16[256,1024]{1,0:T(8,128)(2,1)} %fusion.30.refs_0_, bf16[256,1024]{1,0:T(8,128)(2,1)} %collective-permute-done.43.refs_1_, bf16[256,1024]{1,0:T(8,128)(2,1)} %copy-done.13, ...), custom_call_target="tpu_custom_call" | custom-call | flops 1 | bytes 1 | tf_op jit(solution)/shard_map/final_error/pallas_call | solution.py:268
  (173 shorter events, 45.8 us)
Async XLA Ops:
  9.8 13.1 %collective-permute-start.8 = (bf16[2,256,256]{2,1,0:T(8,128)(2,1)S(1)}, bf16[2,256,256]{2,1,0:T(8,128)(2,1)S(1)}, u32[]{:S(2)}, u32[]{:S(2)}) collective-permute-start(bf16[2,256,256]{2,1,0:T(8,128)(2,1)S(1)} %pad_maximum_fusion.1.refs_1_), channel_id=1, source_target_pairs={{0,2},{1,3},{2,4},{3,5},{4,6},{5,7},{6,0},{7,1},{8,10},{9,11},{10,... | collective-permute-start | bytes 786440 | tf_op jit(solution)/shard_map/ppermute | solution.py:303
  13.1 9.8 %collective-permute-start.1 = (bf16[1,256,256]{2,1,0:T(8,128)(2,1)S(1)}, bf16[1,256,256]{2,1,0:T(8,128)(2,1)S(1)}, u32[]{:S(2)}, u32[]{:S(2)}) collective-permute-start(bf16[1,256,256]{2,1,0:T(8,128)(2,1)S(1)} %collective-permute-done.refs_6_), channel_id=1, source_target_pairs={{0,2},{1,3},{2,4},{3,5},{4,6},{5,7},{6,0},{7,1},{8,10},{9,11},{10,... | collective-permute-start | bytes 393224 | tf_op jit(solution)/shard_map/ppermute | solution.py:303
  14.5 9.7 %collective-permute-start.14 = (bf16[1,256,256]{2,1,0:T(8,128)(2,1)S(1)}, bf16[1,256,256]{2,1,0:T(8,128)(2,1)S(1)}, u32[]{:S(2)}, u32[]{:S(2)}) collective-permute-start(bf16[1,256,256]{2,1,0:T(8,128)(2,1)S(1)} %get-tuple-element.49.refs_0_), channel_id=1, source_target_pairs={{0,1},{1,0},{2,3},{3,2},{4,5},{5,4},{6,7},{7,6},{8,9},{9,8},{10,11... | collective-permute-start | bytes 393224 | tf_op jit(solution)/shard_map/ppermute | solution.py:306
  22.9 10.6 %collective-permute-start.9 = (bf16[2,256,256]{2,1,0:T(8,128)(2,1)S(1)}, bf16[2,256,256]{2,1,0:T(8,128)(2,1)S(1)}, u32[]{:S(2)}, u32[]{:S(2)}) collective-permute-start(bf16[2,256,256]{2,1,0:T(8,128)(2,1)S(1)} %collective-permute-done.8.refs_7_), channel_id=1, source_target_pairs={{0,2},{1,3},{2,4},{3,5},{4,6},{5,7},{6,0},{7,1},{8,10},{9,11},{10,... | collective-permute-start | bytes 786440 | tf_op jit(solution)/shard_map/ppermute | solution.py:303
  26.9 13.0 %collective-permute-start.15 = (bf16[2,256,256]{2,1,0:T(8,128)(2,1)S(1)}, bf16[2,256,256]{2,1,0:T(8,128)(2,1)S(1)}, u32[]{:S(2)}, u32[]{:S(2)}) collective-permute-start(bf16[2,256,256]{2,1,0:T(8,128)(2,1)S(1)} %pad_maximum_fusion.1.refs_1_), channel_id=1, source_target_pairs={{0,1},{1,0},{2,3},{3,2},{4,5},{5,4},{6,7},{7,6},{8,9},{9,8},{10,11... | collective-permute-start | bytes 786440 | tf_op jit(solution)/shard_map/ppermute | solution.py:306
  27.0 10.2 %collective-permute-start.2 = (bf16[256,256]{1,0:T(8,128)(2,1)S(1)}, bf16[256,256]{1,0:T(8,128)(2,1)S(1)}, u32[]{:S(2)}, u32[]{:S(2)}) collective-permute-start(bf16[256,256]{1,0:T(8,128)(2,1)S(1)} %get-tuple-element.54), channel_id=1, source_target_pairs={{0,8},{8,0},{16,24},{24,16},{1,9},{9,1},{17,25},{25,17},{2,10},{10... | collective-permute-start | bytes 393224 | tf_op jit(solution)/shard_map/ppermute | solution.py:313
  33.0 8.9 %collective-permute-start.19 = (bf16[1,256,256]{2,1,0:T(8,128)(2,1)S(1)}, bf16[1,256,256]{2,1,0:T(8,128)(2,1)}, u32[]{:S(2)}, u32[]{:S(2)}) collective-permute-start(bf16[1,256,256]{2,1,0:T(8,128)(2,1)S(1)} %collective-permute-done.12.refs_8_), channel_id=1, source_target_pairs={{0,1},{1,0},{2,3},{3,2},{4,5},{5,4},{6,7},{7,6},{8,9},{9,8},{10,11... | collective-permute-start | bytes 393224 | tf_op jit(solution)/shard_map/ppermute | solution.py:306
  33.6 17.2 %collective-permute-start.10 = (bf16[2,256,256]{2,1,0:T(8,128)(2,1)S(1)}, bf16[2,256,256]{2,1,0:T(8,128)(2,1)S(1)}, u32[]{:S(2)}, u32[]{:S(2)}) collective-permute-start(bf16[2,256,256]{2,1,0:T(8,128)(2,1)S(1)} %collective-permute-done.9.refs_1_), channel_id=1, source_target_pairs={{0,2},{1,3},{2,4},{3,5},{4,6},{5,7},{6,0},{7,1},{8,10},{9,11},{10,... | collective-permute-start | bytes 786440 | tf_op jit(solution)/shard_map/ppermute | solution.py:303
  37.2 12.6 %collective-permute-start.13 = (bf16[1,256,256]{2,1,0:T(8,128)(2,1)S(1)}, bf16[1,256,256]{2,1,0:T(8,128)(2,1)S(1)}, u32[]{:S(2)}, u32[]{:S(2)}) collective-permute-start(bf16[1,256,256]{2,1,0:T(8,128)(2,1)S(1)} %collective-permute-done.12.refs_8_), channel_id=1, source_target_pairs={{0,2},{1,3},{2,4},{3,5},{4,6},{5,7},{6,0},{7,1},{8,10},{9,11},{10,... | collective-permute-start | bytes 393224 | tf_op jit(solution)/shard_map/ppermute | solution.py:303
  39.9 11.2 %collective-permute-start.5 = (bf16[1,256,256]{2,1,0:T(8,128)(2,1)S(1)}, bf16[1,256,256]{2,1,0:T(8,128)(2,1)S(1)}, u32[]{:S(2)}, u32[]{:S(2)}) collective-permute-start(bf16[1,256,256]{2,1,0:T(8,128)(2,1)S(1)} %collective-permute-done.1.refs_0_), channel_id=1, source_target_pairs={{0,2},{1,3},{2,4},{3,5},{4,6},{5,7},{6,0},{7,1},{8,10},{9,11},{10,... | collective-permute-start | bytes 393224 | tf_op jit(solution)/shard_map/ppermute | solution.py:303
  41.9 9.4 %collective-permute-start.23 = (bf16[1,256,256]{2,1,0:T(8,128)(2,1)S(1)}, bf16[1,256,256]{2,1,0:T(8,128)(2,1)S(1)}, u32[]{:S(2)}, u32[]{:S(2)}) collective-permute-start(bf16[1,256,256]{2,1,0:T(8,128)(2,1)S(1)} %collective-permute-done.1.refs_0_), channel_id=1, source_target_pairs={{0,1},{1,0},{2,3},{3,2},{4,5},{5,4},{6,7},{7,6},{8,9},{9,8},{10,11... | collective-permute-start | bytes 393224 | tf_op jit(solution)/shard_map/ppermute | solution.py:306
  50.5 11.1 %collective-permute-start.24 = (bf16[2,256,256]{2,1,0:T(8,128)(2,1)S(1)}, bf16[2,256,256]{2,1,0:T(8,128)(2,1)S(1)}, u32[]{:S(2)}, u32[]{:S(2)}) collective-permute-start(bf16[2,256,256]{2,1,0:T(8,128)(2,1)S(1)} %collective-permute-done.9.refs_1_), channel_id=1, source_target_pairs={{0,1},{1,0},{2,3},{3,2},{4,5},{5,4},{6,7},{7,6},{8,9},{9,8},{10,11... | collective-permute-start | bytes 786440 | tf_op jit(solution)/shard_map/ppermute | solution.py:306
  50.8 10.9 %collective-permute-start.27 = (bf16[2,256,256]{2,1,0:T(8,128)(2,1)S(1)}, bf16[2,256,256]{2,1,0:T(8,128)(2,1)S(1)}, u32[]{:S(2)}, u32[]{:S(2)}) collective-permute-start(bf16[2,256,256]{2,1,0:T(8,128)(2,1)S(1)} %collective-permute-done.10.refs_7_), channel_id=1, source_target_pairs={{0,1},{1,0},{2,3},{3,2},{4,5},{5,4},{6,7},{7,6},{8,9},{9,8},{10,11... | collective-permute-start | bytes 786440 | tf_op jit(solution)/shard_map/ppermute | solution.py:306
  51.3 9.0 %collective-permute-start.25 = (bf16[1,256,256]{2,1,0:T(8,128)(2,1)S(1)}, bf16[1,256,256]{2,1,0:T(8,128)(2,1)S(1)}, u32[]{:S(2)}, u32[]{:S(2)}) collective-permute-start(bf16[1,256,256]{2,1,0:T(8,128)(2,1)S(1)} %collective-permute-done.13.refs_2_), channel_id=1, source_target_pairs={{0,1},{1,0},{2,3},{3,2},{4,5},{5,4},{6,7},{7,6},{8,9},{9,8},{10,11... | collective-permute-start | bytes 393224 | tf_op jit(solution)/shard_map/ppermute | solution.py:306
  59.0 19.5 %collective-permute-start.21 = (bf16[4,256,256]{2,1,0:T(8,128)(2,1)S(1)}, bf16[4,256,256]{2,1,0:T(8,128)(2,1)S(1)}, u32[]{:S(2)}, u32[]{:S(2)}) collective-permute-start(bf16[4,256,256]{2,1,0:T(8,128)(2,1)S(1)} %pad_maximum_fusion.refs_0_), channel_id=1, source_target_pairs={{0,2},{1,3},{2,4},{3,5},{4,6},{5,7},{8,10},{9,11},{10,12},{11,13},... | collective-permute-start | bytes 1572872 | tf_op jit(solution)/shard_map/ppermute | solution.py:303
  60.3 18.2 %collective-permute-start.22 = (bf16[4,256,256]{2,1,0:T(8,128)(2,1)S(1)}, bf16[4,256,256]{2,1,0:T(8,128)(2,1)S(1)}, u32[]{:S(2)}, u32[]{:S(2)}) collective-permute-start(bf16[4,256,256]{2,1,0:T(8,128)(2,1)S(1)} %pad_maximum_fusion.refs_0_), channel_id=1, source_target_pairs={{2,0},{3,1},{4,2},{5,3},{6,4},{7,5},{10,8},{11,9},{12,10},{13,11},... | collective-permute-start | bytes 1572872 | tf_op jit(solution)/shard_map/ppermute | solution.py:303
  76.0 25.8 %collective-permute-start.40 = (bf16[4,256,256]{2,1,0:T(8,128)(2,1)S(1)}, bf16[4,256,256]{2,1,0:T(8,128)(2,1)S(1)}, u32[]{:S(2)}, u32[]{:S(2)}) collective-permute-start(bf16[4,256,256]{2,1,0:T(8,128)(2,1)S(1)} %pad_maximum_fusion.refs_0_), channel_id=1, source_target_pairs={{0,1},{1,0},{2,3},{3,2},{4,5},{5,4},{6,7},{7,6},{8,9},{9,8},{10,11... | collective-permute-start | bytes 1572872 | tf_op jit(solution)/shard_map/ppermute | solution.py:306
  78.0 19.2 %collective-permute-start.34 = (bf16[256,1024]{1,0:T(8,128)(2,1)S(1)}, bf16[256,1024]{1,0:T(8,128)(2,1)S(1)}, u32[]{:S(2)}, u32[]{:S(2)}) collective-permute-start(bf16[256,1024]{1,0:T(8,128)(2,1)S(1)} %fusion.18), channel_id=1, source_target_pairs={{0,1},{1,0},{2,3},{3,2},{4,5},{5,4},{6,7},{7,6},{8,9},{9,8},{10,11... | collective-permute-start | bytes 1572872 | tf_op jit(solution)/shard_map/ppermute | solution.py:306
  78.5 13.3 %collective-permute-start.29 = (bf16[4,256,256]{2,1,0:T(8,128)(2,1)S(1)}, bf16[4,256,256]{2,1,0:T(8,128)(2,1)S(1)}, u32[]{:S(2)}, u32[]{:S(2)}) collective-permute-start(bf16[4,256,256]{2,1,0:T(8,128)(2,1)S(1)} %collective-permute-done.21.refs_2_), channel_id=1, source_target_pairs={{2,4},{3,5},{4,6},{5,7},{10,12},{11,13},{12,14},{13,15},{18,20},{1... | collective-permute-start | bytes 1572872 | tf_op jit(solution)/shard_map/ppermute | solution.py:303
  79.2 17.8 %collective-permute-start.30 = (bf16[4,256,256]{2,1,0:T(8,128)(2,1)S(1)}, bf16[4,256,256]{2,1,0:T(8,128)(2,1)S(1)}, u32[]{:S(2)}, u32[]{:S(2)}) collective-permute-start(bf16[4,256,256]{2,1,0:T(8,128)(2,1)S(1)} %collective-permute-done.22.refs_4_), channel_id=1, source_target_pairs={{2,0},{3,1},{4,2},{5,3},{10,8},{11,9},{12,10},{13,11},{18,16},{19,... | collective-permute-start | bytes 1572872 | tf_op jit(solution)/shard_map/ppermute | solution.py:303
  81.8 17.7 %collective-permute-start.36 = (bf16[256,1024]{1,0:T(8,128)(2,1)S(1)}, bf16[256,1024]{1,0:T(8,128)(2,1)S(1)}, u32[]{:S(2)}, u32[]{:S(2)}) collective-permute-start(bf16[256,1024]{1,0:T(8,128)(2,1)S(1)} %fusion.36), channel_id=1, source_target_pairs={{0,2},{1,3},{6,4},{7,5},{8,10},{9,11},{14,12},{15,13},{16,18},{17,... | collective-permute-start | bytes 1572872 | tf_op jit(solution)/shard_map/ppermute | solution.py:303
  91.8 14.6 %collective-permute-start.37 = (bf16[256,1024]{1,0:T(8,128)(2,1)S(1)}, bf16[256,1024]{1,0:T(8,128)(2,1)S(1)}, u32[]{:S(2)}, u32[]{:S(2)}) collective-permute-start(bf16[256,1024]{1,0:T(8,128)(2,1)S(1)} %fusion.27), channel_id=1, source_target_pairs={{0,1},{1,0},{2,3},{3,2},{4,5},{5,4},{6,7},{7,6},{8,9},{9,8},{10,11... | collective-permute-start | bytes 1572872 | tf_op jit(solution)/shard_map/ppermute | solution.py:306
  97.0 15.5 %collective-permute-start.41 = (bf16[4,256,256]{2,1,0:T(8,128)(2,1)S(1)}, bf16[4,256,256]{2,1,0:T(8,128)(2,1)S(1)}, u32[]{:S(2)}, u32[]{:S(2)}) collective-permute-start(bf16[4,256,256]{2,1,0:T(8,128)(2,1)S(1)} %collective-permute-done.21.refs_2_), channel_id=1, source_target_pairs={{0,1},{1,0},{2,3},{3,2},{4,5},{5,4},{6,7},{7,6},{8,9},{9,8},{10,11... | collective-permute-start | bytes 1572872 | tf_op jit(solution)/shard_map/ppermute | solution.py:306
  97.2 15.4 %collective-permute-start.42 = (bf16[4,256,256]{2,1,0:T(8,128)(2,1)S(1)}, bf16[4,256,256]{2,1,0:T(8,128)(2,1)S(1)}, u32[]{:S(2)}, u32[]{:S(2)}) collective-permute-start(bf16[4,256,256]{2,1,0:T(8,128)(2,1)S(1)} %collective-permute-done.22.refs_4_), channel_id=1, source_target_pairs={{0,1},{1,0},{2,3},{3,2},{4,5},{5,4},{6,7},{7,6},{8,9},{9,8},{10,11... | collective-permute-start | bytes 1572872 | tf_op jit(solution)/shard_map/ppermute | solution.py:306
  99.5 15.2 %collective-permute-start.32 = (bf16[4,256,256]{2,1,0:T(8,128)(2,1)S(1)}, bf16[4,256,256]{2,1,0:T(8,128)(2,1)S(1)}, u32[]{:S(2)}, u32[]{:S(2)}) collective-permute-start(bf16[4,256,256]{2,1,0:T(8,128)(2,1)S(1)} %add.220.refs_0_), channel_id=1, source_target_pairs={{4,6},{5,7},{2,0},{3,1},{12,14},{13,15},{10,8},{11,9},{20,22},{21,... | collective-permute-start | bytes 1572872 | tf_op jit(solution)/shard_map/ppermute | solution.py:303
  101.8 21.9 %collective-permute-start.38 = (bf16[256,1024]{1,0:T(8,128)(2,1)}, bf16[256,1024]{1,0:T(8,128)(2,1)S(1)}, u32[]{:S(2)}, u32[]{:S(2)}) collective-permute-start(bf16[256,1024]{1,0:T(8,128)(2,1)} %add_convert_fusion.2), channel_id=1, source_target_pairs={{0,2},{1,3},{2,4},{3,5},{8,10},{9,11},{10,12},{11,13},{16,18},{17,... | collective-permute-start | bytes 1572872 | tf_op jit(solution)/shard_map/ppermute | solution.py:303
  106.4 17.3 %collective-permute-start.39 = (bf16[256,1024]{1,0:T(8,128)(2,1)}, bf16[256,1024]{1,0:T(8,128)(2,1)}, u32[]{:S(2)}, u32[]{:S(2)}) collective-permute-start(bf16[256,1024]{1,0:T(8,128)(2,1)} %add_convert_fusion.2), channel_id=1, source_target_pairs={{4,2},{5,3},{6,4},{7,5},{12,10},{13,11},{14,12},{15,13},{20,18},{2... | collective-permute-start | bytes 1572872 | tf_op jit(solution)/shard_map/ppermute | solution.py:303
  112.5 12.8 %collective-permute-start.43 = (bf16[256,1024]{1,0:T(8,128)(2,1)S(1)}, bf16[256,1024]{1,0:T(8,128)(2,1)}, u32[]{:S(2)}, u32[]{:S(2)}) collective-permute-start(bf16[256,1024]{1,0:T(8,128)(2,1)S(1)} %fusion.33), channel_id=1, source_target_pairs={{0,1},{1,0},{2,3},{3,2},{4,5},{5,4},{6,7},{7,6},{8,9},{9,8},{10,11... | collective-permute-start | bytes 1572872 | tf_op jit(solution)/shard_map/ppermute | solution.py:306
  112.6 17.8 %collective-permute-start.31 = (bf16[4,256,256]{2,1,0:T(8,128)(2,1)S(1)}, bf16[4,256,256]{2,1,0:T(8,128)(2,1)S(1)}, u32[]{:S(2)}, u32[]{:S(2)}) collective-permute-start(bf16[4,256,256]{2,1,0:T(8,128)(2,1)S(1)} %add.220.refs_0_), channel_id=1, source_target_pairs={{0,1},{1,0},{2,3},{3,2},{4,5},{5,4},{6,7},{7,6},{8,9},{9,8},{10,11... | collective-permute-start | bytes 1572872 | tf_op jit(solution)/shard_map/ppermute | solution.py:306
  114.7 15.8 %collective-permute-start.33 = (bf16[4,256,256]{2,1,0:T(8,128)(2,1)S(1)}, bf16[4,256,256]{2,1,0:T(8,128)(2,1)}, u32[]{:S(2)}, u32[]{:S(2)}) collective-permute-start(bf16[4,256,256]{2,1,0:T(8,128)(2,1)S(1)} %collective-permute-done.32.refs_2_), channel_id=1, source_target_pairs={{0,1},{1,0},{2,3},{3,2},{4,5},{5,4},{6,7},{7,6},{8,9},{9,8},{10,11... | collective-permute-start | bytes 1572872 | tf_op jit(solution)/shard_map/ppermute | solution.py:306
  125.4 29.2 %collective-permute-start.44 = (bf16[256,1024]{1,0:T(8,128)(2,1)S(1)}, bf16[256,1024]{1,0:T(8,128)(2,1)S(1)}, u32[]{:S(2)}, u32[]{:S(2)}) collective-permute-start(bf16[256,1024]{1,0:T(8,128)(2,1)S(1)} %get-tuple-element.38), channel_id=1, source_target_pairs={{0,2},{1,3},{2,4},{3,5},{4,6},{5,7},{8,10},{9,11},{10,12},{11,13},... | collective-permute-start | bytes 1572872 | tf_op jit(solution)/shard_map/ppermute | solution.py:303
  128.5 26.1 %collective-permute-start.45 = (bf16[256,1024]{1,0:T(8,128)(2,1)S(1)}, bf16[256,1024]{1,0:T(8,128)(2,1)}, u32[]{:S(2)}, u32[]{:S(2)}) collective-permute-start(bf16[256,1024]{1,0:T(8,128)(2,1)S(1)} %get-tuple-element.39), channel_id=1, source_target_pairs={{2,0},{3,1},{4,2},{5,3},{6,4},{7,5},{10,8},{11,9},{12,10},{13,11},... | collective-permute-start | bytes 1572872 | tf_op jit(solution)/shard_map/ppermute | solution.py:303
  (53 other events, 621.2 us)

commit v4 on v0

v4 whole, which is shorter than its diff:
```python
import functools

import jax
import jax.numpy as jnp
from jax import lax
from jax.experimental import pallas as pl
from jax.experimental.pallas import tpu as pltpu
from jax.sharding import PartitionSpec as P

BLOCK = 128
TILE = 128
X_STREAMS = ((0,), (1, 2), (3,))
PIECES = 8
PARAMS = pltpu.CompilerParams(vmem_limit_bytes=24 << 20)
F32 = jnp.float32
BF16 = jnp.bfloat16
LIGHT = pl.CostEstimate(flops=1, bytes_accessed=1, transcendentals=0)
VMEM = pl.BlockSpec(memory_space=pltpu.VMEM)
SMEM = pl.BlockSpec(memory_space=pltpu.SMEM)


def cost(flops, moved):
    return pl.CostEstimate(flops=flops, bytes_accessed=moved, transcendentals=0)


def after(value, *others):
    return lax.optimization_barrier((value, others))[0]


def kernel_call(body, outs, args, name, hint=LIGHT, scratch=()):
    return pl.pallas_call(
        body,
        in_specs=[SMEM] + [VMEM] * (len(args) - 1),
        out_specs=[VMEM] * len(outs),
        out_shape=[jax.ShapeDtypeStruct(shape, kind) for shape, kind in outs],
        scratch_shapes=list(scratch),
        compiler_params=PARAMS,
        cost_estimate=hint,
        name=name,
    )(*args)


def load_body(w_ref, through_ref, out_ref, same_ref, sems):
    step = w_ref.shape[0] // PIECES
    copies = []
    for n in range(PIECES):
        part = pl.ds(n * step, step)
        copies.append(pltpu.make_async_copy(w_ref.at[part], out_ref.at[part], sems.at[n]))
    for copy in copies:
        copy.start()
    for copy in copies:
        copy.wait()


def load(w, through, room):
    anywhere = pl.BlockSpec(memory_space=pl.ANY)
    return pl.pallas_call(
        load_body,
        in_specs=[anywhere, anywhere],
        out_specs=[VMEM, anywhere],
        out_shape=[
            pltpu.VMEM(w.shape, w.dtype),
            jax.ShapeDtypeStruct(through.shape, through.dtype),
        ],
        scratch_shapes=[pltpu.SemaphoreType.DMA((PIECES,))],
        input_output_aliases={1: 1},
        compiler_params=pltpu.CompilerParams(vmem_limit_bytes=room << 20),
        cost_estimate=cost(0, 2 * w.size),
        name="load",
    )(w, through)


FIXED = 3


def pieces(refs, streams):
    return [refs[a].at[b] for a, stream in enumerate(streams) for b in range(len(stream))]


def aligned(index, width):
    return pl.ds(pl.multiple_of(index * width, width), width)


def enc_body(streams, count, first, last, n_feat, at, table, *refs):
    size = len(streams)
    slots = [pieces(refs[q * size:(q + 1) * size], streams) for q in range(count)]
    w_ref, bias_ref, hit_ref = refs[count * size:count * size + 3]
    refs = refs[count * size + 3:]
    carry_ref = None
    if not first:
        carry_ref, seen_ref, refs = refs[0], refs[1], refs[2:]
    out_ref, own_ref = refs[:2]
    total_ref = refs[2] if last else out_ref
    n_tok, width = len(slots[0]), slots[0][0].shape[1]
    if not first:
        own_ref[...] = seen_ref[...]
    for q, blocks in enumerate(slots):
        source = table[at + q]
        total = carry_ref if q == 0 else total_ref
        total = None if total is None else total[...]
        for s, x in enumerate(blocks):
            w = w_ref[(table[0] ^ s) * n_feat + source]
            term = jnp.dot(x[...], w, preferred_element_type=F32)
            total = term if total is None else total + term
        total_ref[...] = total
        for s, x in enumerate(blocks):

            @pl.when(((table[0] ^ s) == table[1]) & (source // n_tok == table[2]))
            def _():
                own_ref[:, aligned(source % n_tok, width)] = x[...]

    if last:
        pre = total_ref[...] + bias_ref[...]
        tiles = hit_ref.shape[0]
        shaped = jnp.maximum(pre, 0.0).reshape(tiles, TILE, -1) * hit_ref[...][:, None, :]
        out_ref[...] = shaped.reshape(pre.shape).astype(BF16)


def encode(table, at, slots, w, bias, hit, carry, streams, last, n_feat):
    width, feats = w.shape[1:]
    rows = slots[0][0].shape[1]
    n_tok = w.shape[0] // n_feat
    args = [table] + [a for slot in slots for a in slot] + [w, bias, hit]
    if carry is not None:
        args += carry
    return kernel_call(
        functools.partial(enc_body, streams, len(slots), carry is None, last, n_feat, at),
        [((rows, feats), BF16 if last else F32), ((rows, n_tok * width), BF16)],
        args,
        "encode",
        LIGHT if last else cost(2 * len(slots) * rows * n_tok * width * feats, 4 << 20),
        [pltpu.VMEM((rows, feats), F32)] if last else [],
    )


def dec_body(at, table, acts_ref, w_ref, *out_refs):
    share = out_refs[0].shape[1]
    for q, out_ref in enumerate(out_refs):
        w = w_ref[:, aligned(table[at + q], share)]
        out_ref[...] = jnp.dot(acts_ref[...], w, preferred_element_type=F32).astype(BF16)


def decode(table, at, acts, w, share, count, hint):
    outs = [((acts.shape[0], share), BF16)] * count
    return kernel_call(functools.partial(dec_body, at), outs, [table, acts, w], "decode", hint)


def proj_body(count, first, last, n_feat, at, table, *refs):
    slots, refs = refs[:count], refs[count:]
    w_ref, acts_ref, x_ref, bias_ref = refs[:4]
    refs = refs[4:]
    if not first:
        carry_ref, seen_ref, refs = refs[0], refs[1], refs[2:]
    out_ref, sum_ref = refs[:2]
    if last:
        out_ref, line_ref, sum_ref = refs
    if first:
        sum_ref[...] = jnp.zeros_like(sum_ref)
    else:
        sum_ref[...] = seen_ref[...]
    for q, g_ref in enumerate(slots):
        n_tok, _, width = g_ref.shape
        source, held = table[at + 2 * q], table[at + 2 * q + 1] == 1

        @pl.when(held)
        def _():
            total = None if q == 0 and first else (carry_ref if q == 0 else out_ref)[...]
            for s in range(n_tok):
                w = w_ref[:, aligned((table[0] ^ s) * n_feat + source, width)]
                term = lax.dot_general(
                    g_ref[s], w, (((1,), (1,)), ((), ())), preferred_element_type=F32
                )
                total = term if total is None else total + term
            out_ref[...] = total

        @pl.when(held & (source // n_tok == table[2]))
        def _():
            cols = aligned(source % n_tok, width)
            term = x_ref[:, cols].astype(F32) - bias_ref[:, cols]
            term = term * g_ref[table[0] ^ table[1]].astype(F32)
            sum_ref[...] += jnp.sum(term, axis=1, keepdims=True)

    if last:
        attr = acts_ref[...].astype(F32) * out_ref[...]
        out_ref[...] = attr
        total = sum_ref[...] - jnp.sum(attr, axis=1, keepdims=True)
        line_ref[...] = jnp.broadcast_to(total, (total.shape[0], TILE)).T[:8]


def project(table, at, slots, w, acts, own_x, bias, carry, last, n_feat):
    rows, feats = acts.shape
    outs = [((rows, feats), F32), ((8, rows), F32) if last else ((rows, 1), F32)]
    return kernel_call(
        functools.partial(proj_body, len(slots), carry is None, last, n_feat, at),
        outs,
        [table, *slots, w, acts, own_x, bias, *(carry or [])],
        "project",
        LIGHT if last else cost(2 * len(slots) * slots[0].size * feats, 4 << 20),
        [pltpu.VMEM((rows, 1), F32)] if last else [],
    )


def line_program(resid, resid_grad, active, w_enc, b_enc, w_dec, b_dec):
    n_tok, n_feat = lax.axis_size("tok"), lax.axis_size("feat")
    i, j = lax.axis_index("tok"), lax.axis_index("feat")
    chips = n_feat // 2
    chip, core = j // 2, j % 2
    width = resid.shape[1]
    rows = resid.shape[0] // n_tok
    feats = w_enc.shape[1]
    share = n_tok * width

    def along(pairs):
        return [(2 * a + c, 2 * b + c) for a, b in pairs for c in range(2)]

    def send(array, pairs):
        return lax.ppermute(array, "feat", along(pairs))

    def cross(array):
        return lax.ppermute(array, "feat", [(a, a ^ 1) for a in range(n_feat)])

    def exchange(array, streams):
        def block(s):
            mine = lax.dynamic_slice_in_dim(array, (i ^ s) * rows, rows, 0)
            if s == 0:
                return mine
            return lax.ppermute(mine, "tok", [(a, a ^ s) for a in range(n_tok)])

        blocks = [block(s) for s in range(n_tok)]
        return [jnp.stack([blocks[s] for s in stream]) for stream in streams]

    def both_cores(place):
        return [2 * place + core, 2 * place + 1 - core]

    def held_slots(*sources):
        values, seen = [], 0
        for place, valid in sources:
            seen = jnp.where(valid, place, seen)
            for source in both_cores(seen):
                values += [source, valid]
        return values

    numbers = [i, j // (n_feat // n_tok), j % (n_feat // n_tok)]
    at = []
    for values in (
        both_cores(chip) + both_cores((chip + chips - 1) % chips),
        both_cores((chip + chips - 2) % chips) + both_cores((chip + chips - 3) % chips),
        both_cores(chip ^ 3)[::-1],
        both_cores(chip ^ 2)[::-1] + both_cores(chip ^ 1)[::-1] + both_cores(chip)[::-1],
        held_slots((chip, True), (chip - 1, chip >= 1), (chip + 1, chip <= chips - 2)),
        held_slots((chip ^ 2, True), (chip ^ 3, (chip == 0) | (chip == chips - 1))),
    ):
        at.append(len(numbers))
        numbers += values
    table = jnp.stack([jnp.asarray(n).astype(jnp.int32) for n in numbers])

    blocks = feats // BLOCK
    block_ids = j * blocks + jnp.arange(blocks, dtype=jnp.int32)
    hits = jnp.any(active[:, :, None] == block_ids[None, None, :], axis=1).astype(F32)
    hit = jnp.repeat(hits, BLOCK, axis=1)
    bias = b_enc.reshape(1, feats)
    b_row = b_dec.reshape(1, share)

    ring = [(a, (a + 1) % chips) for a in range(chips)]
    near_x = [exchange(resid, X_STREAMS)]
    w_in, near_x[0][2] = load(w_enc.reshape(n_tok * n_feat, width, feats), near_x[0][2], 46)
    far_x = [[cross(a) for a in near_x[0]]]
    carry = None
    for k in range(1, chips):
        held = near_x[-1]
        if k == 2:
            w_out, held[2] = load(w_dec, held[2], 36)
        if k == 3:
            held = [held[0], held[1], after(held[2], shard_g)]
        near_x.append([send(a, ring) for a in held])
        if k == 2:
            shard_g, = exchange(after(resid_grad, near_x[2][0]), ((0, 1, 2, 3),))
        if k == 3:
            slots = [near_x[0], far_x[0], near_x[1], far_x[1]]
            carry = encode(
                table, at[0], slots, w_in, bias, hit, None, X_STREAMS, False, n_feat
            )
            late = after(near_x[3][2], carry)
            far_x.append([cross(near_x[3][0]), cross(near_x[3][1]), cross(late)])
        else:
            far_x.append([cross(a) for a in near_x[-1]])

    up_pairs = [(a, a + 1) for a in range(chips - 1)]
    down_pairs = [(a + 1, a) for a in range(chips - 1)]
    shard_g = after(shard_g, near_x[-1])
    up_1, down_1 = send(shard_g, up_pairs), send(shard_g, down_pairs)

    slots = [near_x[2], far_x[2], near_x[3], far_x[3]]
    acts, own_x = encode(table, at[1], slots, w_in, bias, hit, carry, X_STREAMS, True, n_feat)

    far_3, near_3 = decode(table, at[2], acts, w_out, share, 2, LIGHT)
    up_1, down_1 = after((up_1, down_1), far_3)
    parts = {3: (near_3, cross(far_3))}
    outs = decode(
        table, at[3], after(acts, far_3), w_out, share, 6, cost(12 * rows * feats * share, 4 << 20)
    )
    for n, k in enumerate((2, 1, 0)):
        parts[k] = (outs[2 * n + 1], cross(outs[2 * n]))

    def pair_sum(k):
        return parts[k][0].astype(F32) + parts[k][1].astype(F32)

    sum_3, sum_1 = pair_sum(3), pair_sum(1)
    come = send(sum_3.astype(BF16), [(0, 1), (3, 2)])
    up_2, down_2 = send(up_1, up_pairs[1:]), send(down_1, down_pairs[:-1])
    two_g = up_2 + down_2
    three_g = send(two_g, [(2, 3), (1, 0)])

    going = (pair_sum(2) + come.astype(F32)).astype(BF16)
    up = send(going, up_pairs[:2])
    down = send(going, down_pairs[1:])

    slots = [shard_g, cross(shard_g), up_1, cross(up_1), down_1, cross(down_1)]
    carry = project(
        table, at[4], slots, w_out, after(acts, going), own_x, b_row, None, False, n_feat
    )
    base = own_x.astype(F32) - b_row - pair_sum(0)

    going_up = (jnp.where(chip == 1, sum_3, sum_1) + up.astype(F32)).astype(BF16)
    going_down = (jnp.where(chip == 2, sum_3, sum_1) + down.astype(F32)).astype(BF16)
    going_up, going_down = after((going_up, going_down), carry, base)
    up = send(going_up, up_pairs)
    down = send(going_down, down_pairs)

    slots = [two_g, cross(two_g), three_g, cross(three_g)]
    feature_attr, attr = project(
        table, at[5], slots, w_out, after(acts, going_up, going_down), own_x, b_row, carry, True, n_feat
    )
    attr = attr[:1]
    attr = attr + cross(attr)
    others = [send(attr, [(a, a ^ k) for a in range(chips)]) for k in range(1, chips)]
    for other in others:
        attr = attr + other

    error = base - (up.astype(F32) + down.astype(F32))
    return feature_attr, error, attr.reshape(rows)


def gathered_program(resid, resid_grad, active, w_enc, b_enc, w_dec, b_dec):
    n_tok = lax.axis_size("tok")
    n_feat = lax.axis_size("feat")
    width = resid.shape[1]

    def rows_of(array):
        part = lax.all_to_all(array, "tok", split_axis=0, concat_axis=1, tiled=True)
        part = part.reshape(part.shape[0], n_tok, 1, width)
        part = lax.all_gather(part, "feat", axis=2, tiled=True)
        return part.reshape(part.shape[0], n_tok * n_feat * width)

    rows_x, rows_g = rows_of(resid), rows_of(resid_grad)
    tok_rows = rows_x.shape[0]
    feat_dev = w_enc.shape[1]
    blocks = feat_dev // BLOCK
    tiles_dev = active.shape[0]
    block_ids = lax.axis_index("feat") * blocks + jnp.arange(blocks, dtype=jnp.int32)
    hits = jnp.any(active[:, :, None] == block_ids[None, None, :], axis=1).astype(F32)
    pre = jnp.dot(rows_x, w_enc, preferred_element_type=F32) + b_enc
    shaped = jnp.maximum(pre, 0.0).reshape(tiles_dev, TILE, blocks, BLOCK) * hits[:, None, :, None]
    acts = shaped.reshape(tok_rows, feat_dev).astype(BF16)
    partial_recon = jnp.dot(acts, w_dec, preferred_element_type=F32)
    recon_share = lax.psum_scatter(
        partial_recon.astype(BF16), "feat", scatter_dimension=1, tiled=True
    ).astype(F32)
    share = recon_share.shape[1]
    start = lax.axis_index("feat") * share
    own_x = lax.dynamic_slice_in_dim(rows_x, start, share, 1)
    own_g = lax.dynamic_slice_in_dim(rows_g, start, share, 1)
    recon = recon_share + b_dec
    error = own_x.astype(F32) - recon
    local_sums = jnp.sum(error * own_g.astype(F32), axis=1)
    error_attr = lax.psum(local_sums, "feat")
    proj = lax.dot_general(rows_g, w_dec, (((1,), (1,)), ((), ())), preferred_element_type=F32)
    return acts.astype(F32) * proj, error, error_attr


def per_device(resid, *rest):
    fits = resid.shape[1] % 128 == 0 and lax.axis_size("tok") == 4 and lax.axis_size("feat") == 8
    return (line_program if fits else gathered_program)(resid, *rest)


def solution(mesh):
    placed = (
        P(None, ("tok", "feat")),
        P(None, ("tok", "feat")),
        P("tok", None),
        P(None, "feat"),
        P("feat"),
        P("feat", None),
        P("feat"),
    )
    return jax.shard_map(
        per_device,
        mesh=mesh,
        in_specs=placed,
        out_specs=(P("tok", "feat"), P("tok", "feat"), P("tok")),
        check_vma=False,
    )
```

time: 191 us -> 160 us (0.84)
  waiting for transfers between devices: 104 us -> 37.2 us
  starting transfers between devices: 0.12 us -> 54.4 us
  blocking collectives: 40.6 us -> 0 us
  Pallas kernels: 0 us -> 28.3 us
  local copies, waits for them, and re-layouts: 9.68 us -> 30.3 us
  matrix products: 19.2 us -> 0 us
  between operations: 13.9 us -> 1.18 us
  other arithmetic: 3.44 us -> 7.93 us
    all_gather x2 -> x0, waiting for transfers between devices: 65.4 us -> none  [the longest x1 34.2 us: per_device(): lax.all_gather(part_x, 'feat', axis=2, tiled=True)]
    ppermute x0 -> x50, starting transfers between devices: none -> 54.4 us  [the longest x22 41.7 us: send(): return lax.ppermute(array, 'feat', along(pairs))]
    reduce_scatter x1 -> x0, waiting for transfers between devices: 38.7 us -> none  [per_device(): lax.psum_scatter(partial_recon.astype(jnp.bfloat16), 'feat', scatter_dime...]
    ppermute x0 -> x50, waiting for transfers between devices: none -> 37.2 us  [the longest x22 30 us: send(): return lax.ppermute(array, 'feat', along(pairs))]
    pallas_call x0 -> x8, Pallas kernels: none -> 28.3 us  [the longest x6 20.2 us: kernel_call(): pl.pallas_call(body, in_specs=[SMEM] + [VMEM] * (len(args) - 1), out_spec...]
    all_to_all x2 -> x0, blocking collectives: 26.3 us -> none  [the longest x1 14.3 us: per_device(): lax.all_to_all(resid, 'tok', split_axis=0, concat_axis=1, tiled=True)]
    unnamed x15 -> x58, local copies, waits for them, and re-layouts: 3.96 us -> 28.3 us
    dot_general x3 -> x0, matrix products: 19.2 us -> none  [the longest x1 7.4 us: per_device(): lax.dot_general(rows_g, w_dec, (((1,), (1,)), ((), ())), preferred_elemen...]
  transfers between devices with their start and end apart: 3 -> 50, of which waited for: 3 -> 15; matrix products, arithmetic and copies ran while one was open for 14% -> 5% of each run, Pallas kernels for 0% -> 18%
where the time goes in v4:
time: 160 us; the launch traced here: 159 us
  starting transfers between devices  54.4 us (34%)
  waiting for transfers between devices  37.2 us (23%)
  local copies, waits for them, and re-layouts  30.3 us (19%)
  Pallas kernels  28.3 us (18%)
  other arithmetic  7.93 us (5%)
    ppermute x22, starting transfers between devices, send(): return lax.ppermute(array, 'feat', along(pairs))  41.7 us
    ppermute x22, waiting for transfers between devices, send(): return lax.ppermute(array, 'feat', along(pairs))  30 us
    unnamed x58, local copies, waits for them, and re-layouts  28.3 us
    pallas_call x6, Pallas kernels, kernel_call(): pl.pallas_call(body, in_specs=[SMEM] + [VMEM] * (len(args) - 1), out_spec...  20.2 us
    pallas_call x2, Pallas kernels, load(): pl.pallas_call(load_body, in_specs=[anywhere, anywhere], out_specs=[VMEM,...  8.18 us
    ppermute x6, starting transfers between devices, block(): return lax.ppermute(mine, 'tok', [(a, a ^ s) for a in range(n_tok)])  8.1 us
    ppermute x6, waiting for transfers between devices, block(): return lax.ppermute(mine, 'tok', [(a, a ^ s) for a in range(n_tok)])  5.97 us
    ppermute x22, starting transfers between devices, cross(): return lax.ppermute(array, 'feat', [(a, a ^ 1) for a in range(n_feat)])  4.57 us
  transfers between devices with their start and end apart: 50, of which 15 were waited for; matrix products, arithmetic and copies ran while one was open for 5% of the time, Pallas kernels for 18%

profile of v4, /device:TPU:0, one launch (start us, length us, event | category | flops | bytes accessed | tf_op | source)
XLA Modules:
  0.0 159.4 jit_solution(8522950457955475293)
XLA Ops:
  1.9 3.0 %collective-permute-start.6 = (bf16[256,256]{1,0:T(8,128)(2,1)S(1)}, bf16[256,256]{1,0:T(8,128)(2,1)S(1)}, u32[]{:S(2)}, u32[]{:S(2)}) collective-permute-start(bf16[256,256]{1,0:T(8,128)(2,1)S(1)} %get-tuple-element.68), channel_id=1, source_target_pairs={{0,8},{8,0},{16,24},{24,16},{1,9},{9,1},{17,25},{25,17},{2,10},{10... | collective-permute-start | bytes 393224 | tf_op jit(solution)/shard_map/ppermute | solution.py:227
  6.4 2.0 %collective-permute-start = (bf16[1,256,256]{2,1,0:T(8,128)(2,1)S(1)}, bf16[1,256,256]{2,1,0:T(8,128)(2,1)S(1)}, u32[]{:S(2)}, u32[]{:S(2)}) collective-permute-start(bf16[1,256,256]{2,1,0:T(8,128)(2,1)S(1)} %get-tuple-element.69.refs_0_), channel_id=1, source_target_pairs={{0,2},{1,3},{2,4},{3,5},{4,6},{5,7},{6,0},{7,1},{8,10},{9,11},{10,... | collective-permute-start | bytes 393224 | tf_op jit(solution)/shard_map/ppermute | solution.py:217
  8.8 3.9 %collective-permute-done.7 = bf16[256,256]{1,0:T(8,128)(2,1)S(1)} collective-permute-done((bf16[256,256]{1,0:T(8,128)(2,1)S(1)}, bf16[256,256]{1,0:T(8,128)(2,1)S(1)}, u32[]{:S(2)}, u32[]{:S(2)}) %collective-permute-start.7) | collective-permute-done | bytes 131104 | tf_op jit(solution)/shard_map/ppermute | solution.py:227
  12.7 1.6 %collective-permute-start.8 = (bf16[2,256,256]{2,1,0:T(8,128)(2,1)S(1)}, bf16[2,256,256]{2,1,0:T(8,128)(2,1)S(1)}, u32[]{:S(2)}, u32[]{:S(2)}) collective-permute-start(bf16[2,256,256]{2,1,0:T(8,128)(2,1)S(1)} %pad_maximum_fusion.1.refs_1_), channel_id=1, source_target_pairs={{0,2},{1,3},{2,4},{3,5},{4,6},{5,7},{6,0},{7,1},{8,10},{9,11},{10,... | collective-permute-start | bytes 786440 | tf_op jit(solution)/shard_map/ppermute | solution.py:217
  15.0 4.1 %load.2 = (bf16[32,256,640]{2,1,0:T(8,128)(2,1)S(1)}, bf16[1,256,256]{2,1,0:T(8,128)(2,1)}) custom-call(bf16[32,256,640]{2,1,0:T(8,128)(2,1)} %bitcast.51, bf16[1,256,256]{2,1,0:T(8,128)(2,1)} %bitcast.46), custom_call_target="tpu_custom_call", output_to_operand_aliasing={{1}: (1, {})} | custom-call | bytes 10485760 | tf_op jit(solution)/shard_map/load/pallas_call | solution.py:57
  19.1 3.9 %copy-done.2 = bf16[32,256,640]{2,1,0:T(8,128)(2,1)} copy-done((bf16[32,256,640]{2,1,0:T(8,128)(2,1)}, bf16[32,256,640]{2,1,0:T(8,128)(2,1)S(1)}, u32[]{:S(2)}) %copy-start.2) | copy-done | bytes 10485784
  23.0 1.6 collective-permute-start.12
  24.6 1.6 collective-permute-start.1
  26.1 3.8 %collective-permute-done.12.through_ref = bf16[1,256,256]{2,1,0:T(8,128)(2,1)S(1)} collective-permute-done((bf16[1,256,256]{2,1,0:T(8,128)(2,1)}, bf16[1,256,256]{2,1,0:T(8,128)(2,1)S(1)}, u32[]{:S(2)}, u32[]{:S(2)}) %collective-permute-start.12) | collective-permute-done | bytes 131104 | tf_op jit(solution)/shard_map/ppermute | solution.py:217
  32.0 1.5 collective-permute-start.3
  33.5 4.1 %load.3 = (bf16[640,8192]{1,0:T(8,128)(2,1)S(1)}, bf16[1,256,256]{2,1,0:T(8,128)(2,1)S(1)}) custom-call(bf16[640,8192]{1,0:T(8,128)(2,1)} %w_ref.1, bf16[1,256,256]{2,1,0:T(8,128)(2,1)S(1)} %collective-permute-done.12.through_ref), custom_call_target="tpu_custom_call", output_to_operand_aliasing={{1}: (1, {})} | custom-call | bytes 10485760 | tf_op jit(solution)/shard_map/load/pallas_call | solution.py:57
  37.6 4.0 %copy-done = bf16[640,8192]{1,0:T(8,128)(2,1)} copy-done((bf16[640,8192]{1,0:T(8,128)(2,1)}, bf16[640,8192]{1,0:T(8,128)(2,1)S(1)}, u32[]{:S(2)}) %copy-start) | copy-done | bytes 10485784
  45.9 1.8 %collective-permute-done.4 = bf16[256,256]{1,0:T(8,128)(2,1)} collective-permute-done((bf16[256,256]{1,0:T(8,128)(2,1)S(1)}, bf16[256,256]{1,0:T(8,128)(2,1)}, u32[]{:S(2)}, u32[]{:S(2)}) %collective-permute-start.4) | collective-permute-done | bytes 131104 | tf_op jit(solution)/shard_map/ppermute | solution.py:227
  48.9 1.8 %collective-permute-done.13.refs_2_ = bf16[1,256,256]{2,1,0:T(8,128)(2,1)} collective-permute-done((bf16[1,256,256]{2,1,0:T(8,128)(2,1)S(1)}, bf16[1,256,256]{2,1,0:T(8,128)(2,1)}, u32[]{:S(2)}, u32[]{:S(2)}) %collective-permute-start.13) | collective-permute-done | bytes 131104 | tf_op jit(solution)/shard_map/ppermute | solution.py:217
  52.7 1.6 collective-permute-start.14
  54.8 6.8 %collective-permute-done.10.refs_7_ = bf16[2,256,256]{2,1,0:T(8,128)(2,1)S(1)} collective-permute-done((bf16[2,256,256]{2,1,0:T(8,128)(2,1)S(1)}, bf16[2,256,256]{2,1,0:T(8,128)(2,1)S(1)}, u32[]{:S(2)}, u32[]{:S(2)}) %collective-permute-start.10) | collective-permute-done | bytes 262176 | tf_op jit(solution)/shard_map/ppermute | solution.py:217
  63.1 4.0 %copy-done.3 = bf16[32,256,640]{2,1,0:T(8,128)(2,1)S(1)} copy-done((bf16[32,256,640]{2,1,0:T(8,128)(2,1)S(1)}, bf16[32,256,640]{2,1,0:T(8,128)(2,1)}, u32[]{:S(2)}) %copy-start.3) | copy-done | bytes 10485784
  68.8 3.0 %encode.2 = (f32[256,640]{1,0:T(8,128)S(1)}, bf16[256,1024]{1,0:T(8,128)(2,1)S(1)}) custom-call(s32[39]{0:T(128)S(1)} %stack.158.table, bf16[1,256,256]{2,1,0:T(8,128)(2,1)S(1)} %get-tuple-element.69.refs_0_, bf16[2,256,256]{2,1,0:T(8,128)(2,1)S(1)} %pad_maximum_fusion.1.refs_1_, bf16[1,256,256]{2,1,0:T(8,128)(2,1)S(1)} %copy-done.13, ...), custom_call_target="tpu_custom_call" | custom-call | flops 1342177280 | bytes 4194304 | tf_op jit(solution)/shard_map/encode/pallas_call | solution.py:31
  75.2 4.0 %copy-done.4 = bf16[32,256,640]{2,1,0:T(8,128)(2,1)S(1)} copy-done((bf16[32,256,640]{2,1,0:T(8,128)(2,1)S(1)}, bf16[32,256,640]{2,1,0:T(8,128)(2,1)}, u32[]{:S(2)}) %copy-start.4) | copy-done | bytes 10485784
  80.1 3.7 %encode.3 = (bf16[256,640]{1,0:T(8,128)(2,1)S(1)}, bf16[256,1024]{1,0:T(8,128)(2,1)S(1)}) custom-call(s32[39]{0:T(128)S(1)} %stack.158.table, bf16[1,256,256]{2,1,0:T(8,128)(2,1)S(1)} %copy-done.15, bf16[2,256,256]{2,1,0:T(8,128)(2,1)S(1)} %collective-permute-done.9.refs_1_, bf16[1,256,256]{2,1,0:T(8,128)(2,1)} %collective-permute-done.13.refs_2_, ...), custom_call_target="tpu_custom_call" | custom-call | flops 1 | bytes 1 | tf_op jit(solution)/shard_map/encode/pallas_call | solution.py:31
  85.6 3.6 %decode.3 = (bf16[256,1024]{1,0:T(8,128)(2,1)S(1)}, bf16[256,1024]{1,0:T(8,128)(2,1)S(1)}, bf16[256,1024]{1,0:T(8,128)(2,1)}, bf16[256,1024]{1,0:T(8,128)(2,1)S(...) custom-call(s32[39]{0:T(128)S(1)} %stack.158.table, ...), custom_call_target="tpu_custom_call" | custom-call | flops 2013265920 | bytes 4194304 | tf_op jit(solution)/shard_map/decode/pallas_call | solution.py:31
  91.9 7.0 %collective-permute-start.37 = (bf16[256,1024]{1,0:T(8,128)(2,1)S(1)}, bf16[256,1024]{1,0:T(8,128)(2,1)S(1)}, u32[]{:S(2)}, u32[]{:S(2)}) collective-permute-start(bf16[256,1024]{1,0:T(8,128)(2,1)S(1)} %fusion), channel_id=1, source_target_pairs={{0,2},{1,3},{6,4},{7,5},{8,10},{9,11},{14,12},{15,13},{16,18},{17,... | collective-permute-start | bytes 1572872 | tf_op jit(solution)/shard_map/ppermute | solution.py:217
  99.5 9.1 %collective-permute-done.30 = bf16[4,256,256]{2,1,0:T(8,128)(2,1)S(1)} collective-permute-done((bf16[4,256,256]{2,1,0:T(8,128)(2,1)S(1)}, bf16[4,256,256]{2,1,0:T(8,128)(2,1)S(1)}, u32[]{:S(2)}, u32[]{:S(2)}) %collective-permute-start.30) | collective-permute-done | bytes 524320 | tf_op jit(solution)/shard_map/ppermute | solution.py:217
  113.1 6.1 %collective-permute-start.38 = (bf16[256,1024]{1,0:T(8,128)(2,1)}, bf16[256,1024]{1,0:T(8,128)(2,1)}, u32[]{:S(2)}, u32[]{:S(2)}) collective-permute-start(bf16[256,1024]{1,0:T(8,128)(2,1)} %add_convert_fusion.2), channel_id=1, source_target_pairs={{0,2},{1,3},{2,4},{3,5},{8,10},{9,11},{10,12},{11,13},{16,18},{17,... | collective-permute-start | bytes 1572872 | tf_op jit(solution)/shard_map/ppermute | solution.py:217
  123.4 1.8 %collective-permute-done.32.refs_2_ = bf16[4,256,256]{2,1,0:T(8,128)(2,1)} collective-permute-done((bf16[4,256,256]{2,1,0:T(8,128)(2,1)S(1)}, bf16[4,256,256]{2,1,0:T(8,128)(2,1)}, u32[]{:S(2)}, u32[]{:S(2)}) %collective-permute-start.32) | collective-permute-done | bytes 524320 | tf_op jit(solution)/shard_map/ppermute | solution.py:217
  125.1 4.0 %copy-done.1 = bf16[640,8192]{1,0:T(8,128)(2,1)S(1)} copy-done((bf16[640,8192]{1,0:T(8,128)(2,1)S(1)}, bf16[640,8192]{1,0:T(8,128)(2,1)}, u32[]{:S(2)}) %copy-start.1) | copy-done | bytes 10485784
  131.2 4.0 %project.2 = (f32[256,640]{1,0:T(8,128)S(1)}, f32[256,1]{1,0:T(8,128)S(1)}) custom-call(s32[39]{0:T(128)S(1)} %stack.158.table, bf16[4,256,256]{2,1,0:T(8,128)(2,1)S(1)} %pad_maximum_fusion.refs_0_, bf16[4,256,256]{2,1,0:T(8,128)(2,1)S(1)} %copy-done.9, bf16[4,256,256]{2,1,0:T(8,128)(2,1)S(1)} %collective-permute-done.15.refs_2_, ...), custom_call_target="tpu_custom_call" | custom-call | flops 2013265920 | bytes 4194304 | tf_op jit(solution)/shard_map/project/pallas_call | solution.py:31
  135.2 2.0 %add_convert_fusion = (bf16[256,1024]{1,0:T(8,128)(2,1)S(1)}, bf16[256,1024]{1,0:T(8,128)(2,1)S(1)}) fusion(bf16[256,1024]{1,0:T(8,128)(2,1)} %collective-permute-done.39, bf16[256,1024]{1,0:T(8,128)(2,1)} %collective-permute-done.35, bf16[256,1024]{1,0:T(8,128)(2,1)S(1)} %copy-done.6, bf16[256,1024]{1,0:T(8,128)(2,1)S(1)} %copy-done.22, ...), kind=kLoop, calls=%fused_computation.2 | loop fusion | flops 3670016 | bytes 4194306 | tf_op jit(solution)/shard_map/convert_element_type | solution.py:325
  137.3 4.2 %collective-permute-start.44 = (bf16[256,1024]{1,0:T(8,128)(2,1)S(1)}, bf16[256,1024]{1,0:T(8,128)(2,1)S(1)}, u32[]{:S(2)}, u32[]{:S(2)}) collective-permute-start(bf16[256,1024]{1,0:T(8,128)(2,1)S(1)} %get-tuple-element.60), channel_id=1, source_target_pairs={{0,2},{1,3},{2,4},{3,5},{4,6},{5,7},{8,10},{9,11},{10,12},{11,13},... | collective-permute-start | bytes 1572872 | tf_op jit(solution)/shard_map/ppermute | solution.py:217
  142.8 4.4 %project.3 = (f32[256,640]{1,0:T(8,128)}, f32[8,256]{1,0:T(8,128)S(1)}) custom-call(s32[39]{0:T(128)S(1)} %stack.158.table, bf16[4,256,256]{2,1,0:T(8,128)(2,1)S(1)} %add.190.refs_0_, bf16[4,256,256]{2,1,0:T(8,128)(2,1)S(1)} %collective-permute-done.31.refs_1_, bf16[4,256,256]{2,1,0:T(8,128)(2,1)} %collective-permute-done.32.refs_2_, ...), custom_call_target="tpu_custom_call" | custom-call | flops 1 | bytes 1 | tf_op jit(solution)/shard_map/project/pallas_call | solution.py:31
  149.8 1.9 %collective-permute-start.48 = (f32[1,256]{1,0:T(1,128)S(1)}, f32[1,256]{1,0:T(1,128)S(1)}, u32[]{:S(2)}, u32[]{:S(2)}) collective-permute-start(f32[1,256]{1,0:T(1,128)S(1)} %slice_add_fusion), channel_id=1, source_target_pairs={{0,4},{1,5},{2,6},{3,7},{4,0},{5,1},{6,2},{7,3},{8,12},{9,13},{10,... | collective-permute-start | bytes 3080 | tf_op jit(solution)/shard_map/ppermute | solution.py:217
  152.7 3.7 %collective-permute-done.47 = f32[1,256]{1,0:T(1,128)S(1)} collective-permute-done((f32[1,256]{1,0:T(1,128)S(1)}, f32[1,256]{1,0:T(1,128)S(1)}, u32[]{:S(2)}, u32[]{:S(2)}) %collective-permute-start.47) | collective-permute-done | bytes 1056 | tf_op jit(solution)/shard_map/ppermute | solution.py:217
  (153 shorter events, 44.8 us)
Async XLA Ops:
  6.4 18.2 %collective-permute-start = (bf16[1,256,256]{2,1,0:T(8,128)(2,1)S(1)}, bf16[1,256,256]{2,1,0:T(8,128)(2,1)S(1)}, u32[]{:S(2)}, u32[]{:S(2)}) collective-permute-start(bf16[1,256,256]{2,1,0:T(8,128)(2,1)S(1)} %get-tuple-element.69.refs_0_), channel_id=1, source_target_pairs={{0,2},{1,3},{2,4},{3,5},{4,6},{5,7},{6,0},{7,1},{8,10},{9,11},{10,... | collective-permute-start | bytes 393224 | tf_op jit(solution)/shard_map/ppermute | solution.py:217
  12.7 18.7 %collective-permute-start.8 = (bf16[2,256,256]{2,1,0:T(8,128)(2,1)S(1)}, bf16[2,256,256]{2,1,0:T(8,128)(2,1)S(1)}, u32[]{:S(2)}, u32[]{:S(2)}) collective-permute-start(bf16[2,256,256]{2,1,0:T(8,128)(2,1)S(1)} %pad_maximum_fusion.1.refs_1_), channel_id=1, source_target_pairs={{0,2},{1,3},{2,4},{3,5},{4,6},{5,7},{6,0},{7,1},{8,10},{9,11},{10,... | collective-permute-start | bytes 786440 | tf_op jit(solution)/shard_map/ppermute | solution.py:217
  30.0 11.7 %collective-permute-start.22 = (bf16[1,256,256]{2,1,0:T(8,128)(2,1)S(1)}, bf16[1,256,256]{2,1,0:T(8,128)(2,1)S(1)}, u32[]{:S(2)}, u32[]{:S(2)}) collective-permute-start(bf16[1,256,256]{2,1,0:T(8,128)(2,1)S(1)} %get-tuple-element.69.refs_0_), channel_id=1, source_target_pairs={{0,1},{1,0},{2,3},{3,2},{4,5},{5,4},{6,7},{7,6},{8,9},{9,8},{10,11... | collective-permute-start | bytes 393224 | tf_op jit(solution)/shard_map/ppermute | solution.py:220
  30.5 12.6 %collective-permute-start.25 = (bf16[1,256,256]{2,1,0:T(8,128)(2,1)S(1)}, bf16[1,256,256]{2,1,0:T(8,128)(2,1)S(1)}, u32[]{:S(2)}, u32[]{:S(2)}) collective-permute-start(bf16[1,256,256]{2,1,0:T(8,128)(2,1)S(1)} %collective-permute-done.refs_6_), channel_id=1, source_target_pairs={{0,1},{1,0},{2,3},{3,2},{4,5},{5,4},{6,7},{7,6},{8,9},{9,8},{10,11... | collective-permute-start | bytes 393224 | tf_op jit(solution)/shard_map/ppermute | solution.py:220
  31.4 19.4 %collective-permute-start.9 = (bf16[2,256,256]{2,1,0:T(8,128)(2,1)S(1)}, bf16[2,256,256]{2,1,0:T(8,128)(2,1)S(1)}, u32[]{:S(2)}, u32[]{:S(2)}) collective-permute-start(bf16[2,256,256]{2,1,0:T(8,128)(2,1)S(1)} %collective-permute-done.8.refs_7_), channel_id=1, source_target_pairs={{0,2},{1,3},{2,4},{3,5},{4,6},{5,7},{6,0},{7,1},{8,10},{9,11},{10,... | collective-permute-start | bytes 786440 | tf_op jit(solution)/shard_map/ppermute | solution.py:217
  31.4 13.8 %collective-permute-start.2 = (bf16[256,256]{1,0:T(8,128)(2,1)S(1)}, bf16[256,256]{1,0:T(8,128)(2,1)S(1)}, u32[]{:S(2)}, u32[]{:S(2)}) collective-permute-start(bf16[256,256]{1,0:T(8,128)(2,1)S(1)} %get-tuple-element.74), channel_id=1, source_target_pairs={{0,8},{8,0},{16,24},{24,16},{1,9},{9,1},{17,25},{25,17},{2,10},{10... | collective-permute-start | bytes 393224 | tf_op jit(solution)/shard_map/ppermute | solution.py:227
  32.0 13.4 %collective-permute-start.3 = (bf16[256,256]{1,0:T(8,128)(2,1)S(1)}, bf16[256,256]{1,0:T(8,128)(2,1)S(1)}, u32[]{:S(2)}, u32[]{:S(2)}) collective-permute-start(bf16[256,256]{1,0:T(8,128)(2,1)S(1)} %get-tuple-element.73), channel_id=1, source_target_pairs={{0,16},{8,24},{16,0},{24,8},{1,17},{9,25},{17,1},{25,9},{2,18},{10... | collective-permute-start | bytes 393224 | tf_op jit(solution)/shard_map/ppermute | solution.py:227
  50.7 11.7 %collective-permute-start.26 = (bf16[2,256,256]{2,1,0:T(8,128)(2,1)S(1)}, bf16[2,256,256]{2,1,0:T(8,128)(2,1)S(1)}, u32[]{:S(2)}, u32[]{:S(2)}) collective-permute-start(bf16[2,256,256]{2,1,0:T(8,128)(2,1)S(1)} %collective-permute-done.8.refs_7_), channel_id=1, source_target_pairs={{0,1},{1,0},{2,3},{3,2},{4,5},{5,4},{6,7},{7,6},{8,9},{9,8},{10,11... | collective-permute-start | bytes 786440 | tf_op jit(solution)/shard_map/ppermute | solution.py:220
  50.8 10.9 %collective-permute-start.10 = (bf16[2,256,256]{2,1,0:T(8,128)(2,1)S(1)}, bf16[2,256,256]{2,1,0:T(8,128)(2,1)S(1)}, u32[]{:S(2)}, u32[]{:S(2)}) collective-permute-start(bf16[2,256,256]{2,1,0:T(8,128)(2,1)S(1)} %collective-permute-done.9.refs_1_), channel_id=1, source_target_pairs={{0,2},{1,3},{2,4},{3,5},{4,6},{5,7},{6,0},{7,1},{8,10},{9,11},{10,... | collective-permute-start | bytes 786440 | tf_op jit(solution)/shard_map/ppermute | solution.py:217
  52.7 19.1 %collective-permute-start.14 = (bf16[1,256,256]{2,1,0:T(8,128)(2,1)}, bf16[1,256,256]{2,1,0:T(8,128)(2,1)}, u32[]{:S(2)}, u32[]{:S(2)}) collective-permute-start(bf16[1,256,256]{2,1,0:T(8,128)(2,1)} %collective-permute-done.13.refs_2_), channel_id=1, source_target_pairs={{0,2},{1,3},{2,4},{3,5},{4,6},{5,7},{6,0},{7,1},{8,10},{9,11},{10,... | collective-permute-start | bytes 393224 | tf_op jit(solution)/shard_map/ppermute | solution.py:217
  54.3 17.6 %collective-permute-start.17 = (bf16[1,256,256]{2,1,0:T(8,128)(2,1)S(1)}, bf16[1,256,256]{2,1,0:T(8,128)(2,1)}, u32[]{:S(2)}, u32[]{:S(2)}) collective-permute-start(bf16[1,256,256]{2,1,0:T(8,128)(2,1)S(1)} %collective-permute-done.1.refs_0_), channel_id=1, source_target_pairs={{0,1},{1,0},{2,3},{3,2},{4,5},{5,4},{6,7},{7,6},{8,9},{9,8},{10,11... | collective-permute-start | bytes 393224 | tf_op jit(solution)/shard_map/ppermute | solution.py:220
  54.5 20.7 %collective-permute-start.18 = (bf16[2,256,256]{2,1,0:T(8,128)(2,1)S(1)}, bf16[2,256,256]{2,1,0:T(8,128)(2,1)S(1)}, u32[]{:S(2)}, u32[]{:S(2)}) collective-permute-start(bf16[2,256,256]{2,1,0:T(8,128)(2,1)S(1)} %collective-permute-done.9.refs_1_), channel_id=1, source_target_pairs={{0,1},{1,0},{2,3},{3,2},{4,5},{5,4},{6,7},{7,6},{8,9},{9,8},{10,11... | collective-permute-start | bytes 786440 | tf_op jit(solution)/shard_map/ppermute | solution.py:220
  61.7 13.6 %collective-permute-start.21 = (bf16[2,256,256]{2,1,0:T(8,128)(2,1)S(1)}, bf16[2,256,256]{2,1,0:T(8,128)(2,1)S(1)}, u32[]{:S(2)}, u32[]{:S(2)}) collective-permute-start(bf16[2,256,256]{2,1,0:T(8,128)(2,1)S(1)} %collective-permute-done.10.refs_7_), channel_id=1, source_target_pairs={{0,1},{1,0},{2,3},{3,2},{4,5},{5,4},{6,7},{7,6},{8,9},{9,8},{10,11... | collective-permute-start | bytes 786440 | tf_op jit(solution)/shard_map/ppermute | solution.py:220
  62.5 10.0 %collective-permute-start.20 = (bf16[1,256,256]{2,1,0:T(8,128)(2,1)}, bf16[1,256,256]{2,1,0:T(8,128)(2,1)S(1)}, u32[]{:S(2)}, u32[]{:S(2)}) collective-permute-start(bf16[1,256,256]{2,1,0:T(8,128)(2,1)} %collective-permute-done.5.refs_6_), channel_id=1, source_target_pairs={{0,1},{1,0},{2,3},{3,2},{4,5},{5,4},{6,7},{7,6},{8,9},{9,8},{10,11... | collective-permute-start | bytes 393224 | tf_op jit(solution)/shard_map/ppermute | solution.py:220
  72.4 17.2 %collective-permute-start.15 = (bf16[4,256,256]{2,1,0:T(8,128)(2,1)S(1)}, bf16[4,256,256]{2,1,0:T(8,128)(2,1)S(1)}, u32[]{:S(2)}, u32[]{:S(2)}) collective-permute-start(bf16[4,256,256]{2,1,0:T(8,128)(2,1)S(1)} %pad_maximum_fusion.refs_0_), channel_id=1, source_target_pairs={{0,2},{1,3},{2,4},{3,5},{4,6},{5,7},{8,10},{9,11},{10,12},{11,13},... | collective-permute-start | bytes 1572872 | tf_op jit(solution)/shard_map/ppermute | solution.py:217
  73.9 15.8 %collective-permute-start.16 = (bf16[4,256,256]{2,1,0:T(8,128)(2,1)S(1)}, bf16[4,256,256]{2,1,0:T(8,128)(2,1)S(1)}, u32[]{:S(2)}, u32[]{:S(2)}) collective-permute-start(bf16[4,256,256]{2,1,0:T(8,128)(2,1)S(1)} %pad_maximum_fusion.refs_0_), channel_id=1, source_target_pairs={{2,0},{3,1},{4,2},{5,3},{6,4},{7,5},{10,8},{11,9},{12,10},{13,11},... | collective-permute-start | bytes 1572872 | tf_op jit(solution)/shard_map/ppermute | solution.py:217
  89.2 19.5 %collective-permute-start.36 = (bf16[256,1024]{1,0:T(8,128)(2,1)S(1)}, bf16[256,1024]{1,0:T(8,128)(2,1)S(1)}, u32[]{:S(2)}, u32[]{:S(2)}) collective-permute-start(bf16[256,1024]{1,0:T(8,128)(2,1)S(1)} %get-tuple-element.53), channel_id=1, source_target_pairs={{0,1},{1,0},{2,3},{3,2},{4,5},{5,4},{6,7},{7,6},{8,9},{9,8},{10,11... | collective-permute-start | bytes 1572872 | tf_op jit(solution)/shard_map/ppermute | solution.py:220
  89.7 9.3 %collective-permute-start.29 = (bf16[4,256,256]{2,1,0:T(8,128)(2,1)S(1)}, bf16[4,256,256]{2,1,0:T(8,128)(2,1)S(1)}, u32[]{:S(2)}, u32[]{:S(2)}) collective-permute-start(bf16[4,256,256]{2,1,0:T(8,128)(2,1)S(1)} %collective-permute-done.15.refs_2_), channel_id=1, source_target_pairs={{2,4},{3,5},{4,6},{5,7},{10,12},{11,13},{12,14},{13,15},{18,20},{1... | collective-permute-start | bytes 1572872 | tf_op jit(solution)/shard_map/ppermute | solution.py:217
  90.4 18.1 %collective-permute-start.30 = (bf16[4,256,256]{2,1,0:T(8,128)(2,1)S(1)}, bf16[4,256,256]{2,1,0:T(8,128)(2,1)S(1)}, u32[]{:S(2)}, u32[]{:S(2)}) collective-permute-start(bf16[4,256,256]{2,1,0:T(8,128)(2,1)S(1)} %collective-permute-done.16.refs_4_), channel_id=1, source_target_pairs={{2,0},{3,1},{4,2},{5,3},{10,8},{11,9},{12,10},{13,11},{18,16},{19,... | collective-permute-start | bytes 1572872 | tf_op jit(solution)/shard_map/ppermute | solution.py:217
  91.9 18.0 %collective-permute-start.37 = (bf16[256,1024]{1,0:T(8,128)(2,1)S(1)}, bf16[256,1024]{1,0:T(8,128)(2,1)S(1)}, u32[]{:S(2)}, u32[]{:S(2)}) collective-permute-start(bf16[256,1024]{1,0:T(8,128)(2,1)S(1)} %fusion), channel_id=1, source_target_pairs={{0,2},{1,3},{6,4},{7,5},{8,10},{9,11},{14,12},{15,13},{16,18},{17,... | collective-permute-start | bytes 1572872 | tf_op jit(solution)/shard_map/ppermute | solution.py:217
  98.9 13.4 %collective-permute-start.40 = (bf16[4,256,256]{2,1,0:T(8,128)(2,1)S(1)}, bf16[4,256,256]{2,1,0:T(8,128)(2,1)S(1)}, u32[]{:S(2)}, u32[]{:S(2)}) collective-permute-start(bf16[4,256,256]{2,1,0:T(8,128)(2,1)S(1)} %pad_maximum_fusion.refs_0_), channel_id=1, source_target_pairs={{0,1},{1,0},{2,3},{3,2},{4,5},{5,4},{6,7},{7,6},{8,9},{9,8},{10,11... | collective-permute-start | bytes 1572872 | tf_op jit(solution)/shard_map/ppermute | solution.py:220
  99.0 14.1 %collective-permute-start.43 = (bf16[256,1024]{1,0:T(8,128)(2,1)S(1)}, bf16[256,1024]{1,0:T(8,128)(2,1)}, u32[]{:S(2)}, u32[]{:S(2)}) collective-permute-start(bf16[256,1024]{1,0:T(8,128)(2,1)S(1)} %get-tuple-element.59), channel_id=1, source_target_pairs={{0,1},{1,0},{2,3},{3,2},{4,5},{5,4},{6,7},{7,6},{8,9},{9,8},{10,11... | collective-permute-start | bytes 1572872 | tf_op jit(solution)/shard_map/ppermute | solution.py:220
  108.6 10.7 %collective-permute-start.41 = (bf16[4,256,256]{2,1,0:T(8,128)(2,1)S(1)}, bf16[4,256,256]{2,1,0:T(8,128)(2,1)S(1)}, u32[]{:S(2)}, u32[]{:S(2)}) collective-permute-start(bf16[4,256,256]{2,1,0:T(8,128)(2,1)S(1)} %collective-permute-done.15.refs_2_), channel_id=1, source_target_pairs={{0,1},{1,0},{2,3},{3,2},{4,5},{5,4},{6,7},{7,6},{8,9},{9,8},{10,11... | collective-permute-start | bytes 1572872 | tf_op jit(solution)/shard_map/ppermute | solution.py:220
  108.7 14.4 %collective-permute-start.42 = (bf16[4,256,256]{2,1,0:T(8,128)(2,1)S(1)}, bf16[4,256,256]{2,1,0:T(8,128)(2,1)}, u32[]{:S(2)}, u32[]{:S(2)}) collective-permute-start(bf16[4,256,256]{2,1,0:T(8,128)(2,1)S(1)} %collective-permute-done.16.refs_4_), channel_id=1, source_target_pairs={{0,1},{1,0},{2,3},{3,2},{4,5},{5,4},{6,7},{7,6},{8,9},{9,8},{10,11... | collective-permute-start | bytes 1572872 | tf_op jit(solution)/shard_map/ppermute | solution.py:220
  110.0 15.2 %collective-permute-start.32 = (bf16[4,256,256]{2,1,0:T(8,128)(2,1)S(1)}, bf16[4,256,256]{2,1,0:T(8,128)(2,1)}, u32[]{:S(2)}, u32[]{:S(2)}) collective-permute-start(bf16[4,256,256]{2,1,0:T(8,128)(2,1)S(1)} %add.190.refs_0_), channel_id=1, source_target_pairs={{4,6},{5,7},{2,0},{3,1},{12,14},{13,15},{10,8},{11,9},{20,22},{21,... | collective-permute-start | bytes 1572872 | tf_op jit(solution)/shard_map/ppermute | solution.py:217
  113.1 22.1 %collective-permute-start.35 = (bf16[256,1024]{1,0:T(8,128)(2,1)}, bf16[256,1024]{1,0:T(8,128)(2,1)}, u32[]{:S(2)}, u32[]{:S(2)}) collective-permute-start(bf16[256,1024]{1,0:T(8,128)(2,1)} %get-tuple-element.51), channel_id=1, source_target_pairs={{0,1},{1,0},{2,3},{3,2},{4,5},{5,4},{6,7},{7,6},{8,9},{9,8},{10,11... | collective-permute-start | bytes 1572872 | tf_op jit(solution)/shard_map/ppermute | solution.py:220
  113.1 22.1 %collective-permute-start.38 = (bf16[256,1024]{1,0:T(8,128)(2,1)}, bf16[256,1024]{1,0:T(8,128)(2,1)}, u32[]{:S(2)}, u32[]{:S(2)}) collective-permute-start(bf16[256,1024]{1,0:T(8,128)(2,1)} %add_convert_fusion.2), channel_id=1, source_target_pairs={{0,2},{1,3},{2,4},{3,5},{8,10},{9,11},{10,12},{11,13},{16,18},{17,... | collective-permute-start | bytes 1572872 | tf_op jit(solution)/shard_map/ppermute | solution.py:217
  120.0 15.1 %collective-permute-start.39 = (bf16[256,1024]{1,0:T(8,128)(2,1)}, bf16[256,1024]{1,0:T(8,128)(2,1)}, u32[]{:S(2)}, u32[]{:S(2)}) collective-permute-start(bf16[256,1024]{1,0:T(8,128)(2,1)} %add_convert_fusion.2), channel_id=1, source_target_pairs={{4,2},{5,3},{6,4},{7,5},{12,10},{13,11},{14,12},{15,13},{20,18},{2... | collective-permute-start | bytes 1572872 | tf_op jit(solution)/shard_map/ppermute | solution.py:217
  123.1 19.7 %collective-permute-start.31 = (bf16[4,256,256]{2,1,0:T(8,128)(2,1)S(1)}, bf16[4,256,256]{2,1,0:T(8,128)(2,1)S(1)}, u32[]{:S(2)}, u32[]{:S(2)}) collective-permute-start(bf16[4,256,256]{2,1,0:T(8,128)(2,1)S(1)} %add.190.refs_0_), channel_id=1, source_target_pairs={{0,1},{1,0},{2,3},{3,2},{4,5},{5,4},{6,7},{7,6},{8,9},{9,8},{10,11... | collective-permute-start | bytes 1572872 | tf_op jit(solution)/shard_map/ppermute | solution.py:220
  125.1 17.6 %collective-permute-start.33 = (bf16[4,256,256]{2,1,0:T(8,128)(2,1)}, bf16[4,256,256]{2,1,0:T(8,128)(2,1)S(1)}, u32[]{:S(2)}, u32[]{:S(2)}) collective-permute-start(bf16[4,256,256]{2,1,0:T(8,128)(2,1)} %collective-permute-done.32.refs_2_), channel_id=1, source_target_pairs={{0,1},{1,0},{2,3},{3,2},{4,5},{5,4},{6,7},{7,6},{8,9},{9,8},{10,11... | collective-permute-start | bytes 1572872 | tf_op jit(solution)/shard_map/ppermute | solution.py:220
  137.3 20.9 %collective-permute-start.44 = (bf16[256,1024]{1,0:T(8,128)(2,1)S(1)}, bf16[256,1024]{1,0:T(8,128)(2,1)S(1)}, u32[]{:S(2)}, u32[]{:S(2)}) collective-permute-start(bf16[256,1024]{1,0:T(8,128)(2,1)S(1)} %get-tuple-element.60), channel_id=1, source_target_pairs={{0,2},{1,3},{2,4},{3,5},{4,6},{5,7},{8,10},{9,11},{10,12},{11,13},... | collective-permute-start | bytes 1572872 | tf_op jit(solution)/shard_map/ppermute | solution.py:217
  141.5 16.7 %collective-permute-start.45 = (bf16[256,1024]{1,0:T(8,128)(2,1)S(1)}, bf16[256,1024]{1,0:T(8,128)(2,1)S(1)}, u32[]{:S(2)}, u32[]{:S(2)}) collective-permute-start(bf16[256,1024]{1,0:T(8,128)(2,1)S(1)} %get-tuple-element.61), channel_id=1, source_target_pairs={{2,0},{3,1},{4,2},{5,3},{6,4},{7,5},{10,8},{11,9},{12,10},{13,11},... | collective-permute-start | bytes 1572872 | tf_op jit(solution)/shard_map/ppermute | solution.py:217
  (46 other events, 453.4 us)

commit v5 on v4

--- a/solution.py
+++ b/solution.py
@@ -9,7 +9,7 @@
 
 BLOCK = 128
 TILE = 128
-X_STREAMS = ((0,), (1, 2), (3,))
+X_STREAMS = ((0, 1), (2, 3))
 PIECES = 8
 PARAMS = pltpu.CompilerParams(vmem_limit_bytes=24 << 20)
 F32 = jnp.float32
@@ -70,7 +70,93 @@
     )(w, through)
 
 
-FIXED = 3
+SLOTS = {"enc_a": 4, "enc_b": 8, "dec_a": 12, "dec_b": 14, "proj_a": 20, "proj_b": 32, "hits": 40}
+
+
+def table_body(n_tok, n_feat, blocks, ids_ref, active_ref, out_ref):
+    i, j = ids_ref[0], ids_ref[1]
+    chips, ratio = n_feat // 2, n_feat // n_tok
+    chip, core = j // 2, j % 2
+
+    def both_cores(place):
+        return [2 * place + core, 2 * place + 1 - core]
+
+    def held_slots(*sources):
+        values, seen = [], 0
+        for place, valid in sources:
+            seen = jnp.where(valid, place, seen)
+            for source in both_cores(seen):
+                values += [source, jnp.where(valid, 1, 0)]
+        return values
+
+    numbers = [i, j // ratio, j % ratio, chip]
+    for k in range(chips):
+        numbers += both_cores((chip + chips - k) % chips)
+    for k in (3, 2, 1, 0):
+        numbers += both_cores(chip ^ k)[::-1]
+    numbers += held_slots((chip, chip >= 0), (chip - 1, chip >= 1), (chip + 1, chip <= chips - 2))
+    numbers += held_slots((chip ^ 2, chip >= 0), (chip ^ 3, (chip == 0) | (chip == chips - 1)))
+    for n, number in enumerate(numbers):
+        out_ref[n] = number
+    tiles, listed = active_ref.shape
+    for t in range(tiles):
+        for b in range(blocks):
+            found = jnp.int32(0)
+            for n in range(listed):
+                found = jnp.where(active_ref[t, n] == j * blocks + b, 1, found)
+            out_ref[SLOTS["hits"] + t * blocks + b] = found
+
+
+def make_table(ids, active, n_tok, n_feat, blocks):
+    size = SLOTS["hits"] + active.shape[0] * blocks
+    return pl.pallas_call(
+        functools.partial(table_body, n_tok, n_feat, blocks),
+        in_specs=[SMEM, SMEM],
+        out_specs=SMEM,
+        out_shape=jax.ShapeDtypeStruct((size,), jnp.int32),
+        compiler_params=PARAMS,
+        cost_estimate=LIGHT,
+        name="table",
+    )(ids, active)
+
+
+def pick_body(table, array_ref, *refs):
+    outs, sems = refs[:-1], refs[-1]
+    rows = outs[0].shape[0]
+    copies = []
+    for s, out_ref in enumerate(outs):
+        part = array_ref.at[aligned(table[0] ^ s, rows)]
+        copies.append(pltpu.make_async_copy(part, out_ref, sems.at[s]))
+    for copy in copies:
+        copy.start()
+    for copy in copies:
+        copy.wait()
+
+
+def pick(table, array, n_tok):
+    shape = (array.shape[0] // n_tok, array.shape[1])
+    return pl.pallas_call(
+        pick_body,
+        in_specs=[SMEM, pl.BlockSpec(memory_space=pl.ANY)],
+        out_specs=[VMEM] * n_tok,
+        out_shape=[jax.ShapeDtypeStruct(shape, array.dtype)] * n_tok,
+        scratch_shapes=[pltpu.SemaphoreType.DMA((n_tok,))],
+        compiler_params=PARAMS,
+        cost_estimate=LIGHT,
+        name="pick",
+    )(table, array)
+
+
+def third_body(chips, table, *refs):
+    near_1, far_1, near_3, far_3, up_ref, down_ref, going_up_ref, going_down_ref = refs
+    chip = table[3]
+    for target, come_ref, turn in ((going_up_ref, up_ref, 1), (going_down_ref, down_ref, chips - 2)):
+        for near_ref, far_ref, chosen in ((near_3, far_3, chip == turn), (near_1, far_1, chip != turn)):
+
+            @pl.when(chosen)
+            def _():
+                total = near_ref[...].astype(F32) + far_ref[...].astype(F32)
+                target[...] = (total + come_ref[...].astype(F32)).astype(BF16)
 
 
 def pieces(refs, streams):
@@ -84,8 +170,8 @@
 def enc_body(streams, count, first, last, n_feat, at, table, *refs):
     size = len(streams)
     slots = [pieces(refs[q * size:(q + 1) * size], streams) for q in range(count)]
-    w_ref, bias_ref, hit_ref = refs[count * size:count * size + 3]
-    refs = refs[count * size + 3:]
+    w_ref, bias_ref = refs[count * size:count * size + 2]
+    refs = refs[count * size + 2:]
     carry_ref = None
     if not first:
         carry_ref, seen_ref, refs = refs[0], refs[1], refs[2:]
@@ -110,17 +196,20 @@
                 own_ref[:, aligned(source % n_tok, width)] = x[...]
 
     if last:
-        pre = total_ref[...] + bias_ref[...]
-        tiles = hit_ref.shape[0]
-        shaped = jnp.maximum(pre, 0.0).reshape(tiles, TILE, -1) * hit_ref[...][:, None, :]
-        out_ref[...] = shaped.reshape(pre.shape).astype(BF16)
-
-
-def encode(table, at, slots, w, bias, hit, carry, streams, last, n_feat):
+        blocks = out_ref.shape[1] // BLOCK
+        for t in range(out_ref.shape[0] // TILE):
+            for b in range(blocks):
+                tile, block = slice(t * TILE, (t + 1) * TILE), slice(b * BLOCK, (b + 1) * BLOCK)
+                pre = total_ref[tile, block] + bias_ref[:, block]
+                live = table[SLOTS["hits"] + t * blocks + b].astype(F32)
+                out_ref[tile, block] = (jnp.maximum(pre, 0.0) * live).astype(BF16)
+
+
+def encode(table, at, slots, w, bias, carry, streams, last, n_feat):
     width, feats = w.shape[1:]
     rows = slots[0][0].shape[1]
     n_tok = w.shape[0] // n_feat
-    args = [table] + [a for slot in slots for a in slot] + [w, bias, hit]
+    args = [table] + [a for slot in slots for a in slot] + [w, bias]
     if carry is not None:
         args += carry
     return kernel_call(
@@ -204,7 +293,6 @@
     n_tok, n_feat = lax.axis_size("tok"), lax.axis_size("feat")
     i, j = lax.axis_index("tok"), lax.axis_index("feat")
     chips = n_feat // 2
-    chip, core = j // 2, j % 2
     width = resid.shape[1]
     rows = resid.shape[0] // n_tok
     feats = w_enc.shape[1]
@@ -220,70 +308,33 @@
         return lax.ppermute(array, "feat", [(a, a ^ 1) for a in range(n_feat)])
 
     def exchange(array, streams):
-        def block(s):
-            mine = lax.dynamic_slice_in_dim(array, (i ^ s) * rows, rows, 0)
-            if s == 0:
-                return mine
-            return lax.ppermute(mine, "tok", [(a, a ^ s) for a in range(n_tok)])
-
-        blocks = [block(s) for s in range(n_tok)]
+        blocks = list(pick(table, array, n_tok))
+        for s in range(1, n_tok):
+            blocks[s] = lax.ppermute(blocks[s], "tok", [(a, a ^ s) for a in range(n_tok)])
         return [jnp.stack([blocks[s] for s in stream]) for stream in streams]
 
-    def both_cores(place):
-        return [2 * place + core, 2 * place + 1 - core]
-
-    def held_slots(*sources):
-        values, seen = [], 0
-        for place, valid in sources:
-            seen = jnp.where(valid, place, seen)
-            for source in both_cores(seen):
-                values += [source, valid]
-        return values
-
-    numbers = [i, j // (n_feat // n_tok), j % (n_feat // n_tok)]
-    at = []
-    for values in (
-        both_cores(chip) + both_cores((chip + chips - 1) % chips),
-        both_cores((chip + chips - 2) % chips) + both_cores((chip + chips - 3) % chips),
-        both_cores(chip ^ 3)[::-1],
-        both_cores(chip ^ 2)[::-1] + both_cores(chip ^ 1)[::-1] + both_cores(chip)[::-1],
-        held_slots((chip, True), (chip - 1, chip >= 1), (chip + 1, chip <= chips - 2)),
-        held_slots((chip ^ 2, True), (chip ^ 3, (chip == 0) | (chip == chips - 1))),
-    ):
-        at.append(len(numbers))
-        numbers += values
-    table = jnp.stack([jnp.asarray(n).astype(jnp.int32) for n in numbers])
-
-    blocks = feats // BLOCK
-    block_ids = j * blocks + jnp.arange(blocks, dtype=jnp.int32)
-    hits = jnp.any(active[:, :, None] == block_ids[None, None, :], axis=1).astype(F32)
-    hit = jnp.repeat(hits, BLOCK, axis=1)
+    table = make_table(jnp.stack([i, j]), active, n_tok, n_feat, feats // BLOCK)
     bias = b_enc.reshape(1, feats)
     b_row = b_dec.reshape(1, share)
 
     ring = [(a, (a + 1) % chips) for a in range(chips)]
     near_x = [exchange(resid, X_STREAMS)]
-    w_in, near_x[0][2] = load(w_enc.reshape(n_tok * n_feat, width, feats), near_x[0][2], 46)
     far_x = [[cross(a) for a in near_x[0]]]
-    carry = None
     for k in range(1, chips):
-        held = near_x[-1]
+        first, second = near_x[-1]
         if k == 2:
-            w_out, held[2] = load(w_dec, held[2], 36)
-        if k == 3:
-            held = [held[0], held[1], after(held[2], shard_g)]
-        near_x.append([send(a, ring) for a in held])
+            w_out, second = load(w_dec, second, 44)
+            first = after(first, second)
+            w_in, first = load(w_enc.reshape(n_tok * n_feat, width, feats), first, 34)
+            near_x[-1] = [first, second]
+            far_x.append([cross(a) for a in near_x[-1]])
+        near_x.append([send(first, ring), send(second, ring)])
         if k == 2:
             shard_g, = exchange(after(resid_grad, near_x[2][0]), ((0, 1, 2, 3),))
-        if k == 3:
-            slots = [near_x[0], far_x[0], near_x[1], far_x[1]]
-            carry = encode(
-                table, at[0], slots, w_in, bias, hit, None, X_STREAMS, False, n_feat
-            )
-            late = after(near_x[3][2], carry)
-            far_x.append([cross(near_x[3][0]), cross(near_x[3][1]), cross(late)])
-        else:
-            far_x.append([cross(a) for a in near_x[-1]])
+    slots = [near_x[0], far_x[0], near_x[1], far_x[1]]
+    carry = encode(table, SLOTS["enc_a"], slots, w_in, bias, None, X_STREAMS, False, n_feat)
+    far_x.append([cross(a) for a in near_x[2]])
+    far_x.append([cross(near_x[3][0]), cross(after(near_x[3][1], carry))])
 
     up_pairs = [(a, a + 1) for a in range(chips - 1)]
     down_pairs = [(a + 1, a) for a in range(chips - 1)]
@@ -291,13 +342,13 @@
     up_1, down_1 = send(shard_g, up_pairs), send(shard_g, down_pairs)
 
     slots = [near_x[2], far_x[2], near_x[3], far_x[3]]
-    acts, own_x = encode(table, at[1], slots, w_in, bias, hit, carry, X_STREAMS, True, n_feat)
-
-    far_3, near_3 = decode(table, at[2], acts, w_out, share, 2, LIGHT)
+    acts, own_x = encode(table, SLOTS["enc_b"], slots, w_in, bias, carry, X_STREAMS, True, n_feat)
+
+    far_3, near_3 = decode(table, SLOTS["dec_a"], acts, w_out, share, 2, LIGHT)
     up_1, down_1 = after((up_1, down_1), far_3)
     parts = {3: (near_3, cross(far_3))}
     outs = decode(
-        table, at[3], after(acts, far_3), w_out, share, 6, cost(12 * rows * feats * share, 4 << 20)
+        table, SLOTS["dec_b"], after(acts, far_3), w_out, share, 6, cost(12 * rows * feats * share, 4 << 20)
     )
     for n, k in enumerate((2, 1, 0)):
         parts[k] = (outs[2 * n + 1], cross(outs[2 * n]))
@@ -305,8 +356,7 @@
     def pair_sum(k):
         return parts[k][0].astype(F32) + parts[k][1].astype(F32)
 
-    sum_3, sum_1 = pair_sum(3), pair_sum(1)
-    come = send(sum_3.astype(BF16), [(0, 1), (3, 2)])
+    come = send(pair_sum(3).astype(BF16), [(0, 1), (3, 2)])
     up_2, down_2 = send(up_1, up_pairs[1:]), send(down_1, down_pairs[:-1])
     two_g = up_2 + down_2
     three_g = send(two_g, [(2, 3), (1, 0)])
@@ -317,19 +367,23 @@
 
     slots = [shard_g, cross(shard_g), up_1, cross(up_1), down_1, cross(down_1)]
     carry = project(
-        table, at[4], slots, w_out, after(acts, going), own_x, b_row, None, False, n_feat
+        table, SLOTS["proj_a"], slots, w_out, after(acts, going), own_x, b_row, None, False, n_feat
     )
     base = own_x.astype(F32) - b_row - pair_sum(0)
 
-    going_up = (jnp.where(chip == 1, sum_3, sum_1) + up.astype(F32)).astype(BF16)
-    going_down = (jnp.where(chip == 2, sum_3, sum_1) + down.astype(F32)).astype(BF16)
+    going_up, going_down = kernel_call(
+        functools.partial(third_body, chips),
+        [((rows, share), BF16)] * 2,
+        [table, *parts[1], *parts[3], up, down],
+        "third",
+    )
     going_up, going_down = after((going_up, going_down), carry, base)
     up = send(going_up, up_pairs)
     down = send(going_down, down_pairs)
 
     slots = [two_g, cross(two_g), three_g, cross(three_g)]
     feature_attr, attr = project(
-        table, at[5], slots, w_out, after(acts, going_up, going_down), own_x, b_row, carry, True, n_feat
+        table, SLOTS["proj_b"], slots, w_out, after(acts, going_up, going_down), own_x, b_row, carry, True, n_feat
     )
     attr = attr[:1]
     attr = attr + cross(attr)

time: 160 us -> 151 us (0.944)
  local copies, waits for them, and re-layouts: 30.3 us -> 14.5 us
  waiting for transfers between devices: 37.2 us -> 48.6 us
  other arithmetic: 7.93 us -> 2.81 us
  Pallas kernels: 28.3 us -> 31.4 us
  starting transfers between devices: 54.4 us -> 51.8 us
    unnamed x58 -> x20, local copies, waits for them, and re-layouts: 28.3 us -> 14.5 us
    ppermute x6, waiting for transfers between devices: 5.97 us -> 11.8 us  [exchange(): lax.ppermute(blocks[s], 'tok', [(a, a ^ s) for a in range(n_tok)])]
    ppermute x22 -> x19, waiting for transfers between devices: 30 us -> 35.6 us  [send(): return lax.ppermute(array, 'feat', along(pairs))]
    pallas_call x0 -> x3, Pallas kernels: none -> 3.85 us  [the longest x2 2.52 us: pick(): pl.pallas_call(pick_body, in_specs=[SMEM, pl.BlockSpec(memory_space=pl.AN...]
    convert_element_type x3 -> x1, other arithmetic: 2.23 us -> 0.19 us  [line_program(): come = send(pair_sum(3).astype(BF16), [(0, 1), (3, 2)])]
    ppermute x22 -> x19, starting transfers between devices: 41.7 us -> 39.8 us  [send(): return lax.ppermute(array, 'feat', along(pairs))]
    ppermute x22 -> x18, starting transfers between devices: 4.57 us -> 3.76 us  [cross(): return lax.ppermute(array, 'feat', [(a, a ^ 1) for a in range(n_feat)])]
    pallas_call x6 -> x7, Pallas kernels: 20.2 us -> 19.4 us  [kernel_call(): pl.pallas_call(body, in_specs=[SMEM] + [VMEM] * (len(args) - 1), out_spec...]
  transfers between devices with their start and end apart: 50 -> 43, of which waited for: 15 -> 12; matrix products, arithmetic and copies ran while one was open for 5% -> 1% of each run, Pallas kernels for 18% -> 19%
where the time goes in v5:
time: 151 us; the launch traced here: 150 us
  starting transfers between devices  51.8 us (34%)
  waiting for transfers between devices  48.6 us (32%)
  Pallas kernels  31.4 us (21%)
  local copies, waits for them, and re-layouts  14.5 us (10%)
  other arithmetic  2.81 us (2%)
    ppermute x19, starting transfers between devices, send(): return lax.ppermute(array, 'feat', along(pairs))  39.8 us
    ppermute x19, waiting for transfers between devices, send(): return lax.ppermute(array, 'feat', along(pairs))  35.6 us
    pallas_call x7, Pallas kernels, kernel_call(): pl.pallas_call(body, in_specs=[SMEM] + [VMEM] * (len(args) - 1), out_spec...  19.4 us
    unnamed x20, local copies, waits for them, and re-layouts  14.5 us
    ppermute x6, waiting for transfers between devices, exchange(): lax.ppermute(blocks[s], 'tok', [(a, a ^ s) for a in range(n_tok)])  11.8 us
    ppermute x6, starting transfers between devices, exchange(): lax.ppermute(blocks[s], 'tok', [(a, a ^ s) for a in range(n_tok)])  8.23 us
    pallas_call x2, Pallas kernels, load(): pl.pallas_call(load_body, in_specs=[anywhere, anywhere], out_specs=[VMEM,...  8.17 us
    ppermute x18, starting transfers between devices, cross(): return lax.ppermute(array, 'feat', [(a, a ^ 1) for a in range(n_feat)])  3.76 us
  transfers between devices with their start and end apart: 43, of which 12 were waited for; matrix products, arithmetic and copies ran while one was open for 1% of the time, Pallas kernels for 19%

profile of v5, /device:TPU:0, one launch (start us, length us, event | category | flops | bytes accessed | tf_op | source)
XLA Modules:
  0.0 150.2 jit_solution(14917959105659546159)
XLA Ops:
  1.4 1.3 table.1
  5.0 3.0 %collective-permute-start.2 = (bf16[256,256]{1,0:T(8,128)(2,1)S(1)}, bf16[256,256]{1,0:T(8,128)(2,1)S(1)}, u32[]{:S(2)}, u32[]{:S(2)}) collective-permute-start(bf16[256,256]{1,0:T(8,128)(2,1)S(1)} %get-tuple-element.46), channel_id=1, source_target_pairs={{0,16},{8,24},{16,0},{24,8},{1,17},{9,25},{17,1},{25,9},{2,18},{10... | collective-permute-start | bytes 393224 | tf_op jit(solution)/shard_map/ppermute | solution.py:313
  8.1 1.4 collective-permute-start.3
  9.6 4.0 %collective-permute-done.2 = bf16[256,256]{1,0:T(8,128)(2,1)S(1)} collective-permute-done((bf16[256,256]{1,0:T(8,128)(2,1)S(1)}, bf16[256,256]{1,0:T(8,128)(2,1)S(1)}, u32[]{:S(2)}, u32[]{:S(2)}) %collective-permute-start.2) | collective-permute-done | bytes 131104 | tf_op jit(solution)/shard_map/ppermute | solution.py:313
  13.6 1.7 %collective-permute-done.3 = bf16[256,256]{1,0:T(8,128)(2,1)S(1)} collective-permute-done((bf16[256,256]{1,0:T(8,128)(2,1)S(1)}, bf16[256,256]{1,0:T(8,128)(2,1)S(1)}, u32[]{:S(2)}, u32[]{:S(2)}) %collective-permute-start.3) | collective-permute-done | bytes 131104 | tf_op jit(solution)/shard_map/ppermute | solution.py:313
  15.4 1.6 %collective-permute-start.4 = (bf16[2,256,256]{2,1,0:T(8,128)(2,1)S(1)}, bf16[2,256,256]{2,1,0:T(8,128)(2,1)S(1)}, u32[]{:S(2)}, u32[]{:S(2)}) collective-permute-start(bf16[2,256,256]{2,1,0:T(8,128)(2,1)S(1)} %pad_maximum_fusion.2.refs_1_), channel_id=1, source_target_pairs={{0,2},{1,3},{2,4},{3,5},{4,6},{5,7},{6,0},{7,1},{8,10},{9,11},{10,... | collective-permute-start | bytes 786440 | tf_op jit(solution)/shard_map/ppermute | solution.py:305
  17.1 1.6 %collective-permute-start.1 = (bf16[2,256,256]{2,1,0:T(8,128)(2,1)S(1)}, bf16[2,256,256]{2,1,0:T(8,128)(2,1)S(1)}, u32[]{:S(2)}, u32[]{:S(2)}) collective-permute-start(bf16[2,256,256]{2,1,0:T(8,128)(2,1)S(1)} %pad_maximum_fusion.1.refs_0_), channel_id=1, source_target_pairs={{0,2},{1,3},{2,4},{3,5},{4,6},{5,7},{6,0},{7,1},{8,10},{9,11},{10,... | collective-permute-start | bytes 786440 | tf_op jit(solution)/shard_map/ppermute | solution.py:305
  18.7 6.7 %collective-permute-done.4.through_ref = bf16[2,256,256]{2,1,0:T(8,128)(2,1)S(1)} collective-permute-done((bf16[2,256,256]{2,1,0:T(8,128)(2,1)S(1)}, bf16[2,256,256]{2,1,0:T(8,128)(2,1)S(1)}, u32[]{:S(2)}, u32[]{:S(2)}) %collective-permute-start.4) | collective-permute-done | bytes 262176 | tf_op jit(solution)/shard_map/ppermute | solution.py:305
  26.1 4.1 %load.2 = (bf16[640,8192]{1,0:T(8,128)(2,1)S(1)}, bf16[2,256,256]{2,1,0:T(8,128)(2,1)}) custom-call(bf16[640,8192]{1,0:T(8,128)(2,1)} %w_ref.1, bf16[2,256,256]{2,1,0:T(8,128)(2,1)} %copy-done.3), custom_call_target="tpu_custom_call", output_to_operand_aliasing={{1}: (1, {})} | custom-call | bytes 10485760 | tf_op jit(solution)/shard_map/load/pallas_call | solution.py:57
  30.3 4.1 %load.3 = (bf16[32,256,640]{2,1,0:T(8,128)(2,1)S(1)}, bf16[2,256,256]{2,1,0:T(8,128)(2,1)S(1)}) custom-call(bf16[32,256,640]{2,1,0:T(8,128)(2,1)} %bitcast.17, bf16[2,256,256]{2,1,0:T(8,128)(2,1)S(1)} %collective-permute-done.1.through_ref), custom_call_target="tpu_custom_call", output_to_operand_aliasing={{1}: (1, {})} | custom-call | bytes 10485760 | tf_op jit(solution)/shard_map/load/pallas_call | solution.py:57
  34.4 4.0 %copy-done = bf16[32,256,640]{2,1,0:T(8,128)(2,1)} copy-done((bf16[32,256,640]{2,1,0:T(8,128)(2,1)}, bf16[32,256,640]{2,1,0:T(8,128)(2,1)S(1)}, u32[]{:S(2)}) %copy-start) | copy-done | bytes 10485784
  40.3 1.6 %collective-permute-start.11 = (bf16[2,256,256]{2,1,0:T(8,128)(2,1)S(1)}, bf16[2,256,256]{2,1,0:T(8,128)(2,1)S(1)}, u32[]{:S(2)}, u32[]{:S(2)}) collective-permute-start(bf16[2,256,256]{2,1,0:T(8,128)(2,1)S(1)} %collective-permute-done.10.refs_1_), channel_id=1, source_target_pairs={{0,2},{1,3},{2,4},{3,5},{4,6},{5,7},{6,0},{7,1},{8,10},{9,11},{10,... | collective-permute-start | bytes 786440 | tf_op jit(solution)/shard_map/ppermute | solution.py:305
  41.9 6.2 %collective-permute-done.5.refs_0_ = bf16[2,256,256]{2,1,0:T(8,128)(2,1)S(1)} collective-permute-done((bf16[2,256,256]{2,1,0:T(8,128)(2,1)S(1)}, bf16[2,256,256]{2,1,0:T(8,128)(2,1)S(1)}, u32[]{:S(2)}, u32[]{:S(2)}) %collective-permute-start.5) | collective-permute-done | bytes 262176 | tf_op jit(solution)/shard_map/ppermute | solution.py:305
  49.3 1.6 %collective-permute-start.6 = (bf16[256,256]{1,0:T(8,128)(2,1)S(1)}, bf16[256,256]{1,0:T(8,128)(2,1)S(1)}, u32[]{:S(2)}, u32[]{:S(2)}) collective-permute-start(bf16[256,256]{1,0:T(8,128)(2,1)S(1)} %get-tuple-element.53), channel_id=1, source_target_pairs={{0,8},{8,0},{16,24},{24,16},{1,9},{9,1},{17,25},{25,17},{2,10},{10... | collective-permute-start | bytes 393224 | tf_op jit(solution)/shard_map/ppermute | solution.py:313
  50.9 1.8 %collective-permute-start.7 = (bf16[256,256]{1,0:T(8,128)(2,1)S(1)}, bf16[256,256]{1,0:T(8,128)(2,1)S(1)}, u32[]{:S(2)}, u32[]{:S(2)}) collective-permute-start(bf16[256,256]{1,0:T(8,128)(2,1)S(1)} %get-tuple-element.54), channel_id=1, source_target_pairs={{0,16},{8,24},{16,0},{24,8},{1,17},{9,25},{17,1},{25,9},{2,18},{10... | collective-permute-start | bytes 393224 | tf_op jit(solution)/shard_map/ppermute | solution.py:313
  52.7 4.0 %copy-done.1 = bf16[32,256,640]{2,1,0:T(8,128)(2,1)S(1)} copy-done((bf16[32,256,640]{2,1,0:T(8,128)(2,1)S(1)}, bf16[32,256,640]{2,1,0:T(8,128)(2,1)}, u32[]{:S(2)}) %copy-start.1) | copy-done | bytes 10485784
  56.7 3.0 %encode.2 = (f32[256,640]{1,0:T(8,128)S(1)}, bf16[256,1024]{1,0:T(8,128)(2,1)S(1)}) custom-call(s32[50]{0:T(128)S(1)} %table.1, bf16[2,256,256]{2,1,0:T(8,128)(2,1)S(1)} %pad_maximum_fusion.1.refs_0_, bf16[2,256,256]{2,1,0:T(8,128)(2,1)S(1)} %pad_maximum_fusion.2.refs_1_, bf16[2,256,256]{2,1,0:T(8,128)(2,1)S(1)} %collective-permute-done.17.refs_2_, ...), custom_call_target="tpu_custom_call" | custom-call | flops 1342177280 | bytes 4194304 | tf_op jit(solution)/shard_map/encode/pallas_call | solution.py:31
  61.1 6.1 %collective-permute-done.8 = bf16[256,256]{1,0:T(8,128)(2,1)S(1)} collective-permute-done((bf16[256,256]{1,0:T(8,128)(2,1)S(1)}, bf16[256,256]{1,0:T(8,128)(2,1)S(1)}, u32[]{:S(2)}, u32[]{:S(2)}) %collective-permute-start.8) | collective-permute-done | bytes 131104 | tf_op jit(solution)/shard_map/ppermute | solution.py:313
  68.5 4.6 %collective-permute-start.12 = (bf16[4,256,256]{2,1,0:T(8,128)(2,1)S(1)}, bf16[4,256,256]{2,1,0:T(8,128)(2,1)S(1)}, u32[]{:S(2)}, u32[]{:S(2)}) collective-permute-start(bf16[4,256,256]{2,1,0:T(8,128)(2,1)S(1)} %pad_maximum_fusion.refs_0_), channel_id=1, source_target_pairs={{0,2},{1,3},{2,4},{3,5},{4,6},{5,7},{8,10},{9,11},{10,12},{11,13},... | collective-permute-start | bytes 1572872 | tf_op jit(solution)/shard_map/ppermute | solution.py:305
  73.2 4.0 %copy-done.2 = bf16[32,256,640]{2,1,0:T(8,128)(2,1)S(1)} copy-done((bf16[32,256,640]{2,1,0:T(8,128)(2,1)S(1)}, bf16[32,256,640]{2,1,0:T(8,128)(2,1)}, u32[]{:S(2)}) %copy-start.2) | copy-done | bytes 10485784
  77.2 3.2 %encode.3 = (bf16[256,640]{1,0:T(8,128)(2,1)S(1)}, bf16[256,1024]{1,0:T(8,128)(2,1)S(1)}) custom-call(s32[50]{0:T(128)S(1)} %table.1, bf16[2,256,256]{2,1,0:T(8,128)(2,1)S(1)} %collective-permute-done.5.refs_0_, bf16[2,256,256]{2,1,0:T(8,128)(2,1)S(1)} %collective-permute-done.10.refs_1_, bf16[2,256,256]{2,1,0:T(8,128)(2,1)S(1)} %collective-permute-done.14.refs_2_, ...), custom_call_target="tpu_custom_call" | custom-call | flops 1 | bytes 1 | tf_op jit(solution)/shard_map/encode/pallas_call | solution.py:31
  80.3 1.5 %decode.2 = (bf16[256,1024]{1,0:T(8,128)(2,1)S(1)}, bf16[256,1024]{1,0:T(8,128)(2,1)S(1)}) custom-call(s32[50]{0:T(128)S(1)} %table.1, bf16[256,640]{1,0:T(8,128)(2,1)S(1)} %get-tuple-element.82.acts_ref.refs_7_.refs_5_, bf16[640,8192]{1,0:T(8,128)(2,1)S(1)} %get-tuple-element.62.w_ref.refs_6_.refs_4_), custom_call_target="tpu_custom_call" | custom-call | flops 1 | bytes 1 | tf_op jit(solution)/shard_map/decode/pallas_call | solution.py:31
  82.0 3.2 %decode.3 = (bf16[256,1024]{1,0:T(8,128)(2,1)S(1)}, bf16[256,1024]{1,0:T(8,128)(2,1)S(1)}, bf16[256,1024]{1,0:T(8,128)(2,1)S(1)}, bf16[256,1024]{1,0:T(8,128)(2,...) custom-call(s32[50]{0:T(128)S(1)} %table.1, ...), custom_call_target="tpu_custom_call" | custom-call | flops 2013265920 | bytes 4194304 | tf_op jit(solution)/shard_map/decode/pallas_call | solution.py:31
  87.9 8.0 %collective-permute-start.30 = (bf16[256,1024]{1,0:T(8,128)(2,1)S(1)}, bf16[256,1024]{1,0:T(8,128)(2,1)S(1)}, u32[]{:S(2)}, u32[]{:S(2)}) collective-permute-start(bf16[256,1024]{1,0:T(8,128)(2,1)S(1)} %add_convert_fusion.1), channel_id=1, source_target_pairs={{0,2},{1,3},{6,4},{7,5},{8,10},{9,11},{14,12},{15,13},{16,18},{17,... | collective-permute-start | bytes 1572872 | tf_op jit(solution)/shard_map/ppermute | solution.py:305
  96.5 9.1 %collective-permute-done.23 = bf16[4,256,256]{2,1,0:T(8,128)(2,1)S(1)} collective-permute-done((bf16[4,256,256]{2,1,0:T(8,128)(2,1)S(1)}, bf16[4,256,256]{2,1,0:T(8,128)(2,1)S(1)}, u32[]{:S(2)}, u32[]{:S(2)}) %collective-permute-start.23) | collective-permute-done | bytes 524320 | tf_op jit(solution)/shard_map/ppermute | solution.py:305
  109.3 5.2 %collective-permute-start.31 = (bf16[256,1024]{1,0:T(8,128)(2,1)S(1)}, bf16[256,1024]{1,0:T(8,128)(2,1)S(1)}, u32[]{:S(2)}, u32[]{:S(2)}) collective-permute-start(bf16[256,1024]{1,0:T(8,128)(2,1)S(1)} %add_convert_fusion), channel_id=1, source_target_pairs={{0,2},{1,3},{2,4},{3,5},{8,10},{9,11},{10,12},{11,13},{16,18},{17,... | collective-permute-start | bytes 1572872 | tf_op jit(solution)/shard_map/ppermute | solution.py:305
  114.8 7.2 %collective-permute-done.25.refs_2_ = bf16[4,256,256]{2,1,0:T(8,128)(2,1)S(1)} collective-permute-done((bf16[4,256,256]{2,1,0:T(8,128)(2,1)S(1)}, bf16[4,256,256]{2,1,0:T(8,128)(2,1)S(1)}, u32[]{:S(2)}, u32[]{:S(2)}) %collective-permute-start.25) | collective-permute-done | bytes 524320 | tf_op jit(solution)/shard_map/ppermute | solution.py:305
  122.3 3.6 %project.2 = (f32[256,640]{1,0:T(8,128)S(1)}, f32[256,1]{1,0:T(8,128)S(1)}) custom-call(s32[50]{0:T(128)S(1)} %table.1, bf16[4,256,256]{2,1,0:T(8,128)(2,1)S(1)} %pad_maximum_fusion.refs_0_, bf16[4,256,256]{2,1,0:T(8,128)(2,1)S(1)} %collective-permute-done.33.refs_1_, bf16[4,256,256]{2,1,0:T(8,128)(2,1)S(1)} %collective-permute-done.12.refs_2_, ...), custom_call_target="tpu_custom_call" | custom-call | flops 2013265920 | bytes 4194304 | tf_op jit(solution)/shard_map/project/pallas_call | solution.py:31
  127.3 4.4 %collective-permute-start.37 = (bf16[256,1024]{1,0:T(8,128)(2,1)S(1)}, bf16[256,1024]{1,0:T(8,128)(2,1)S(1)}, u32[]{:S(2)}, u32[]{:S(2)}) collective-permute-start(bf16[256,1024]{1,0:T(8,128)(2,1)S(1)} %get-tuple-element.80), channel_id=1, source_target_pairs={{0,2},{1,3},{2,4},{3,5},{4,6},{5,7},{8,10},{9,11},{10,12},{11,13},... | collective-permute-start | bytes 1572872 | tf_op jit(solution)/shard_map/ppermute | solution.py:305
  133.0 3.9 %project.3 = (f32[256,640]{1,0:T(8,128)}, f32[8,256]{1,0:T(8,128)S(1)}) custom-call(s32[50]{0:T(128)S(1)} %table.1, bf16[4,256,256]{2,1,0:T(8,128)(2,1)S(1)} %add.30.refs_0_, bf16[4,256,256]{2,1,0:T(8,128)(2,1)S(1)} %collective-permute-done.24.refs_1_, bf16[4,256,256]{2,1,0:T(8,128)(2,1)S(1)} %collective-permute-done.25.refs_2_, ...), custom_call_target="tpu_custom_call" | custom-call | flops 1 | bytes 1 | tf_op jit(solution)/shard_map/project/pallas_call | solution.py:31
  138.1 4.4 %collective-permute-start.42 = (f32[1,256]{1,0:T(1,128)S(1)}, f32[1,256]{1,0:T(1,128)S(1)}, u32[]{:S(2)}, u32[]{:S(2)}) collective-permute-start(f32[1,256]{1,0:T(1,128)S(1)} %slice_add_fusion), channel_id=1, source_target_pairs={{0,6},{1,7},{2,4},{3,5},{4,2},{5,3},{6,0},{7,1},{8,14},{9,15},{10,... | collective-permute-start | bytes 3080 | tf_op jit(solution)/shard_map/ppermute | solution.py:305
  143.0 5.1 %collective-permute-done.42 = f32[1,256]{1,0:T(1,128)S(1)} collective-permute-done((f32[1,256]{1,0:T(1,128)S(1)}, f32[1,256]{1,0:T(1,128)S(1)}, u32[]{:S(2)}, u32[]{:S(2)}) %collective-permute-start.42) | collective-permute-done | bytes 1056 | tf_op jit(solution)/shard_map/ppermute | solution.py:305
  (99 shorter events, 23.9 us)
Async XLA Ops:
  15.4 10.0 %collective-permute-start.4 = (bf16[2,256,256]{2,1,0:T(8,128)(2,1)S(1)}, bf16[2,256,256]{2,1,0:T(8,128)(2,1)S(1)}, u32[]{:S(2)}, u32[]{:S(2)}) collective-permute-start(bf16[2,256,256]{2,1,0:T(8,128)(2,1)S(1)} %pad_maximum_fusion.2.refs_1_), channel_id=1, source_target_pairs={{0,2},{1,3},{2,4},{3,5},{4,6},{5,7},{6,0},{7,1},{8,10},{9,11},{10,... | collective-permute-start | bytes 786440 | tf_op jit(solution)/shard_map/ppermute | solution.py:305
  17.1 13.2 %collective-permute-start.1 = (bf16[2,256,256]{2,1,0:T(8,128)(2,1)S(1)}, bf16[2,256,256]{2,1,0:T(8,128)(2,1)S(1)}, u32[]{:S(2)}, u32[]{:S(2)}) collective-permute-start(bf16[2,256,256]{2,1,0:T(8,128)(2,1)S(1)} %pad_maximum_fusion.1.refs_0_), channel_id=1, source_target_pairs={{0,2},{1,3},{2,4},{3,5},{4,6},{5,7},{6,0},{7,1},{8,10},{9,11},{10,... | collective-permute-start | bytes 786440 | tf_op jit(solution)/shard_map/ppermute | solution.py:305
  18.7 21.5 %collective-permute-start.18 = (bf16[2,256,256]{2,1,0:T(8,128)(2,1)S(1)}, bf16[2,256,256]{2,1,0:T(8,128)(2,1)S(1)}, u32[]{:S(2)}, u32[]{:S(2)}) collective-permute-start(bf16[2,256,256]{2,1,0:T(8,128)(2,1)S(1)} %pad_maximum_fusion.2.refs_1_), channel_id=1, source_target_pairs={{0,1},{1,0},{2,3},{3,2},{4,5},{5,4},{6,7},{7,6},{8,9},{9,8},{10,11... | collective-permute-start | bytes 786440 | tf_op jit(solution)/shard_map/ppermute | solution.py:308
  30.2 10.1 %collective-permute-start.10 = (bf16[2,256,256]{2,1,0:T(8,128)(2,1)}, bf16[2,256,256]{2,1,0:T(8,128)(2,1)S(1)}, u32[]{:S(2)}, u32[]{:S(2)}) collective-permute-start(bf16[2,256,256]{2,1,0:T(8,128)(2,1)} %get-tuple-element.48.refs_5_), channel_id=1, source_target_pairs={{0,2},{1,3},{2,4},{3,5},{4,6},{5,7},{6,0},{7,1},{8,10},{9,11},{10,... | collective-permute-start | bytes 786440 | tf_op jit(solution)/shard_map/ppermute | solution.py:305
  39.7 9.6 %collective-permute-start.17 = (bf16[2,256,256]{2,1,0:T(8,128)(2,1)S(1)}, bf16[2,256,256]{2,1,0:T(8,128)(2,1)S(1)}, u32[]{:S(2)}, u32[]{:S(2)}) collective-permute-start(bf16[2,256,256]{2,1,0:T(8,128)(2,1)S(1)} %pad_maximum_fusion.1.refs_0_), channel_id=1, source_target_pairs={{0,1},{1,0},{2,3},{3,2},{4,5},{5,4},{6,7},{7,6},{8,9},{9,8},{10,11... | collective-permute-start | bytes 786440 | tf_op jit(solution)/shard_map/ppermute | solution.py:308
  39.7 11.2 %collective-permute-start.20 = (bf16[2,256,256]{2,1,0:T(8,128)(2,1)S(1)}, bf16[2,256,256]{2,1,0:T(8,128)(2,1)S(1)}, u32[]{:S(2)}, u32[]{:S(2)}) collective-permute-start(bf16[2,256,256]{2,1,0:T(8,128)(2,1)S(1)} %copy-done.4), channel_id=1, source_target_pairs={{0,1},{1,0},{2,3},{3,2},{4,5},{5,4},{6,7},{7,6},{8,9},{9,8},{10,11... | collective-permute-start | bytes 786440 | tf_op jit(solution)/shard_map/ppermute | solution.py:308
  40.2 12.4 %collective-permute-start.19 = (bf16[2,256,256]{2,1,0:T(8,128)(2,1)S(1)}, bf16[2,256,256]{2,1,0:T(8,128)(2,1)S(1)}, u32[]{:S(2)}, u32[]{:S(2)}) collective-permute-start(bf16[2,256,256]{2,1,0:T(8,128)(2,1)S(1)} %get-tuple-element.50.refs_4_), channel_id=1, source_target_pairs={{0,1},{1,0},{2,3},{3,2},{4,5},{5,4},{6,7},{7,6},{8,9},{9,8},{10,11... | collective-permute-start | bytes 786440 | tf_op jit(solution)/shard_map/ppermute | solution.py:308
  40.3 19.4 %collective-permute-start.11 = (bf16[2,256,256]{2,1,0:T(8,128)(2,1)S(1)}, bf16[2,256,256]{2,1,0:T(8,128)(2,1)S(1)}, u32[]{:S(2)}, u32[]{:S(2)}) collective-permute-start(bf16[2,256,256]{2,1,0:T(8,128)(2,1)S(1)} %collective-permute-done.10.refs_1_), channel_id=1, source_target_pairs={{0,2},{1,3},{2,4},{3,5},{4,6},{5,7},{6,0},{7,1},{8,10},{9,11},{10,... | collective-permute-start | bytes 786440 | tf_op jit(solution)/shard_map/ppermute | solution.py:305
  48.0 12.3 %collective-permute-start.9 = (bf16[2,256,256]{2,1,0:T(8,128)(2,1)S(1)}, bf16[2,256,256]{2,1,0:T(8,128)(2,1)S(1)}, u32[]{:S(2)}, u32[]{:S(2)}) collective-permute-start(bf16[2,256,256]{2,1,0:T(8,128)(2,1)S(1)} %collective-permute-done.5.refs_0_), channel_id=1, source_target_pairs={{0,2},{1,3},{2,4},{3,5},{4,6},{5,7},{6,0},{7,1},{8,10},{9,11},{10,... | collective-permute-start | bytes 786440 | tf_op jit(solution)/shard_map/ppermute | solution.py:305
  49.3 10.9 %collective-permute-start.6 = (bf16[256,256]{1,0:T(8,128)(2,1)S(1)}, bf16[256,256]{1,0:T(8,128)(2,1)S(1)}, u32[]{:S(2)}, u32[]{:S(2)}) collective-permute-start(bf16[256,256]{1,0:T(8,128)(2,1)S(1)} %get-tuple-element.53), channel_id=1, source_target_pairs={{0,8},{8,0},{16,24},{24,16},{1,9},{9,1},{17,25},{25,17},{2,10},{10... | collective-permute-start | bytes 393224 | tf_op jit(solution)/shard_map/ppermute | solution.py:313
  50.9 9.9 %collective-permute-start.7 = (bf16[256,256]{1,0:T(8,128)(2,1)S(1)}, bf16[256,256]{1,0:T(8,128)(2,1)S(1)}, u32[]{:S(2)}, u32[]{:S(2)}) collective-permute-start(bf16[256,256]{1,0:T(8,128)(2,1)S(1)} %get-tuple-element.54), channel_id=1, source_target_pairs={{0,16},{8,24},{16,0},{24,8},{1,17},{9,25},{17,1},{25,9},{2,18},{10... | collective-permute-start | bytes 393224 | tf_op jit(solution)/shard_map/ppermute | solution.py:313
  52.7 15.9 %collective-permute-start.15 = (bf16[2,256,256]{2,1,0:T(8,128)(2,1)S(1)}, bf16[2,256,256]{2,1,0:T(8,128)(2,1)S(1)}, u32[]{:S(2)}, u32[]{:S(2)}) collective-permute-start(bf16[2,256,256]{2,1,0:T(8,128)(2,1)S(1)} %collective-permute-done.10.refs_1_), channel_id=1, source_target_pairs={{0,1},{1,0},{2,3},{3,2},{4,5},{5,4},{6,7},{7,6},{8,9},{9,8},{10,11... | collective-permute-start | bytes 786440 | tf_op jit(solution)/shard_map/ppermute | solution.py:308
  59.7 13.5 %collective-permute-start.14 = (bf16[2,256,256]{2,1,0:T(8,128)(2,1)S(1)}, bf16[2,256,256]{2,1,0:T(8,128)(2,1)S(1)}, u32[]{:S(2)}, u32[]{:S(2)}) collective-permute-start(bf16[2,256,256]{2,1,0:T(8,128)(2,1)S(1)} %collective-permute-done.5.refs_0_), channel_id=1, source_target_pairs={{0,1},{1,0},{2,3},{3,2},{4,5},{5,4},{6,7},{7,6},{8,9},{9,8},{10,11... | collective-permute-start | bytes 786440 | tf_op jit(solution)/shard_map/ppermute | solution.py:308
  60.3 12.9 %collective-permute-start.21 = (bf16[2,256,256]{2,1,0:T(8,128)(2,1)S(1)}, bf16[2,256,256]{2,1,0:T(8,128)(2,1)S(1)}, u32[]{:S(2)}, u32[]{:S(2)}) collective-permute-start(bf16[2,256,256]{2,1,0:T(8,128)(2,1)S(1)} %collective-permute-done.11.refs_5_), channel_id=1, source_target_pairs={{0,1},{1,0},{2,3},{3,2},{4,5},{5,4},{6,7},{7,6},{8,9},{9,8},{10,11... | collective-permute-start | bytes 786440 | tf_op jit(solution)/shard_map/ppermute | solution.py:308
  60.3 12.8 %collective-permute-start.16 = (bf16[2,256,256]{2,1,0:T(8,128)(2,1)S(1)}, bf16[2,256,256]{2,1,0:T(8,128)(2,1)S(1)}, u32[]{:S(2)}, u32[]{:S(2)}) collective-permute-start(bf16[2,256,256]{2,1,0:T(8,128)(2,1)S(1)} %collective-permute-done.9.refs_4_), channel_id=1, source_target_pairs={{0,1},{1,0},{2,3},{3,2},{4,5},{5,4},{6,7},{7,6},{8,9},{9,8},{10,11... | collective-permute-start | bytes 786440 | tf_op jit(solution)/shard_map/ppermute | solution.py:308
  67.2 18.5 %collective-permute-start.13 = (bf16[4,256,256]{2,1,0:T(8,128)(2,1)S(1)}, bf16[4,256,256]{2,1,0:T(8,128)(2,1)S(1)}, u32[]{:S(2)}, u32[]{:S(2)}) collective-permute-start(bf16[4,256,256]{2,1,0:T(8,128)(2,1)S(1)} %pad_maximum_fusion.refs_0_), channel_id=1, source_target_pairs={{2,0},{3,1},{4,2},{5,3},{6,4},{7,5},{10,8},{11,9},{12,10},{13,11},... | collective-permute-start | bytes 1572872 | tf_op jit(solution)/shard_map/ppermute | solution.py:305
  68.5 17.2 %collective-permute-start.12 = (bf16[4,256,256]{2,1,0:T(8,128)(2,1)S(1)}, bf16[4,256,256]{2,1,0:T(8,128)(2,1)S(1)}, u32[]{:S(2)}, u32[]{:S(2)}) collective-permute-start(bf16[4,256,256]{2,1,0:T(8,128)(2,1)S(1)} %pad_maximum_fusion.refs_0_), channel_id=1, source_target_pairs={{0,2},{1,3},{2,4},{3,5},{4,6},{5,7},{8,10},{9,11},{10,12},{11,13},... | collective-permute-start | bytes 1572872 | tf_op jit(solution)/shard_map/ppermute | solution.py:305
  85.2 20.5 %collective-permute-start.29 = (bf16[256,1024]{1,0:T(8,128)(2,1)S(1)}, bf16[256,1024]{1,0:T(8,128)(2,1)S(1)}, u32[]{:S(2)}, u32[]{:S(2)}) collective-permute-start(bf16[256,1024]{1,0:T(8,128)(2,1)S(1)} %get-tuple-element.71), channel_id=1, source_target_pairs={{0,1},{1,0},{2,3},{3,2},{4,5},{5,4},{6,7},{7,6},{8,9},{9,8},{10,11... | collective-permute-start | bytes 1572872 | tf_op jit(solution)/shard_map/ppermute | solution.py:308
  85.7 10.3 %collective-permute-start.22 = (bf16[4,256,256]{2,1,0:T(8,128)(2,1)S(1)}, bf16[4,256,256]{2,1,0:T(8,128)(2,1)S(1)}, u32[]{:S(2)}, u32[]{:S(2)}) collective-permute-start(bf16[4,256,256]{2,1,0:T(8,128)(2,1)S(1)} %collective-permute-done.12.refs_2_), channel_id=1, source_target_pairs={{2,4},{3,5},{4,6},{5,7},{10,12},{11,13},{12,14},{13,15},{18,20},{1... | collective-permute-start | bytes 1572872 | tf_op jit(solution)/shard_map/ppermute | solution.py:305
  86.4 19.1 %collective-permute-start.23 = (bf16[4,256,256]{2,1,0:T(8,128)(2,1)S(1)}, bf16[4,256,256]{2,1,0:T(8,128)(2,1)S(1)}, u32[]{:S(2)}, u32[]{:S(2)}) collective-permute-start(bf16[4,256,256]{2,1,0:T(8,128)(2,1)S(1)} %collective-permute-done.13.refs_4_), channel_id=1, source_target_pairs={{2,0},{3,1},{4,2},{5,3},{10,8},{11,9},{12,10},{13,11},{18,16},{19,... | collective-permute-start | bytes 1572872 | tf_op jit(solution)/shard_map/ppermute | solution.py:305
  87.9 19.0 %collective-permute-start.30 = (bf16[256,1024]{1,0:T(8,128)(2,1)S(1)}, bf16[256,1024]{1,0:T(8,128)(2,1)S(1)}, u32[]{:S(2)}, u32[]{:S(2)}) collective-permute-start(bf16[256,1024]{1,0:T(8,128)(2,1)S(1)} %add_convert_fusion.1), channel_id=1, source_target_pairs={{0,2},{1,3},{6,4},{7,5},{8,10},{9,11},{14,12},{15,13},{16,18},{17,... | collective-permute-start | bytes 1572872 | tf_op jit(solution)/shard_map/ppermute | solution.py:305
  95.9 12.6 %collective-permute-start.33 = (bf16[4,256,256]{2,1,0:T(8,128)(2,1)S(1)}, bf16[4,256,256]{2,1,0:T(8,128)(2,1)S(1)}, u32[]{:S(2)}, u32[]{:S(2)}) collective-permute-start(bf16[4,256,256]{2,1,0:T(8,128)(2,1)S(1)} %pad_maximum_fusion.refs_0_), channel_id=1, source_target_pairs={{0,1},{1,0},{2,3},{3,2},{4,5},{5,4},{6,7},{7,6},{8,9},{9,8},{10,11... | collective-permute-start | bytes 1572872 | tf_op jit(solution)/shard_map/ppermute | solution.py:308
  96.0 12.6 %collective-permute-start.36 = (bf16[256,1024]{1,0:T(8,128)(2,1)S(1)}, bf16[256,1024]{1,0:T(8,128)(2,1)S(1)}, u32[]{:S(2)}, u32[]{:S(2)}) collective-permute-start(bf16[256,1024]{1,0:T(8,128)(2,1)S(1)} %get-tuple-element.79), channel_id=1, source_target_pairs={{0,1},{1,0},{2,3},{3,2},{4,5},{5,4},{6,7},{7,6},{8,9},{9,8},{10,11... | collective-permute-start | bytes 1572872 | tf_op jit(solution)/shard_map/ppermute | solution.py:308
  107.0 15.1 %collective-permute-start.25 = (bf16[4,256,256]{2,1,0:T(8,128)(2,1)S(1)}, bf16[4,256,256]{2,1,0:T(8,128)(2,1)S(1)}, u32[]{:S(2)}, u32[]{:S(2)}) collective-permute-start(bf16[4,256,256]{2,1,0:T(8,128)(2,1)S(1)} %add.30.refs_0_), channel_id=1, source_target_pairs={{4,6},{5,7},{2,0},{3,1},{12,14},{13,15},{10,8},{11,9},{20,22},{21,... | collective-permute-start | bytes 1572872 | tf_op jit(solution)/shard_map/ppermute | solution.py:305
  108.5 17.4 %collective-permute-start.27 = (bf16[256,1024]{1,0:T(8,128)(2,1)S(1)}, bf16[256,1024]{1,0:T(8,128)(2,1)S(1)}, u32[]{:S(2)}, u32[]{:S(2)}) collective-permute-start(bf16[256,1024]{1,0:T(8,128)(2,1)S(1)} %get-tuple-element.68), channel_id=1, source_target_pairs={{0,1},{1,0},{2,3},{3,2},{4,5},{5,4},{6,7},{7,6},{8,9},{9,8},{10,11... | collective-permute-start | bytes 1572872 | tf_op jit(solution)/shard_map/ppermute | solution.py:308
  108.6 17.3 %collective-permute-start.32 = (bf16[256,1024]{1,0:T(8,128)(2,1)S(1)}, bf16[256,1024]{1,0:T(8,128)(2,1)S(1)}, u32[]{:S(2)}, u32[]{:S(2)}) collective-permute-start(bf16[256,1024]{1,0:T(8,128)(2,1)S(1)} %add_convert_fusion), channel_id=1, source_target_pairs={{4,2},{5,3},{6,4},{7,5},{12,10},{13,11},{14,12},{15,13},{20,18},{2... | collective-permute-start | bytes 1572872 | tf_op jit(solution)/shard_map/ppermute | solution.py:305
  109.3 17.0 %collective-permute-start.31 = (bf16[256,1024]{1,0:T(8,128)(2,1)S(1)}, bf16[256,1024]{1,0:T(8,128)(2,1)S(1)}, u32[]{:S(2)}, u32[]{:S(2)}) collective-permute-start(bf16[256,1024]{1,0:T(8,128)(2,1)S(1)} %add_convert_fusion), channel_id=1, source_target_pairs={{0,2},{1,3},{2,4},{3,5},{8,10},{9,11},{10,12},{11,13},{16,18},{17,... | collective-permute-start | bytes 1572872 | tf_op jit(solution)/shard_map/ppermute | solution.py:305
  114.6 18.4 %collective-permute-start.24 = (bf16[4,256,256]{2,1,0:T(8,128)(2,1)S(1)}, bf16[4,256,256]{2,1,0:T(8,128)(2,1)S(1)}, u32[]{:S(2)}, u32[]{:S(2)}) collective-permute-start(bf16[4,256,256]{2,1,0:T(8,128)(2,1)S(1)} %add.30.refs_0_), channel_id=1, source_target_pairs={{0,1},{1,0},{2,3},{3,2},{4,5},{5,4},{6,7},{7,6},{8,9},{9,8},{10,11... | collective-permute-start | bytes 1572872 | tf_op jit(solution)/shard_map/ppermute | solution.py:308
  122.0 11.0 %collective-permute-start.26 = (bf16[4,256,256]{2,1,0:T(8,128)(2,1)S(1)}, bf16[4,256,256]{2,1,0:T(8,128)(2,1)S(1)}, u32[]{:S(2)}, u32[]{:S(2)}) collective-permute-start(bf16[4,256,256]{2,1,0:T(8,128)(2,1)S(1)} %collective-permute-done.25.refs_2_), channel_id=1, source_target_pairs={{0,1},{1,0},{2,3},{3,2},{4,5},{5,4},{6,7},{7,6},{8,9},{9,8},{10,11... | collective-permute-start | bytes 1572872 | tf_op jit(solution)/shard_map/ppermute | solution.py:308
  127.3 21.7 %collective-permute-start.37 = (bf16[256,1024]{1,0:T(8,128)(2,1)S(1)}, bf16[256,1024]{1,0:T(8,128)(2,1)S(1)}, u32[]{:S(2)}, u32[]{:S(2)}) collective-permute-start(bf16[256,1024]{1,0:T(8,128)(2,1)S(1)} %get-tuple-element.80), channel_id=1, source_target_pairs={{0,2},{1,3},{2,4},{3,5},{4,6},{5,7},{8,10},{9,11},{10,12},{11,13},... | collective-permute-start | bytes 1572872 | tf_op jit(solution)/shard_map/ppermute | solution.py:305
  131.7 17.3 %collective-permute-start.38 = (bf16[256,1024]{1,0:T(8,128)(2,1)S(1)}, bf16[256,1024]{1,0:T(8,128)(2,1)S(1)}, u32[]{:S(2)}, u32[]{:S(2)}) collective-permute-start(bf16[256,1024]{1,0:T(8,128)(2,1)S(1)} %get-tuple-element.81), channel_id=1, source_target_pairs={{2,0},{3,1},{4,2},{5,3},{6,4},{7,5},{10,8},{11,9},{12,10},{13,11},... | collective-permute-start | bytes 1572872 | tf_op jit(solution)/shard_map/ppermute | solution.py:305
  138.1 10.0 %collective-permute-start.42 = (f32[1,256]{1,0:T(1,128)S(1)}, f32[1,256]{1,0:T(1,128)S(1)}, u32[]{:S(2)}, u32[]{:S(2)}) collective-permute-start(f32[1,256]{1,0:T(1,128)S(1)} %slice_add_fusion), channel_id=1, source_target_pairs={{0,6},{1,7},{2,4},{3,5},{4,2},{5,3},{6,0},{7,1},{8,14},{9,15},{10,... | collective-permute-start | bytes 3080 | tf_op jit(solution)/shard_map/ppermute | solution.py:305
  (21 other events, 199.9 us)

commit v6 on v5

--- a/solution.py
+++ b/solution.py
@@ -11,7 +11,7 @@
 TILE = 128
 X_STREAMS = ((0, 1), (2, 3))
 PIECES = 8
-PARAMS = pltpu.CompilerParams(vmem_limit_bytes=24 << 20)
+PARAMS = pltpu.CompilerParams(vmem_limit_bytes=20 << 20)
 F32 = jnp.float32
 BF16 = jnp.bfloat16
 LIGHT = pl.CostEstimate(flops=1, bytes_accessed=1, transcendentals=0)
@@ -307,8 +307,8 @@
     def cross(array):
         return lax.ppermute(array, "feat", [(a, a ^ 1) for a in range(n_feat)])
 
-    def exchange(array, streams):
-        blocks = list(pick(table, array, n_tok))
+    def exchange(blocks, streams):
+        blocks = list(blocks)
         for s in range(1, n_tok):
             blocks[s] = lax.ppermute(blocks[s], "tok", [(a, a ^ s) for a in range(n_tok)])
         return [jnp.stack([blocks[s] for s in stream]) for stream in streams]
@@ -318,22 +318,25 @@
     b_row = b_dec.reshape(1, share)
 
     ring = [(a, (a + 1) % chips) for a in range(chips)]
-    near_x = [exchange(resid, X_STREAMS)]
+    cut_x = [lax.dynamic_slice_in_dim(resid, (i ^ s) * rows, rows, 0) for s in range(n_tok)]
+    near_x = [exchange(cut_x, X_STREAMS)]
     far_x = [[cross(a) for a in near_x[0]]]
     for k in range(1, chips):
         first, second = near_x[-1]
+        if k == 1:
+            second = after(second, table)
         if k == 2:
-            w_out, second = load(w_dec, second, 44)
-            first = after(first, second)
-            w_in, first = load(w_enc.reshape(n_tok * n_feat, width, feats), first, 34)
-            near_x[-1] = [first, second]
+            w_out, first = load(w_dec, first, 44)
+            shard_g, = exchange(pick(table, after(resid_grad, first), n_tok), ((0, 1, 2, 3),))
+        if k == 3:
+            w_in, first = load(w_enc.reshape(n_tok * n_feat, width, feats), first, 36)
+            second = after(second, shard_g)
+        near_x[-1] = [first, second]
+        if k > 1:
             far_x.append([cross(a) for a in near_x[-1]])
         near_x.append([send(first, ring), send(second, ring)])
-        if k == 2:
-            shard_g, = exchange(after(resid_grad, near_x[2][0]), ((0, 1, 2, 3),))
     slots = [near_x[0], far_x[0], near_x[1], far_x[1]]
     carry = encode(table, SLOTS["enc_a"], slots, w_in, bias, None, X_STREAMS, False, n_feat)
-    far_x.append([cross(a) for a in near_x[2]])
     far_x.append([cross(near_x[3][0]), cross(after(near_x[3][1], carry))])
 
     up_pairs = [(a, a + 1) for a in range(chips - 1)]

time: 151 us -> 134 us (0.89)
  local copies, waits for them, and re-layouts: 14.5 us -> 2.6 us
  waiting for transfers between devices: 48.6 us -> 43.8 us
  starting transfers between devices: 51.8 us -> 53.6 us
    unnamed x20 -> x12, local copies, waits for them, and re-layouts: 14.5 us -> 1.4 us
    ppermute x6, waiting for transfers between devices: 11.8 us -> 7.09 us  [exchange(): lax.ppermute(blocks[s], 'tok', [(a, a ^ s) for a in range(n_tok)])]
    ppermute x6, starting transfers between devices: 8.23 us -> 11.8 us  [exchange(): lax.ppermute(blocks[s], 'tok', [(a, a ^ s) for a in range(n_tok)])]
  transfers between devices with their start and end apart: 43 -> 43, of which waited for: 12 -> 14; matrix products, arithmetic and copies ran while one was open for 1% -> 1% of each run, Pallas kernels for 19% -> 22%
where the time goes in v6:
time: 134 us
  starting transfers between devices  53.6 us (40%)
  waiting for transfers between devices  43.8 us (33%)
  Pallas kernels  30.1 us (22%)
  other arithmetic  2.81 us (2%)
  local copies, waits for them, and re-layouts  2.6 us (2%)
    ppermute x19, starting transfers between devices, send(): return lax.ppermute(array, 'feat', along(pairs))  38.4 us
    ppermute x19, waiting for transfers between devices, send(): return lax.ppermute(array, 'feat', along(pairs))  35.5 us
    pallas_call x7, Pallas kernels, kernel_call(): pl.pallas_call(body, in_specs=[SMEM] + [VMEM] * (len(args) - 1), out_spec...  19.3 us
    ppermute x6, starting transfers between devices, exchange(): lax.ppermute(blocks[s], 'tok', [(a, a ^ s) for a in range(n_tok)])  11.8 us
    pallas_call x2, Pallas kernels, load(): pl.pallas_call(load_body, in_specs=[anywhere, anywhere], out_specs=[VMEM,...  8.16 us
    ppermute x6, waiting for transfers between devices, exchange(): lax.ppermute(blocks[s], 'tok', [(a, a ^ s) for a in range(n_tok)])  7.09 us
    ppermute x18, starting transfers between devices, cross(): return lax.ppermute(array, 'feat', [(a, a ^ 1) for a in range(n_feat)])  3.41 us
  transfers between devices with their start and end apart: 43, of which 14 were waited for; matrix products, arithmetic and copies ran while one was open for 1% of the time, Pallas kernels for 22%

profile of v6, /device:TPU:0, one launch (start us, length us, event | category | flops | bytes accessed | tf_op | source)
XLA Modules:
  0.0 133.9 jit_solution(13010271791950935299)
XLA Ops:
  1.9 3.0 %collective-permute-start = (bf16[256,256]{1,0:T(8,128)(2,1)S(1)}, bf16[256,256]{1,0:T(8,128)(2,1)S(1)}, u32[]{:S(2)}, u32[]{:S(2)}) collective-permute-start(bf16[256,256]{1,0:T(8,128)(2,1)S(1)} %get-tuple-element.80), channel_id=1, source_target_pairs={{0,8},{8,0},{16,24},{24,16},{1,9},{9,1},{17,25},{25,17},{2,10},{10... | collective-permute-start | bytes 393224 | tf_op jit(solution)/shard_map/ppermute | solution.py:313
  4.9 1.5 %collective-permute-start.8 = (bf16[256,256]{1,0:T(8,128)(2,1)S(1)}, bf16[256,256]{1,0:T(8,128)(2,1)S(1)}, u32[]{:S(2)}, u32[]{:S(2)}) collective-permute-start(bf16[256,256]{1,0:T(8,128)(2,1)S(1)} %get-tuple-element.82), channel_id=1, source_target_pairs={{0,24},{8,16},{16,8},{24,0},{1,25},{9,17},{17,9},{25,1},{2,26},{10... | collective-permute-start | bytes 393224 | tf_op jit(solution)/shard_map/ppermute | solution.py:313
  8.8 2.1 %collective-permute-start.1 = (bf16[2,256,256]{2,1,0:T(8,128)(2,1)S(1)}, bf16[2,256,256]{2,1,0:T(8,128)(2,1)S(1)}, u32[]{:S(2)}, u32[]{:S(2)}) collective-permute-start(bf16[2,256,256]{2,1,0:T(8,128)(2,1)S(1)} %pad_maximum_fusion.1.refs_0_), channel_id=1, source_target_pairs={{0,2},{1,3},{2,4},{3,5},{4,6},{5,7},{6,0},{7,1},{8,10},{9,11},{10,... | collective-permute-start | bytes 786440 | tf_op jit(solution)/shard_map/ppermute | solution.py:305
  10.9 1.6 %collective-permute-done.8 = bf16[256,256]{1,0:T(8,128)(2,1)S(1)} collective-permute-done((bf16[256,256]{1,0:T(8,128)(2,1)S(1)}, bf16[256,256]{1,0:T(8,128)(2,1)S(1)}, u32[]{:S(2)}, u32[]{:S(2)}) %collective-permute-start.8) | collective-permute-done | bytes 131104 | tf_op jit(solution)/shard_map/ppermute | solution.py:313
  12.5 1.4 %collective-permute-done.7 = bf16[256,256]{1,0:T(8,128)(2,1)S(1)} collective-permute-done((bf16[256,256]{1,0:T(8,128)(2,1)S(1)}, bf16[256,256]{1,0:T(8,128)(2,1)S(1)}, u32[]{:S(2)}, u32[]{:S(2)}) %collective-permute-start.7) | collective-permute-done | bytes 131104 | tf_op jit(solution)/shard_map/ppermute | solution.py:313
  13.9 1.6 %collective-permute-start.9 = (bf16[2,256,256]{2,1,0:T(8,128)(2,1)S(1)}, bf16[2,256,256]{2,1,0:T(8,128)(2,1)S(1)}, u32[]{:S(2)}, u32[]{:S(2)}) collective-permute-start(bf16[2,256,256]{2,1,0:T(8,128)(2,1)S(1)} %pad_maximum_fusion.2.refs_1_), channel_id=1, source_target_pairs={{0,2},{1,3},{2,4},{3,5},{4,6},{5,7},{6,0},{7,1},{8,10},{9,11},{10,... | collective-permute-start | bytes 786440 | tf_op jit(solution)/shard_map/ppermute | solution.py:305
  15.5 3.2 %collective-permute-done.1.through_ref = bf16[2,256,256]{2,1,0:T(8,128)(2,1)S(1)} collective-permute-done((bf16[2,256,256]{2,1,0:T(8,128)(2,1)S(1)}, bf16[2,256,256]{2,1,0:T(8,128)(2,1)S(1)}, u32[]{:S(2)}, u32[]{:S(2)}) %collective-permute-start.1) | collective-permute-done | bytes 262176 | tf_op jit(solution)/shard_map/ppermute | solution.py:305
  19.4 4.1 %load.2 = (bf16[640,8192]{1,0:T(8,128)(2,1)S(1)}, bf16[2,256,256]{2,1,0:T(8,128)(2,1)}) custom-call(bf16[640,8192]{1,0:T(8,128)(2,1)} %w_ref.1, bf16[2,256,256]{2,1,0:T(8,128)(2,1)} %copy-done), custom_call_target="tpu_custom_call", output_to_operand_aliasing={{1}: (1, {})} | custom-call | bytes 10485760 | tf_op jit(solution)/shard_map/load/pallas_call | solution.py:57
  24.8 1.6 %collective-permute-start.2 = (bf16[256,256]{1,0:T(8,128)(2,1)S(1)}, bf16[256,256]{1,0:T(8,128)(2,1)S(1)}, u32[]{:S(2)}, u32[]{:S(2)}) collective-permute-start(bf16[256,256]{1,0:T(8,128)(2,1)S(1)} %get-tuple-element.44), channel_id=1, source_target_pairs={{0,8},{8,0},{16,24},{24,16},{1,9},{9,1},{17,25},{25,17},{2,10},{10... | collective-permute-start | bytes 393224 | tf_op jit(solution)/shard_map/ppermute | solution.py:313
  27.6 2.6 %collective-permute-start.3 = (bf16[256,256]{1,0:T(8,128)(2,1)S(1)}, bf16[256,256]{1,0:T(8,128)(2,1)S(1)}, u32[]{:S(2)}, u32[]{:S(2)}) collective-permute-start(bf16[256,256]{1,0:T(8,128)(2,1)S(1)} %get-tuple-element.45), channel_id=1, source_target_pairs={{0,16},{8,24},{16,0},{24,8},{1,17},{9,25},{17,1},{25,9},{2,18},{10... | collective-permute-start | bytes 393224 | tf_op jit(solution)/shard_map/ppermute | solution.py:313
  30.2 3.1 %collective-permute-start.4 = (bf16[256,256]{1,0:T(8,128)(2,1)S(1)}, bf16[256,256]{1,0:T(8,128)(2,1)S(1)}, u32[]{:S(2)}, u32[]{:S(2)}) collective-permute-start(bf16[256,256]{1,0:T(8,128)(2,1)S(1)} %get-tuple-element.46), channel_id=1, source_target_pairs={{0,24},{8,16},{16,8},{24,0},{1,25},{9,17},{17,9},{25,1},{2,26},{10... | collective-permute-start | bytes 393224 | tf_op jit(solution)/shard_map/ppermute | solution.py:313
  33.3 3.9 %collective-permute-done.3 = bf16[256,256]{1,0:T(8,128)(2,1)S(1)} collective-permute-done((bf16[256,256]{1,0:T(8,128)(2,1)S(1)}, bf16[256,256]{1,0:T(8,128)(2,1)S(1)}, u32[]{:S(2)}, u32[]{:S(2)}) %collective-permute-start.3) | collective-permute-done | bytes 131104 | tf_op jit(solution)/shard_map/ppermute | solution.py:313
  39.5 4.1 %load.3 = (bf16[32,256,640]{2,1,0:T(8,128)(2,1)S(1)}, bf16[2,256,256]{2,1,0:T(8,128)(2,1)S(1)}) custom-call(bf16[32,256,640]{2,1,0:T(8,128)(2,1)} %bitcast.17, bf16[2,256,256]{2,1,0:T(8,128)(2,1)S(1)} %collective-permute-done.5.through_ref), custom_call_target="tpu_custom_call", output_to_operand_aliasing={{1}: (1, {})} | custom-call | bytes 10485760 | tf_op jit(solution)/shard_map/load/pallas_call | solution.py:57
  43.6 2.1 %collective-permute-start.6 = (bf16[2,256,256]{2,1,0:T(8,128)(2,1)S(1)}, bf16[2,256,256]{2,1,0:T(8,128)(2,1)S(1)}, u32[]{:S(2)}, u32[]{:S(2)}) collective-permute-start(bf16[2,256,256]{2,1,0:T(8,128)(2,1)S(1)} %get-tuple-element.47.refs_0_), channel_id=1, source_target_pairs={{0,2},{1,3},{2,4},{3,5},{4,6},{5,7},{6,0},{7,1},{8,10},{9,11},{10,... | collective-permute-start | bytes 786440 | tf_op jit(solution)/shard_map/ppermute | solution.py:305
  46.3 3.0 %encode.2 = (f32[256,640]{1,0:T(8,128)S(1)}, bf16[256,1024]{1,0:T(8,128)(2,1)S(1)}) custom-call(s32[50]{0:T(128)S(1)} %table.1, bf16[2,256,256]{2,1,0:T(8,128)(2,1)S(1)} %pad_maximum_fusion.1.refs_0_, bf16[2,256,256]{2,1,0:T(8,128)(2,1)S(1)} %pad_maximum_fusion.2.refs_1_, bf16[2,256,256]{2,1,0:T(8,128)(2,1)S(1)} %collective-permute-done.17.refs_2_, ...), custom_call_target="tpu_custom_call" | custom-call | flops 1342177280 | bytes 4194304 | tf_op jit(solution)/shard_map/encode/pallas_call | solution.py:31
  49.4 4.5 %collective-permute-done.6.refs_4_ = bf16[2,256,256]{2,1,0:T(8,128)(2,1)S(1)} collective-permute-done((bf16[2,256,256]{2,1,0:T(8,128)(2,1)S(1)}, bf16[2,256,256]{2,1,0:T(8,128)(2,1)S(1)}, u32[]{:S(2)}, u32[]{:S(2)}) %collective-permute-start.6) | collective-permute-done | bytes 262176 | tf_op jit(solution)/shard_map/ppermute | solution.py:305
  54.0 2.0 %collective-permute-start.12 = (bf16[4,256,256]{2,1,0:T(8,128)(2,1)S(1)}, bf16[4,256,256]{2,1,0:T(8,128)(2,1)S(1)}, u32[]{:S(2)}, u32[]{:S(2)}) collective-permute-start(bf16[4,256,256]{2,1,0:T(8,128)(2,1)S(1)} %pad_maximum_fusion.refs_0_), channel_id=1, source_target_pairs={{0,2},{1,3},{2,4},{3,5},{4,6},{5,7},{8,10},{9,11},{10,12},{11,13},... | collective-permute-start | bytes 1572872 | tf_op jit(solution)/shard_map/ppermute | solution.py:305
  57.3 3.2 %encode.3 = (bf16[256,640]{1,0:T(8,128)(2,1)S(1)}, bf16[256,1024]{1,0:T(8,128)(2,1)S(1)}) custom-call(s32[50]{0:T(128)S(1)} %table.1, bf16[2,256,256]{2,1,0:T(8,128)(2,1)S(1)} %get-tuple-element.47.refs_0_, bf16[2,256,256]{2,1,0:T(8,128)(2,1)S(1)} %collective-permute-done.10.refs_1_, bf16[2,256,256]{2,1,0:T(8,128)(2,1)S(1)} %collective-permute-done.14.refs_2_, ...), custom_call_target="tpu_custom_call" | custom-call | flops 1 | bytes 1 | tf_op jit(solution)/shard_map/encode/pallas_call | solution.py:31
  60.5 1.5 %decode.2 = (bf16[256,1024]{1,0:T(8,128)(2,1)S(1)}, bf16[256,1024]{1,0:T(8,128)(2,1)S(1)}) custom-call(s32[50]{0:T(128)S(1)} %table.1, bf16[256,640]{1,0:T(8,128)(2,1)S(1)} %get-tuple-element.76.acts_ref.refs_7_.refs_5_, bf16[640,8192]{1,0:T(8,128)(2,1)S(1)} %get-tuple-element.56.w_ref.refs_6_.refs_4_), custom_call_target="tpu_custom_call" | custom-call | flops 1 | bytes 1 | tf_op jit(solution)/shard_map/decode/pallas_call | solution.py:31
  62.4 3.2 %decode.3 = (bf16[256,1024]{1,0:T(8,128)(2,1)S(1)}, bf16[256,1024]{1,0:T(8,128)(2,1)S(1)}, bf16[256,1024]{1,0:T(8,128)(2,1)S(1)}, bf16[256,1024]{1,0:T(8,128)(2,...) custom-call(s32[50]{0:T(128)S(1)} %table.1, ...), custom_call_target="tpu_custom_call" | custom-call | flops 2013265920 | bytes 4194304 | tf_op jit(solution)/shard_map/decode/pallas_call | solution.py:31
  65.9 1.9 %collective-permute-done.12.refs_2_ = bf16[4,256,256]{2,1,0:T(8,128)(2,1)S(1)} collective-permute-done((bf16[4,256,256]{2,1,0:T(8,128)(2,1)S(1)}, bf16[4,256,256]{2,1,0:T(8,128)(2,1)S(1)}, u32[]{:S(2)}, u32[]{:S(2)}) %collective-permute-start.12) | collective-permute-done | bytes 524320 | tf_op jit(solution)/shard_map/ppermute | solution.py:305
  67.8 4.2 %collective-permute-done.13.refs_4_ = bf16[4,256,256]{2,1,0:T(8,128)(2,1)S(1)} collective-permute-done((bf16[4,256,256]{2,1,0:T(8,128)(2,1)S(1)}, bf16[4,256,256]{2,1,0:T(8,128)(2,1)S(1)}, u32[]{:S(2)}, u32[]{:S(2)}) %collective-permute-start.13) | collective-permute-done | bytes 524320 | tf_op jit(solution)/shard_map/ppermute | solution.py:305
  74.2 5.8 %collective-permute-start.30 = (bf16[256,1024]{1,0:T(8,128)(2,1)S(1)}, bf16[256,1024]{1,0:T(8,128)(2,1)S(1)}, u32[]{:S(2)}, u32[]{:S(2)}) collective-permute-start(bf16[256,1024]{1,0:T(8,128)(2,1)S(1)} %add_convert_fusion.1), channel_id=1, source_target_pairs={{0,2},{1,3},{6,4},{7,5},{8,10},{9,11},{14,12},{15,13},{16,18},{17,... | collective-permute-start | bytes 1572872 | tf_op jit(solution)/shard_map/ppermute | solution.py:305
  80.6 8.5 %collective-permute-done.23 = bf16[4,256,256]{2,1,0:T(8,128)(2,1)S(1)} collective-permute-done((bf16[4,256,256]{2,1,0:T(8,128)(2,1)S(1)}, bf16[4,256,256]{2,1,0:T(8,128)(2,1)S(1)}, u32[]{:S(2)}, u32[]{:S(2)}) %collective-permute-start.23) | collective-permute-done | bytes 524320 | tf_op jit(solution)/shard_map/ppermute | solution.py:305
  92.1 4.6 %collective-permute-start.31 = (bf16[256,1024]{1,0:T(8,128)(2,1)S(1)}, bf16[256,1024]{1,0:T(8,128)(2,1)S(1)}, u32[]{:S(2)}, u32[]{:S(2)}) collective-permute-start(bf16[256,1024]{1,0:T(8,128)(2,1)S(1)} %add_convert_fusion), channel_id=1, source_target_pairs={{0,2},{1,3},{2,4},{3,5},{8,10},{9,11},{10,12},{11,13},{16,18},{17,... | collective-permute-start | bytes 1572872 | tf_op jit(solution)/shard_map/ppermute | solution.py:305
  97.7 7.8 %collective-permute-done.25.refs_2_ = bf16[4,256,256]{2,1,0:T(8,128)(2,1)S(1)} collective-permute-done((bf16[4,256,256]{2,1,0:T(8,128)(2,1)S(1)}, bf16[4,256,256]{2,1,0:T(8,128)(2,1)S(1)}, u32[]{:S(2)}, u32[]{:S(2)}) %collective-permute-start.25) | collective-permute-done | bytes 524320 | tf_op jit(solution)/shard_map/ppermute | solution.py:305
  105.8 3.6 %project.2 = (f32[256,640]{1,0:T(8,128)S(1)}, f32[256,1]{1,0:T(8,128)S(1)}) custom-call(s32[50]{0:T(128)S(1)} %table.1, bf16[4,256,256]{2,1,0:T(8,128)(2,1)S(1)} %pad_maximum_fusion.refs_0_, bf16[4,256,256]{2,1,0:T(8,128)(2,1)S(1)} %collective-permute-done.33.refs_1_, bf16[4,256,256]{2,1,0:T(8,128)(2,1)S(1)} %collective-permute-done.12.refs_2_, ...), custom_call_target="tpu_custom_call" | custom-call | flops 2013265920 | bytes 4194304 | tf_op jit(solution)/shard_map/project/pallas_call | solution.py:31
  110.4 6.9 %collective-permute-start.37 = (bf16[256,1024]{1,0:T(8,128)(2,1)S(1)}, bf16[256,1024]{1,0:T(8,128)(2,1)S(1)}, u32[]{:S(2)}, u32[]{:S(2)}) collective-permute-start(bf16[256,1024]{1,0:T(8,128)(2,1)S(1)} %get-tuple-element.74), channel_id=1, source_target_pairs={{0,2},{1,3},{2,4},{3,5},{4,6},{5,7},{8,10},{9,11},{10,12},{11,13},... | collective-permute-start | bytes 1572872 | tf_op jit(solution)/shard_map/ppermute | solution.py:305
  118.6 3.9 %project.3 = (f32[256,640]{1,0:T(8,128)}, f32[8,256]{1,0:T(8,128)S(1)}) custom-call(s32[50]{0:T(128)S(1)} %table.1, bf16[4,256,256]{2,1,0:T(8,128)(2,1)S(1)} %add.46.refs_0_, bf16[4,256,256]{2,1,0:T(8,128)(2,1)S(1)} %collective-permute-done.24.refs_1_, bf16[4,256,256]{2,1,0:T(8,128)(2,1)S(1)} %collective-permute-done.25.refs_2_, ...), custom_call_target="tpu_custom_call" | custom-call | flops 1 | bytes 1 | tf_op jit(solution)/shard_map/project/pallas_call | solution.py:31
  123.6 1.5 %collective-permute-start.40 = (f32[1,256]{1,0:T(1,128)S(1)}, f32[1,256]{1,0:T(1,128)S(1)}, u32[]{:S(2)}, u32[]{:S(2)}) collective-permute-start(f32[1,256]{1,0:T(1,128)S(1)} %slice_add_fusion), channel_id=1, source_target_pairs={{0,2},{1,3},{2,0},{3,1},{4,6},{5,7},{6,4},{7,5},{8,10},{9,11},{10,... | collective-permute-start | bytes 3080 | tf_op jit(solution)/shard_map/ppermute | solution.py:305
  125.8 2.2 %collective-permute-start.42 = (f32[1,256]{1,0:T(1,128)S(1)}, f32[1,256]{1,0:T(1,128)S(1)}, u32[]{:S(2)}, u32[]{:S(2)}) collective-permute-start(f32[1,256]{1,0:T(1,128)S(1)} %slice_add_fusion), channel_id=1, source_target_pairs={{0,6},{1,7},{2,4},{3,5},{4,2},{5,3},{6,0},{7,1},{8,14},{9,15},{10,... | collective-permute-start | bytes 3080 | tf_op jit(solution)/shard_map/ppermute | solution.py:305
  128.0 4.2 %collective-permute-done.40 = f32[1,256]{1,0:T(1,128)S(1)} collective-permute-done((f32[1,256]{1,0:T(1,128)S(1)}, f32[1,256]{1,0:T(1,128)S(1)}, u32[]{:S(2)}, u32[]{:S(2)}) %collective-permute-start.40) | collective-permute-done | bytes 1056 | tf_op jit(solution)/shard_map/ppermute | solution.py:305
  (91 shorter events, 24.8 us)
Async XLA Ops:
  8.8 9.9 %collective-permute-start.1 = (bf16[2,256,256]{2,1,0:T(8,128)(2,1)S(1)}, bf16[2,256,256]{2,1,0:T(8,128)(2,1)S(1)}, u32[]{:S(2)}, u32[]{:S(2)}) collective-permute-start(bf16[2,256,256]{2,1,0:T(8,128)(2,1)S(1)} %pad_maximum_fusion.1.refs_0_), channel_id=1, source_target_pairs={{0,2},{1,3},{2,4},{3,5},{4,6},{5,7},{6,0},{7,1},{8,10},{9,11},{10,... | collective-permute-start | bytes 786440 | tf_op jit(solution)/shard_map/ppermute | solution.py:305
  13.9 12.4 %collective-permute-start.9 = (bf16[2,256,256]{2,1,0:T(8,128)(2,1)S(1)}, bf16[2,256,256]{2,1,0:T(8,128)(2,1)S(1)}, u32[]{:S(2)}, u32[]{:S(2)}) collective-permute-start(bf16[2,256,256]{2,1,0:T(8,128)(2,1)S(1)} %pad_maximum_fusion.2.refs_1_), channel_id=1, source_target_pairs={{0,2},{1,3},{2,4},{3,5},{4,6},{5,7},{6,0},{7,1},{8,10},{9,11},{10,... | collective-permute-start | bytes 786440 | tf_op jit(solution)/shard_map/ppermute | solution.py:305
  26.3 11.4 %collective-permute-start.10 = (bf16[2,256,256]{2,1,0:T(8,128)(2,1)S(1)}, bf16[2,256,256]{2,1,0:T(8,128)(2,1)S(1)}, u32[]{:S(2)}, u32[]{:S(2)}) collective-permute-start(bf16[2,256,256]{2,1,0:T(8,128)(2,1)S(1)} %collective-permute-done.9.refs_5_), channel_id=1, source_target_pairs={{0,2},{1,3},{2,4},{3,5},{4,6},{5,7},{6,0},{7,1},{8,10},{9,11},{10,... | collective-permute-start | bytes 786440 | tf_op jit(solution)/shard_map/ppermute | solution.py:305
  26.3 12.1 %collective-permute-start.5 = (bf16[2,256,256]{2,1,0:T(8,128)(2,1)}, bf16[2,256,256]{2,1,0:T(8,128)(2,1)S(1)}, u32[]{:S(2)}, u32[]{:S(2)}) collective-permute-start(bf16[2,256,256]{2,1,0:T(8,128)(2,1)} %get-tuple-element.41.refs_4_), channel_id=1, source_target_pairs={{0,2},{1,3},{2,4},{3,5},{4,6},{5,7},{6,0},{7,1},{8,10},{9,11},{10,... | collective-permute-start | bytes 786440 | tf_op jit(solution)/shard_map/ppermute | solution.py:305
  27.6 15.9 %collective-permute-start.17 = (bf16[2,256,256]{2,1,0:T(8,128)(2,1)S(1)}, bf16[2,256,256]{2,1,0:T(8,128)(2,1)S(1)}, u32[]{:S(2)}, u32[]{:S(2)}) collective-permute-start(bf16[2,256,256]{2,1,0:T(8,128)(2,1)S(1)} %pad_maximum_fusion.1.refs_0_), channel_id=1, source_target_pairs={{0,1},{1,0},{2,3},{3,2},{4,5},{5,4},{6,7},{7,6},{8,9},{9,8},{10,11... | collective-permute-start | bytes 786440 | tf_op jit(solution)/shard_map/ppermute | solution.py:308
  27.6 9.5 %collective-permute-start.3 = (bf16[256,256]{1,0:T(8,128)(2,1)S(1)}, bf16[256,256]{1,0:T(8,128)(2,1)S(1)}, u32[]{:S(2)}, u32[]{:S(2)}) collective-permute-start(bf16[256,256]{1,0:T(8,128)(2,1)S(1)} %get-tuple-element.45), channel_id=1, source_target_pairs={{0,16},{8,24},{16,0},{24,8},{1,17},{9,25},{17,1},{25,9},{2,18},{10... | collective-permute-start | bytes 393224 | tf_op jit(solution)/shard_map/ppermute | solution.py:313
  37.2 8.5 %collective-permute-start.18 = (bf16[2,256,256]{2,1,0:T(8,128)(2,1)S(1)}, bf16[2,256,256]{2,1,0:T(8,128)(2,1)S(1)}, u32[]{:S(2)}, u32[]{:S(2)}) collective-permute-start(bf16[2,256,256]{2,1,0:T(8,128)(2,1)S(1)} %pad_maximum_fusion.2.refs_1_), channel_id=1, source_target_pairs={{0,1},{1,0},{2,3},{3,2},{4,5},{5,4},{6,7},{7,6},{8,9},{9,8},{10,11... | collective-permute-start | bytes 786440 | tf_op jit(solution)/shard_map/ppermute | solution.py:308
  37.2 8.6 %collective-permute-start.20 = (bf16[2,256,256]{2,1,0:T(8,128)(2,1)S(1)}, bf16[2,256,256]{2,1,0:T(8,128)(2,1)S(1)}, u32[]{:S(2)}, u32[]{:S(2)}) collective-permute-start(bf16[2,256,256]{2,1,0:T(8,128)(2,1)S(1)} %collective-permute-done.9.refs_5_), channel_id=1, source_target_pairs={{0,1},{1,0},{2,3},{3,2},{4,5},{5,4},{6,7},{7,6},{8,9},{9,8},{10,11... | collective-permute-start | bytes 786440 | tf_op jit(solution)/shard_map/ppermute | solution.py:308
  37.7 8.6 %collective-permute-start.19 = (bf16[2,256,256]{2,1,0:T(8,128)(2,1)}, bf16[2,256,256]{2,1,0:T(8,128)(2,1)S(1)}, u32[]{:S(2)}, u32[]{:S(2)}) collective-permute-start(bf16[2,256,256]{2,1,0:T(8,128)(2,1)} %get-tuple-element.41.refs_4_), channel_id=1, source_target_pairs={{0,1},{1,0},{2,3},{3,2},{4,5},{5,4},{6,7},{7,6},{8,9},{9,8},{10,11... | collective-permute-start | bytes 786440 | tf_op jit(solution)/shard_map/ppermute | solution.py:308
  38.5 10.8 %collective-permute-start.11 = (bf16[2,256,256]{2,1,0:T(8,128)(2,1)S(1)}, bf16[2,256,256]{2,1,0:T(8,128)(2,1)S(1)}, u32[]{:S(2)}, u32[]{:S(2)}) collective-permute-start(bf16[2,256,256]{2,1,0:T(8,128)(2,1)S(1)} %collective-permute-done.10.refs_1_), channel_id=1, source_target_pairs={{0,2},{1,3},{2,4},{3,5},{4,6},{5,7},{6,0},{7,1},{8,10},{9,11},{10,... | collective-permute-start | bytes 786440 | tf_op jit(solution)/shard_map/ppermute | solution.py:305
  43.6 10.4 %collective-permute-start.6 = (bf16[2,256,256]{2,1,0:T(8,128)(2,1)S(1)}, bf16[2,256,256]{2,1,0:T(8,128)(2,1)S(1)}, u32[]{:S(2)}, u32[]{:S(2)}) collective-permute-start(bf16[2,256,256]{2,1,0:T(8,128)(2,1)S(1)} %get-tuple-element.47.refs_0_), channel_id=1, source_target_pairs={{0,2},{1,3},{2,4},{3,5},{4,6},{5,7},{6,0},{7,1},{8,10},{9,11},{10,... | collective-permute-start | bytes 786440 | tf_op jit(solution)/shard_map/ppermute | solution.py:305
  45.7 10.3 %collective-permute-start.15 = (bf16[2,256,256]{2,1,0:T(8,128)(2,1)S(1)}, bf16[2,256,256]{2,1,0:T(8,128)(2,1)S(1)}, u32[]{:S(2)}, u32[]{:S(2)}) collective-permute-start(bf16[2,256,256]{2,1,0:T(8,128)(2,1)S(1)} %collective-permute-done.10.refs_1_), channel_id=1, source_target_pairs={{0,1},{1,0},{2,3},{3,2},{4,5},{5,4},{6,7},{7,6},{8,9},{9,8},{10,11... | collective-permute-start | bytes 786440 | tf_op jit(solution)/shard_map/ppermute | solution.py:308
  45.8 11.5 %collective-permute-start.14 = (bf16[2,256,256]{2,1,0:T(8,128)(2,1)S(1)}, bf16[2,256,256]{2,1,0:T(8,128)(2,1)S(1)}, u32[]{:S(2)}, u32[]{:S(2)}) collective-permute-start(bf16[2,256,256]{2,1,0:T(8,128)(2,1)S(1)} %get-tuple-element.47.refs_0_), channel_id=1, source_target_pairs={{0,1},{1,0},{2,3},{3,2},{4,5},{5,4},{6,7},{7,6},{8,9},{9,8},{10,11... | collective-permute-start | bytes 786440 | tf_op jit(solution)/shard_map/ppermute | solution.py:308
  54.0 13.8 %collective-permute-start.12 = (bf16[4,256,256]{2,1,0:T(8,128)(2,1)S(1)}, bf16[4,256,256]{2,1,0:T(8,128)(2,1)S(1)}, u32[]{:S(2)}, u32[]{:S(2)}) collective-permute-start(bf16[4,256,256]{2,1,0:T(8,128)(2,1)S(1)} %pad_maximum_fusion.refs_0_), channel_id=1, source_target_pairs={{0,2},{1,3},{2,4},{3,5},{4,6},{5,7},{8,10},{9,11},{10,12},{11,13},... | collective-permute-start | bytes 1572872 | tf_op jit(solution)/shard_map/ppermute | solution.py:305
  56.0 15.9 %collective-permute-start.13 = (bf16[4,256,256]{2,1,0:T(8,128)(2,1)S(1)}, bf16[4,256,256]{2,1,0:T(8,128)(2,1)S(1)}, u32[]{:S(2)}, u32[]{:S(2)}) collective-permute-start(bf16[4,256,256]{2,1,0:T(8,128)(2,1)S(1)} %pad_maximum_fusion.refs_0_), channel_id=1, source_target_pairs={{2,0},{3,1},{4,2},{5,3},{6,4},{7,5},{10,8},{11,9},{12,10},{13,11},... | collective-permute-start | bytes 1572872 | tf_op jit(solution)/shard_map/ppermute | solution.py:305
  62.1 11.9 %collective-permute-start.28 = (bf16[256,1024]{1,0:T(8,128)(2,1)S(1)}, bf16[256,1024]{1,0:T(8,128)(2,1)S(1)}, u32[]{:S(2)}, u32[]{:S(2)}) collective-permute-start(bf16[256,1024]{1,0:T(8,128)(2,1)S(1)} %get-tuple-element.57), channel_id=1, source_target_pairs={{0,1},{1,0},{2,3},{3,2},{4,5},{5,4},{6,7},{7,6},{8,9},{9,8},{10,11... | collective-permute-start | bytes 1572872 | tf_op jit(solution)/shard_map/ppermute | solution.py:308
  65.5 23.6 %collective-permute-start.29 = (bf16[256,1024]{1,0:T(8,128)(2,1)S(1)}, bf16[256,1024]{1,0:T(8,128)(2,1)S(1)}, u32[]{:S(2)}, u32[]{:S(2)}) collective-permute-start(bf16[256,1024]{1,0:T(8,128)(2,1)S(1)} %get-tuple-element.65), channel_id=1, source_target_pairs={{0,1},{1,0},{2,3},{3,2},{4,5},{5,4},{6,7},{7,6},{8,9},{9,8},{10,11... | collective-permute-start | bytes 1572872 | tf_op jit(solution)/shard_map/ppermute | solution.py:308
  72.0 8.1 %collective-permute-start.22 = (bf16[4,256,256]{2,1,0:T(8,128)(2,1)S(1)}, bf16[4,256,256]{2,1,0:T(8,128)(2,1)S(1)}, u32[]{:S(2)}, u32[]{:S(2)}) collective-permute-start(bf16[4,256,256]{2,1,0:T(8,128)(2,1)S(1)} %collective-permute-done.12.refs_2_), channel_id=1, source_target_pairs={{2,4},{3,5},{4,6},{5,7},{10,12},{11,13},{12,14},{13,15},{18,20},{1... | collective-permute-start | bytes 1572872 | tf_op jit(solution)/shard_map/ppermute | solution.py:305
  72.6 16.4 %collective-permute-start.23 = (bf16[4,256,256]{2,1,0:T(8,128)(2,1)S(1)}, bf16[4,256,256]{2,1,0:T(8,128)(2,1)S(1)}, u32[]{:S(2)}, u32[]{:S(2)}) collective-permute-start(bf16[4,256,256]{2,1,0:T(8,128)(2,1)S(1)} %collective-permute-done.13.refs_4_), channel_id=1, source_target_pairs={{2,0},{3,1},{4,2},{5,3},{10,8},{11,9},{12,10},{13,11},{18,16},{19,... | collective-permute-start | bytes 1572872 | tf_op jit(solution)/shard_map/ppermute | solution.py:305
  74.2 16.3 %collective-permute-start.30 = (bf16[256,1024]{1,0:T(8,128)(2,1)S(1)}, bf16[256,1024]{1,0:T(8,128)(2,1)S(1)}, u32[]{:S(2)}, u32[]{:S(2)}) collective-permute-start(bf16[256,1024]{1,0:T(8,128)(2,1)S(1)} %add_convert_fusion.1), channel_id=1, source_target_pairs={{0,2},{1,3},{6,4},{7,5},{8,10},{9,11},{14,12},{15,13},{16,18},{17,... | collective-permute-start | bytes 1572872 | tf_op jit(solution)/shard_map/ppermute | solution.py:305
  80.0 12.0 %collective-permute-start.33 = (bf16[4,256,256]{2,1,0:T(8,128)(2,1)S(1)}, bf16[4,256,256]{2,1,0:T(8,128)(2,1)S(1)}, u32[]{:S(2)}, u32[]{:S(2)}) collective-permute-start(bf16[4,256,256]{2,1,0:T(8,128)(2,1)S(1)} %pad_maximum_fusion.refs_0_), channel_id=1, source_target_pairs={{0,1},{1,0},{2,3},{3,2},{4,5},{5,4},{6,7},{7,6},{8,9},{9,8},{10,11... | collective-permute-start | bytes 1572872 | tf_op jit(solution)/shard_map/ppermute | solution.py:308
  80.1 12.0 %collective-permute-start.36 = (bf16[256,1024]{1,0:T(8,128)(2,1)S(1)}, bf16[256,1024]{1,0:T(8,128)(2,1)S(1)}, u32[]{:S(2)}, u32[]{:S(2)}) collective-permute-start(bf16[256,1024]{1,0:T(8,128)(2,1)S(1)} %get-tuple-element.73), channel_id=1, source_target_pairs={{0,1},{1,0},{2,3},{3,2},{4,5},{5,4},{6,7},{7,6},{8,9},{9,8},{10,11... | collective-permute-start | bytes 1572872 | tf_op jit(solution)/shard_map/ppermute | solution.py:308
  89.2 8.2 %collective-permute-start.35 = (bf16[4,256,256]{2,1,0:T(8,128)(2,1)S(1)}, bf16[4,256,256]{2,1,0:T(8,128)(2,1)S(1)}, u32[]{:S(2)}, u32[]{:S(2)}) collective-permute-start(bf16[4,256,256]{2,1,0:T(8,128)(2,1)S(1)} %collective-permute-done.13.refs_4_), channel_id=1, source_target_pairs={{0,1},{1,0},{2,3},{3,2},{4,5},{5,4},{6,7},{7,6},{8,9},{9,8},{10,11... | collective-permute-start | bytes 1572872 | tf_op jit(solution)/shard_map/ppermute | solution.py:308
  90.4 15.1 %collective-permute-start.25 = (bf16[4,256,256]{2,1,0:T(8,128)(2,1)S(1)}, bf16[4,256,256]{2,1,0:T(8,128)(2,1)S(1)}, u32[]{:S(2)}, u32[]{:S(2)}) collective-permute-start(bf16[4,256,256]{2,1,0:T(8,128)(2,1)S(1)} %add.46.refs_0_), channel_id=1, source_target_pairs={{4,6},{5,7},{2,0},{3,1},{12,14},{13,15},{10,8},{11,9},{20,22},{21,... | collective-permute-start | bytes 1572872 | tf_op jit(solution)/shard_map/ppermute | solution.py:305
  92.0 17.4 %collective-permute-start.27 = (bf16[256,1024]{1,0:T(8,128)(2,1)S(1)}, bf16[256,1024]{1,0:T(8,128)(2,1)S(1)}, u32[]{:S(2)}, u32[]{:S(2)}) collective-permute-start(bf16[256,1024]{1,0:T(8,128)(2,1)S(1)} %get-tuple-element.62), channel_id=1, source_target_pairs={{0,1},{1,0},{2,3},{3,2},{4,5},{5,4},{6,7},{7,6},{8,9},{9,8},{10,11... | collective-permute-start | bytes 1572872 | tf_op jit(solution)/shard_map/ppermute | solution.py:308
  92.1 17.3 %collective-permute-start.31 = (bf16[256,1024]{1,0:T(8,128)(2,1)S(1)}, bf16[256,1024]{1,0:T(8,128)(2,1)S(1)}, u32[]{:S(2)}, u32[]{:S(2)}) collective-permute-start(bf16[256,1024]{1,0:T(8,128)(2,1)S(1)} %add_convert_fusion), channel_id=1, source_target_pairs={{0,2},{1,3},{2,4},{3,5},{8,10},{9,11},{10,12},{11,13},{16,18},{17,... | collective-permute-start | bytes 1572872 | tf_op jit(solution)/shard_map/ppermute | solution.py:305
  96.7 12.7 %collective-permute-start.32 = (bf16[256,1024]{1,0:T(8,128)(2,1)S(1)}, bf16[256,1024]{1,0:T(8,128)(2,1)S(1)}, u32[]{:S(2)}, u32[]{:S(2)}) collective-permute-start(bf16[256,1024]{1,0:T(8,128)(2,1)S(1)} %add_convert_fusion), channel_id=1, source_target_pairs={{4,2},{5,3},{6,4},{7,5},{12,10},{13,11},{14,12},{15,13},{20,18},{2... | collective-permute-start | bytes 1572872 | tf_op jit(solution)/shard_map/ppermute | solution.py:305
  97.4 21.1 %collective-permute-start.24 = (bf16[4,256,256]{2,1,0:T(8,128)(2,1)S(1)}, bf16[4,256,256]{2,1,0:T(8,128)(2,1)S(1)}, u32[]{:S(2)}, u32[]{:S(2)}) collective-permute-start(bf16[4,256,256]{2,1,0:T(8,128)(2,1)S(1)} %add.46.refs_0_), channel_id=1, source_target_pairs={{0,1},{1,0},{2,3},{3,2},{4,5},{5,4},{6,7},{7,6},{8,9},{9,8},{10,11... | collective-permute-start | bytes 1572872 | tf_op jit(solution)/shard_map/ppermute | solution.py:308
  105.5 13.1 %collective-permute-start.26 = (bf16[4,256,256]{2,1,0:T(8,128)(2,1)S(1)}, bf16[4,256,256]{2,1,0:T(8,128)(2,1)S(1)}, u32[]{:S(2)}, u32[]{:S(2)}) collective-permute-start(bf16[4,256,256]{2,1,0:T(8,128)(2,1)S(1)} %collective-permute-done.25.refs_2_), channel_id=1, source_target_pairs={{0,1},{1,0},{2,3},{3,2},{4,5},{5,4},{6,7},{7,6},{8,9},{9,8},{10,11... | collective-permute-start | bytes 1572872 | tf_op jit(solution)/shard_map/ppermute | solution.py:308
  110.4 22.4 %collective-permute-start.37 = (bf16[256,1024]{1,0:T(8,128)(2,1)S(1)}, bf16[256,1024]{1,0:T(8,128)(2,1)S(1)}, u32[]{:S(2)}, u32[]{:S(2)}) collective-permute-start(bf16[256,1024]{1,0:T(8,128)(2,1)S(1)} %get-tuple-element.74), channel_id=1, source_target_pairs={{0,2},{1,3},{2,4},{3,5},{4,6},{5,7},{8,10},{9,11},{10,12},{11,13},... | collective-permute-start | bytes 1572872 | tf_op jit(solution)/shard_map/ppermute | solution.py:305
  117.2 15.5 %collective-permute-start.38 = (bf16[256,1024]{1,0:T(8,128)(2,1)S(1)}, bf16[256,1024]{1,0:T(8,128)(2,1)S(1)}, u32[]{:S(2)}, u32[]{:S(2)}) collective-permute-start(bf16[256,1024]{1,0:T(8,128)(2,1)S(1)} %get-tuple-element.75), channel_id=1, source_target_pairs={{2,0},{3,1},{4,2},{5,3},{6,4},{7,5},{10,8},{11,9},{12,10},{13,11},... | collective-permute-start | bytes 1572872 | tf_op jit(solution)/shard_map/ppermute | solution.py:305
  123.6 8.6 %collective-permute-start.40 = (f32[1,256]{1,0:T(1,128)S(1)}, f32[1,256]{1,0:T(1,128)S(1)}, u32[]{:S(2)}, u32[]{:S(2)}) collective-permute-start(f32[1,256]{1,0:T(1,128)S(1)} %slice_add_fusion), channel_id=1, source_target_pairs={{0,2},{1,3},{2,0},{3,1},{4,6},{5,7},{6,4},{7,5},{8,10},{9,11},{10,... | collective-permute-start | bytes 3080 | tf_op jit(solution)/shard_map/ppermute | solution.py:305
  (17 other events, 190.4 us)

commit v7 on v6

--- a/solution.py
+++ b/solution.py
@@ -148,15 +148,22 @@
 
 
 def third_body(chips, table, *refs):
-    near_1, far_1, near_3, far_3, up_ref, down_ref, going_up_ref, going_down_ref = refs
+    near_1, far_1, near_3, far_3, up_ref, down_ref = refs[:3] + (refs[3:-4],) + refs[-4:-2]
     chip = table[3]
-    for target, come_ref, turn in ((going_up_ref, up_ref, 1), (going_down_ref, down_ref, chips - 2)):
-        for near_ref, far_ref, chosen in ((near_3, far_3, chip == turn), (near_1, far_1, chip != turn)):
-
-            @pl.when(chosen)
-            def _():
-                total = near_ref[...].astype(F32) + far_ref[...].astype(F32)
-                target[...] = (total + come_ref[...].astype(F32)).astype(BF16)
+    for target, come_ref, turn in ((refs[-2], up_ref, 1), (refs[-1], down_ref, chips - 2)):
+
+        @pl.when(chip == turn)
+        def _():
+            rows = far_3[0].shape[0]
+            for h, far_ref in enumerate(far_3):
+                part = slice(h * rows, (h + 1) * rows)
+                total = near_3[part].astype(F32) + far_ref[...].astype(F32)
+                target[part] = (total + come_ref[part].astype(F32)).astype(BF16)
+
+        @pl.when(chip != turn)
+        def _():
+            total = near_1[...].astype(F32) + far_1[...].astype(F32)
+            target[...] = (total + come_ref[...].astype(F32)).astype(BF16)
 
 
 def pieces(refs, streams):
@@ -229,9 +236,28 @@
         out_ref[...] = jnp.dot(acts_ref[...], w, preferred_element_type=F32).astype(BF16)
 
 
-def decode(table, at, acts, w, share, count, hint):
+def decode(table, at, acts, w, share, count):
     outs = [((acts.shape[0], share), BF16)] * count
+    hint = cost(2 * count * acts.size * share, 4 << 20)
     return kernel_call(functools.partial(dec_body, at), outs, [table, acts, w], "decode", hint)
+
+
+def first_body(at, table, acts_ref, w_ref, *out_refs):
+    share = out_refs[0].shape[1]
+    for q, targets in enumerate((out_refs[:-1], out_refs[-1:])):
+        w = w_ref[:, aligned(table[at + q], share)]
+        part = jnp.dot(acts_ref[...], w, preferred_element_type=F32).astype(BF16)
+        rows = part.shape[0] // len(targets)
+        for h, out_ref in enumerate(targets):
+            out_ref[...] = part[h * rows:(h + 1) * rows]
+
+
+def sum_body(table, near_ref, *refs):
+    far_refs, out_ref = refs[:-1], refs[-1]
+    rows = far_refs[0].shape[0]
+    for h, far_ref in enumerate(far_refs):
+        part = slice(h * rows, (h + 1) * rows)
+        out_ref[part] = (near_ref[part].astype(F32) + far_ref[...].astype(F32)).astype(BF16)
 
 
 def proj_body(count, first, last, n_feat, at, table, *refs):
@@ -326,10 +352,13 @@
         if k == 1:
             second = after(second, table)
         if k == 2:
-            w_out, first = load(w_dec, first, 44)
+            w_out, far_x[0][0] = load(w_dec, far_x[0][0], 44)
+            first = after(first, far_x[0][0])
             shard_g, = exchange(pick(table, after(resid_grad, first), n_tok), ((0, 1, 2, 3),))
         if k == 3:
-            w_in, first = load(w_enc.reshape(n_tok * n_feat, width, feats), first, 36)
+            far_x[0][1] = after(far_x[0][1], far_x[1][0])
+            w_in, far_x[0][1] = load(w_enc.reshape(n_tok * n_feat, width, feats), far_x[0][1], 36)
+            first = after(first, far_x[0][1])
             second = after(second, shard_g)
         near_x[-1] = [first, second]
         if k > 1:
@@ -341,30 +370,35 @@
 
     up_pairs = [(a, a + 1) for a in range(chips - 1)]
     down_pairs = [(a + 1, a) for a in range(chips - 1)]
-    shard_g = after(shard_g, near_x[-1])
+    shard_g = after(shard_g, near_x[-1], carry)
     up_1, down_1 = send(shard_g, up_pairs), send(shard_g, down_pairs)
 
     slots = [near_x[2], far_x[2], near_x[3], far_x[3]]
     acts, own_x = encode(table, SLOTS["enc_b"], slots, w_in, bias, carry, X_STREAMS, True, n_feat)
 
-    far_3, near_3 = decode(table, SLOTS["dec_a"], acts, w_out, share, 2, LIGHT)
+    *far_3, near_3 = kernel_call(
+        functools.partial(first_body, SLOTS["dec_a"]),
+        [((rows // 2, share), BF16)] * 2 + [((rows, share), BF16)],
+        [table, acts, w_out],
+        "decode",
+    )
     up_1, down_1 = after((up_1, down_1), far_3)
-    parts = {3: (near_3, cross(far_3))}
-    outs = decode(
-        table, SLOTS["dec_b"], after(acts, far_3), w_out, share, 6, cost(12 * rows * feats * share, 4 << 20)
-    )
+    far_in = [cross(a) for a in far_3]
+    start, = kernel_call(sum_body, [((rows, share), BF16)], [table, near_3, *far_in], "sum")
+    parts = {}
+    outs = decode(table, SLOTS["dec_b"], after(acts, start), w_out, share, 6)
     for n, k in enumerate((2, 1, 0)):
         parts[k] = (outs[2 * n + 1], cross(outs[2 * n]))
 
     def pair_sum(k):
         return parts[k][0].astype(F32) + parts[k][1].astype(F32)
 
-    come = send(pair_sum(3).astype(BF16), [(0, 1), (3, 2)])
+    come = send(start, [(0, 1), (3, 2)])
     up_2, down_2 = send(up_1, up_pairs[1:]), send(down_1, down_pairs[:-1])
+    going = (pair_sum(2) + come.astype(F32)).astype(BF16)
     two_g = up_2 + down_2
     three_g = send(two_g, [(2, 3), (1, 0)])
 
-    going = (pair_sum(2) + come.astype(F32)).astype(BF16)
     up = send(going, up_pairs[:2])
     down = send(going, down_pairs[1:])
 
@@ -377,7 +411,7 @@
     going_up, going_down = kernel_call(
         functools.partial(third_body, chips),
         [((rows, share), BF16)] * 2,
-        [table, *parts[1], *parts[3], up, down],
+        [table, *parts[1], near_3, *far_in, up, down],
         "third",
     )
     going_up, going_down = after((going_up, going_down), carry, base)

time: 134 us -> 137 us (1.022)
  waiting for transfers between devices: 43.8 us -> 50.6 us
  starting transfers between devices: 53.6 us -> 48.5 us
    ppermute x19, waiting for transfers between devices: 35.5 us -> 40.6 us  [send(): return lax.ppermute(array, 'feat', along(pairs))]
    ppermute x19, starting transfers between devices: 38.4 us -> 35 us  [send(): return lax.ppermute(array, 'feat', along(pairs))]
    ppermute x6, starting transfers between devices: 11.8 us -> 10.2 us  [exchange(): lax.ppermute(blocks[s], 'tok', [(a, a ^ s) for a in range(n_tok)])]
    ppermute x18 -> x19, waiting for transfers between devices: 1.18 us -> 2.64 us  [cross(): return lax.ppermute(array, 'feat', [(a, a ^ 1) for a in range(n_feat)])]
    pallas_call x7 -> x8, Pallas kernels: 19.3 us -> 20 us  [kernel_call(): pl.pallas_call(body, in_specs=[SMEM] + [VMEM] * (len(args) - 1), out_spec...]
    ppermute x18 -> x19, starting transfers between devices: 3.41 us -> 3.31 us  [cross(): return lax.ppermute(array, 'feat', [(a, a ^ 1) for a in range(n_feat)])]
  transfers between devices with their start and end apart: 43 -> 44, of which waited for: 14 -> 18; matrix products, arithmetic and copies ran while one was open for 1% -> 2% of each run, Pallas kernels for 22% -> 23%
where the time goes in v7:
time: 137 us; the launch traced here: 136 us
  waiting for transfers between devices  50.6 us (37%)
  starting transfers between devices  48.5 us (35%)
  Pallas kernels  30.7 us (22%)
  other arithmetic  2.64 us (2%)
  local copies, waits for them, and re-layouts  2.6 us (2%)
    ppermute x19, waiting for transfers between devices, send(): return lax.ppermute(array, 'feat', along(pairs))  40.6 us
    ppermute x19, starting transfers between devices, send(): return lax.ppermute(array, 'feat', along(pairs))  35 us
    pallas_call x8, Pallas kernels, kernel_call(): pl.pallas_call(body, in_specs=[SMEM] + [VMEM] * (len(args) - 1), out_spec...  20 us
    ppermute x6, starting transfers between devices, exchange(): lax.ppermute(blocks[s], 'tok', [(a, a ^ s) for a in range(n_tok)])  10.2 us
    pallas_call x2, Pallas kernels, load(): pl.pallas_call(load_body, in_specs=[anywhere, anywhere], out_specs=[VMEM,...  8.17 us
    ppermute x6, waiting for transfers between devices, exchange(): lax.ppermute(blocks[s], 'tok', [(a, a ^ s) for a in range(n_tok)])  7.33 us
    ppermute x19, starting transfers between devices, cross(): return lax.ppermute(array, 'feat', [(a, a ^ 1) for a in range(n_feat)])  3.31 us
  transfers between devices with their start and end apart: 44, of which 18 were waited for; matrix products, arithmetic and copies ran while one was open for 2% of the time, Pallas kernels for 23%

profile of v7, /device:TPU:0, one launch (start us, length us, event | category | flops | bytes accessed | tf_op | source)
XLA Modules:
  0.0 136.2 jit_solution(15428405403302752988)
XLA Ops:
  1.9 3.0 %collective-permute-start = (bf16[256,256]{1,0:T(8,128)(2,1)S(1)}, bf16[256,256]{1,0:T(8,128)(2,1)S(1)}, u32[]{:S(2)}, u32[]{:S(2)}) collective-permute-start(bf16[256,256]{1,0:T(8,128)(2,1)S(1)} %get-tuple-element.88), channel_id=1, source_target_pairs={{0,8},{8,0},{16,24},{24,16},{1,9},{9,1},{17,25},{25,17},{2,10},{10... | collective-permute-start | bytes 393224 | tf_op jit(solution)/shard_map/ppermute | solution.py:339
  4.9 1.5 %collective-permute-start.8 = (bf16[256,256]{1,0:T(8,128)(2,1)S(1)}, bf16[256,256]{1,0:T(8,128)(2,1)S(1)}, u32[]{:S(2)}, u32[]{:S(2)}) collective-permute-start(bf16[256,256]{1,0:T(8,128)(2,1)S(1)} %get-tuple-element.90), channel_id=1, source_target_pairs={{0,24},{8,16},{16,8},{24,0},{1,25},{9,17},{17,9},{25,1},{2,26},{10... | collective-permute-start | bytes 393224 | tf_op jit(solution)/shard_map/ppermute | solution.py:339
  6.4 2.4 %collective-permute-done = bf16[256,256]{1,0:T(8,128)(2,1)S(1)} collective-permute-done((bf16[256,256]{1,0:T(8,128)(2,1)S(1)}, bf16[256,256]{1,0:T(8,128)(2,1)S(1)}, u32[]{:S(2)}, u32[]{:S(2)}) %collective-permute-start) | collective-permute-done | bytes 131104 | tf_op jit(solution)/shard_map/ppermute | solution.py:339
  8.9 2.1 %collective-permute-start.1 = (bf16[2,256,256]{2,1,0:T(8,128)(2,1)S(1)}, bf16[2,256,256]{2,1,0:T(8,128)(2,1)S(1)}, u32[]{:S(2)}, u32[]{:S(2)}) collective-permute-start(bf16[2,256,256]{2,1,0:T(8,128)(2,1)S(1)} %pad_maximum_fusion.1.refs_0_), channel_id=1, source_target_pairs={{0,2},{1,3},{2,4},{3,5},{4,6},{5,7},{6,0},{7,1},{8,10},{9,11},{10,... | collective-permute-start | bytes 786440 | tf_op jit(solution)/shard_map/ppermute | solution.py:331
  13.9 1.6 %collective-permute-start.12 = (bf16[2,256,256]{2,1,0:T(8,128)(2,1)S(1)}, bf16[2,256,256]{2,1,0:T(8,128)(2,1)S(1)}, u32[]{:S(2)}, u32[]{:S(2)}) collective-permute-start(bf16[2,256,256]{2,1,0:T(8,128)(2,1)S(1)} %pad_maximum_fusion.2.refs_1_), channel_id=1, source_target_pairs={{0,2},{1,3},{2,4},{3,5},{4,6},{5,7},{6,0},{7,1},{8,10},{9,11},{10,... | collective-permute-start | bytes 786440 | tf_op jit(solution)/shard_map/ppermute | solution.py:331
  16.2 4.1 %load.2 = (bf16[640,8192]{1,0:T(8,128)(2,1)S(1)}, bf16[2,256,256]{2,1,0:T(8,128)(2,1)}) custom-call(bf16[640,8192]{1,0:T(8,128)(2,1)} %w_ref.1, bf16[2,256,256]{2,1,0:T(8,128)(2,1)} %copy-done), custom_call_target="tpu_custom_call", output_to_operand_aliasing={{1}: (1, {})} | custom-call | bytes 10485760 | tf_op jit(solution)/shard_map/load/pallas_call | solution.py:57
  21.6 2.0 %collective-permute-start.3 = (bf16[256,256]{1,0:T(8,128)(2,1)S(1)}, bf16[256,256]{1,0:T(8,128)(2,1)S(1)}, u32[]{:S(2)}, u32[]{:S(2)}) collective-permute-start(bf16[256,256]{1,0:T(8,128)(2,1)S(1)} %get-tuple-element.49), channel_id=1, source_target_pairs={{0,8},{8,0},{16,24},{24,16},{1,9},{9,1},{17,25},{25,17},{2,10},{10... | collective-permute-start | bytes 393224 | tf_op jit(solution)/shard_map/ppermute | solution.py:339
  23.6 1.5 %collective-permute-start.4 = (bf16[256,256]{1,0:T(8,128)(2,1)S(1)}, bf16[256,256]{1,0:T(8,128)(2,1)S(1)}, u32[]{:S(2)}, u32[]{:S(2)}) collective-permute-start(bf16[256,256]{1,0:T(8,128)(2,1)S(1)} %get-tuple-element.50), channel_id=1, source_target_pairs={{0,16},{8,24},{16,0},{24,8},{1,17},{9,25},{17,1},{25,9},{2,18},{10... | collective-permute-start | bytes 393224 | tf_op jit(solution)/shard_map/ppermute | solution.py:339
  26.6 1.6 %collective-permute-start.6 = (bf16[2,256,256]{2,1,0:T(8,128)(2,1)S(1)}, bf16[2,256,256]{2,1,0:T(8,128)(2,1)S(1)}, u32[]{:S(2)}, u32[]{:S(2)}) collective-permute-start(bf16[2,256,256]{2,1,0:T(8,128)(2,1)S(1)} %collective-permute-done.1.refs_4_), channel_id=1, source_target_pairs={{0,2},{1,3},{2,4},{3,5},{4,6},{5,7},{6,0},{7,1},{8,10},{9,11},{10,... | collective-permute-start | bytes 786440 | tf_op jit(solution)/shard_map/ppermute | solution.py:331
  28.6 2.1 %collective-permute-start.5 = (bf16[256,256]{1,0:T(8,128)(2,1)S(1)}, bf16[256,256]{1,0:T(8,128)(2,1)S(1)}, u32[]{:S(2)}, u32[]{:S(2)}) collective-permute-start(bf16[256,256]{1,0:T(8,128)(2,1)S(1)} %get-tuple-element.51), channel_id=1, source_target_pairs={{0,24},{8,16},{16,8},{24,0},{1,25},{9,17},{17,9},{25,1},{2,26},{10... | collective-permute-start | bytes 393224 | tf_op jit(solution)/shard_map/ppermute | solution.py:339
  30.8 3.7 %collective-permute-done.5 = bf16[256,256]{1,0:T(8,128)(2,1)S(1)} collective-permute-done((bf16[256,256]{1,0:T(8,128)(2,1)S(1)}, bf16[256,256]{1,0:T(8,128)(2,1)S(1)}, u32[]{:S(2)}, u32[]{:S(2)}) %collective-permute-start.5) | collective-permute-done | bytes 131104 | tf_op jit(solution)/shard_map/ppermute | solution.py:339
  34.6 2.1 %collective-permute-done.13.refs_1_ = bf16[2,256,256]{2,1,0:T(8,128)(2,1)S(1)} collective-permute-done((bf16[2,256,256]{2,1,0:T(8,128)(2,1)S(1)}, bf16[2,256,256]{2,1,0:T(8,128)(2,1)S(1)}, u32[]{:S(2)}, u32[]{:S(2)}) %collective-permute-start.13) | collective-permute-done | bytes 262176 | tf_op jit(solution)/shard_map/ppermute | solution.py:331
  36.6 4.1 %load.3 = (bf16[32,256,640]{2,1,0:T(8,128)(2,1)S(1)}, bf16[2,256,256]{2,1,0:T(8,128)(2,1)S(1)}) custom-call(bf16[32,256,640]{2,1,0:T(8,128)(2,1)} %bitcast.17, bf16[2,256,256]{2,1,0:T(8,128)(2,1)S(1)} %collective-permute-done.9.through_ref), custom_call_target="tpu_custom_call", output_to_operand_aliasing={{1}: (1, {})} | custom-call | bytes 10485760 | tf_op jit(solution)/shard_map/load/pallas_call | solution.py:57
  40.7 1.5 %collective-permute-done.6.refs_0_ = bf16[2,256,256]{2,1,0:T(8,128)(2,1)S(1)} collective-permute-done((bf16[2,256,256]{2,1,0:T(8,128)(2,1)S(1)}, bf16[2,256,256]{2,1,0:T(8,128)(2,1)S(1)}, u32[]{:S(2)}, u32[]{:S(2)}) %collective-permute-start.6) | collective-permute-done | bytes 262176 | tf_op jit(solution)/shard_map/ppermute | solution.py:331
  42.8 3.0 %encode.2 = (f32[256,640]{1,0:T(8,128)S(1)}, bf16[256,1024]{1,0:T(8,128)(2,1)S(1)}) custom-call(s32[50]{0:T(128)S(1)} %table.1, bf16[2,256,256]{2,1,0:T(8,128)(2,1)S(1)} %pad_maximum_fusion.1.refs_0_, bf16[2,256,256]{2,1,0:T(8,128)(2,1)S(1)} %pad_maximum_fusion.2.refs_1_, bf16[2,256,256]{2,1,0:T(8,128)(2,1)S(1)} %copy-done.1, ...), custom_call_target="tpu_custom_call" | custom-call | flops 1342177280 | bytes 4194304 | tf_op jit(solution)/shard_map/encode/pallas_call | solution.py:31
  45.8 2.1 %collective-permute-done.14.refs_5_ = bf16[2,256,256]{2,1,0:T(8,128)(2,1)S(1)} collective-permute-done((bf16[2,256,256]{2,1,0:T(8,128)(2,1)S(1)}, bf16[2,256,256]{2,1,0:T(8,128)(2,1)S(1)}, u32[]{:S(2)}, u32[]{:S(2)}) %collective-permute-start.14) | collective-permute-done | bytes 262176 | tf_op jit(solution)/shard_map/ppermute | solution.py:331
  47.9 4.7 %collective-permute-done.11.refs_4_ = bf16[2,256,256]{2,1,0:T(8,128)(2,1)S(1)} collective-permute-done((bf16[2,256,256]{2,1,0:T(8,128)(2,1)S(1)}, bf16[2,256,256]{2,1,0:T(8,128)(2,1)S(1)}, u32[]{:S(2)}, u32[]{:S(2)}) %collective-permute-start.11) | collective-permute-done | bytes 262176 | tf_op jit(solution)/shard_map/ppermute | solution.py:331
  55.2 3.2 %encode.3 = (bf16[256,640]{1,0:T(8,128)(2,1)S(1)}, bf16[256,1024]{1,0:T(8,128)(2,1)S(1)}) custom-call(s32[50]{0:T(128)S(1)} %table.1, bf16[2,256,256]{2,1,0:T(8,128)(2,1)S(1)} %collective-permute-done.6.refs_0_, bf16[2,256,256]{2,1,0:T(8,128)(2,1)S(1)} %collective-permute-done.13.refs_1_, bf16[2,256,256]{2,1,0:T(8,128)(2,1)S(1)} %collective-permute-done.18.refs_2_, ...), custom_call_target="tpu_custom_call" | custom-call | flops 1 | bytes 1 | tf_op jit(solution)/shard_map/encode/pallas_call | solution.py:31
  58.4 1.5 %decode.2 = (bf16[128,1024]{1,0:T(8,128)(2,1)S(1)}, bf16[128,1024]{1,0:T(8,128)(2,1)S(1)}, bf16[256,1024]{1,0:T(8,128)(2,1)S(1)}) custom-call(s32[50]{0:T(128)S(1)} %table.1, bf16[256,640]{1,0:T(8,128)(2,1)S(1)} %get-tuple-element.84.acts_ref.refs_7_.refs_5_, bf16[640,8192]{1,0:T(8,128)(2,1)S(1)} %get-tuple-element.63.w_ref.refs_6_.refs_4_), custom_call_target="tpu_custom_call" | custom-call | flops 1 | bytes 1 | tf_op jit(solution)/shard_map/decode/pallas_call | solution.py:31
  62.7 3.2 %collective-permute-done.16.refs_2_ = bf16[4,256,256]{2,1,0:T(8,128)(2,1)S(1)} collective-permute-done((bf16[4,256,256]{2,1,0:T(8,128)(2,1)S(1)}, bf16[4,256,256]{2,1,0:T(8,128)(2,1)S(1)}, u32[]{:S(2)}, u32[]{:S(2)}) %collective-permute-start.16) | collective-permute-done | bytes 524320 | tf_op jit(solution)/shard_map/ppermute | solution.py:331
  65.9 4.2 %collective-permute-done.17.refs_4_ = bf16[4,256,256]{2,1,0:T(8,128)(2,1)S(1)} collective-permute-done((bf16[4,256,256]{2,1,0:T(8,128)(2,1)S(1)}, bf16[4,256,256]{2,1,0:T(8,128)(2,1)S(1)}, u32[]{:S(2)}, u32[]{:S(2)}) %collective-permute-start.17) | collective-permute-done | bytes 524320 | tf_op jit(solution)/shard_map/ppermute | solution.py:331
  72.1 3.2 %decode.3 = (bf16[256,1024]{1,0:T(8,128)(2,1)S(1)}, bf16[256,1024]{1,0:T(8,128)(2,1)S(1)}, bf16[256,1024]{1,0:T(8,128)(2,1)S(1)}, bf16[256,1024]{1,0:T(8,128)(2,...) custom-call(s32[50]{0:T(128)S(1)} %table.1, ...), custom_call_target="tpu_custom_call" | custom-call | flops 2013265920 | bytes 4194304 | tf_op jit(solution)/shard_map/decode/pallas_call | solution.py:31
  75.4 5.3 %collective-permute-start.31 = (bf16[256,1024]{1,0:T(8,128)(2,1)S(1)}, bf16[256,1024]{1,0:T(8,128)(2,1)S(1)}, u32[]{:S(2)}, u32[]{:S(2)}) collective-permute-start(bf16[256,1024]{1,0:T(8,128)(2,1)S(1)} %sum.1), channel_id=1, source_target_pairs={{0,2},{1,3},{6,4},{7,5},{8,10},{9,11},{14,12},{15,13},{16,18},{17,... | collective-permute-start | bytes 1572872 | tf_op jit(solution)/shard_map/ppermute | solution.py:331
  81.2 5.4 %collective-permute-done.23 = bf16[4,256,256]{2,1,0:T(8,128)(2,1)S(1)} collective-permute-done((bf16[4,256,256]{2,1,0:T(8,128)(2,1)S(1)}, bf16[4,256,256]{2,1,0:T(8,128)(2,1)S(1)}, u32[]{:S(2)}, u32[]{:S(2)}) %collective-permute-start.23) | collective-permute-done | bytes 524320 | tf_op jit(solution)/shard_map/ppermute | solution.py:331
  87.3 5.1 %collective-permute-done.31 = bf16[256,1024]{1,0:T(8,128)(2,1)S(1)} collective-permute-done((bf16[256,1024]{1,0:T(8,128)(2,1)S(1)}, bf16[256,1024]{1,0:T(8,128)(2,1)S(1)}, u32[]{:S(2)}, u32[]{:S(2)}) %collective-permute-start.31) | collective-permute-done | bytes 524320 | tf_op jit(solution)/shard_map/ppermute | solution.py:331
  94.1 4.6 %collective-permute-start.32 = (bf16[256,1024]{1,0:T(8,128)(2,1)S(1)}, bf16[256,1024]{1,0:T(8,128)(2,1)S(1)}, u32[]{:S(2)}, u32[]{:S(2)}) collective-permute-start(bf16[256,1024]{1,0:T(8,128)(2,1)S(1)} %add_convert_fusion), channel_id=1, source_target_pairs={{0,2},{1,3},{2,4},{3,5},{8,10},{9,11},{10,12},{11,13},{16,18},{17,... | collective-permute-start | bytes 1572872 | tf_op jit(solution)/shard_map/ppermute | solution.py:331
  99.7 8.3 %collective-permute-done.25.refs_2_ = bf16[4,256,256]{2,1,0:T(8,128)(2,1)S(1)} collective-permute-done((bf16[4,256,256]{2,1,0:T(8,128)(2,1)S(1)}, bf16[4,256,256]{2,1,0:T(8,128)(2,1)S(1)}, u32[]{:S(2)}, u32[]{:S(2)}) %collective-permute-start.25) | collective-permute-done | bytes 524320 | tf_op jit(solution)/shard_map/ppermute | solution.py:331
  108.2 3.6 %project.2 = (f32[256,640]{1,0:T(8,128)S(1)}, f32[256,1]{1,0:T(8,128)S(1)}) custom-call(s32[50]{0:T(128)S(1)} %table.1, bf16[4,256,256]{2,1,0:T(8,128)(2,1)S(1)} %pad_maximum_fusion.refs_0_, bf16[4,256,256]{2,1,0:T(8,128)(2,1)S(1)} %collective-permute-done.34.refs_1_, bf16[4,256,256]{2,1,0:T(8,128)(2,1)S(1)} %collective-permute-done.16.refs_2_, ...), custom_call_target="tpu_custom_call" | custom-call | flops 2013265920 | bytes 4194304 | tf_op jit(solution)/shard_map/project/pallas_call | solution.py:31
  112.8 6.7 %collective-permute-start.38 = (bf16[256,1024]{1,0:T(8,128)(2,1)S(1)}, bf16[256,1024]{1,0:T(8,128)(2,1)S(1)}, u32[]{:S(2)}, u32[]{:S(2)}) collective-permute-start(bf16[256,1024]{1,0:T(8,128)(2,1)S(1)} %get-tuple-element.82), channel_id=1, source_target_pairs={{0,2},{1,3},{2,4},{3,5},{4,6},{5,7},{8,10},{9,11},{10,12},{11,13},... | collective-permute-start | bytes 1572872 | tf_op jit(solution)/shard_map/ppermute | solution.py:331
  120.8 3.9 %project.3 = (f32[256,640]{1,0:T(8,128)}, f32[8,256]{1,0:T(8,128)S(1)}) custom-call(s32[50]{0:T(128)S(1)} %table.1, bf16[4,256,256]{2,1,0:T(8,128)(2,1)S(1)} %add.43.refs_0_, bf16[4,256,256]{2,1,0:T(8,128)(2,1)S(1)} %collective-permute-done.24.refs_1_, bf16[4,256,256]{2,1,0:T(8,128)(2,1)S(1)} %collective-permute-done.25.refs_2_, ...), custom_call_target="tpu_custom_call" | custom-call | flops 1 | bytes 1 | tf_op jit(solution)/shard_map/project/pallas_call | solution.py:31
  128.1 2.2 %collective-permute-start.43 = (f32[1,256]{1,0:T(1,128)S(1)}, f32[1,256]{1,0:T(1,128)S(1)}, u32[]{:S(2)}, u32[]{:S(2)}) collective-permute-start(f32[1,256]{1,0:T(1,128)S(1)} %slice_add_fusion), channel_id=1, source_target_pairs={{0,6},{1,7},{2,4},{3,5},{4,2},{5,3},{6,0},{7,1},{8,14},{9,15},{10,... | collective-permute-start | bytes 3080 | tf_op jit(solution)/shard_map/ppermute | solution.py:331
  130.3 4.1 %collective-permute-done.39 = bf16[256,1024]{1,0:T(8,128)(2,1)S(1)} collective-permute-done((bf16[256,1024]{1,0:T(8,128)(2,1)S(1)}, bf16[256,1024]{1,0:T(8,128)(2,1)S(1)}, u32[]{:S(2)}, u32[]{:S(2)}) %collective-permute-start.39) | collective-permute-done | bytes 524320 | tf_op jit(solution)/shard_map/ppermute | solution.py:331
  (93 shorter events, 27.6 us)
Async XLA Ops:
  4.9 8.2 %collective-permute-start.8 = (bf16[256,256]{1,0:T(8,128)(2,1)S(1)}, bf16[256,256]{1,0:T(8,128)(2,1)S(1)}, u32[]{:S(2)}, u32[]{:S(2)}) collective-permute-start(bf16[256,256]{1,0:T(8,128)(2,1)S(1)} %get-tuple-element.90), channel_id=1, source_target_pairs={{0,24},{8,16},{16,8},{24,0},{1,25},{9,17},{17,9},{25,1},{2,26},{10... | collective-permute-start | bytes 393224 | tf_op jit(solution)/shard_map/ppermute | solution.py:339
  8.9 11.4 %collective-permute-start.1 = (bf16[2,256,256]{2,1,0:T(8,128)(2,1)S(1)}, bf16[2,256,256]{2,1,0:T(8,128)(2,1)S(1)}, u32[]{:S(2)}, u32[]{:S(2)}) collective-permute-start(bf16[2,256,256]{2,1,0:T(8,128)(2,1)S(1)} %pad_maximum_fusion.1.refs_0_), channel_id=1, source_target_pairs={{0,2},{1,3},{2,4},{3,5},{4,6},{5,7},{6,0},{7,1},{8,10},{9,11},{10,... | collective-permute-start | bytes 786440 | tf_op jit(solution)/shard_map/ppermute | solution.py:331
  13.9 11.8 %collective-permute-start.12 = (bf16[2,256,256]{2,1,0:T(8,128)(2,1)S(1)}, bf16[2,256,256]{2,1,0:T(8,128)(2,1)S(1)}, u32[]{:S(2)}, u32[]{:S(2)}) collective-permute-start(bf16[2,256,256]{2,1,0:T(8,128)(2,1)S(1)} %pad_maximum_fusion.2.refs_1_), channel_id=1, source_target_pairs={{0,2},{1,3},{2,4},{3,5},{4,6},{5,7},{6,0},{7,1},{8,10},{9,11},{10,... | collective-permute-start | bytes 786440 | tf_op jit(solution)/shard_map/ppermute | solution.py:331
  25.2 9.4 %collective-permute-start.9 = (bf16[2,256,256]{2,1,0:T(8,128)(2,1)S(1)}, bf16[2,256,256]{2,1,0:T(8,128)(2,1)S(1)}, u32[]{:S(2)}, u32[]{:S(2)}) collective-permute-start(bf16[2,256,256]{2,1,0:T(8,128)(2,1)S(1)} %pad_maximum_fusion.2.refs_1_), channel_id=1, source_target_pairs={{0,1},{1,0},{2,3},{3,2},{4,5},{5,4},{6,7},{7,6},{8,9},{9,8},{10,11... | collective-permute-start | bytes 786440 | tf_op jit(solution)/shard_map/ppermute | solution.py:334
  25.2 9.4 %collective-permute-start.10 = (bf16[2,256,256]{2,1,0:T(8,128)(2,1)S(1)}, bf16[2,256,256]{2,1,0:T(8,128)(2,1)S(1)}, u32[]{:S(2)}, u32[]{:S(2)}) collective-permute-start(bf16[2,256,256]{2,1,0:T(8,128)(2,1)S(1)} %collective-permute-done.1.refs_4_), channel_id=1, source_target_pairs={{0,1},{1,0},{2,3},{3,2},{4,5},{5,4},{6,7},{7,6},{8,9},{9,8},{10,11... | collective-permute-start | bytes 786440 | tf_op jit(solution)/shard_map/ppermute | solution.py:334
  25.7 11.0 %collective-permute-start.13 = (bf16[2,256,256]{2,1,0:T(8,128)(2,1)S(1)}, bf16[2,256,256]{2,1,0:T(8,128)(2,1)S(1)}, u32[]{:S(2)}, u32[]{:S(2)}) collective-permute-start(bf16[2,256,256]{2,1,0:T(8,128)(2,1)S(1)} %collective-permute-done.12.refs_5_), channel_id=1, source_target_pairs={{0,2},{1,3},{2,4},{3,5},{4,6},{5,7},{6,0},{7,1},{8,10},{9,11},{10,... | collective-permute-start | bytes 786440 | tf_op jit(solution)/shard_map/ppermute | solution.py:331
  26.6 15.6 %collective-permute-start.6 = (bf16[2,256,256]{2,1,0:T(8,128)(2,1)S(1)}, bf16[2,256,256]{2,1,0:T(8,128)(2,1)S(1)}, u32[]{:S(2)}, u32[]{:S(2)}) collective-permute-start(bf16[2,256,256]{2,1,0:T(8,128)(2,1)S(1)} %collective-permute-done.1.refs_4_), channel_id=1, source_target_pairs={{0,2},{1,3},{2,4},{3,5},{4,6},{5,7},{6,0},{7,1},{8,10},{9,11},{10,... | collective-permute-start | bytes 786440 | tf_op jit(solution)/shard_map/ppermute | solution.py:331
  34.5 8.3 %collective-permute-start.15 = (bf16[2,256,256]{2,1,0:T(8,128)(2,1)S(1)}, bf16[2,256,256]{2,1,0:T(8,128)(2,1)S(1)}, u32[]{:S(2)}, u32[]{:S(2)}) collective-permute-start(bf16[2,256,256]{2,1,0:T(8,128)(2,1)S(1)} %collective-permute-done.12.refs_5_), channel_id=1, source_target_pairs={{0,1},{1,0},{2,3},{3,2},{4,5},{5,4},{6,7},{7,6},{8,9},{9,8},{10,11... | collective-permute-start | bytes 786440 | tf_op jit(solution)/shard_map/ppermute | solution.py:334
  36.6 11.2 %collective-permute-start.14 = (bf16[2,256,256]{2,1,0:T(8,128)(2,1)S(1)}, bf16[2,256,256]{2,1,0:T(8,128)(2,1)S(1)}, u32[]{:S(2)}, u32[]{:S(2)}) collective-permute-start(bf16[2,256,256]{2,1,0:T(8,128)(2,1)S(1)} %collective-permute-done.13.refs_1_), channel_id=1, source_target_pairs={{0,2},{1,3},{2,4},{3,5},{4,6},{5,7},{6,0},{7,1},{8,10},{9,11},{10,... | collective-permute-start | bytes 786440 | tf_op jit(solution)/shard_map/ppermute | solution.py:331
  42.3 10.3 %collective-permute-start.11 = (bf16[2,256,256]{2,1,0:T(8,128)(2,1)S(1)}, bf16[2,256,256]{2,1,0:T(8,128)(2,1)S(1)}, u32[]{:S(2)}, u32[]{:S(2)}) collective-permute-start(bf16[2,256,256]{2,1,0:T(8,128)(2,1)S(1)} %collective-permute-done.6.refs_0_), channel_id=1, source_target_pairs={{0,2},{1,3},{2,4},{3,5},{4,6},{5,7},{6,0},{7,1},{8,10},{9,11},{10,... | collective-permute-start | bytes 786440 | tf_op jit(solution)/shard_map/ppermute | solution.py:331
  42.3 11.6 %collective-permute-start.18 = (bf16[2,256,256]{2,1,0:T(8,128)(2,1)S(1)}, bf16[2,256,256]{2,1,0:T(8,128)(2,1)S(1)}, u32[]{:S(2)}, u32[]{:S(2)}) collective-permute-start(bf16[2,256,256]{2,1,0:T(8,128)(2,1)S(1)} %collective-permute-done.6.refs_0_), channel_id=1, source_target_pairs={{0,1},{1,0},{2,3},{3,2},{4,5},{5,4},{6,7},{7,6},{8,9},{9,8},{10,11... | collective-permute-start | bytes 786440 | tf_op jit(solution)/shard_map/ppermute | solution.py:334
  42.3 12.9 %collective-permute-start.19 = (bf16[2,256,256]{2,1,0:T(8,128)(2,1)S(1)}, bf16[2,256,256]{2,1,0:T(8,128)(2,1)S(1)}, u32[]{:S(2)}, u32[]{:S(2)}) collective-permute-start(bf16[2,256,256]{2,1,0:T(8,128)(2,1)S(1)} %collective-permute-done.13.refs_1_), channel_id=1, source_target_pairs={{0,1},{1,0},{2,3},{3,2},{4,5},{5,4},{6,7},{7,6},{8,9},{9,8},{10,11... | collective-permute-start | bytes 786440 | tf_op jit(solution)/shard_map/ppermute | solution.py:334
  52.5 13.4 %collective-permute-start.16 = (bf16[4,256,256]{2,1,0:T(8,128)(2,1)S(1)}, bf16[4,256,256]{2,1,0:T(8,128)(2,1)S(1)}, u32[]{:S(2)}, u32[]{:S(2)}) collective-permute-start(bf16[4,256,256]{2,1,0:T(8,128)(2,1)S(1)} %pad_maximum_fusion.refs_0_), channel_id=1, source_target_pairs={{0,2},{1,3},{2,4},{3,5},{4,6},{5,7},{8,10},{9,11},{10,12},{11,13},... | collective-permute-start | bytes 1572872 | tf_op jit(solution)/shard_map/ppermute | solution.py:331
  53.9 16.2 %collective-permute-start.17 = (bf16[4,256,256]{2,1,0:T(8,128)(2,1)S(1)}, bf16[4,256,256]{2,1,0:T(8,128)(2,1)S(1)}, u32[]{:S(2)}, u32[]{:S(2)}) collective-permute-start(bf16[4,256,256]{2,1,0:T(8,128)(2,1)S(1)} %pad_maximum_fusion.refs_0_), channel_id=1, source_target_pairs={{2,0},{3,1},{4,2},{5,3},{6,4},{7,5},{10,8},{11,9},{12,10},{13,11},... | collective-permute-start | bytes 1572872 | tf_op jit(solution)/shard_map/ppermute | solution.py:331
  70.1 10.8 %collective-permute-start.22 = (bf16[4,256,256]{2,1,0:T(8,128)(2,1)S(1)}, bf16[4,256,256]{2,1,0:T(8,128)(2,1)S(1)}, u32[]{:S(2)}, u32[]{:S(2)}) collective-permute-start(bf16[4,256,256]{2,1,0:T(8,128)(2,1)S(1)} %collective-permute-done.16.refs_2_), channel_id=1, source_target_pairs={{2,4},{3,5},{4,6},{5,7},{10,12},{11,13},{12,14},{13,15},{18,20},{1... | collective-permute-start | bytes 1572872 | tf_op jit(solution)/shard_map/ppermute | solution.py:331
  70.8 15.8 %collective-permute-start.23 = (bf16[4,256,256]{2,1,0:T(8,128)(2,1)S(1)}, bf16[4,256,256]{2,1,0:T(8,128)(2,1)S(1)}, u32[]{:S(2)}, u32[]{:S(2)}) collective-permute-start(bf16[4,256,256]{2,1,0:T(8,128)(2,1)S(1)} %collective-permute-done.17.refs_4_), channel_id=1, source_target_pairs={{2,0},{3,1},{4,2},{5,3},{10,8},{11,9},{12,10},{13,11},{18,16},{19,... | collective-permute-start | bytes 1572872 | tf_op jit(solution)/shard_map/ppermute | solution.py:331
  75.3 11.5 %collective-permute-start.30 = (bf16[256,1024]{1,0:T(8,128)(2,1)S(1)}, bf16[256,1024]{1,0:T(8,128)(2,1)S(1)}, u32[]{:S(2)}, u32[]{:S(2)}) collective-permute-start(bf16[256,1024]{1,0:T(8,128)(2,1)S(1)} %get-tuple-element.73), channel_id=1, source_target_pairs={{0,1},{1,0},{2,3},{3,2},{4,5},{5,4},{6,7},{7,6},{8,9},{9,8},{10,11... | collective-permute-start | bytes 1572872 | tf_op jit(solution)/shard_map/ppermute | solution.py:334
  75.4 17.1 %collective-permute-start.31 = (bf16[256,1024]{1,0:T(8,128)(2,1)S(1)}, bf16[256,1024]{1,0:T(8,128)(2,1)S(1)}, u32[]{:S(2)}, u32[]{:S(2)}) collective-permute-start(bf16[256,1024]{1,0:T(8,128)(2,1)S(1)} %sum.1), channel_id=1, source_target_pairs={{0,2},{1,3},{6,4},{7,5},{8,10},{9,11},{14,12},{15,13},{16,18},{17,... | collective-permute-start | bytes 1572872 | tf_op jit(solution)/shard_map/ppermute | solution.py:331
  80.6 13.3 %collective-permute-start.34 = (bf16[4,256,256]{2,1,0:T(8,128)(2,1)S(1)}, bf16[4,256,256]{2,1,0:T(8,128)(2,1)S(1)}, u32[]{:S(2)}, u32[]{:S(2)}) collective-permute-start(bf16[4,256,256]{2,1,0:T(8,128)(2,1)S(1)} %pad_maximum_fusion.refs_0_), channel_id=1, source_target_pairs={{0,1},{1,0},{2,3},{3,2},{4,5},{5,4},{6,7},{7,6},{8,9},{9,8},{10,11... | collective-permute-start | bytes 1572872 | tf_op jit(solution)/shard_map/ppermute | solution.py:334
  80.9 13.2 %collective-permute-start.37 = (bf16[256,1024]{1,0:T(8,128)(2,1)S(1)}, bf16[256,1024]{1,0:T(8,128)(2,1)S(1)}, u32[]{:S(2)}, u32[]{:S(2)}) collective-permute-start(bf16[256,1024]{1,0:T(8,128)(2,1)S(1)} %get-tuple-element.81), channel_id=1, source_target_pairs={{0,1},{1,0},{2,3},{3,2},{4,5},{5,4},{6,7},{7,6},{8,9},{9,8},{10,11... | collective-permute-start | bytes 1572872 | tf_op jit(solution)/shard_map/ppermute | solution.py:334
  86.6 12.1 %collective-permute-start.35 = (bf16[4,256,256]{2,1,0:T(8,128)(2,1)S(1)}, bf16[4,256,256]{2,1,0:T(8,128)(2,1)S(1)}, u32[]{:S(2)}, u32[]{:S(2)}) collective-permute-start(bf16[4,256,256]{2,1,0:T(8,128)(2,1)S(1)} %collective-permute-done.16.refs_2_), channel_id=1, source_target_pairs={{0,1},{1,0},{2,3},{3,2},{4,5},{5,4},{6,7},{7,6},{8,9},{9,8},{10,11... | collective-permute-start | bytes 1572872 | tf_op jit(solution)/shard_map/ppermute | solution.py:334
  86.8 12.7 %collective-permute-start.36 = (bf16[4,256,256]{2,1,0:T(8,128)(2,1)S(1)}, bf16[4,256,256]{2,1,0:T(8,128)(2,1)S(1)}, u32[]{:S(2)}, u32[]{:S(2)}) collective-permute-start(bf16[4,256,256]{2,1,0:T(8,128)(2,1)S(1)} %collective-permute-done.17.refs_4_), channel_id=1, source_target_pairs={{0,1},{1,0},{2,3},{3,2},{4,5},{5,4},{6,7},{7,6},{8,9},{9,8},{10,11... | collective-permute-start | bytes 1572872 | tf_op jit(solution)/shard_map/ppermute | solution.py:334
  92.4 15.5 %collective-permute-start.25 = (bf16[4,256,256]{2,1,0:T(8,128)(2,1)S(1)}, bf16[4,256,256]{2,1,0:T(8,128)(2,1)S(1)}, u32[]{:S(2)}, u32[]{:S(2)}) collective-permute-start(bf16[4,256,256]{2,1,0:T(8,128)(2,1)S(1)} %add.43.refs_0_), channel_id=1, source_target_pairs={{4,6},{5,7},{2,0},{3,1},{12,14},{13,15},{10,8},{11,9},{20,22},{21,... | collective-permute-start | bytes 1572872 | tf_op jit(solution)/shard_map/ppermute | solution.py:331
  94.0 17.9 %collective-permute-start.29 = (bf16[256,1024]{1,0:T(8,128)(2,1)S(1)}, bf16[256,1024]{1,0:T(8,128)(2,1)S(1)}, u32[]{:S(2)}, u32[]{:S(2)}) collective-permute-start(bf16[256,1024]{1,0:T(8,128)(2,1)S(1)} %get-tuple-element.71), channel_id=1, source_target_pairs={{0,1},{1,0},{2,3},{3,2},{4,5},{5,4},{6,7},{7,6},{8,9},{9,8},{10,11... | collective-permute-start | bytes 1572872 | tf_op jit(solution)/shard_map/ppermute | solution.py:334
  94.1 17.8 %collective-permute-start.32 = (bf16[256,1024]{1,0:T(8,128)(2,1)S(1)}, bf16[256,1024]{1,0:T(8,128)(2,1)S(1)}, u32[]{:S(2)}, u32[]{:S(2)}) collective-permute-start(bf16[256,1024]{1,0:T(8,128)(2,1)S(1)} %add_convert_fusion), channel_id=1, source_target_pairs={{0,2},{1,3},{2,4},{3,5},{8,10},{9,11},{10,12},{11,13},{16,18},{17,... | collective-permute-start | bytes 1572872 | tf_op jit(solution)/shard_map/ppermute | solution.py:331
  98.7 13.2 %collective-permute-start.33 = (bf16[256,1024]{1,0:T(8,128)(2,1)S(1)}, bf16[256,1024]{1,0:T(8,128)(2,1)S(1)}, u32[]{:S(2)}, u32[]{:S(2)}) collective-permute-start(bf16[256,1024]{1,0:T(8,128)(2,1)S(1)} %add_convert_fusion), channel_id=1, source_target_pairs={{4,2},{5,3},{6,4},{7,5},{12,10},{13,11},{14,12},{15,13},{20,18},{2... | collective-permute-start | bytes 1572872 | tf_op jit(solution)/shard_map/ppermute | solution.py:331
  99.4 21.4 %collective-permute-start.24 = (bf16[4,256,256]{2,1,0:T(8,128)(2,1)S(1)}, bf16[4,256,256]{2,1,0:T(8,128)(2,1)S(1)}, u32[]{:S(2)}, u32[]{:S(2)}) collective-permute-start(bf16[4,256,256]{2,1,0:T(8,128)(2,1)S(1)} %add.43.refs_0_), channel_id=1, source_target_pairs={{0,1},{1,0},{2,3},{3,2},{4,5},{5,4},{6,7},{7,6},{8,9},{9,8},{10,11... | collective-permute-start | bytes 1572872 | tf_op jit(solution)/shard_map/ppermute | solution.py:334
  107.9 12.9 %collective-permute-start.26 = (bf16[4,256,256]{2,1,0:T(8,128)(2,1)S(1)}, bf16[4,256,256]{2,1,0:T(8,128)(2,1)S(1)}, u32[]{:S(2)}, u32[]{:S(2)}) collective-permute-start(bf16[4,256,256]{2,1,0:T(8,128)(2,1)S(1)} %collective-permute-done.25.refs_2_), channel_id=1, source_target_pairs={{0,1},{1,0},{2,3},{3,2},{4,5},{5,4},{6,7},{7,6},{8,9},{9,8},{10,11... | collective-permute-start | bytes 1572872 | tf_op jit(solution)/shard_map/ppermute | solution.py:334
  112.8 17.4 %collective-permute-start.38 = (bf16[256,1024]{1,0:T(8,128)(2,1)S(1)}, bf16[256,1024]{1,0:T(8,128)(2,1)S(1)}, u32[]{:S(2)}, u32[]{:S(2)}) collective-permute-start(bf16[256,1024]{1,0:T(8,128)(2,1)S(1)} %get-tuple-element.82), channel_id=1, source_target_pairs={{0,2},{1,3},{2,4},{3,5},{4,6},{5,7},{8,10},{9,11},{10,12},{11,13},... | collective-permute-start | bytes 1572872 | tf_op jit(solution)/shard_map/ppermute | solution.py:331
  119.5 14.9 %collective-permute-start.39 = (bf16[256,1024]{1,0:T(8,128)(2,1)S(1)}, bf16[256,1024]{1,0:T(8,128)(2,1)S(1)}, u32[]{:S(2)}, u32[]{:S(2)}) collective-permute-start(bf16[256,1024]{1,0:T(8,128)(2,1)S(1)} %get-tuple-element.83), channel_id=1, source_target_pairs={{2,0},{3,1},{4,2},{5,3},{6,4},{7,5},{10,8},{11,9},{12,10},{13,11},... | collective-permute-start | bytes 1572872 | tf_op jit(solution)/shard_map/ppermute | solution.py:331
  125.9 9.7 %collective-permute-start.41 = (f32[1,256]{1,0:T(1,128)S(1)}, f32[1,256]{1,0:T(1,128)S(1)}, u32[]{:S(2)}, u32[]{:S(2)}) collective-permute-start(f32[1,256]{1,0:T(1,128)S(1)} %slice_add_fusion), channel_id=1, source_target_pairs={{0,2},{1,3},{2,0},{3,1},{4,6},{5,7},{6,4},{7,5},{8,10},{9,11},{10,... | collective-permute-start | bytes 3080 | tf_op jit(solution)/shard_map/ppermute | solution.py:331
  127.3 8.3 %collective-permute-start.42 = (f32[1,256]{1,0:T(1,128)S(1)}, f32[1,256]{1,0:T(1,128)S(1)}, u32[]{:S(2)}, u32[]{:S(2)}) collective-permute-start(f32[1,256]{1,0:T(1,128)S(1)} %slice_add_fusion), channel_id=1, source_target_pairs={{0,4},{1,5},{2,6},{3,7},{4,0},{5,1},{6,2},{7,3},{8,12},{9,13},{10,... | collective-permute-start | bytes 3080 | tf_op jit(solution)/shard_map/ppermute | solution.py:331
  (18 other events, 178.9 us)

commit v8 on v7

--- a/solution.py
+++ b/solution.py
@@ -70,7 +70,7 @@
     )(w, through)
 
 
-SLOTS = {"enc_a": 4, "enc_b": 8, "dec_a": 12, "dec_b": 14, "proj_a": 20, "proj_b": 32, "hits": 40}
+SLOTS = {"enc_a": 4, "enc_b": 8, "dec": 12, "proj_a": 20, "proj_b": 32, "hits": 40}
 
 
 def table_body(n_tok, n_feat, blocks, ids_ref, active_ref, out_ref):
@@ -231,20 +231,7 @@
 
 def dec_body(at, table, acts_ref, w_ref, *out_refs):
     share = out_refs[0].shape[1]
-    for q, out_ref in enumerate(out_refs):
-        w = w_ref[:, aligned(table[at + q], share)]
-        out_ref[...] = jnp.dot(acts_ref[...], w, preferred_element_type=F32).astype(BF16)
-
-
-def decode(table, at, acts, w, share, count):
-    outs = [((acts.shape[0], share), BF16)] * count
-    hint = cost(2 * count * acts.size * share, 4 << 20)
-    return kernel_call(functools.partial(dec_body, at), outs, [table, acts, w], "decode", hint)
-
-
-def first_body(at, table, acts_ref, w_ref, *out_refs):
-    share = out_refs[0].shape[1]
-    for q, targets in enumerate((out_refs[:-1], out_refs[-1:])):
+    for q, targets in enumerate([out_refs[:2]] + [(out_ref,) for out_ref in out_refs[2:]]):
         w = w_ref[:, aligned(table[at + q], share)]
         part = jnp.dot(acts_ref[...], w, preferred_element_type=F32).astype(BF16)
         rows = part.shape[0] // len(targets)
@@ -354,18 +341,19 @@
         if k == 2:
             w_out, far_x[0][0] = load(w_dec, far_x[0][0], 44)
             first = after(first, far_x[0][0])
-            shard_g, = exchange(pick(table, after(resid_grad, first), n_tok), ((0, 1, 2, 3),))
         if k == 3:
             far_x[0][1] = after(far_x[0][1], far_x[1][0])
             w_in, far_x[0][1] = load(w_enc.reshape(n_tok * n_feat, width, feats), far_x[0][1], 36)
             first = after(first, far_x[0][1])
-            second = after(second, shard_g)
+            shard_g, = exchange(pick(table, after(resid_grad, first), n_tok), ((0, 1, 2, 3),))
         near_x[-1] = [first, second]
         if k > 1:
             far_x.append([cross(a) for a in near_x[-1]])
         near_x.append([send(first, ring), send(second, ring)])
     slots = [near_x[0], far_x[0], near_x[1], far_x[1]]
-    carry = encode(table, SLOTS["enc_a"], slots, w_in, bias, None, X_STREAMS, False, n_feat)
+    carry = encode(
+        after(table, shard_g), SLOTS["enc_a"], slots, w_in, bias, None, X_STREAMS, False, n_feat
+    )
     far_x.append([cross(near_x[3][0]), cross(after(near_x[3][1], carry))])
 
     up_pairs = [(a, a + 1) for a in range(chips - 1)]
@@ -376,19 +364,17 @@
     slots = [near_x[2], far_x[2], near_x[3], far_x[3]]
     acts, own_x = encode(table, SLOTS["enc_b"], slots, w_in, bias, carry, X_STREAMS, True, n_feat)
 
-    *far_3, near_3 = kernel_call(
-        functools.partial(first_body, SLOTS["dec_a"]),
-        [((rows // 2, share), BF16)] * 2 + [((rows, share), BF16)],
+    far_3_a, far_3_b, near_3, *outs = kernel_call(
+        functools.partial(dec_body, SLOTS["dec"]),
+        [((rows // 2, share), BF16)] * 2 + [((rows, share), BF16)] * (2 * chips - 1),
         [table, acts, w_out],
         "decode",
     )
-    up_1, down_1 = after((up_1, down_1), far_3)
-    far_in = [cross(a) for a in far_3]
+    up_1, down_1 = after((up_1, down_1), far_3_a)
+    far_in = [cross(far_3_a), cross(far_3_b)]
     start, = kernel_call(sum_body, [((rows, share), BF16)], [table, near_3, *far_in], "sum")
-    parts = {}
-    outs = decode(table, SLOTS["dec_b"], after(acts, start), w_out, share, 6)
-    for n, k in enumerate((2, 1, 0)):
-        parts[k] = (outs[2 * n + 1], cross(outs[2 * n]))
+    outs = after(outs, start)
+    parts = {k: (outs[2 * n + 1], cross(outs[2 * n])) for n, k in enumerate((2, 1, 0))}
 
     def pair_sum(k):
         return parts[k][0].astype(F32) + parts[k][1].astype(F32)

time: 137 us -> 133 us (0.971)
  starting transfers between devices: 48.5 us -> 45.9 us
    ppermute x6, starting transfers between devices: 10.2 us -> 8.56 us  [exchange(): lax.ppermute(blocks[s], 'tok', [(a, a ^ s) for a in range(n_tok)])]
    pallas_call x8 -> x7, Pallas kernels: 20 us -> 19.3 us  [kernel_call(): pl.pallas_call(body, in_specs=[SMEM] + [VMEM] * (len(args) - 1), out_spec...]
  transfers between devices with their start and end apart: 44 -> 44, of which waited for: 18 -> 19; matrix products, arithmetic and copies ran while one was open for 2% -> 2% of each run, Pallas kernels for 23% -> 23%
where the time goes in v8:
time: 133 us; the launch traced here: 132 us
  waiting for transfers between devices  50.1 us (38%)
  starting transfers between devices  45.9 us (35%)
  Pallas kernels  30.1 us (23%)
  other arithmetic  2.62 us (2%)
  local copies, waits for them, and re-layouts  2.55 us (2%)
    ppermute x19, waiting for transfers between devices, send(): return lax.ppermute(array, 'feat', along(pairs))  39.7 us
    ppermute x19, starting transfers between devices, send(): return lax.ppermute(array, 'feat', along(pairs))  34.4 us
    pallas_call x7, Pallas kernels, kernel_call(): pl.pallas_call(body, in_specs=[SMEM] + [VMEM] * (len(args) - 1), out_spec...  19.3 us
    ppermute x6, starting transfers between devices, exchange(): lax.ppermute(blocks[s], 'tok', [(a, a ^ s) for a in range(n_tok)])  8.56 us
    pallas_call x2, Pallas kernels, load(): pl.pallas_call(load_body, in_specs=[anywhere, anywhere], out_specs=[VMEM,...  8.17 us
    ppermute x6, waiting for transfers between devices, exchange(): lax.ppermute(blocks[s], 'tok', [(a, a ^ s) for a in range(n_tok)])  7.6 us
    ppermute x19, starting transfers between devices, cross(): return lax.ppermute(array, 'feat', [(a, a ^ 1) for a in range(n_feat)])  2.87 us
    ppermute x19, waiting for transfers between devices, cross(): return lax.ppermute(array, 'feat', [(a, a ^ 1) for a in range(n_feat)])  2.87 us
  transfers between devices with their start and end apart: 44, of which 19 were waited for; matrix products, arithmetic and copies ran while one was open for 2% of the time, Pallas kernels for 23%

profile of v8, /device:TPU:0, one launch (start us, length us, event | category | flops | bytes accessed | tf_op | source)
XLA Modules:
  0.0 132.3 jit_solution(3245271753561173432)
XLA Ops:
  1.8 3.0 %collective-permute-start = (bf16[256,256]{1,0:T(8,128)(2,1)S(1)}, bf16[256,256]{1,0:T(8,128)(2,1)S(1)}, u32[]{:S(2)}, u32[]{:S(2)}) collective-permute-start(bf16[256,256]{1,0:T(8,128)(2,1)S(1)} %get-tuple-element.98), channel_id=1, source_target_pairs={{0,8},{8,0},{16,24},{24,16},{1,9},{9,1},{17,25},{25,17},{2,10},{10... | collective-permute-start | bytes 393224 | tf_op jit(solution)/shard_map/ppermute | solution.py:326
  4.8 1.5 %collective-permute-start.4 = (bf16[256,256]{1,0:T(8,128)(2,1)S(1)}, bf16[256,256]{1,0:T(8,128)(2,1)S(1)}, u32[]{:S(2)}, u32[]{:S(2)}) collective-permute-start(bf16[256,256]{1,0:T(8,128)(2,1)S(1)} %get-tuple-element.97), channel_id=1, source_target_pairs={{0,16},{8,24},{16,0},{24,8},{1,17},{9,25},{17,1},{25,9},{2,18},{10... | collective-permute-start | bytes 393224 | tf_op jit(solution)/shard_map/ppermute | solution.py:326
  6.3 2.4 %collective-permute-done = bf16[256,256]{1,0:T(8,128)(2,1)S(1)} collective-permute-done((bf16[256,256]{1,0:T(8,128)(2,1)S(1)}, bf16[256,256]{1,0:T(8,128)(2,1)S(1)}, u32[]{:S(2)}, u32[]{:S(2)}) %collective-permute-start) | collective-permute-done | bytes 131104 | tf_op jit(solution)/shard_map/ppermute | solution.py:326
  8.8 1.9 %collective-permute-start.1 = (bf16[2,256,256]{2,1,0:T(8,128)(2,1)S(1)}, bf16[2,256,256]{2,1,0:T(8,128)(2,1)S(1)}, u32[]{:S(2)}, u32[]{:S(2)}) collective-permute-start(bf16[2,256,256]{2,1,0:T(8,128)(2,1)S(1)} %pad_maximum_fusion.1.refs_0_), channel_id=1, source_target_pairs={{0,2},{1,3},{2,4},{3,5},{4,6},{5,7},{6,0},{7,1},{8,10},{9,11},{10,... | collective-permute-start | bytes 786440 | tf_op jit(solution)/shard_map/ppermute | solution.py:318
  11.4 1.3 %table.1 = s32[50]{0:T(128)S(1)} custom-call(s32[2]{0:T(128)S(1)} %pad_add_fusion.ids_ref, s32[2,20]{1,0:T(2,128)S(1)} %copy-done.4), custom_call_target="tpu_custom_call" | custom-call | flops 1 | bytes 1 | tf_op jit(solution)/shard_map/table/pallas_call | solution.py:112
  12.8 1.6 %collective-permute-start.12 = (bf16[2,256,256]{2,1,0:T(8,128)(2,1)S(1)}, bf16[2,256,256]{2,1,0:T(8,128)(2,1)S(1)}, u32[]{:S(2)}, u32[]{:S(2)}) collective-permute-start(bf16[2,256,256]{2,1,0:T(8,128)(2,1)S(1)} %pad_maximum_fusion.2.refs_1_), channel_id=1, source_target_pairs={{0,2},{1,3},{2,4},{3,5},{4,6},{5,7},{6,0},{7,1},{8,10},{9,11},{10,... | collective-permute-start | bytes 786440 | tf_op jit(solution)/shard_map/ppermute | solution.py:318
  15.2 4.1 %load.2 = (bf16[640,8192]{1,0:T(8,128)(2,1)S(1)}, bf16[2,256,256]{2,1,0:T(8,128)(2,1)}) custom-call(bf16[640,8192]{1,0:T(8,128)(2,1)} %w_ref.1, bf16[2,256,256]{2,1,0:T(8,128)(2,1)} %copy-done), custom_call_target="tpu_custom_call", output_to_operand_aliasing={{1}: (1, {})} | custom-call | bytes 10485760 | tf_op jit(solution)/shard_map/load/pallas_call | solution.py:57
  19.9 1.6 %collective-permute-start.3 = (bf16[2,256,256]{2,1,0:T(8,128)(2,1)S(1)}, bf16[2,256,256]{2,1,0:T(8,128)(2,1)S(1)}, u32[]{:S(2)}, u32[]{:S(2)}) collective-permute-start(bf16[2,256,256]{2,1,0:T(8,128)(2,1)S(1)} %collective-permute-done.1.refs_4_), channel_id=1, source_target_pairs={{0,2},{1,3},{2,4},{3,5},{4,6},{5,7},{6,0},{7,1},{8,10},{9,11},{10,... | collective-permute-start | bytes 786440 | tf_op jit(solution)/shard_map/ppermute | solution.py:318
  21.4 4.0 %collective-permute-done.12.refs_5_ = bf16[2,256,256]{2,1,0:T(8,128)(2,1)S(1)} collective-permute-done((bf16[2,256,256]{2,1,0:T(8,128)(2,1)S(1)}, bf16[2,256,256]{2,1,0:T(8,128)(2,1)S(1)}, u32[]{:S(2)}, u32[]{:S(2)}) %collective-permute-start.12) | collective-permute-done | bytes 262176 | tf_op jit(solution)/shard_map/ppermute | solution.py:318
  25.5 4.1 %load.3 = (bf16[32,256,640]{2,1,0:T(8,128)(2,1)S(1)}, bf16[2,256,256]{2,1,0:T(8,128)(2,1)S(1)}) custom-call(bf16[32,256,640]{2,1,0:T(8,128)(2,1)} %bitcast.17, bf16[2,256,256]{2,1,0:T(8,128)(2,1)S(1)} %collective-permute-done.6.through_ref), custom_call_target="tpu_custom_call", output_to_operand_aliasing={{1}: (1, {})} | custom-call | bytes 10485760 | tf_op jit(solution)/shard_map/load/pallas_call | solution.py:57
  29.6 1.5 %collective-permute-done.3.refs_0_ = bf16[2,256,256]{2,1,0:T(8,128)(2,1)S(1)} collective-permute-done((bf16[2,256,256]{2,1,0:T(8,128)(2,1)S(1)}, bf16[2,256,256]{2,1,0:T(8,128)(2,1)S(1)}, u32[]{:S(2)}, u32[]{:S(2)}) %collective-permute-start.3) | collective-permute-done | bytes 262176 | tf_op jit(solution)/shard_map/ppermute | solution.py:318
  32.4 3.3 %collective-permute-start.10 = (bf16[256,256]{1,0:T(8,128)(2,1)S(1)}, bf16[256,256]{1,0:T(8,128)(2,1)S(1)}, u32[]{:S(2)}, u32[]{:S(2)}) collective-permute-start(bf16[256,256]{1,0:T(8,128)(2,1)S(1)} %get-tuple-element.59), channel_id=1, source_target_pairs={{0,24},{8,16},{16,8},{24,0},{1,25},{9,17},{17,9},{25,1},{2,26},{10... | collective-permute-start | bytes 393224 | tf_op jit(solution)/shard_map/ppermute | solution.py:326
  36.5 3.1 %collective-permute-done.10 = bf16[256,256]{1,0:T(8,128)(2,1)S(1)} collective-permute-done((bf16[256,256]{1,0:T(8,128)(2,1)S(1)}, bf16[256,256]{1,0:T(8,128)(2,1)S(1)}, u32[]{:S(2)}, u32[]{:S(2)}) %collective-permute-start.10) | collective-permute-done | bytes 131104 | tf_op jit(solution)/shard_map/ppermute | solution.py:326
  39.6 2.0 %collective-permute-done.8 = bf16[256,256]{1,0:T(8,128)(2,1)S(1)} collective-permute-done((bf16[256,256]{1,0:T(8,128)(2,1)S(1)}, bf16[256,256]{1,0:T(8,128)(2,1)S(1)}, u32[]{:S(2)}, u32[]{:S(2)}) %collective-permute-start.8) | collective-permute-done | bytes 131104 | tf_op jit(solution)/shard_map/ppermute | solution.py:326
  41.8 3.0 %encode.2 = (f32[256,640]{1,0:T(8,128)S(1)}, bf16[256,1024]{1,0:T(8,128)(2,1)S(1)}) custom-call(s32[50]{0:T(128)S(1)} %table.1, bf16[2,256,256]{2,1,0:T(8,128)(2,1)S(1)} %pad_maximum_fusion.1.refs_0_, bf16[2,256,256]{2,1,0:T(8,128)(2,1)S(1)} %pad_maximum_fusion.2.refs_1_, bf16[2,256,256]{2,1,0:T(8,128)(2,1)S(1)} %copy-done.1, ...), custom_call_target="tpu_custom_call" | custom-call | flops 1342177280 | bytes 4194304 | tf_op jit(solution)/shard_map/encode/pallas_call | solution.py:31
  44.8 2.6 %collective-permute-done.14.refs_5_ = bf16[2,256,256]{2,1,0:T(8,128)(2,1)S(1)} collective-permute-done((bf16[2,256,256]{2,1,0:T(8,128)(2,1)S(1)}, bf16[2,256,256]{2,1,0:T(8,128)(2,1)S(1)}, u32[]{:S(2)}, u32[]{:S(2)}) %collective-permute-start.14) | collective-permute-done | bytes 262176 | tf_op jit(solution)/shard_map/ppermute | solution.py:318
  47.4 4.6 %collective-permute-done.11.refs_4_ = bf16[2,256,256]{2,1,0:T(8,128)(2,1)S(1)} collective-permute-done((bf16[2,256,256]{2,1,0:T(8,128)(2,1)S(1)}, bf16[2,256,256]{2,1,0:T(8,128)(2,1)S(1)}, u32[]{:S(2)}, u32[]{:S(2)}) %collective-permute-start.11) | collective-permute-done | bytes 262176 | tf_op jit(solution)/shard_map/ppermute | solution.py:318
  52.0 1.3 collective-permute-start.16
  57.0 3.2 %encode.3 = (bf16[256,640]{1,0:T(8,128)(2,1)S(1)}, bf16[256,1024]{1,0:T(8,128)(2,1)S(1)}) custom-call(s32[50]{0:T(128)S(1)} %table.1, bf16[2,256,256]{2,1,0:T(8,128)(2,1)S(1)} %collective-permute-done.3.refs_0_, bf16[2,256,256]{2,1,0:T(8,128)(2,1)S(1)} %collective-permute-done.13.refs_1_, bf16[2,256,256]{2,1,0:T(8,128)(2,1)S(1)} %collective-permute-done.18.refs_2_, ...), custom_call_target="tpu_custom_call" | custom-call | flops 1 | bytes 1 | tf_op jit(solution)/shard_map/encode/pallas_call | solution.py:31
  60.2 4.0 %decode.1 = (bf16[128,1024]{1,0:T(8,128)(2,1)S(1)}, bf16[128,1024]{1,0:T(8,128)(2,1)S(1)}, bf16[256,1024]{1,0:T(8,128)(2,1)S(1)}, bf16[256,1024]{1,0:T(8,128)(2,...) custom-call(s32[50]{0:T(128)S(1)} %table.1, ...), custom_call_target="tpu_custom_call" | custom-call | flops 1 | bytes 1 | tf_op jit(solution)/shard_map/decode/pallas_call | solution.py:31
  64.8 3.4 %collective-permute-done.17.refs_4_ = bf16[4,256,256]{2,1,0:T(8,128)(2,1)S(1)} collective-permute-done((bf16[4,256,256]{2,1,0:T(8,128)(2,1)S(1)}, bf16[4,256,256]{2,1,0:T(8,128)(2,1)S(1)}, u32[]{:S(2)}, u32[]{:S(2)}) %collective-permute-start.17) | collective-permute-done | bytes 524320 | tf_op jit(solution)/shard_map/ppermute | solution.py:318
  70.9 5.9 %collective-permute-start.31 = (bf16[256,1024]{1,0:T(8,128)(2,1)S(1)}, bf16[256,1024]{1,0:T(8,128)(2,1)S(1)}, u32[]{:S(2)}, u32[]{:S(2)}) collective-permute-start(bf16[256,1024]{1,0:T(8,128)(2,1)S(1)} %sum.1), channel_id=1, source_target_pairs={{0,2},{1,3},{6,4},{7,5},{8,10},{9,11},{14,12},{15,13},{16,18},{17,... | collective-permute-start | bytes 1572872 | tf_op jit(solution)/shard_map/ppermute | solution.py:318
  77.4 6.5 %collective-permute-done.23 = bf16[4,256,256]{2,1,0:T(8,128)(2,1)S(1)} collective-permute-done((bf16[4,256,256]{2,1,0:T(8,128)(2,1)S(1)}, bf16[4,256,256]{2,1,0:T(8,128)(2,1)S(1)}, u32[]{:S(2)}, u32[]{:S(2)}) %collective-permute-start.23) | collective-permute-done | bytes 524320 | tf_op jit(solution)/shard_map/ppermute | solution.py:318
  84.5 4.0 %collective-permute-done.31 = bf16[256,1024]{1,0:T(8,128)(2,1)S(1)} collective-permute-done((bf16[256,1024]{1,0:T(8,128)(2,1)S(1)}, bf16[256,1024]{1,0:T(8,128)(2,1)S(1)}, u32[]{:S(2)}, u32[]{:S(2)}) %collective-permute-start.31) | collective-permute-done | bytes 524320 | tf_op jit(solution)/shard_map/ppermute | solution.py:318
  90.2 4.6 %collective-permute-start.32 = (bf16[256,1024]{1,0:T(8,128)(2,1)S(1)}, bf16[256,1024]{1,0:T(8,128)(2,1)S(1)}, u32[]{:S(2)}, u32[]{:S(2)}) collective-permute-start(bf16[256,1024]{1,0:T(8,128)(2,1)S(1)} %add_convert_fusion), channel_id=1, source_target_pairs={{0,2},{1,3},{2,4},{3,5},{8,10},{9,11},{10,12},{11,13},{16,18},{17,... | collective-permute-start | bytes 1572872 | tf_op jit(solution)/shard_map/ppermute | solution.py:318
  95.8 8.3 %collective-permute-done.25.refs_2_ = bf16[4,256,256]{2,1,0:T(8,128)(2,1)S(1)} collective-permute-done((bf16[4,256,256]{2,1,0:T(8,128)(2,1)S(1)}, bf16[4,256,256]{2,1,0:T(8,128)(2,1)S(1)}, u32[]{:S(2)}, u32[]{:S(2)}) %collective-permute-start.25) | collective-permute-done | bytes 524320 | tf_op jit(solution)/shard_map/ppermute | solution.py:318
  104.4 3.6 %project.2 = (f32[256,640]{1,0:T(8,128)S(1)}, f32[256,1]{1,0:T(8,128)S(1)}) custom-call(s32[50]{0:T(128)S(1)} %table.1, bf16[4,256,256]{2,1,0:T(8,128)(2,1)S(1)} %pad_maximum_fusion.refs_0_, bf16[4,256,256]{2,1,0:T(8,128)(2,1)S(1)} %collective-permute-done.34.refs_1_, bf16[4,256,256]{2,1,0:T(8,128)(2,1)S(1)} %collective-permute-done.16.refs_2_, ...), custom_call_target="tpu_custom_call" | custom-call | flops 2013265920 | bytes 4194304 | tf_op jit(solution)/shard_map/project/pallas_call | solution.py:31
  109.0 6.7 %collective-permute-start.38 = (bf16[256,1024]{1,0:T(8,128)(2,1)S(1)}, bf16[256,1024]{1,0:T(8,128)(2,1)S(1)}, u32[]{:S(2)}, u32[]{:S(2)}) collective-permute-start(bf16[256,1024]{1,0:T(8,128)(2,1)S(1)} %get-tuple-element.92), channel_id=1, source_target_pairs={{0,2},{1,3},{2,4},{3,5},{4,6},{5,7},{8,10},{9,11},{10,12},{11,13},... | collective-permute-start | bytes 1572872 | tf_op jit(solution)/shard_map/ppermute | solution.py:318
  117.0 3.9 %project.3 = (f32[256,640]{1,0:T(8,128)}, f32[8,256]{1,0:T(8,128)S(1)}) custom-call(s32[50]{0:T(128)S(1)} %table.1, bf16[4,256,256]{2,1,0:T(8,128)(2,1)S(1)} %add.43.refs_0_, bf16[4,256,256]{2,1,0:T(8,128)(2,1)S(1)} %collective-permute-done.24.refs_1_, bf16[4,256,256]{2,1,0:T(8,128)(2,1)S(1)} %collective-permute-done.25.refs_2_, ...), custom_call_target="tpu_custom_call" | custom-call | flops 1 | bytes 1 | tf_op jit(solution)/shard_map/project/pallas_call | solution.py:31
  122.0 1.5 %collective-permute-start.41 = (f32[1,256]{1,0:T(1,128)S(1)}, f32[1,256]{1,0:T(1,128)S(1)}, u32[]{:S(2)}, u32[]{:S(2)}) collective-permute-start(f32[1,256]{1,0:T(1,128)S(1)} %slice_add_fusion), channel_id=1, source_target_pairs={{0,2},{1,3},{2,0},{3,1},{4,6},{5,7},{6,4},{7,5},{8,10},{9,11},{10,... | collective-permute-start | bytes 3080 | tf_op jit(solution)/shard_map/ppermute | solution.py:318
  124.2 2.2 %collective-permute-start.43 = (f32[1,256]{1,0:T(1,128)S(1)}, f32[1,256]{1,0:T(1,128)S(1)}, u32[]{:S(2)}, u32[]{:S(2)}) collective-permute-start(f32[1,256]{1,0:T(1,128)S(1)} %slice_add_fusion), channel_id=1, source_target_pairs={{0,6},{1,7},{2,4},{3,5},{4,2},{5,3},{6,0},{7,1},{8,14},{9,15},{10,... | collective-permute-start | bytes 3080 | tf_op jit(solution)/shard_map/ppermute | solution.py:318
  126.4 4.1 %collective-permute-done.39 = bf16[256,1024]{1,0:T(8,128)(2,1)S(1)} collective-permute-done((bf16[256,1024]{1,0:T(8,128)(2,1)S(1)}, bf16[256,1024]{1,0:T(8,128)(2,1)S(1)}, u32[]{:S(2)}, u32[]{:S(2)}) %collective-permute-start.39) | collective-permute-done | bytes 524320 | tf_op jit(solution)/shard_map/ppermute | solution.py:318
  (92 shorter events, 22.6 us)
Async XLA Ops:
  1.8 6.9 %collective-permute-start = (bf16[256,256]{1,0:T(8,128)(2,1)S(1)}, bf16[256,256]{1,0:T(8,128)(2,1)S(1)}, u32[]{:S(2)}, u32[]{:S(2)}) collective-permute-start(bf16[256,256]{1,0:T(8,128)(2,1)S(1)} %get-tuple-element.98), channel_id=1, source_target_pairs={{0,8},{8,0},{16,24},{24,16},{1,9},{9,1},{17,25},{25,17},{2,10},{10... | collective-permute-start | bytes 393224 | tf_op jit(solution)/shard_map/ppermute | solution.py:326
  4.8 8.0 %collective-permute-start.4 = (bf16[256,256]{1,0:T(8,128)(2,1)S(1)}, bf16[256,256]{1,0:T(8,128)(2,1)S(1)}, u32[]{:S(2)}, u32[]{:S(2)}) collective-permute-start(bf16[256,256]{1,0:T(8,128)(2,1)S(1)} %get-tuple-element.97), channel_id=1, source_target_pairs={{0,16},{8,24},{16,0},{24,8},{1,17},{9,25},{17,1},{25,9},{2,18},{10... | collective-permute-start | bytes 393224 | tf_op jit(solution)/shard_map/ppermute | solution.py:326
  8.8 11.0 %collective-permute-start.1 = (bf16[2,256,256]{2,1,0:T(8,128)(2,1)S(1)}, bf16[2,256,256]{2,1,0:T(8,128)(2,1)S(1)}, u32[]{:S(2)}, u32[]{:S(2)}) collective-permute-start(bf16[2,256,256]{2,1,0:T(8,128)(2,1)S(1)} %pad_maximum_fusion.1.refs_0_), channel_id=1, source_target_pairs={{0,2},{1,3},{2,4},{3,5},{4,6},{5,7},{6,0},{7,1},{8,10},{9,11},{10,... | collective-permute-start | bytes 786440 | tf_op jit(solution)/shard_map/ppermute | solution.py:318
  12.8 12.6 %collective-permute-start.12 = (bf16[2,256,256]{2,1,0:T(8,128)(2,1)S(1)}, bf16[2,256,256]{2,1,0:T(8,128)(2,1)S(1)}, u32[]{:S(2)}, u32[]{:S(2)}) collective-permute-start(bf16[2,256,256]{2,1,0:T(8,128)(2,1)S(1)} %pad_maximum_fusion.2.refs_1_), channel_id=1, source_target_pairs={{0,2},{1,3},{2,4},{3,5},{4,6},{5,7},{6,0},{7,1},{8,10},{9,11},{10,... | collective-permute-start | bytes 786440 | tf_op jit(solution)/shard_map/ppermute | solution.py:318
  14.5 11.0 %collective-permute-start.6 = (bf16[2,256,256]{2,1,0:T(8,128)(2,1)S(1)}, bf16[2,256,256]{2,1,0:T(8,128)(2,1)S(1)}, u32[]{:S(2)}, u32[]{:S(2)}) collective-permute-start(bf16[2,256,256]{2,1,0:T(8,128)(2,1)S(1)} %pad_maximum_fusion.2.refs_1_), channel_id=1, source_target_pairs={{0,1},{1,0},{2,3},{3,2},{4,5},{5,4},{6,7},{7,6},{8,9},{9,8},{10,11... | collective-permute-start | bytes 786440 | tf_op jit(solution)/shard_map/ppermute | solution.py:321
  19.9 11.2 %collective-permute-start.3 = (bf16[2,256,256]{2,1,0:T(8,128)(2,1)S(1)}, bf16[2,256,256]{2,1,0:T(8,128)(2,1)S(1)}, u32[]{:S(2)}, u32[]{:S(2)}) collective-permute-start(bf16[2,256,256]{2,1,0:T(8,128)(2,1)S(1)} %collective-permute-done.1.refs_4_), channel_id=1, source_target_pairs={{0,2},{1,3},{2,4},{3,5},{4,6},{5,7},{6,0},{7,1},{8,10},{9,11},{10,... | collective-permute-start | bytes 786440 | tf_op jit(solution)/shard_map/ppermute | solution.py:318
  25.5 11.0 %collective-permute-start.13 = (bf16[2,256,256]{2,1,0:T(8,128)(2,1)S(1)}, bf16[2,256,256]{2,1,0:T(8,128)(2,1)S(1)}, u32[]{:S(2)}, u32[]{:S(2)}) collective-permute-start(bf16[2,256,256]{2,1,0:T(8,128)(2,1)S(1)} %collective-permute-done.12.refs_5_), channel_id=1, source_target_pairs={{0,2},{1,3},{2,4},{3,5},{4,6},{5,7},{6,0},{7,1},{8,10},{9,11},{10,... | collective-permute-start | bytes 786440 | tf_op jit(solution)/shard_map/ppermute | solution.py:318
  32.4 7.2 %collective-permute-start.10 = (bf16[256,256]{1,0:T(8,128)(2,1)S(1)}, bf16[256,256]{1,0:T(8,128)(2,1)S(1)}, u32[]{:S(2)}, u32[]{:S(2)}) collective-permute-start(bf16[256,256]{1,0:T(8,128)(2,1)S(1)} %get-tuple-element.59), channel_id=1, source_target_pairs={{0,24},{8,16},{16,8},{24,0},{1,25},{9,17},{17,9},{25,1},{2,26},{10... | collective-permute-start | bytes 393224 | tf_op jit(solution)/shard_map/ppermute | solution.py:326
  36.5 11.0 %collective-permute-start.14 = (bf16[2,256,256]{2,1,0:T(8,128)(2,1)S(1)}, bf16[2,256,256]{2,1,0:T(8,128)(2,1)S(1)}, u32[]{:S(2)}, u32[]{:S(2)}) collective-permute-start(bf16[2,256,256]{2,1,0:T(8,128)(2,1)S(1)} %collective-permute-done.13.refs_1_), channel_id=1, source_target_pairs={{0,2},{1,3},{2,4},{3,5},{4,6},{5,7},{6,0},{7,1},{8,10},{9,11},{10,... | collective-permute-start | bytes 786440 | tf_op jit(solution)/shard_map/ppermute | solution.py:318
  39.6 12.4 %collective-permute-start.11 = (bf16[2,256,256]{2,1,0:T(8,128)(2,1)S(1)}, bf16[2,256,256]{2,1,0:T(8,128)(2,1)S(1)}, u32[]{:S(2)}, u32[]{:S(2)}) collective-permute-start(bf16[2,256,256]{2,1,0:T(8,128)(2,1)S(1)} %collective-permute-done.3.refs_0_), channel_id=1, source_target_pairs={{0,2},{1,3},{2,4},{3,5},{4,6},{5,7},{6,0},{7,1},{8,10},{9,11},{10,... | collective-permute-start | bytes 786440 | tf_op jit(solution)/shard_map/ppermute | solution.py:318
  41.6 13.7 %collective-permute-start.18 = (bf16[2,256,256]{2,1,0:T(8,128)(2,1)S(1)}, bf16[2,256,256]{2,1,0:T(8,128)(2,1)S(1)}, u32[]{:S(2)}, u32[]{:S(2)}) collective-permute-start(bf16[2,256,256]{2,1,0:T(8,128)(2,1)S(1)} %collective-permute-done.3.refs_0_), channel_id=1, source_target_pairs={{0,1},{1,0},{2,3},{3,2},{4,5},{5,4},{6,7},{7,6},{8,9},{9,8},{10,11... | collective-permute-start | bytes 786440 | tf_op jit(solution)/shard_map/ppermute | solution.py:321
  52.0 12.8 %collective-permute-start.16 = (bf16[4,256,256]{2,1,0:T(8,128)(2,1)S(1)}, bf16[4,256,256]{2,1,0:T(8,128)(2,1)S(1)}, u32[]{:S(2)}, u32[]{:S(2)}) collective-permute-start(bf16[4,256,256]{2,1,0:T(8,128)(2,1)S(1)} %pad_maximum_fusion.refs_0_), channel_id=1, source_target_pairs={{0,2},{1,3},{2,4},{3,5},{4,6},{5,7},{8,10},{9,11},{10,12},{11,13},... | collective-permute-start | bytes 1572872 | tf_op jit(solution)/shard_map/ppermute | solution.py:318
  53.3 14.8 %collective-permute-start.17 = (bf16[4,256,256]{2,1,0:T(8,128)(2,1)S(1)}, bf16[4,256,256]{2,1,0:T(8,128)(2,1)S(1)}, u32[]{:S(2)}, u32[]{:S(2)}) collective-permute-start(bf16[4,256,256]{2,1,0:T(8,128)(2,1)S(1)} %pad_maximum_fusion.refs_0_), channel_id=1, source_target_pairs={{2,0},{3,1},{4,2},{5,3},{6,4},{7,5},{10,8},{11,9},{12,10},{13,11},... | collective-permute-start | bytes 1572872 | tf_op jit(solution)/shard_map/ppermute | solution.py:318
  68.1 8.9 %collective-permute-start.22 = (bf16[4,256,256]{2,1,0:T(8,128)(2,1)S(1)}, bf16[4,256,256]{2,1,0:T(8,128)(2,1)S(1)}, u32[]{:S(2)}, u32[]{:S(2)}) collective-permute-start(bf16[4,256,256]{2,1,0:T(8,128)(2,1)S(1)} %collective-permute-done.16.refs_2_), channel_id=1, source_target_pairs={{2,4},{3,5},{4,6},{5,7},{10,12},{11,13},{12,14},{13,15},{18,20},{1... | collective-permute-start | bytes 1572872 | tf_op jit(solution)/shard_map/ppermute | solution.py:318
  68.8 15.0 %collective-permute-start.23 = (bf16[4,256,256]{2,1,0:T(8,128)(2,1)S(1)}, bf16[4,256,256]{2,1,0:T(8,128)(2,1)S(1)}, u32[]{:S(2)}, u32[]{:S(2)}) collective-permute-start(bf16[4,256,256]{2,1,0:T(8,128)(2,1)S(1)} %collective-permute-done.17.refs_4_), channel_id=1, source_target_pairs={{2,0},{3,1},{4,2},{5,3},{10,8},{11,9},{12,10},{13,11},{18,16},{19,... | collective-permute-start | bytes 1572872 | tf_op jit(solution)/shard_map/ppermute | solution.py:318
  70.8 13.1 %collective-permute-start.30 = (bf16[256,1024]{1,0:T(8,128)(2,1)S(1)}, bf16[256,1024]{1,0:T(8,128)(2,1)S(1)}, u32[]{:S(2)}, u32[]{:S(2)}) collective-permute-start(bf16[256,1024]{1,0:T(8,128)(2,1)S(1)} %get-tuple-element.83), channel_id=1, source_target_pairs={{0,1},{1,0},{2,3},{3,2},{4,5},{5,4},{6,7},{7,6},{8,9},{9,8},{10,11... | collective-permute-start | bytes 1572872 | tf_op jit(solution)/shard_map/ppermute | solution.py:321
  70.9 17.6 %collective-permute-start.31 = (bf16[256,1024]{1,0:T(8,128)(2,1)S(1)}, bf16[256,1024]{1,0:T(8,128)(2,1)S(1)}, u32[]{:S(2)}, u32[]{:S(2)}) collective-permute-start(bf16[256,1024]{1,0:T(8,128)(2,1)S(1)} %sum.1), channel_id=1, source_target_pairs={{0,2},{1,3},{6,4},{7,5},{8,10},{9,11},{14,12},{15,13},{16,18},{17,... | collective-permute-start | bytes 1572872 | tf_op jit(solution)/shard_map/ppermute | solution.py:318
  76.8 13.3 %collective-permute-start.34 = (bf16[4,256,256]{2,1,0:T(8,128)(2,1)S(1)}, bf16[4,256,256]{2,1,0:T(8,128)(2,1)S(1)}, u32[]{:S(2)}, u32[]{:S(2)}) collective-permute-start(bf16[4,256,256]{2,1,0:T(8,128)(2,1)S(1)} %pad_maximum_fusion.refs_0_), channel_id=1, source_target_pairs={{0,1},{1,0},{2,3},{3,2},{4,5},{5,4},{6,7},{7,6},{8,9},{9,8},{10,11... | collective-permute-start | bytes 1572872 | tf_op jit(solution)/shard_map/ppermute | solution.py:321
  77.0 13.2 %collective-permute-start.37 = (bf16[256,1024]{1,0:T(8,128)(2,1)S(1)}, bf16[256,1024]{1,0:T(8,128)(2,1)S(1)}, u32[]{:S(2)}, u32[]{:S(2)}) collective-permute-start(bf16[256,1024]{1,0:T(8,128)(2,1)S(1)} %get-tuple-element.91), channel_id=1, source_target_pairs={{0,1},{1,0},{2,3},{3,2},{4,5},{5,4},{6,7},{7,6},{8,9},{9,8},{10,11... | collective-permute-start | bytes 1572872 | tf_op jit(solution)/shard_map/ppermute | solution.py:321
  83.8 11.0 %collective-permute-start.35 = (bf16[4,256,256]{2,1,0:T(8,128)(2,1)S(1)}, bf16[4,256,256]{2,1,0:T(8,128)(2,1)S(1)}, u32[]{:S(2)}, u32[]{:S(2)}) collective-permute-start(bf16[4,256,256]{2,1,0:T(8,128)(2,1)S(1)} %collective-permute-done.16.refs_2_), channel_id=1, source_target_pairs={{0,1},{1,0},{2,3},{3,2},{4,5},{5,4},{6,7},{7,6},{8,9},{9,8},{10,11... | collective-permute-start | bytes 1572872 | tf_op jit(solution)/shard_map/ppermute | solution.py:321
  84.0 11.6 %collective-permute-start.36 = (bf16[4,256,256]{2,1,0:T(8,128)(2,1)S(1)}, bf16[4,256,256]{2,1,0:T(8,128)(2,1)S(1)}, u32[]{:S(2)}, u32[]{:S(2)}) collective-permute-start(bf16[4,256,256]{2,1,0:T(8,128)(2,1)S(1)} %collective-permute-done.17.refs_4_), channel_id=1, source_target_pairs={{0,1},{1,0},{2,3},{3,2},{4,5},{5,4},{6,7},{7,6},{8,9},{9,8},{10,11... | collective-permute-start | bytes 1572872 | tf_op jit(solution)/shard_map/ppermute | solution.py:321
  88.6 15.5 %collective-permute-start.25 = (bf16[4,256,256]{2,1,0:T(8,128)(2,1)S(1)}, bf16[4,256,256]{2,1,0:T(8,128)(2,1)S(1)}, u32[]{:S(2)}, u32[]{:S(2)}) collective-permute-start(bf16[4,256,256]{2,1,0:T(8,128)(2,1)S(1)} %add.43.refs_0_), channel_id=1, source_target_pairs={{4,6},{5,7},{2,0},{3,1},{12,14},{13,15},{10,8},{11,9},{20,22},{21,... | collective-permute-start | bytes 1572872 | tf_op jit(solution)/shard_map/ppermute | solution.py:318
  90.1 17.9 %collective-permute-start.29 = (bf16[256,1024]{1,0:T(8,128)(2,1)S(1)}, bf16[256,1024]{1,0:T(8,128)(2,1)S(1)}, u32[]{:S(2)}, u32[]{:S(2)}) collective-permute-start(bf16[256,1024]{1,0:T(8,128)(2,1)S(1)} %get-tuple-element.81), channel_id=1, source_target_pairs={{0,1},{1,0},{2,3},{3,2},{4,5},{5,4},{6,7},{7,6},{8,9},{9,8},{10,11... | collective-permute-start | bytes 1572872 | tf_op jit(solution)/shard_map/ppermute | solution.py:321
  90.2 17.8 %collective-permute-start.32 = (bf16[256,1024]{1,0:T(8,128)(2,1)S(1)}, bf16[256,1024]{1,0:T(8,128)(2,1)S(1)}, u32[]{:S(2)}, u32[]{:S(2)}) collective-permute-start(bf16[256,1024]{1,0:T(8,128)(2,1)S(1)} %add_convert_fusion), channel_id=1, source_target_pairs={{0,2},{1,3},{2,4},{3,5},{8,10},{9,11},{10,12},{11,13},{16,18},{17,... | collective-permute-start | bytes 1572872 | tf_op jit(solution)/shard_map/ppermute | solution.py:318
  94.8 13.2 %collective-permute-start.33 = (bf16[256,1024]{1,0:T(8,128)(2,1)S(1)}, bf16[256,1024]{1,0:T(8,128)(2,1)S(1)}, u32[]{:S(2)}, u32[]{:S(2)}) collective-permute-start(bf16[256,1024]{1,0:T(8,128)(2,1)S(1)} %add_convert_fusion), channel_id=1, source_target_pairs={{4,2},{5,3},{6,4},{7,5},{12,10},{13,11},{14,12},{15,13},{20,18},{2... | collective-permute-start | bytes 1572872 | tf_op jit(solution)/shard_map/ppermute | solution.py:318
  95.6 21.4 %collective-permute-start.24 = (bf16[4,256,256]{2,1,0:T(8,128)(2,1)S(1)}, bf16[4,256,256]{2,1,0:T(8,128)(2,1)S(1)}, u32[]{:S(2)}, u32[]{:S(2)}) collective-permute-start(bf16[4,256,256]{2,1,0:T(8,128)(2,1)S(1)} %add.43.refs_0_), channel_id=1, source_target_pairs={{0,1},{1,0},{2,3},{3,2},{4,5},{5,4},{6,7},{7,6},{8,9},{9,8},{10,11... | collective-permute-start | bytes 1572872 | tf_op jit(solution)/shard_map/ppermute | solution.py:321
  104.1 12.9 %collective-permute-start.26 = (bf16[4,256,256]{2,1,0:T(8,128)(2,1)S(1)}, bf16[4,256,256]{2,1,0:T(8,128)(2,1)S(1)}, u32[]{:S(2)}, u32[]{:S(2)}) collective-permute-start(bf16[4,256,256]{2,1,0:T(8,128)(2,1)S(1)} %collective-permute-done.25.refs_2_), channel_id=1, source_target_pairs={{0,1},{1,0},{2,3},{3,2},{4,5},{5,4},{6,7},{7,6},{8,9},{9,8},{10,11... | collective-permute-start | bytes 1572872 | tf_op jit(solution)/shard_map/ppermute | solution.py:321
  109.0 17.4 %collective-permute-start.38 = (bf16[256,1024]{1,0:T(8,128)(2,1)S(1)}, bf16[256,1024]{1,0:T(8,128)(2,1)S(1)}, u32[]{:S(2)}, u32[]{:S(2)}) collective-permute-start(bf16[256,1024]{1,0:T(8,128)(2,1)S(1)} %get-tuple-element.92), channel_id=1, source_target_pairs={{0,2},{1,3},{2,4},{3,5},{4,6},{5,7},{8,10},{9,11},{10,12},{11,13},... | collective-permute-start | bytes 1572872 | tf_op jit(solution)/shard_map/ppermute | solution.py:318
  115.7 14.9 %collective-permute-start.39 = (bf16[256,1024]{1,0:T(8,128)(2,1)S(1)}, bf16[256,1024]{1,0:T(8,128)(2,1)S(1)}, u32[]{:S(2)}, u32[]{:S(2)}) collective-permute-start(bf16[256,1024]{1,0:T(8,128)(2,1)S(1)} %get-tuple-element.93), channel_id=1, source_target_pairs={{2,0},{3,1},{4,2},{5,3},{6,4},{7,5},{10,8},{11,9},{12,10},{13,11},... | collective-permute-start | bytes 1572872 | tf_op jit(solution)/shard_map/ppermute | solution.py:318
  122.0 9.7 %collective-permute-start.41 = (f32[1,256]{1,0:T(1,128)S(1)}, f32[1,256]{1,0:T(1,128)S(1)}, u32[]{:S(2)}, u32[]{:S(2)}) collective-permute-start(f32[1,256]{1,0:T(1,128)S(1)} %slice_add_fusion), channel_id=1, source_target_pairs={{0,2},{1,3},{2,0},{3,1},{4,6},{5,7},{6,4},{7,5},{8,10},{9,11},{10,... | collective-permute-start | bytes 3080 | tf_op jit(solution)/shard_map/ppermute | solution.py:318
  123.5 8.2 %collective-permute-start.42 = (f32[1,256]{1,0:T(1,128)S(1)}, f32[1,256]{1,0:T(1,128)S(1)}, u32[]{:S(2)}, u32[]{:S(2)}) collective-permute-start(f32[1,256]{1,0:T(1,128)S(1)} %slice_add_fusion), channel_id=1, source_target_pairs={{0,4},{1,5},{2,6},{3,7},{4,0},{5,1},{6,2},{7,3},{8,12},{9,13},{10,... | collective-permute-start | bytes 3080 | tf_op jit(solution)/shard_map/ppermute | solution.py:318
  124.2 7.5 %collective-permute-start.43 = (f32[1,256]{1,0:T(1,128)S(1)}, f32[1,256]{1,0:T(1,128)S(1)}, u32[]{:S(2)}, u32[]{:S(2)}) collective-permute-start(f32[1,256]{1,0:T(1,128)S(1)} %slice_add_fusion), channel_id=1, source_target_pairs={{0,6},{1,7},{2,4},{3,5},{4,2},{5,3},{6,0},{7,1},{8,14},{9,15},{10,... | collective-permute-start | bytes 3080 | tf_op jit(solution)/shard_map/ppermute | solution.py:318
  (18 other events, 166.9 us)

commit v9 on v8

--- a/solution.py
+++ b/solution.py
@@ -352,9 +352,9 @@
         near_x.append([send(first, ring), send(second, ring)])
     slots = [near_x[0], far_x[0], near_x[1], far_x[1]]
     carry = encode(
-        after(table, shard_g), SLOTS["enc_a"], slots, w_in, bias, None, X_STREAMS, False, n_feat
-    )
-    far_x.append([cross(near_x[3][0]), cross(after(near_x[3][1], carry))])
+        table, SLOTS["enc_a"], slots, w_in, bias, None, X_STREAMS, False, n_feat
+    )
+    far_x.append([cross(after(near_x[3][0], shard_g)), cross(after(near_x[3][1], carry))])
 
     up_pairs = [(a, a + 1) for a in range(chips - 1)]
     down_pairs = [(a + 1, a) for a in range(chips - 1)]

time: 133 us -> 132 us (level)
  waiting for transfers between devices: 50.1 us -> 43 us
  starting transfers between devices: 45.9 us -> 52.2 us
    ppermute x6, waiting for transfers between devices: 7.6 us -> 3.32 us  [exchange(): lax.ppermute(blocks[s], 'tok', [(a, a ^ s) for a in range(n_tok)])]
    ppermute x19, starting transfers between devices: 34.4 us -> 38.5 us  [send(): return lax.ppermute(array, 'feat', along(pairs))]
    ppermute x19, waiting for transfers between devices: 39.7 us -> 36.9 us  [send(): return lax.ppermute(array, 'feat', along(pairs))]
    ppermute x6, starting transfers between devices: 8.56 us -> 10.6 us  [exchange(): lax.ppermute(blocks[s], 'tok', [(a, a ^ s) for a in range(n_tok)])]
  transfers between devices with their start and end apart: 44 -> 44, of which waited for: 19 -> 16; matrix products, arithmetic and copies ran while one was open for 2% -> 2% of each run, Pallas kernels for 23% -> 23%
where the time goes in v9:
time: 132 us
  starting transfers between devices  52.2 us (40%)
  waiting for transfers between devices  43 us (33%)
  Pallas kernels  30 us (23%)
  other arithmetic  2.65 us (2%)
  local copies, waits for them, and re-layouts  2.55 us (2%)
    ppermute x19, starting transfers between devices, send(): return lax.ppermute(array, 'feat', along(pairs))  38.5 us
    ppermute x19, waiting for transfers between devices, send(): return lax.ppermute(array, 'feat', along(pairs))  36.9 us
    pallas_call x7, Pallas kernels, kernel_call(): pl.pallas_call(body, in_specs=[SMEM] + [VMEM] * (len(args) - 1), out_spec...  19.3 us
    ppermute x6, starting transfers between devices, exchange(): lax.ppermute(blocks[s], 'tok', [(a, a ^ s) for a in range(n_tok)])  10.6 us
    pallas_call x2, Pallas kernels, load(): pl.pallas_call(load_body, in_specs=[anywhere, anywhere], out_specs=[VMEM,...  8.17 us
    ppermute x6, waiting for transfers between devices, exchange(): lax.ppermute(blocks[s], 'tok', [(a, a ^ s) for a in range(n_tok)])  3.32 us
    ppermute x19, starting transfers between devices, cross(): return lax.ppermute(array, 'feat', [(a, a ^ 1) for a in range(n_feat)])  3.06 us
    ppermute x19, waiting for transfers between devices, cross(): return lax.ppermute(array, 'feat', [(a, a ^ 1) for a in range(n_feat)])  2.87 us
  transfers between devices with their start and end apart: 44, of which 16 were waited for; matrix products, arithmetic and copies ran while one was open for 2% of the time, Pallas kernels for 23%

profile of v9, /device:TPU:0, one launch (start us, length us, event | category | flops | bytes accessed | tf_op | source)
XLA Modules:
  0.0 131.6 jit_solution(3514758010508436922)
XLA Ops:
  1.8 3.0 %collective-permute-start = (bf16[256,256]{1,0:T(8,128)(2,1)S(1)}, bf16[256,256]{1,0:T(8,128)(2,1)S(1)}, u32[]{:S(2)}, u32[]{:S(2)}) collective-permute-start(bf16[256,256]{1,0:T(8,128)(2,1)S(1)} %get-tuple-element.98), channel_id=1, source_target_pairs={{0,8},{8,0},{16,24},{24,16},{1,9},{9,1},{17,25},{25,17},{2,10},{10... | collective-permute-start | bytes 393224 | tf_op jit(solution)/shard_map/ppermute | solution.py:326
  4.8 1.5 %collective-permute-start.4 = (bf16[256,256]{1,0:T(8,128)(2,1)S(1)}, bf16[256,256]{1,0:T(8,128)(2,1)S(1)}, u32[]{:S(2)}, u32[]{:S(2)}) collective-permute-start(bf16[256,256]{1,0:T(8,128)(2,1)S(1)} %get-tuple-element.97), channel_id=1, source_target_pairs={{0,16},{8,24},{16,0},{24,8},{1,17},{9,25},{17,1},{25,9},{2,18},{10... | collective-permute-start | bytes 393224 | tf_op jit(solution)/shard_map/ppermute | solution.py:326
  6.3 2.4 %collective-permute-done = bf16[256,256]{1,0:T(8,128)(2,1)S(1)} collective-permute-done((bf16[256,256]{1,0:T(8,128)(2,1)S(1)}, bf16[256,256]{1,0:T(8,128)(2,1)S(1)}, u32[]{:S(2)}, u32[]{:S(2)}) %collective-permute-start) | collective-permute-done | bytes 131104 | tf_op jit(solution)/shard_map/ppermute | solution.py:326
  8.8 1.9 %collective-permute-start.1 = (bf16[2,256,256]{2,1,0:T(8,128)(2,1)S(1)}, bf16[2,256,256]{2,1,0:T(8,128)(2,1)S(1)}, u32[]{:S(2)}, u32[]{:S(2)}) collective-permute-start(bf16[2,256,256]{2,1,0:T(8,128)(2,1)S(1)} %pad_maximum_fusion.1.refs_0_), channel_id=1, source_target_pairs={{0,2},{1,3},{2,4},{3,5},{4,6},{5,7},{6,0},{7,1},{8,10},{9,11},{10,... | collective-permute-start | bytes 786440 | tf_op jit(solution)/shard_map/ppermute | solution.py:318
  11.4 1.3 %table.1 = s32[50]{0:T(128)S(1)} custom-call(s32[2]{0:T(128)S(1)} %pad_add_fusion.ids_ref, s32[2,20]{1,0:T(2,128)S(1)} %copy-done.4), custom_call_target="tpu_custom_call" | custom-call | flops 1 | bytes 1 | tf_op jit(solution)/shard_map/table/pallas_call | solution.py:112
  12.8 1.6 %collective-permute-start.12 = (bf16[2,256,256]{2,1,0:T(8,128)(2,1)S(1)}, bf16[2,256,256]{2,1,0:T(8,128)(2,1)S(1)}, u32[]{:S(2)}, u32[]{:S(2)}) collective-permute-start(bf16[2,256,256]{2,1,0:T(8,128)(2,1)S(1)} %pad_maximum_fusion.2.refs_1_), channel_id=1, source_target_pairs={{0,2},{1,3},{2,4},{3,5},{4,6},{5,7},{6,0},{7,1},{8,10},{9,11},{10,... | collective-permute-start | bytes 786440 | tf_op jit(solution)/shard_map/ppermute | solution.py:318
  15.2 4.1 %load.2 = (bf16[640,8192]{1,0:T(8,128)(2,1)S(1)}, bf16[2,256,256]{2,1,0:T(8,128)(2,1)}) custom-call(bf16[640,8192]{1,0:T(8,128)(2,1)} %w_ref.1, bf16[2,256,256]{2,1,0:T(8,128)(2,1)} %copy-done), custom_call_target="tpu_custom_call", output_to_operand_aliasing={{1}: (1, {})} | custom-call | bytes 10485760 | tf_op jit(solution)/shard_map/load/pallas_call | solution.py:57
  19.9 1.6 %collective-permute-start.3 = (bf16[2,256,256]{2,1,0:T(8,128)(2,1)S(1)}, bf16[2,256,256]{2,1,0:T(8,128)(2,1)S(1)}, u32[]{:S(2)}, u32[]{:S(2)}) collective-permute-start(bf16[2,256,256]{2,1,0:T(8,128)(2,1)S(1)} %collective-permute-done.1.refs_4_), channel_id=1, source_target_pairs={{0,2},{1,3},{2,4},{3,5},{4,6},{5,7},{6,0},{7,1},{8,10},{9,11},{10,... | collective-permute-start | bytes 786440 | tf_op jit(solution)/shard_map/ppermute | solution.py:318
  21.4 4.0 %collective-permute-done.12.refs_5_ = bf16[2,256,256]{2,1,0:T(8,128)(2,1)S(1)} collective-permute-done((bf16[2,256,256]{2,1,0:T(8,128)(2,1)S(1)}, bf16[2,256,256]{2,1,0:T(8,128)(2,1)S(1)}, u32[]{:S(2)}, u32[]{:S(2)}) %collective-permute-start.12) | collective-permute-done | bytes 262176 | tf_op jit(solution)/shard_map/ppermute | solution.py:318
  25.5 4.1 %load.3 = (bf16[32,256,640]{2,1,0:T(8,128)(2,1)S(1)}, bf16[2,256,256]{2,1,0:T(8,128)(2,1)S(1)}) custom-call(bf16[32,256,640]{2,1,0:T(8,128)(2,1)} %bitcast.17, bf16[2,256,256]{2,1,0:T(8,128)(2,1)S(1)} %collective-permute-done.6.through_ref), custom_call_target="tpu_custom_call", output_to_operand_aliasing={{1}: (1, {})} | custom-call | bytes 10485760 | tf_op jit(solution)/shard_map/load/pallas_call | solution.py:57
  29.6 1.5 %collective-permute-done.3.refs_0_ = bf16[2,256,256]{2,1,0:T(8,128)(2,1)S(1)} collective-permute-done((bf16[2,256,256]{2,1,0:T(8,128)(2,1)S(1)}, bf16[2,256,256]{2,1,0:T(8,128)(2,1)S(1)}, u32[]{:S(2)}, u32[]{:S(2)}) %collective-permute-start.3) | collective-permute-done | bytes 262176 | tf_op jit(solution)/shard_map/ppermute | solution.py:318
  32.4 2.3 %collective-permute-start.8 = (bf16[256,256]{1,0:T(8,128)(2,1)S(1)}, bf16[256,256]{1,0:T(8,128)(2,1)S(1)}, u32[]{:S(2)}, u32[]{:S(2)}) collective-permute-start(bf16[256,256]{1,0:T(8,128)(2,1)S(1)} %get-tuple-element.57), channel_id=1, source_target_pairs={{0,8},{8,0},{16,24},{24,16},{1,9},{9,1},{17,25},{25,17},{2,10},{10... | collective-permute-start | bytes 393224 | tf_op jit(solution)/shard_map/ppermute | solution.py:326
  34.7 1.8 %collective-permute-done.13.refs_1_ = bf16[2,256,256]{2,1,0:T(8,128)(2,1)S(1)} collective-permute-done((bf16[2,256,256]{2,1,0:T(8,128)(2,1)S(1)}, bf16[2,256,256]{2,1,0:T(8,128)(2,1)S(1)}, u32[]{:S(2)}, u32[]{:S(2)}) %collective-permute-start.13) | collective-permute-done | bytes 262176 | tf_op jit(solution)/shard_map/ppermute | solution.py:318
  37.7 1.5 %collective-permute-start.9 = (bf16[256,256]{1,0:T(8,128)(2,1)S(1)}, bf16[256,256]{1,0:T(8,128)(2,1)S(1)}, u32[]{:S(2)}, u32[]{:S(2)}) collective-permute-start(bf16[256,256]{1,0:T(8,128)(2,1)S(1)} %get-tuple-element.58), channel_id=1, source_target_pairs={{0,16},{8,24},{16,0},{24,8},{1,17},{9,25},{17,1},{25,9},{2,18},{10... | collective-permute-start | bytes 393224 | tf_op jit(solution)/shard_map/ppermute | solution.py:326
  39.3 2.2 %collective-permute-start.10 = (bf16[256,256]{1,0:T(8,128)(2,1)S(1)}, bf16[256,256]{1,0:T(8,128)(2,1)S(1)}, u32[]{:S(2)}, u32[]{:S(2)}) collective-permute-start(bf16[256,256]{1,0:T(8,128)(2,1)S(1)} %get-tuple-element.59), channel_id=1, source_target_pairs={{0,24},{8,16},{16,8},{24,0},{1,25},{9,17},{17,9},{25,1},{2,26},{10... | collective-permute-start | bytes 393224 | tf_op jit(solution)/shard_map/ppermute | solution.py:326
  41.6 3.0 %encode.2 = (f32[256,640]{1,0:T(8,128)S(1)}, bf16[256,1024]{1,0:T(8,128)(2,1)S(1)}) custom-call(s32[50]{0:T(128)S(1)} %table.1, bf16[2,256,256]{2,1,0:T(8,128)(2,1)S(1)} %pad_maximum_fusion.1.refs_0_, bf16[2,256,256]{2,1,0:T(8,128)(2,1)S(1)} %pad_maximum_fusion.2.refs_1_, bf16[2,256,256]{2,1,0:T(8,128)(2,1)S(1)} %copy-done.1, ...), custom_call_target="tpu_custom_call" | custom-call | flops 1342177280 | bytes 4194304 | tf_op jit(solution)/shard_map/encode/pallas_call | solution.py:31
  45.6 1.8 %collective-permute-done.14.refs_5_ = bf16[2,256,256]{2,1,0:T(8,128)(2,1)S(1)} collective-permute-done((bf16[2,256,256]{2,1,0:T(8,128)(2,1)S(1)}, bf16[2,256,256]{2,1,0:T(8,128)(2,1)S(1)}, u32[]{:S(2)}, u32[]{:S(2)}) %collective-permute-start.14) | collective-permute-done | bytes 262176 | tf_op jit(solution)/shard_map/ppermute | solution.py:318
  47.4 4.5 %collective-permute-done.11.refs_4_ = bf16[2,256,256]{2,1,0:T(8,128)(2,1)S(1)} collective-permute-done((bf16[2,256,256]{2,1,0:T(8,128)(2,1)S(1)}, bf16[2,256,256]{2,1,0:T(8,128)(2,1)S(1)}, u32[]{:S(2)}, u32[]{:S(2)}) %collective-permute-start.11) | collective-permute-done | bytes 262176 | tf_op jit(solution)/shard_map/ppermute | solution.py:318
  53.2 4.6 %collective-permute-start.16 = (bf16[4,256,256]{2,1,0:T(8,128)(2,1)S(1)}, bf16[4,256,256]{2,1,0:T(8,128)(2,1)S(1)}, u32[]{:S(2)}, u32[]{:S(2)}) collective-permute-start(bf16[4,256,256]{2,1,0:T(8,128)(2,1)S(1)} %pad_maximum_fusion.refs_0_), channel_id=1, source_target_pairs={{0,2},{1,3},{2,4},{3,5},{4,6},{5,7},{8,10},{9,11},{10,12},{11,13},... | collective-permute-start | bytes 1572872 | tf_op jit(solution)/shard_map/ppermute | solution.py:318
  60.2 3.2 %encode.3 = (bf16[256,640]{1,0:T(8,128)(2,1)S(1)}, bf16[256,1024]{1,0:T(8,128)(2,1)S(1)}) custom-call(s32[50]{0:T(128)S(1)} %table.1, bf16[2,256,256]{2,1,0:T(8,128)(2,1)S(1)} %collective-permute-done.3.refs_0_, bf16[2,256,256]{2,1,0:T(8,128)(2,1)S(1)} %collective-permute-done.13.refs_1_, bf16[2,256,256]{2,1,0:T(8,128)(2,1)S(1)} %collective-permute-done.18.refs_2_, ...), custom_call_target="tpu_custom_call" | custom-call | flops 1 | bytes 1 | tf_op jit(solution)/shard_map/encode/pallas_call | solution.py:31
  63.3 4.0 %decode.1 = (bf16[128,1024]{1,0:T(8,128)(2,1)S(1)}, bf16[128,1024]{1,0:T(8,128)(2,1)S(1)}, bf16[256,1024]{1,0:T(8,128)(2,1)S(1)}, bf16[256,1024]{1,0:T(8,128)(2,...) custom-call(s32[50]{0:T(128)S(1)} %table.1, ...), custom_call_target="tpu_custom_call" | custom-call | flops 1 | bytes 1 | tf_op jit(solution)/shard_map/decode/pallas_call | solution.py:31
  68.6 1.3 collective-permute-start.23
  70.8 6.3 %collective-permute-start.31 = (bf16[256,1024]{1,0:T(8,128)(2,1)S(1)}, bf16[256,1024]{1,0:T(8,128)(2,1)S(1)}, u32[]{:S(2)}, u32[]{:S(2)}) collective-permute-start(bf16[256,1024]{1,0:T(8,128)(2,1)S(1)} %sum.1), channel_id=1, source_target_pairs={{0,2},{1,3},{6,4},{7,5},{8,10},{9,11},{14,12},{15,13},{16,18},{17,... | collective-permute-start | bytes 1572872 | tf_op jit(solution)/shard_map/ppermute | solution.py:318
  77.8 6.7 %collective-permute-done.23 = bf16[4,256,256]{2,1,0:T(8,128)(2,1)S(1)} collective-permute-done((bf16[4,256,256]{2,1,0:T(8,128)(2,1)S(1)}, bf16[4,256,256]{2,1,0:T(8,128)(2,1)S(1)}, u32[]{:S(2)}, u32[]{:S(2)}) %collective-permute-start.23) | collective-permute-done | bytes 524320 | tf_op jit(solution)/shard_map/ppermute | solution.py:318
  85.2 3.7 %collective-permute-done.31 = bf16[256,1024]{1,0:T(8,128)(2,1)S(1)} collective-permute-done((bf16[256,1024]{1,0:T(8,128)(2,1)S(1)}, bf16[256,1024]{1,0:T(8,128)(2,1)S(1)}, u32[]{:S(2)}, u32[]{:S(2)}) %collective-permute-start.31) | collective-permute-done | bytes 524320 | tf_op jit(solution)/shard_map/ppermute | solution.py:318
  91.3 5.2 %collective-permute-start.32 = (bf16[256,1024]{1,0:T(8,128)(2,1)S(1)}, bf16[256,1024]{1,0:T(8,128)(2,1)S(1)}, u32[]{:S(2)}, u32[]{:S(2)}) collective-permute-start(bf16[256,1024]{1,0:T(8,128)(2,1)S(1)} %add_convert_fusion), channel_id=1, source_target_pairs={{0,2},{1,3},{2,4},{3,5},{8,10},{9,11},{10,12},{11,13},{16,18},{17,... | collective-permute-start | bytes 1572872 | tf_op jit(solution)/shard_map/ppermute | solution.py:318
  96.8 7.7 %collective-permute-done.25.refs_2_ = bf16[4,256,256]{2,1,0:T(8,128)(2,1)S(1)} collective-permute-done((bf16[4,256,256]{2,1,0:T(8,128)(2,1)S(1)}, bf16[4,256,256]{2,1,0:T(8,128)(2,1)S(1)}, u32[]{:S(2)}, u32[]{:S(2)}) %collective-permute-start.25) | collective-permute-done | bytes 524320 | tf_op jit(solution)/shard_map/ppermute | solution.py:318
  104.8 3.6 %project.2 = (f32[256,640]{1,0:T(8,128)S(1)}, f32[256,1]{1,0:T(8,128)S(1)}) custom-call(s32[50]{0:T(128)S(1)} %table.1, bf16[4,256,256]{2,1,0:T(8,128)(2,1)S(1)} %pad_maximum_fusion.refs_0_, bf16[4,256,256]{2,1,0:T(8,128)(2,1)S(1)} %collective-permute-done.34.refs_1_, bf16[4,256,256]{2,1,0:T(8,128)(2,1)S(1)} %collective-permute-done.16.refs_2_, ...), custom_call_target="tpu_custom_call" | custom-call | flops 2013265920 | bytes 4194304 | tf_op jit(solution)/shard_map/project/pallas_call | solution.py:31
  109.4 4.5 %collective-permute-start.38 = (bf16[256,1024]{1,0:T(8,128)(2,1)S(1)}, bf16[256,1024]{1,0:T(8,128)(2,1)S(1)}, u32[]{:S(2)}, u32[]{:S(2)}) collective-permute-start(bf16[256,1024]{1,0:T(8,128)(2,1)S(1)} %get-tuple-element.92), channel_id=1, source_target_pairs={{0,2},{1,3},{2,4},{3,5},{4,6},{5,7},{8,10},{9,11},{10,12},{11,13},... | collective-permute-start | bytes 1572872 | tf_op jit(solution)/shard_map/ppermute | solution.py:318
  115.2 3.9 %project.3 = (f32[256,640]{1,0:T(8,128)}, f32[8,256]{1,0:T(8,128)S(1)}) custom-call(s32[50]{0:T(128)S(1)} %table.1, bf16[4,256,256]{2,1,0:T(8,128)(2,1)S(1)} %add.43.refs_0_, bf16[4,256,256]{2,1,0:T(8,128)(2,1)S(1)} %collective-permute-done.24.refs_1_, bf16[4,256,256]{2,1,0:T(8,128)(2,1)S(1)} %collective-permute-done.25.refs_2_, ...), custom_call_target="tpu_custom_call" | custom-call | flops 1 | bytes 1 | tf_op jit(solution)/shard_map/project/pallas_call | solution.py:31
  120.2 4.5 %collective-permute-start.43 = (f32[1,256]{1,0:T(1,128)S(1)}, f32[1,256]{1,0:T(1,128)S(1)}, u32[]{:S(2)}, u32[]{:S(2)}) collective-permute-start(f32[1,256]{1,0:T(1,128)S(1)} %slice_add_fusion), channel_id=1, source_target_pairs={{0,6},{1,7},{2,4},{3,5},{4,2},{5,3},{6,0},{7,1},{8,14},{9,15},{10,... | collective-permute-start | bytes 3080 | tf_op jit(solution)/shard_map/ppermute | solution.py:318
  125.3 4.5 %collective-permute-done.39 = bf16[256,1024]{1,0:T(8,128)(2,1)S(1)} collective-permute-done((bf16[256,1024]{1,0:T(8,128)(2,1)S(1)}, bf16[256,1024]{1,0:T(8,128)(2,1)S(1)}, u32[]{:S(2)}, u32[]{:S(2)}) %collective-permute-start.39) | collective-permute-done | bytes 524320 | tf_op jit(solution)/shard_map/ppermute | solution.py:318
  (92 shorter events, 22.7 us)
Async XLA Ops:
  1.8 6.9 %collective-permute-start = (bf16[256,256]{1,0:T(8,128)(2,1)S(1)}, bf16[256,256]{1,0:T(8,128)(2,1)S(1)}, u32[]{:S(2)}, u32[]{:S(2)}) collective-permute-start(bf16[256,256]{1,0:T(8,128)(2,1)S(1)} %get-tuple-element.98), channel_id=1, source_target_pairs={{0,8},{8,0},{16,24},{24,16},{1,9},{9,1},{17,25},{25,17},{2,10},{10... | collective-permute-start | bytes 393224 | tf_op jit(solution)/shard_map/ppermute | solution.py:326
  4.8 8.0 %collective-permute-start.4 = (bf16[256,256]{1,0:T(8,128)(2,1)S(1)}, bf16[256,256]{1,0:T(8,128)(2,1)S(1)}, u32[]{:S(2)}, u32[]{:S(2)}) collective-permute-start(bf16[256,256]{1,0:T(8,128)(2,1)S(1)} %get-tuple-element.97), channel_id=1, source_target_pairs={{0,16},{8,24},{16,0},{24,8},{1,17},{9,25},{17,1},{25,9},{2,18},{10... | collective-permute-start | bytes 393224 | tf_op jit(solution)/shard_map/ppermute | solution.py:326
  8.8 11.0 %collective-permute-start.1 = (bf16[2,256,256]{2,1,0:T(8,128)(2,1)S(1)}, bf16[2,256,256]{2,1,0:T(8,128)(2,1)S(1)}, u32[]{:S(2)}, u32[]{:S(2)}) collective-permute-start(bf16[2,256,256]{2,1,0:T(8,128)(2,1)S(1)} %pad_maximum_fusion.1.refs_0_), channel_id=1, source_target_pairs={{0,2},{1,3},{2,4},{3,5},{4,6},{5,7},{6,0},{7,1},{8,10},{9,11},{10,... | collective-permute-start | bytes 786440 | tf_op jit(solution)/shard_map/ppermute | solution.py:318
  12.8 12.6 %collective-permute-start.12 = (bf16[2,256,256]{2,1,0:T(8,128)(2,1)S(1)}, bf16[2,256,256]{2,1,0:T(8,128)(2,1)S(1)}, u32[]{:S(2)}, u32[]{:S(2)}) collective-permute-start(bf16[2,256,256]{2,1,0:T(8,128)(2,1)S(1)} %pad_maximum_fusion.2.refs_1_), channel_id=1, source_target_pairs={{0,2},{1,3},{2,4},{3,5},{4,6},{5,7},{6,0},{7,1},{8,10},{9,11},{10,... | collective-permute-start | bytes 786440 | tf_op jit(solution)/shard_map/ppermute | solution.py:318
  14.5 11.0 %collective-permute-start.6 = (bf16[2,256,256]{2,1,0:T(8,128)(2,1)S(1)}, bf16[2,256,256]{2,1,0:T(8,128)(2,1)S(1)}, u32[]{:S(2)}, u32[]{:S(2)}) collective-permute-start(bf16[2,256,256]{2,1,0:T(8,128)(2,1)S(1)} %pad_maximum_fusion.2.refs_1_), channel_id=1, source_target_pairs={{0,1},{1,0},{2,3},{3,2},{4,5},{5,4},{6,7},{7,6},{8,9},{9,8},{10,11... | collective-permute-start | bytes 786440 | tf_op jit(solution)/shard_map/ppermute | solution.py:321
  19.9 11.2 %collective-permute-start.3 = (bf16[2,256,256]{2,1,0:T(8,128)(2,1)S(1)}, bf16[2,256,256]{2,1,0:T(8,128)(2,1)S(1)}, u32[]{:S(2)}, u32[]{:S(2)}) collective-permute-start(bf16[2,256,256]{2,1,0:T(8,128)(2,1)S(1)} %collective-permute-done.1.refs_4_), channel_id=1, source_target_pairs={{0,2},{1,3},{2,4},{3,5},{4,6},{5,7},{6,0},{7,1},{8,10},{9,11},{10,... | collective-permute-start | bytes 786440 | tf_op jit(solution)/shard_map/ppermute | solution.py:318
  25.5 11.0 %collective-permute-start.13 = (bf16[2,256,256]{2,1,0:T(8,128)(2,1)S(1)}, bf16[2,256,256]{2,1,0:T(8,128)(2,1)S(1)}, u32[]{:S(2)}, u32[]{:S(2)}) collective-permute-start(bf16[2,256,256]{2,1,0:T(8,128)(2,1)S(1)} %collective-permute-done.12.refs_5_), channel_id=1, source_target_pairs={{0,2},{1,3},{2,4},{3,5},{4,6},{5,7},{6,0},{7,1},{8,10},{9,11},{10,... | collective-permute-start | bytes 786440 | tf_op jit(solution)/shard_map/ppermute | solution.py:318
  25.5 13.8 %collective-permute-start.15 = (bf16[2,256,256]{2,1,0:T(8,128)(2,1)S(1)}, bf16[2,256,256]{2,1,0:T(8,128)(2,1)S(1)}, u32[]{:S(2)}, u32[]{:S(2)}) collective-permute-start(bf16[2,256,256]{2,1,0:T(8,128)(2,1)S(1)} %collective-permute-done.12.refs_5_), channel_id=1, source_target_pairs={{0,1},{1,0},{2,3},{3,2},{4,5},{5,4},{6,7},{7,6},{8,9},{9,8},{10,11... | collective-permute-start | bytes 786440 | tf_op jit(solution)/shard_map/ppermute | solution.py:321
  32.4 9.1 %collective-permute-start.8 = (bf16[256,256]{1,0:T(8,128)(2,1)S(1)}, bf16[256,256]{1,0:T(8,128)(2,1)S(1)}, u32[]{:S(2)}, u32[]{:S(2)}) collective-permute-start(bf16[256,256]{1,0:T(8,128)(2,1)S(1)} %get-tuple-element.57), channel_id=1, source_target_pairs={{0,8},{8,0},{16,24},{24,16},{1,9},{9,1},{17,25},{25,17},{2,10},{10... | collective-permute-start | bytes 393224 | tf_op jit(solution)/shard_map/ppermute | solution.py:326
  36.5 11.0 %collective-permute-start.14 = (bf16[2,256,256]{2,1,0:T(8,128)(2,1)S(1)}, bf16[2,256,256]{2,1,0:T(8,128)(2,1)S(1)}, u32[]{:S(2)}, u32[]{:S(2)}) collective-permute-start(bf16[2,256,256]{2,1,0:T(8,128)(2,1)S(1)} %collective-permute-done.13.refs_1_), channel_id=1, source_target_pairs={{0,2},{1,3},{2,4},{3,5},{4,6},{5,7},{6,0},{7,1},{8,10},{9,11},{10,... | collective-permute-start | bytes 786440 | tf_op jit(solution)/shard_map/ppermute | solution.py:318
  36.5 15.5 %collective-permute-start.11 = (bf16[2,256,256]{2,1,0:T(8,128)(2,1)S(1)}, bf16[2,256,256]{2,1,0:T(8,128)(2,1)S(1)}, u32[]{:S(2)}, u32[]{:S(2)}) collective-permute-start(bf16[2,256,256]{2,1,0:T(8,128)(2,1)S(1)} %collective-permute-done.3.refs_0_), channel_id=1, source_target_pairs={{0,2},{1,3},{2,4},{3,5},{4,6},{5,7},{6,0},{7,1},{8,10},{9,11},{10,... | collective-permute-start | bytes 786440 | tf_op jit(solution)/shard_map/ppermute | solution.py:318
  37.7 7.8 %collective-permute-start.9 = (bf16[256,256]{1,0:T(8,128)(2,1)S(1)}, bf16[256,256]{1,0:T(8,128)(2,1)S(1)}, u32[]{:S(2)}, u32[]{:S(2)}) collective-permute-start(bf16[256,256]{1,0:T(8,128)(2,1)S(1)} %get-tuple-element.58), channel_id=1, source_target_pairs={{0,16},{8,24},{16,0},{24,8},{1,17},{9,25},{17,1},{25,9},{2,18},{10... | collective-permute-start | bytes 393224 | tf_op jit(solution)/shard_map/ppermute | solution.py:326
  41.5 16.9 %collective-permute-start.19 = (bf16[2,256,256]{2,1,0:T(8,128)(2,1)S(1)}, bf16[2,256,256]{2,1,0:T(8,128)(2,1)S(1)}, u32[]{:S(2)}, u32[]{:S(2)}) collective-permute-start(bf16[2,256,256]{2,1,0:T(8,128)(2,1)S(1)} %collective-permute-done.13.refs_1_), channel_id=1, source_target_pairs={{0,1},{1,0},{2,3},{3,2},{4,5},{5,4},{6,7},{7,6},{8,9},{9,8},{10,11... | collective-permute-start | bytes 786440 | tf_op jit(solution)/shard_map/ppermute | solution.py:321
  51.9 16.0 %collective-permute-start.17 = (bf16[4,256,256]{2,1,0:T(8,128)(2,1)S(1)}, bf16[4,256,256]{2,1,0:T(8,128)(2,1)S(1)}, u32[]{:S(2)}, u32[]{:S(2)}) collective-permute-start(bf16[4,256,256]{2,1,0:T(8,128)(2,1)S(1)} %pad_maximum_fusion.refs_0_), channel_id=1, source_target_pairs={{2,0},{3,1},{4,2},{5,3},{6,4},{7,5},{10,8},{11,9},{12,10},{13,11},... | collective-permute-start | bytes 1572872 | tf_op jit(solution)/shard_map/ppermute | solution.py:318
  53.2 14.7 %collective-permute-start.16 = (bf16[4,256,256]{2,1,0:T(8,128)(2,1)S(1)}, bf16[4,256,256]{2,1,0:T(8,128)(2,1)S(1)}, u32[]{:S(2)}, u32[]{:S(2)}) collective-permute-start(bf16[4,256,256]{2,1,0:T(8,128)(2,1)S(1)} %pad_maximum_fusion.refs_0_), channel_id=1, source_target_pairs={{0,2},{1,3},{2,4},{3,5},{4,6},{5,7},{8,10},{9,11},{10,12},{11,13},... | collective-permute-start | bytes 1572872 | tf_op jit(solution)/shard_map/ppermute | solution.py:318
  68.0 9.5 %collective-permute-start.22 = (bf16[4,256,256]{2,1,0:T(8,128)(2,1)S(1)}, bf16[4,256,256]{2,1,0:T(8,128)(2,1)S(1)}, u32[]{:S(2)}, u32[]{:S(2)}) collective-permute-start(bf16[4,256,256]{2,1,0:T(8,128)(2,1)S(1)} %collective-permute-done.16.refs_2_), channel_id=1, source_target_pairs={{2,4},{3,5},{4,6},{5,7},{10,12},{11,13},{12,14},{13,15},{18,20},{1... | collective-permute-start | bytes 1572872 | tf_op jit(solution)/shard_map/ppermute | solution.py:318
  68.6 15.8 %collective-permute-start.23 = (bf16[4,256,256]{2,1,0:T(8,128)(2,1)S(1)}, bf16[4,256,256]{2,1,0:T(8,128)(2,1)S(1)}, u32[]{:S(2)}, u32[]{:S(2)}) collective-permute-start(bf16[4,256,256]{2,1,0:T(8,128)(2,1)S(1)} %collective-permute-done.17.refs_4_), channel_id=1, source_target_pairs={{2,0},{3,1},{4,2},{5,3},{10,8},{11,9},{12,10},{13,11},{18,16},{19,... | collective-permute-start | bytes 1572872 | tf_op jit(solution)/shard_map/ppermute | solution.py:318
  70.6 14.0 %collective-permute-start.30 = (bf16[256,1024]{1,0:T(8,128)(2,1)S(1)}, bf16[256,1024]{1,0:T(8,128)(2,1)S(1)}, u32[]{:S(2)}, u32[]{:S(2)}) collective-permute-start(bf16[256,1024]{1,0:T(8,128)(2,1)S(1)} %get-tuple-element.83), channel_id=1, source_target_pairs={{0,1},{1,0},{2,3},{3,2},{4,5},{5,4},{6,7},{7,6},{8,9},{9,8},{10,11... | collective-permute-start | bytes 1572872 | tf_op jit(solution)/shard_map/ppermute | solution.py:321
  70.8 18.1 %collective-permute-start.31 = (bf16[256,1024]{1,0:T(8,128)(2,1)S(1)}, bf16[256,1024]{1,0:T(8,128)(2,1)S(1)}, u32[]{:S(2)}, u32[]{:S(2)}) collective-permute-start(bf16[256,1024]{1,0:T(8,128)(2,1)S(1)} %sum.1), channel_id=1, source_target_pairs={{0,2},{1,3},{6,4},{7,5},{8,10},{9,11},{14,12},{15,13},{16,18},{17,... | collective-permute-start | bytes 1572872 | tf_op jit(solution)/shard_map/ppermute | solution.py:318
  77.2 13.3 %collective-permute-start.34 = (bf16[4,256,256]{2,1,0:T(8,128)(2,1)S(1)}, bf16[4,256,256]{2,1,0:T(8,128)(2,1)S(1)}, u32[]{:S(2)}, u32[]{:S(2)}) collective-permute-start(bf16[4,256,256]{2,1,0:T(8,128)(2,1)S(1)} %pad_maximum_fusion.refs_0_), channel_id=1, source_target_pairs={{0,1},{1,0},{2,3},{3,2},{4,5},{5,4},{6,7},{7,6},{8,9},{9,8},{10,11... | collective-permute-start | bytes 1572872 | tf_op jit(solution)/shard_map/ppermute | solution.py:321
  77.5 13.2 %collective-permute-start.37 = (bf16[256,1024]{1,0:T(8,128)(2,1)S(1)}, bf16[256,1024]{1,0:T(8,128)(2,1)S(1)}, u32[]{:S(2)}, u32[]{:S(2)}) collective-permute-start(bf16[256,1024]{1,0:T(8,128)(2,1)S(1)} %get-tuple-element.91), channel_id=1, source_target_pairs={{0,1},{1,0},{2,3},{3,2},{4,5},{5,4},{6,7},{7,6},{8,9},{9,8},{10,11... | collective-permute-start | bytes 1572872 | tf_op jit(solution)/shard_map/ppermute | solution.py:321
  84.5 6.8 %collective-permute-start.35 = (bf16[4,256,256]{2,1,0:T(8,128)(2,1)S(1)}, bf16[4,256,256]{2,1,0:T(8,128)(2,1)S(1)}, u32[]{:S(2)}, u32[]{:S(2)}) collective-permute-start(bf16[4,256,256]{2,1,0:T(8,128)(2,1)S(1)} %collective-permute-done.16.refs_2_), channel_id=1, source_target_pairs={{0,1},{1,0},{2,3},{3,2},{4,5},{5,4},{6,7},{7,6},{8,9},{9,8},{10,11... | collective-permute-start | bytes 1572872 | tf_op jit(solution)/shard_map/ppermute | solution.py:321
  84.6 11.9 %collective-permute-start.36 = (bf16[4,256,256]{2,1,0:T(8,128)(2,1)S(1)}, bf16[4,256,256]{2,1,0:T(8,128)(2,1)S(1)}, u32[]{:S(2)}, u32[]{:S(2)}) collective-permute-start(bf16[4,256,256]{2,1,0:T(8,128)(2,1)S(1)} %collective-permute-done.17.refs_4_), channel_id=1, source_target_pairs={{0,1},{1,0},{2,3},{3,2},{4,5},{5,4},{6,7},{7,6},{8,9},{9,8},{10,11... | collective-permute-start | bytes 1572872 | tf_op jit(solution)/shard_map/ppermute | solution.py:321
  89.0 15.5 %collective-permute-start.25 = (bf16[4,256,256]{2,1,0:T(8,128)(2,1)S(1)}, bf16[4,256,256]{2,1,0:T(8,128)(2,1)S(1)}, u32[]{:S(2)}, u32[]{:S(2)}) collective-permute-start(bf16[4,256,256]{2,1,0:T(8,128)(2,1)S(1)} %add.43.refs_0_), channel_id=1, source_target_pairs={{4,6},{5,7},{2,0},{3,1},{12,14},{13,15},{10,8},{11,9},{20,22},{21,... | collective-permute-start | bytes 1572872 | tf_op jit(solution)/shard_map/ppermute | solution.py:318
  90.5 17.9 %collective-permute-start.29 = (bf16[256,1024]{1,0:T(8,128)(2,1)S(1)}, bf16[256,1024]{1,0:T(8,128)(2,1)S(1)}, u32[]{:S(2)}, u32[]{:S(2)}) collective-permute-start(bf16[256,1024]{1,0:T(8,128)(2,1)S(1)} %get-tuple-element.81), channel_id=1, source_target_pairs={{0,1},{1,0},{2,3},{3,2},{4,5},{5,4},{6,7},{7,6},{8,9},{9,8},{10,11... | collective-permute-start | bytes 1572872 | tf_op jit(solution)/shard_map/ppermute | solution.py:321
  90.6 17.8 %collective-permute-start.33 = (bf16[256,1024]{1,0:T(8,128)(2,1)S(1)}, bf16[256,1024]{1,0:T(8,128)(2,1)S(1)}, u32[]{:S(2)}, u32[]{:S(2)}) collective-permute-start(bf16[256,1024]{1,0:T(8,128)(2,1)S(1)} %add_convert_fusion), channel_id=1, source_target_pairs={{4,2},{5,3},{6,4},{7,5},{12,10},{13,11},{14,12},{15,13},{20,18},{2... | collective-permute-start | bytes 1572872 | tf_op jit(solution)/shard_map/ppermute | solution.py:318
  91.3 17.1 %collective-permute-start.32 = (bf16[256,1024]{1,0:T(8,128)(2,1)S(1)}, bf16[256,1024]{1,0:T(8,128)(2,1)S(1)}, u32[]{:S(2)}, u32[]{:S(2)}) collective-permute-start(bf16[256,1024]{1,0:T(8,128)(2,1)S(1)} %add_convert_fusion), channel_id=1, source_target_pairs={{0,2},{1,3},{2,4},{3,5},{8,10},{9,11},{10,12},{11,13},{16,18},{17,... | collective-permute-start | bytes 1572872 | tf_op jit(solution)/shard_map/ppermute | solution.py:318
  96.6 18.6 %collective-permute-start.24 = (bf16[4,256,256]{2,1,0:T(8,128)(2,1)S(1)}, bf16[4,256,256]{2,1,0:T(8,128)(2,1)S(1)}, u32[]{:S(2)}, u32[]{:S(2)}) collective-permute-start(bf16[4,256,256]{2,1,0:T(8,128)(2,1)S(1)} %add.43.refs_0_), channel_id=1, source_target_pairs={{0,1},{1,0},{2,3},{3,2},{4,5},{5,4},{6,7},{7,6},{8,9},{9,8},{10,11... | collective-permute-start | bytes 1572872 | tf_op jit(solution)/shard_map/ppermute | solution.py:321
  104.5 10.7 %collective-permute-start.26 = (bf16[4,256,256]{2,1,0:T(8,128)(2,1)S(1)}, bf16[4,256,256]{2,1,0:T(8,128)(2,1)S(1)}, u32[]{:S(2)}, u32[]{:S(2)}) collective-permute-start(bf16[4,256,256]{2,1,0:T(8,128)(2,1)S(1)} %collective-permute-done.25.refs_2_), channel_id=1, source_target_pairs={{0,1},{1,0},{2,3},{3,2},{4,5},{5,4},{6,7},{7,6},{8,9},{9,8},{10,11... | collective-permute-start | bytes 1572872 | tf_op jit(solution)/shard_map/ppermute | solution.py:321
  109.4 15.9 %collective-permute-start.38 = (bf16[256,1024]{1,0:T(8,128)(2,1)S(1)}, bf16[256,1024]{1,0:T(8,128)(2,1)S(1)}, u32[]{:S(2)}, u32[]{:S(2)}) collective-permute-start(bf16[256,1024]{1,0:T(8,128)(2,1)S(1)} %get-tuple-element.92), channel_id=1, source_target_pairs={{0,2},{1,3},{2,4},{3,5},{4,6},{5,7},{8,10},{9,11},{10,12},{11,13},... | collective-permute-start | bytes 1572872 | tf_op jit(solution)/shard_map/ppermute | solution.py:318
  113.9 15.9 %collective-permute-start.39 = (bf16[256,1024]{1,0:T(8,128)(2,1)S(1)}, bf16[256,1024]{1,0:T(8,128)(2,1)S(1)}, u32[]{:S(2)}, u32[]{:S(2)}) collective-permute-start(bf16[256,1024]{1,0:T(8,128)(2,1)S(1)} %get-tuple-element.93), channel_id=1, source_target_pairs={{2,0},{3,1},{4,2},{5,3},{6,4},{7,5},{10,8},{11,9},{12,10},{13,11},... | collective-permute-start | bytes 1572872 | tf_op jit(solution)/shard_map/ppermute | solution.py:318
  120.2 10.8 %collective-permute-start.43 = (f32[1,256]{1,0:T(1,128)S(1)}, f32[1,256]{1,0:T(1,128)S(1)}, u32[]{:S(2)}, u32[]{:S(2)}) collective-permute-start(f32[1,256]{1,0:T(1,128)S(1)} %slice_add_fusion), channel_id=1, source_target_pairs={{0,6},{1,7},{2,4},{3,5},{4,2},{5,3},{6,0},{7,1},{8,14},{9,15},{10,... | collective-permute-start | bytes 3080 | tf_op jit(solution)/shard_map/ppermute | solution.py:318
  (18 other events, 159.8 us)

commit v10 on v8

--- a/solution.py
+++ b/solution.py
@@ -333,27 +333,31 @@
     ring = [(a, (a + 1) % chips) for a in range(chips)]
     cut_x = [lax.dynamic_slice_in_dim(resid, (i ^ s) * rows, rows, 0) for s in range(n_tok)]
     near_x = [exchange(cut_x, X_STREAMS)]
+    cut_g = [lax.dynamic_slice_in_dim(resid_grad, (i ^ s) * rows, rows, 0) for s in range(n_tok)]
+    shard_g, = exchange(cut_g, ((0, 1, 2, 3),))
     far_x = [[cross(a) for a in near_x[0]]]
     for k in range(1, chips):
         first, second = near_x[-1]
         if k == 1:
             second = after(second, table)
         if k == 2:
+            second = after(second, shard_g)
             w_out, far_x[0][0] = load(w_dec, far_x[0][0], 44)
             first = after(first, far_x[0][0])
         if k == 3:
             far_x[0][1] = after(far_x[0][1], far_x[1][0])
             w_in, far_x[0][1] = load(w_enc.reshape(n_tok * n_feat, width, feats), far_x[0][1], 36)
             first = after(first, far_x[0][1])
-            shard_g, = exchange(pick(table, after(resid_grad, first), n_tok), ((0, 1, 2, 3),))
+            far_x.append([cross(first), cross(second)])
+            slots = [near_x[0], far_x[0], near_x[1], far_x[1]]
+            carry = encode(
+                table, SLOTS["enc_a"], slots, w_in, bias, None, X_STREAMS, False, n_feat
+            )
+            second = after(second, carry)
         near_x[-1] = [first, second]
-        if k > 1:
+        if k == 2:
             far_x.append([cross(a) for a in near_x[-1]])
         near_x.append([send(first, ring), send(second, ring)])
-    slots = [near_x[0], far_x[0], near_x[1], far_x[1]]
-    carry = encode(
-        after(table, shard_g), SLOTS["enc_a"], slots, w_in, bias, None, X_STREAMS, False, n_feat
-    )
     far_x.append([cross(near_x[3][0]), cross(after(near_x[3][1], carry))])
 
     up_pairs = [(a, a + 1) for a in range(chips - 1)]

time: 133 us -> 139 us (1.045)
  waiting for transfers between devices: 50.1 us -> 53.8 us
  starting transfers between devices: 45.9 us -> 48.9 us
    ppermute x19, waiting for transfers between devices: 39.7 us -> 46.1 us  [send(): return lax.ppermute(array, 'feat', along(pairs))]
    ppermute x6, waiting for transfers between devices: 7.6 us -> 4.84 us  [exchange(): lax.ppermute(blocks[s], 'tok', [(a, a ^ s) for a in range(n_tok)])]
    ppermute x19, starting transfers between devices: 34.4 us -> 36.9 us  [send(): return lax.ppermute(array, 'feat', along(pairs))]
  transfers between devices with their start and end apart: 44 -> 44, of which waited for: 19 -> 16; matrix products, arithmetic and copies ran while one was open for 2% -> 2% of each run, Pallas kernels for 23% -> 21%
where the time goes in v10:
time: 139 us; the launch traced here: 138 us
  waiting for transfers between devices  53.8 us (39%)
  starting transfers between devices  48.9 us (35%)
  Pallas kernels  28.8 us (21%)
  local copies, waits for them, and re-layouts  3.11 us (2%)
  other arithmetic  2.66 us (2%)
    ppermute x19, waiting for transfers between devices, send(): return lax.ppermute(array, 'feat', along(pairs))  46.1 us
    ppermute x19, starting transfers between devices, send(): return lax.ppermute(array, 'feat', along(pairs))  36.9 us
    pallas_call x7, Pallas kernels, kernel_call(): pl.pallas_call(body, in_specs=[SMEM] + [VMEM] * (len(args) - 1), out_spec...  19.3 us
    ppermute x6, starting transfers between devices, exchange(): lax.ppermute(blocks[s], 'tok', [(a, a ^ s) for a in range(n_tok)])  8.46 us
    pallas_call x2, Pallas kernels, load(): pl.pallas_call(load_body, in_specs=[anywhere, anywhere], out_specs=[VMEM,...  8.17 us
    ppermute x6, waiting for transfers between devices, exchange(): lax.ppermute(blocks[s], 'tok', [(a, a ^ s) for a in range(n_tok)])  4.84 us
    ppermute x19, starting transfers between devices, cross(): return lax.ppermute(array, 'feat', [(a, a ^ 1) for a in range(n_feat)])  3.54 us
    ppermute x19, waiting for transfers between devices, cross(): return lax.ppermute(array, 'feat', [(a, a ^ 1) for a in range(n_feat)])  2.87 us
  transfers between devices with their start and end apart: 44, of which 16 were waited for; matrix products, arithmetic and copies ran while one was open for 2% of the time, Pallas kernels for 21%

profile of v10, /device:TPU:0, one launch (start us, length us, event | category | flops | bytes accessed | tf_op | source)
XLA Modules:
  0.0 138.3 jit_solution(14317814977024307670)
XLA Ops:
  1.8 3.0 %collective-permute-start.3 = (bf16[256,256]{1,0:T(8,128)(2,1)S(1)}, bf16[256,256]{1,0:T(8,128)(2,1)S(1)}, u32[]{:S(2)}, u32[]{:S(2)}) collective-permute-start(bf16[256,256]{1,0:T(8,128)(2,1)S(1)} %get-tuple-element.90), channel_id=1, source_target_pairs={{0,8},{8,0},{16,24},{24,16},{1,9},{9,1},{17,25},{25,17},{2,10},{10... | collective-permute-start | bytes 393224 | tf_op jit(solution)/shard_map/ppermute | solution.py:326
  4.8 1.5 %collective-permute-start.7 = (bf16[256,256]{1,0:T(8,128)(2,1)S(1)}, bf16[256,256]{1,0:T(8,128)(2,1)S(1)}, u32[]{:S(2)}, u32[]{:S(2)}) collective-permute-start(bf16[256,256]{1,0:T(8,128)(2,1)S(1)} %get-tuple-element.89), channel_id=1, source_target_pairs={{0,16},{8,24},{16,0},{24,8},{1,17},{9,25},{17,1},{25,9},{2,18},{10... | collective-permute-start | bytes 393224 | tf_op jit(solution)/shard_map/ppermute | solution.py:326
  6.4 2.4 %collective-permute-done.3 = bf16[256,256]{1,0:T(8,128)(2,1)S(1)} collective-permute-done((bf16[256,256]{1,0:T(8,128)(2,1)S(1)}, bf16[256,256]{1,0:T(8,128)(2,1)S(1)}, u32[]{:S(2)}, u32[]{:S(2)}) %collective-permute-start.3) | collective-permute-done | bytes 131104 | tf_op jit(solution)/shard_map/ppermute | solution.py:326
  9.6 1.3 table.1
  10.9 1.9 %collective-permute-start.4 = (bf16[2,256,256]{2,1,0:T(8,128)(2,1)S(1)}, bf16[2,256,256]{2,1,0:T(8,128)(2,1)S(1)}, u32[]{:S(2)}, u32[]{:S(2)}) collective-permute-start(bf16[2,256,256]{2,1,0:T(8,128)(2,1)S(1)} %pad_maximum_fusion.1.refs_0_), channel_id=1, source_target_pairs={{0,2},{1,3},{2,4},{3,5},{4,6},{5,7},{6,0},{7,1},{8,10},{9,11},{10,... | collective-permute-start | bytes 786440 | tf_op jit(solution)/shard_map/ppermute | solution.py:318
  12.8 1.6 %collective-permute-start.12 = (bf16[2,256,256]{2,1,0:T(8,128)(2,1)S(1)}, bf16[2,256,256]{2,1,0:T(8,128)(2,1)S(1)}, u32[]{:S(2)}, u32[]{:S(2)}) collective-permute-start(bf16[2,256,256]{2,1,0:T(8,128)(2,1)S(1)} %pad_maximum_fusion.2.refs_1_), channel_id=1, source_target_pairs={{0,2},{1,3},{2,4},{3,5},{4,6},{5,7},{6,0},{7,1},{8,10},{9,11},{10,... | collective-permute-start | bytes 786440 | tf_op jit(solution)/shard_map/ppermute | solution.py:318
  15.6 2.3 %collective-permute-start = (bf16[256,256]{1,0:T(8,128)(2,1)S(1)}, bf16[256,256]{1,0:T(8,128)(2,1)S(1)}, u32[]{:S(2)}, u32[]{:S(2)}) collective-permute-start(bf16[256,256]{1,0:T(8,128)(2,1)S(1)} %get-tuple-element.94), channel_id=1, source_target_pairs={{0,8},{8,0},{16,24},{24,16},{1,9},{9,1},{17,25},{25,17},{2,10},{10... | collective-permute-start | bytes 393224 | tf_op jit(solution)/shard_map/ppermute | solution.py:326
  19.6 4.1 %load.2 = (bf16[640,8192]{1,0:T(8,128)(2,1)S(1)}, bf16[2,256,256]{2,1,0:T(8,128)(2,1)}) custom-call(bf16[640,8192]{1,0:T(8,128)(2,1)} %w_ref.1, bf16[2,256,256]{2,1,0:T(8,128)(2,1)} %copy-done), custom_call_target="tpu_custom_call", output_to_operand_aliasing={{1}: (1, {})} | custom-call | bytes 10485760 | tf_op jit(solution)/shard_map/load/pallas_call | solution.py:57
  25.4 1.4 %collective-permute-done.1 = bf16[256,256]{1,0:T(8,128)(2,1)S(1)} collective-permute-done((bf16[256,256]{1,0:T(8,128)(2,1)S(1)}, bf16[256,256]{1,0:T(8,128)(2,1)S(1)}, u32[]{:S(2)}, u32[]{:S(2)}) %collective-permute-start.1) | collective-permute-done | bytes 131104 | tf_op jit(solution)/shard_map/ppermute | solution.py:326
  28.8 4.1 %load.3 = (bf16[32,256,640]{2,1,0:T(8,128)(2,1)S(1)}, bf16[2,256,256]{2,1,0:T(8,128)(2,1)S(1)}) custom-call(bf16[32,256,640]{2,1,0:T(8,128)(2,1)} %bitcast.17, bf16[2,256,256]{2,1,0:T(8,128)(2,1)S(1)} %collective-permute-done.9.through_ref), custom_call_target="tpu_custom_call", output_to_operand_aliasing={{1}: (1, {})} | custom-call | bytes 10485760 | tf_op jit(solution)/shard_map/load/pallas_call | solution.py:57
  32.9 3.0 %encode.2 = (f32[256,640]{1,0:T(8,128)S(1)}, bf16[256,1024]{1,0:T(8,128)(2,1)S(1)}) custom-call(s32[50]{0:T(128)S(1)} %table.1, bf16[2,256,256]{2,1,0:T(8,128)(2,1)S(1)} %pad_maximum_fusion.1.refs_0_, bf16[2,256,256]{2,1,0:T(8,128)(2,1)S(1)} %pad_maximum_fusion.2.refs_1_, bf16[2,256,256]{2,1,0:T(8,128)(2,1)S(1)} %copy-done.1, ...), custom_call_target="tpu_custom_call" | custom-call | flops 1342177280 | bytes 4194304 | tf_op jit(solution)/shard_map/encode/pallas_call | solution.py:31
  35.9 2.4 %collective-permute-done.13.refs_1_ = bf16[2,256,256]{2,1,0:T(8,128)(2,1)S(1)} collective-permute-done((bf16[2,256,256]{2,1,0:T(8,128)(2,1)S(1)}, bf16[2,256,256]{2,1,0:T(8,128)(2,1)S(1)}, u32[]{:S(2)}, u32[]{:S(2)}) %collective-permute-start.13) | collective-permute-done | bytes 262176 | tf_op jit(solution)/shard_map/ppermute | solution.py:318
  38.3 5.2 %collective-permute-done.6.refs_0_ = bf16[2,256,256]{2,1,0:T(8,128)(2,1)S(1)} collective-permute-done((bf16[2,256,256]{2,1,0:T(8,128)(2,1)S(1)}, bf16[2,256,256]{2,1,0:T(8,128)(2,1)S(1)}, u32[]{:S(2)}, u32[]{:S(2)}) %collective-permute-start.6) | collective-permute-done | bytes 262176 | tf_op jit(solution)/shard_map/ppermute | solution.py:318
  43.5 11.0 %collective-permute-done.11.refs_4_ = bf16[2,256,256]{2,1,0:T(8,128)(2,1)S(1)} collective-permute-done((bf16[2,256,256]{2,1,0:T(8,128)(2,1)S(1)}, bf16[2,256,256]{2,1,0:T(8,128)(2,1)S(1)}, u32[]{:S(2)}, u32[]{:S(2)}) %collective-permute-start.11) | collective-permute-done | bytes 262176 | tf_op jit(solution)/shard_map/ppermute | solution.py:318
  54.5 4.3 %collective-permute-done.15.refs_5_ = bf16[2,256,256]{2,1,0:T(8,128)(2,1)S(1)} collective-permute-done((bf16[2,256,256]{2,1,0:T(8,128)(2,1)S(1)}, bf16[2,256,256]{2,1,0:T(8,128)(2,1)S(1)}, u32[]{:S(2)}, u32[]{:S(2)}) %collective-permute-start.15) | collective-permute-done | bytes 262176 | tf_op jit(solution)/shard_map/ppermute | solution.py:318
  58.9 1.3 collective-permute-start.17
  60.1 4.6 %collective-permute-start.16 = (bf16[4,256,256]{2,1,0:T(8,128)(2,1)S(1)}, bf16[4,256,256]{2,1,0:T(8,128)(2,1)S(1)}, u32[]{:S(2)}, u32[]{:S(2)}) collective-permute-start(bf16[4,256,256]{2,1,0:T(8,128)(2,1)S(1)} %pad_maximum_fusion.refs_0_), channel_id=1, source_target_pairs={{0,2},{1,3},{2,4},{3,5},{4,6},{5,7},{8,10},{9,11},{10,12},{11,13},... | collective-permute-start | bytes 1572872 | tf_op jit(solution)/shard_map/ppermute | solution.py:318
  67.1 3.2 %encode.3 = (bf16[256,640]{1,0:T(8,128)(2,1)S(1)}, bf16[256,1024]{1,0:T(8,128)(2,1)S(1)}) custom-call(s32[50]{0:T(128)S(1)} %table.1, bf16[2,256,256]{2,1,0:T(8,128)(2,1)S(1)} %collective-permute-done.6.refs_0_, bf16[2,256,256]{2,1,0:T(8,128)(2,1)S(1)} %collective-permute-done.13.refs_1_, bf16[2,256,256]{2,1,0:T(8,128)(2,1)S(1)} %collective-permute-done.18.refs_2_, ...), custom_call_target="tpu_custom_call" | custom-call | flops 1 | bytes 1 | tf_op jit(solution)/shard_map/encode/pallas_call | solution.py:31
  70.3 4.0 %decode.1 = (bf16[128,1024]{1,0:T(8,128)(2,1)S(1)}, bf16[128,1024]{1,0:T(8,128)(2,1)S(1)}, bf16[256,1024]{1,0:T(8,128)(2,1)S(1)}, bf16[256,1024]{1,0:T(8,128)(2,...) custom-call(s32[50]{0:T(128)S(1)} %table.1, ...), custom_call_target="tpu_custom_call" | custom-call | flops 1 | bytes 1 | tf_op jit(solution)/shard_map/decode/pallas_call | solution.py:31
  75.6 1.3 collective-permute-start.23
  77.7 6.2 %collective-permute-start.31 = (bf16[256,1024]{1,0:T(8,128)(2,1)S(1)}, bf16[256,1024]{1,0:T(8,128)(2,1)S(1)}, u32[]{:S(2)}, u32[]{:S(2)}) collective-permute-start(bf16[256,1024]{1,0:T(8,128)(2,1)S(1)} %sum.1), channel_id=1, source_target_pairs={{0,2},{1,3},{6,4},{7,5},{8,10},{9,11},{14,12},{15,13},{16,18},{17,... | collective-permute-start | bytes 1572872 | tf_op jit(solution)/shard_map/ppermute | solution.py:318
  84.5 6.9 %collective-permute-done.23 = bf16[4,256,256]{2,1,0:T(8,128)(2,1)S(1)} collective-permute-done((bf16[4,256,256]{2,1,0:T(8,128)(2,1)S(1)}, bf16[4,256,256]{2,1,0:T(8,128)(2,1)S(1)}, u32[]{:S(2)}, u32[]{:S(2)}) %collective-permute-start.23) | collective-permute-done | bytes 524320 | tf_op jit(solution)/shard_map/ppermute | solution.py:318
  92.1 3.6 %collective-permute-done.31 = bf16[256,1024]{1,0:T(8,128)(2,1)S(1)} collective-permute-done((bf16[256,1024]{1,0:T(8,128)(2,1)S(1)}, bf16[256,1024]{1,0:T(8,128)(2,1)S(1)}, u32[]{:S(2)}, u32[]{:S(2)}) %collective-permute-start.31) | collective-permute-done | bytes 524320 | tf_op jit(solution)/shard_map/ppermute | solution.py:318
  95.7 1.3 collective-permute-start.25
  98.1 5.2 %collective-permute-start.32 = (bf16[256,1024]{1,0:T(8,128)(2,1)S(1)}, bf16[256,1024]{1,0:T(8,128)(2,1)S(1)}, u32[]{:S(2)}, u32[]{:S(2)}) collective-permute-start(bf16[256,1024]{1,0:T(8,128)(2,1)S(1)} %add_convert_fusion), channel_id=1, source_target_pairs={{0,2},{1,3},{2,4},{3,5},{8,10},{9,11},{10,12},{11,13},{16,18},{17,... | collective-permute-start | bytes 1572872 | tf_op jit(solution)/shard_map/ppermute | solution.py:318
  103.6 7.7 %collective-permute-done.25.refs_2_ = bf16[4,256,256]{2,1,0:T(8,128)(2,1)S(1)} collective-permute-done((bf16[4,256,256]{2,1,0:T(8,128)(2,1)S(1)}, bf16[4,256,256]{2,1,0:T(8,128)(2,1)S(1)}, u32[]{:S(2)}, u32[]{:S(2)}) %collective-permute-start.25) | collective-permute-done | bytes 524320 | tf_op jit(solution)/shard_map/ppermute | solution.py:318
  111.5 3.6 %project.2 = (f32[256,640]{1,0:T(8,128)S(1)}, f32[256,1]{1,0:T(8,128)S(1)}) custom-call(s32[50]{0:T(128)S(1)} %table.1, bf16[4,256,256]{2,1,0:T(8,128)(2,1)S(1)} %pad_maximum_fusion.refs_0_, bf16[4,256,256]{2,1,0:T(8,128)(2,1)S(1)} %collective-permute-done.34.refs_1_, bf16[4,256,256]{2,1,0:T(8,128)(2,1)S(1)} %collective-permute-done.16.refs_2_, ...), custom_call_target="tpu_custom_call" | custom-call | flops 2013265920 | bytes 4194304 | tf_op jit(solution)/shard_map/project/pallas_call | solution.py:31
  116.1 4.5 %collective-permute-start.38 = (bf16[256,1024]{1,0:T(8,128)(2,1)S(1)}, bf16[256,1024]{1,0:T(8,128)(2,1)S(1)}, u32[]{:S(2)}, u32[]{:S(2)}) collective-permute-start(bf16[256,1024]{1,0:T(8,128)(2,1)S(1)} %get-tuple-element.84), channel_id=1, source_target_pairs={{0,2},{1,3},{2,4},{3,5},{4,6},{5,7},{8,10},{9,11},{10,12},{11,13},... | collective-permute-start | bytes 1572872 | tf_op jit(solution)/shard_map/ppermute | solution.py:318
  120.6 1.3 collective-permute-start.39
  122.0 3.9 %project.3 = (f32[256,640]{1,0:T(8,128)}, f32[8,256]{1,0:T(8,128)S(1)}) custom-call(s32[50]{0:T(128)S(1)} %table.1, bf16[4,256,256]{2,1,0:T(8,128)(2,1)S(1)} %add.47.refs_0_, bf16[4,256,256]{2,1,0:T(8,128)(2,1)S(1)} %collective-permute-done.24.refs_1_, bf16[4,256,256]{2,1,0:T(8,128)(2,1)S(1)} %collective-permute-done.25.refs_2_, ...), custom_call_target="tpu_custom_call" | custom-call | flops 1 | bytes 1 | tf_op jit(solution)/shard_map/project/pallas_call | solution.py:31
  127.0 4.5 %collective-permute-start.43 = (f32[1,256]{1,0:T(1,128)S(1)}, f32[1,256]{1,0:T(1,128)S(1)}, u32[]{:S(2)}, u32[]{:S(2)}) collective-permute-start(f32[1,256]{1,0:T(1,128)S(1)} %slice_add_fusion), channel_id=1, source_target_pairs={{0,6},{1,7},{2,4},{3,5},{4,2},{5,3},{6,0},{7,1},{8,14},{9,15},{10,... | collective-permute-start | bytes 3080 | tf_op jit(solution)/shard_map/ppermute | solution.py:318
  132.0 4.5 %collective-permute-done.39 = bf16[256,1024]{1,0:T(8,128)(2,1)S(1)} collective-permute-done((bf16[256,1024]{1,0:T(8,128)(2,1)S(1)}, bf16[256,1024]{1,0:T(8,128)(2,1)S(1)}, u32[]{:S(2)}, u32[]{:S(2)}) %collective-permute-start.39) | collective-permute-done | bytes 524320 | tf_op jit(solution)/shard_map/ppermute | solution.py:318
  (90 shorter events, 20.3 us)
Async XLA Ops:
  1.8 6.9 %collective-permute-start.3 = (bf16[256,256]{1,0:T(8,128)(2,1)S(1)}, bf16[256,256]{1,0:T(8,128)(2,1)S(1)}, u32[]{:S(2)}, u32[]{:S(2)}) collective-permute-start(bf16[256,256]{1,0:T(8,128)(2,1)S(1)} %get-tuple-element.90), channel_id=1, source_target_pairs={{0,8},{8,0},{16,24},{24,16},{1,9},{9,1},{17,25},{25,17},{2,10},{10... | collective-permute-start | bytes 393224 | tf_op jit(solution)/shard_map/ppermute | solution.py:326
  4.8 8.0 %collective-permute-start.7 = (bf16[256,256]{1,0:T(8,128)(2,1)S(1)}, bf16[256,256]{1,0:T(8,128)(2,1)S(1)}, u32[]{:S(2)}, u32[]{:S(2)}) collective-permute-start(bf16[256,256]{1,0:T(8,128)(2,1)S(1)} %get-tuple-element.89), channel_id=1, source_target_pairs={{0,16},{8,24},{16,0},{24,8},{1,17},{9,25},{17,1},{25,9},{2,18},{10... | collective-permute-start | bytes 393224 | tf_op jit(solution)/shard_map/ppermute | solution.py:326
  8.7 10.2 %collective-permute-start.5 = (bf16[2,256,256]{2,1,0:T(8,128)(2,1)S(1)}, bf16[2,256,256]{2,1,0:T(8,128)(2,1)S(1)}, u32[]{:S(2)}, u32[]{:S(2)}) collective-permute-start(bf16[2,256,256]{2,1,0:T(8,128)(2,1)S(1)} %pad_maximum_fusion.1.refs_0_), channel_id=1, source_target_pairs={{0,1},{1,0},{2,3},{3,2},{4,5},{5,4},{6,7},{7,6},{8,9},{9,8},{10,11... | collective-permute-start | bytes 786440 | tf_op jit(solution)/shard_map/ppermute | solution.py:321
  10.9 12.8 %collective-permute-start.4 = (bf16[2,256,256]{2,1,0:T(8,128)(2,1)S(1)}, bf16[2,256,256]{2,1,0:T(8,128)(2,1)S(1)}, u32[]{:S(2)}, u32[]{:S(2)}) collective-permute-start(bf16[2,256,256]{2,1,0:T(8,128)(2,1)S(1)} %pad_maximum_fusion.1.refs_0_), channel_id=1, source_target_pairs={{0,2},{1,3},{2,4},{3,5},{4,6},{5,7},{6,0},{7,1},{8,10},{9,11},{10,... | collective-permute-start | bytes 786440 | tf_op jit(solution)/shard_map/ppermute | solution.py:318
  12.8 14.6 %collective-permute-start.12 = (bf16[2,256,256]{2,1,0:T(8,128)(2,1)S(1)}, bf16[2,256,256]{2,1,0:T(8,128)(2,1)S(1)}, u32[]{:S(2)}, u32[]{:S(2)}) collective-permute-start(bf16[2,256,256]{2,1,0:T(8,128)(2,1)S(1)} %pad_maximum_fusion.2.refs_1_), channel_id=1, source_target_pairs={{0,2},{1,3},{2,4},{3,5},{4,6},{5,7},{6,0},{7,1},{8,10},{9,11},{10,... | collective-permute-start | bytes 786440 | tf_op jit(solution)/shard_map/ppermute | solution.py:318
  15.6 8.3 %collective-permute-start = (bf16[256,256]{1,0:T(8,128)(2,1)S(1)}, bf16[256,256]{1,0:T(8,128)(2,1)S(1)}, u32[]{:S(2)}, u32[]{:S(2)}) collective-permute-start(bf16[256,256]{1,0:T(8,128)(2,1)S(1)} %get-tuple-element.94), channel_id=1, source_target_pairs={{0,8},{8,0},{16,24},{24,16},{1,9},{9,1},{17,25},{25,17},{2,10},{10... | collective-permute-start | bytes 393224 | tf_op jit(solution)/shard_map/ppermute | solution.py:326
  17.9 7.5 %collective-permute-start.2 = (bf16[256,256]{1,0:T(8,128)(2,1)S(1)}, bf16[256,256]{1,0:T(8,128)(2,1)S(1)}, u32[]{:S(2)}, u32[]{:S(2)}) collective-permute-start(bf16[256,256]{1,0:T(8,128)(2,1)S(1)} %get-tuple-element.95), channel_id=1, source_target_pairs={{0,24},{8,16},{16,8},{24,0},{1,25},{9,17},{17,9},{25,1},{2,26},{10... | collective-permute-start | bytes 393224 | tf_op jit(solution)/shard_map/ppermute | solution.py:326
  18.9 7.9 %collective-permute-start.1 = (bf16[256,256]{1,0:T(8,128)(2,1)S(1)}, bf16[256,256]{1,0:T(8,128)(2,1)S(1)}, u32[]{:S(2)}, u32[]{:S(2)}) collective-permute-start(bf16[256,256]{1,0:T(8,128)(2,1)S(1)} %get-tuple-element.96), channel_id=1, source_target_pairs={{0,16},{8,24},{16,0},{24,8},{1,17},{9,25},{17,1},{25,9},{2,18},{10... | collective-permute-start | bytes 393224 | tf_op jit(solution)/shard_map/ppermute | solution.py:326
  27.4 10.9 %collective-permute-start.13 = (bf16[2,256,256]{2,1,0:T(8,128)(2,1)S(1)}, bf16[2,256,256]{2,1,0:T(8,128)(2,1)S(1)}, u32[]{:S(2)}, u32[]{:S(2)}) collective-permute-start(bf16[2,256,256]{2,1,0:T(8,128)(2,1)S(1)} %collective-permute-done.12.refs_5_), channel_id=1, source_target_pairs={{0,2},{1,3},{2,4},{3,5},{4,6},{5,7},{6,0},{7,1},{8,10},{9,11},{10,... | collective-permute-start | bytes 786440 | tf_op jit(solution)/shard_map/ppermute | solution.py:318
  28.6 14.9 %collective-permute-start.6 = (bf16[2,256,256]{2,1,0:T(8,128)(2,1)S(1)}, bf16[2,256,256]{2,1,0:T(8,128)(2,1)S(1)}, u32[]{:S(2)}, u32[]{:S(2)}) collective-permute-start(bf16[2,256,256]{2,1,0:T(8,128)(2,1)S(1)} %collective-permute-done.4.refs_4_), channel_id=1, source_target_pairs={{0,2},{1,3},{2,4},{3,5},{4,6},{5,7},{6,0},{7,1},{8,10},{9,11},{10,... | collective-permute-start | bytes 786440 | tf_op jit(solution)/shard_map/ppermute | solution.py:318
  43.5 11.0 %collective-permute-start.11 = (bf16[2,256,256]{2,1,0:T(8,128)(2,1)S(1)}, bf16[2,256,256]{2,1,0:T(8,128)(2,1)S(1)}, u32[]{:S(2)}, u32[]{:S(2)}) collective-permute-start(bf16[2,256,256]{2,1,0:T(8,128)(2,1)S(1)} %collective-permute-done.6.refs_0_), channel_id=1, source_target_pairs={{0,2},{1,3},{2,4},{3,5},{4,6},{5,7},{6,0},{7,1},{8,10},{9,11},{10,... | collective-permute-start | bytes 786440 | tf_op jit(solution)/shard_map/ppermute | solution.py:318
  43.5 15.3 %collective-permute-start.15 = (bf16[2,256,256]{2,1,0:T(8,128)(2,1)S(1)}, bf16[2,256,256]{2,1,0:T(8,128)(2,1)S(1)}, u32[]{:S(2)}, u32[]{:S(2)}) collective-permute-start(bf16[2,256,256]{2,1,0:T(8,128)(2,1)S(1)} %collective-permute-done.13.refs_1_), channel_id=1, source_target_pairs={{0,2},{1,3},{2,4},{3,5},{4,6},{5,7},{6,0},{7,1},{8,10},{9,11},{10,... | collective-permute-start | bytes 786440 | tf_op jit(solution)/shard_map/ppermute | solution.py:318
  43.5 21.8 %collective-permute-start.19 = (bf16[2,256,256]{2,1,0:T(8,128)(2,1)S(1)}, bf16[2,256,256]{2,1,0:T(8,128)(2,1)S(1)}, u32[]{:S(2)}, u32[]{:S(2)}) collective-permute-start(bf16[2,256,256]{2,1,0:T(8,128)(2,1)S(1)} %collective-permute-done.13.refs_1_), channel_id=1, source_target_pairs={{0,1},{1,0},{2,3},{3,2},{4,5},{5,4},{6,7},{7,6},{8,9},{9,8},{10,11... | collective-permute-start | bytes 786440 | tf_op jit(solution)/shard_map/ppermute | solution.py:321
  58.9 16.0 %collective-permute-start.17 = (bf16[4,256,256]{2,1,0:T(8,128)(2,1)S(1)}, bf16[4,256,256]{2,1,0:T(8,128)(2,1)S(1)}, u32[]{:S(2)}, u32[]{:S(2)}) collective-permute-start(bf16[4,256,256]{2,1,0:T(8,128)(2,1)S(1)} %pad_maximum_fusion.refs_0_), channel_id=1, source_target_pairs={{2,0},{3,1},{4,2},{5,3},{6,4},{7,5},{10,8},{11,9},{12,10},{13,11},... | collective-permute-start | bytes 1572872 | tf_op jit(solution)/shard_map/ppermute | solution.py:318
  60.1 14.7 %collective-permute-start.16 = (bf16[4,256,256]{2,1,0:T(8,128)(2,1)S(1)}, bf16[4,256,256]{2,1,0:T(8,128)(2,1)S(1)}, u32[]{:S(2)}, u32[]{:S(2)}) collective-permute-start(bf16[4,256,256]{2,1,0:T(8,128)(2,1)S(1)} %pad_maximum_fusion.refs_0_), channel_id=1, source_target_pairs={{0,2},{1,3},{2,4},{3,5},{4,6},{5,7},{8,10},{9,11},{10,12},{11,13},... | collective-permute-start | bytes 1572872 | tf_op jit(solution)/shard_map/ppermute | solution.py:318
  74.9 9.3 %collective-permute-start.22 = (bf16[4,256,256]{2,1,0:T(8,128)(2,1)S(1)}, bf16[4,256,256]{2,1,0:T(8,128)(2,1)S(1)}, u32[]{:S(2)}, u32[]{:S(2)}) collective-permute-start(bf16[4,256,256]{2,1,0:T(8,128)(2,1)S(1)} %collective-permute-done.16.refs_2_), channel_id=1, source_target_pairs={{2,4},{3,5},{4,6},{5,7},{10,12},{11,13},{12,14},{13,15},{18,20},{1... | collective-permute-start | bytes 1572872 | tf_op jit(solution)/shard_map/ppermute | solution.py:318
  75.6 15.8 %collective-permute-start.23 = (bf16[4,256,256]{2,1,0:T(8,128)(2,1)S(1)}, bf16[4,256,256]{2,1,0:T(8,128)(2,1)S(1)}, u32[]{:S(2)}, u32[]{:S(2)}) collective-permute-start(bf16[4,256,256]{2,1,0:T(8,128)(2,1)S(1)} %collective-permute-done.17.refs_4_), channel_id=1, source_target_pairs={{2,0},{3,1},{4,2},{5,3},{10,8},{11,9},{12,10},{13,11},{18,16},{19,... | collective-permute-start | bytes 1572872 | tf_op jit(solution)/shard_map/ppermute | solution.py:318
  77.6 14.0 %collective-permute-start.30 = (bf16[256,1024]{1,0:T(8,128)(2,1)S(1)}, bf16[256,1024]{1,0:T(8,128)(2,1)S(1)}, u32[]{:S(2)}, u32[]{:S(2)}) collective-permute-start(bf16[256,1024]{1,0:T(8,128)(2,1)S(1)} %get-tuple-element.75), channel_id=1, source_target_pairs={{0,1},{1,0},{2,3},{3,2},{4,5},{5,4},{6,7},{7,6},{8,9},{9,8},{10,11... | collective-permute-start | bytes 1572872 | tf_op jit(solution)/shard_map/ppermute | solution.py:321
  77.7 18.0 %collective-permute-start.31 = (bf16[256,1024]{1,0:T(8,128)(2,1)S(1)}, bf16[256,1024]{1,0:T(8,128)(2,1)S(1)}, u32[]{:S(2)}, u32[]{:S(2)}) collective-permute-start(bf16[256,1024]{1,0:T(8,128)(2,1)S(1)} %sum.1), channel_id=1, source_target_pairs={{0,2},{1,3},{6,4},{7,5},{8,10},{9,11},{14,12},{15,13},{16,18},{17,... | collective-permute-start | bytes 1572872 | tf_op jit(solution)/shard_map/ppermute | solution.py:318
  83.9 13.3 %collective-permute-start.34 = (bf16[4,256,256]{2,1,0:T(8,128)(2,1)S(1)}, bf16[4,256,256]{2,1,0:T(8,128)(2,1)S(1)}, u32[]{:S(2)}, u32[]{:S(2)}) collective-permute-start(bf16[4,256,256]{2,1,0:T(8,128)(2,1)S(1)} %pad_maximum_fusion.refs_0_), channel_id=1, source_target_pairs={{0,1},{1,0},{2,3},{3,2},{4,5},{5,4},{6,7},{7,6},{8,9},{9,8},{10,11... | collective-permute-start | bytes 1572872 | tf_op jit(solution)/shard_map/ppermute | solution.py:321
  84.2 13.2 %collective-permute-start.37 = (bf16[256,1024]{1,0:T(8,128)(2,1)S(1)}, bf16[256,1024]{1,0:T(8,128)(2,1)S(1)}, u32[]{:S(2)}, u32[]{:S(2)}) collective-permute-start(bf16[256,1024]{1,0:T(8,128)(2,1)S(1)} %get-tuple-element.83), channel_id=1, source_target_pairs={{0,1},{1,0},{2,3},{3,2},{4,5},{5,4},{6,7},{7,6},{8,9},{9,8},{10,11... | collective-permute-start | bytes 1572872 | tf_op jit(solution)/shard_map/ppermute | solution.py:321
  91.4 6.7 %collective-permute-start.35 = (bf16[4,256,256]{2,1,0:T(8,128)(2,1)S(1)}, bf16[4,256,256]{2,1,0:T(8,128)(2,1)S(1)}, u32[]{:S(2)}, u32[]{:S(2)}) collective-permute-start(bf16[4,256,256]{2,1,0:T(8,128)(2,1)S(1)} %collective-permute-done.16.refs_2_), channel_id=1, source_target_pairs={{0,1},{1,0},{2,3},{3,2},{4,5},{5,4},{6,7},{7,6},{8,9},{9,8},{10,11... | collective-permute-start | bytes 1572872 | tf_op jit(solution)/shard_map/ppermute | solution.py:321
  91.6 11.7 %collective-permute-start.36 = (bf16[4,256,256]{2,1,0:T(8,128)(2,1)S(1)}, bf16[4,256,256]{2,1,0:T(8,128)(2,1)S(1)}, u32[]{:S(2)}, u32[]{:S(2)}) collective-permute-start(bf16[4,256,256]{2,1,0:T(8,128)(2,1)S(1)} %collective-permute-done.17.refs_4_), channel_id=1, source_target_pairs={{0,1},{1,0},{2,3},{3,2},{4,5},{5,4},{6,7},{7,6},{8,9},{9,8},{10,11... | collective-permute-start | bytes 1572872 | tf_op jit(solution)/shard_map/ppermute | solution.py:321
  95.7 15.5 %collective-permute-start.25 = (bf16[4,256,256]{2,1,0:T(8,128)(2,1)S(1)}, bf16[4,256,256]{2,1,0:T(8,128)(2,1)S(1)}, u32[]{:S(2)}, u32[]{:S(2)}) collective-permute-start(bf16[4,256,256]{2,1,0:T(8,128)(2,1)S(1)} %add.47.refs_0_), channel_id=1, source_target_pairs={{4,6},{5,7},{2,0},{3,1},{12,14},{13,15},{10,8},{11,9},{20,22},{21,... | collective-permute-start | bytes 1572872 | tf_op jit(solution)/shard_map/ppermute | solution.py:318
  97.3 17.9 %collective-permute-start.29 = (bf16[256,1024]{1,0:T(8,128)(2,1)S(1)}, bf16[256,1024]{1,0:T(8,128)(2,1)S(1)}, u32[]{:S(2)}, u32[]{:S(2)}) collective-permute-start(bf16[256,1024]{1,0:T(8,128)(2,1)S(1)} %get-tuple-element.73), channel_id=1, source_target_pairs={{0,1},{1,0},{2,3},{3,2},{4,5},{5,4},{6,7},{7,6},{8,9},{9,8},{10,11... | collective-permute-start | bytes 1572872 | tf_op jit(solution)/shard_map/ppermute | solution.py:321
  97.4 17.8 %collective-permute-start.33 = (bf16[256,1024]{1,0:T(8,128)(2,1)S(1)}, bf16[256,1024]{1,0:T(8,128)(2,1)S(1)}, u32[]{:S(2)}, u32[]{:S(2)}) collective-permute-start(bf16[256,1024]{1,0:T(8,128)(2,1)S(1)} %add_convert_fusion), channel_id=1, source_target_pairs={{4,2},{5,3},{6,4},{7,5},{12,10},{13,11},{14,12},{15,13},{20,18},{2... | collective-permute-start | bytes 1572872 | tf_op jit(solution)/shard_map/ppermute | solution.py:318
  98.1 17.1 %collective-permute-start.32 = (bf16[256,1024]{1,0:T(8,128)(2,1)S(1)}, bf16[256,1024]{1,0:T(8,128)(2,1)S(1)}, u32[]{:S(2)}, u32[]{:S(2)}) collective-permute-start(bf16[256,1024]{1,0:T(8,128)(2,1)S(1)} %add_convert_fusion), channel_id=1, source_target_pairs={{0,2},{1,3},{2,4},{3,5},{8,10},{9,11},{10,12},{11,13},{16,18},{17,... | collective-permute-start | bytes 1572872 | tf_op jit(solution)/shard_map/ppermute | solution.py:318
  103.3 18.6 %collective-permute-start.24 = (bf16[4,256,256]{2,1,0:T(8,128)(2,1)S(1)}, bf16[4,256,256]{2,1,0:T(8,128)(2,1)S(1)}, u32[]{:S(2)}, u32[]{:S(2)}) collective-permute-start(bf16[4,256,256]{2,1,0:T(8,128)(2,1)S(1)} %add.47.refs_0_), channel_id=1, source_target_pairs={{0,1},{1,0},{2,3},{3,2},{4,5},{5,4},{6,7},{7,6},{8,9},{9,8},{10,11... | collective-permute-start | bytes 1572872 | tf_op jit(solution)/shard_map/ppermute | solution.py:321
  111.3 10.7 %collective-permute-start.26 = (bf16[4,256,256]{2,1,0:T(8,128)(2,1)S(1)}, bf16[4,256,256]{2,1,0:T(8,128)(2,1)S(1)}, u32[]{:S(2)}, u32[]{:S(2)}) collective-permute-start(bf16[4,256,256]{2,1,0:T(8,128)(2,1)S(1)} %collective-permute-done.25.refs_2_), channel_id=1, source_target_pairs={{0,1},{1,0},{2,3},{3,2},{4,5},{5,4},{6,7},{7,6},{8,9},{9,8},{10,11... | collective-permute-start | bytes 1572872 | tf_op jit(solution)/shard_map/ppermute | solution.py:321
  116.1 15.9 %collective-permute-start.38 = (bf16[256,1024]{1,0:T(8,128)(2,1)S(1)}, bf16[256,1024]{1,0:T(8,128)(2,1)S(1)}, u32[]{:S(2)}, u32[]{:S(2)}) collective-permute-start(bf16[256,1024]{1,0:T(8,128)(2,1)S(1)} %get-tuple-element.84), channel_id=1, source_target_pairs={{0,2},{1,3},{2,4},{3,5},{4,6},{5,7},{8,10},{9,11},{10,12},{11,13},... | collective-permute-start | bytes 1572872 | tf_op jit(solution)/shard_map/ppermute | solution.py:318
  120.6 15.9 %collective-permute-start.39 = (bf16[256,1024]{1,0:T(8,128)(2,1)S(1)}, bf16[256,1024]{1,0:T(8,128)(2,1)S(1)}, u32[]{:S(2)}, u32[]{:S(2)}) collective-permute-start(bf16[256,1024]{1,0:T(8,128)(2,1)S(1)} %get-tuple-element.85), channel_id=1, source_target_pairs={{2,0},{3,1},{4,2},{5,3},{6,4},{7,5},{10,8},{11,9},{12,10},{13,11},... | collective-permute-start | bytes 1572872 | tf_op jit(solution)/shard_map/ppermute | solution.py:318
  127.0 10.8 %collective-permute-start.43 = (f32[1,256]{1,0:T(1,128)S(1)}, f32[1,256]{1,0:T(1,128)S(1)}, u32[]{:S(2)}, u32[]{:S(2)}) collective-permute-start(f32[1,256]{1,0:T(1,128)S(1)} %slice_add_fusion), channel_id=1, source_target_pairs={{0,6},{1,7},{2,4},{3,5},{4,2},{5,3},{6,0},{7,1},{8,14},{9,15},{10,... | collective-permute-start | bytes 3080 | tf_op jit(solution)/shard_map/ppermute | solution.py:318
  (17 other events, 125.5 us)

commit v11 on v8

--- a/solution.py
+++ b/solution.py
@@ -333,26 +333,28 @@
     ring = [(a, (a + 1) % chips) for a in range(chips)]
     cut_x = [lax.dynamic_slice_in_dim(resid, (i ^ s) * rows, rows, 0) for s in range(n_tok)]
     near_x = [exchange(cut_x, X_STREAMS)]
+    cut_g = [lax.dynamic_slice_in_dim(resid_grad, (i ^ s) * rows, rows, 0) for s in range(n_tok)]
+    shard_g, = exchange(cut_g, ((0, 1, 2, 3),))
     far_x = [[cross(a) for a in near_x[0]]]
     for k in range(1, chips):
         first, second = near_x[-1]
         if k == 1:
             second = after(second, table)
         if k == 2:
+            second = after(second, shard_g)
             w_out, far_x[0][0] = load(w_dec, far_x[0][0], 44)
             first = after(first, far_x[0][0])
         if k == 3:
             far_x[0][1] = after(far_x[0][1], far_x[1][0])
             w_in, far_x[0][1] = load(w_enc.reshape(n_tok * n_feat, width, feats), far_x[0][1], 36)
             first = after(first, far_x[0][1])
-            shard_g, = exchange(pick(table, after(resid_grad, first), n_tok), ((0, 1, 2, 3),))
         near_x[-1] = [first, second]
         if k > 1:
             far_x.append([cross(a) for a in near_x[-1]])
         near_x.append([send(first, ring), send(second, ring)])
     slots = [near_x[0], far_x[0], near_x[1], far_x[1]]
     carry = encode(
-        after(table, shard_g), SLOTS["enc_a"], slots, w_in, bias, None, X_STREAMS, False, n_feat
+        after(table, near_x[3][0]), SLOTS["enc_a"], slots, w_in, bias, None, X_STREAMS, False, n_feat
     )
     far_x.append([cross(near_x[3][0]), cross(after(near_x[3][1], carry))])
 

time: 133 us -> 132 us (level)
  waiting for transfers between devices: 50.1 us -> 48.1 us
  starting transfers between devices: 45.9 us -> 47.8 us
    ppermute x6, waiting for transfers between devices: 7.6 us -> 4.21 us  [exchange(): lax.ppermute(blocks[s], 'tok', [(a, a ^ s) for a in range(n_tok)])]
    ppermute x19, starting transfers between devices: 34.4 us -> 36.3 us  [send(): return lax.ppermute(array, 'feat', along(pairs))]
    ppermute x19, waiting for transfers between devices: 39.7 us -> 41 us  [send(): return lax.ppermute(array, 'feat', along(pairs))]
  transfers between devices with their start and end apart: 44 -> 44, of which waited for: 19 -> 17; matrix products, arithmetic and copies ran while one was open for 2% -> 2% of each run, Pallas kernels for 23% -> 22%
where the time goes in v11:
time: 132 us; the launch traced here: 131 us
  waiting for transfers between devices  48.1 us (36%)
  starting transfers between devices  47.8 us (36%)
  Pallas kernels  28.8 us (22%)
  local copies, waits for them, and re-layouts  2.97 us (2%)
  other arithmetic  2.65 us (2%)
    ppermute x19, waiting for transfers between devices, send(): return lax.ppermute(array, 'feat', along(pairs))  41 us
    ppermute x19, starting transfers between devices, send(): return lax.ppermute(array, 'feat', along(pairs))  36.3 us
    pallas_call x7, Pallas kernels, kernel_call(): pl.pallas_call(body, in_specs=[SMEM] + [VMEM] * (len(args) - 1), out_spec...  19.3 us
    pallas_call x2, Pallas kernels, load(): pl.pallas_call(load_body, in_specs=[anywhere, anywhere], out_specs=[VMEM,...  8.17 us
    ppermute x6, starting transfers between devices, exchange(): lax.ppermute(blocks[s], 'tok', [(a, a ^ s) for a in range(n_tok)])  8.1 us
    ppermute x6, waiting for transfers between devices, exchange(): lax.ppermute(blocks[s], 'tok', [(a, a ^ s) for a in range(n_tok)])  4.21 us
    ppermute x19, starting transfers between devices, cross(): return lax.ppermute(array, 'feat', [(a, a ^ 1) for a in range(n_feat)])  3.42 us
    ppermute x19, waiting for transfers between devices, cross(): return lax.ppermute(array, 'feat', [(a, a ^ 1) for a in range(n_feat)])  2.87 us
  transfers between devices with their start and end apart: 44, of which 17 were waited for; matrix products, arithmetic and copies ran while one was open for 2% of the time, Pallas kernels for 22%

profile of v11, /device:TPU:0, one launch (start us, length us, event | category | flops | bytes accessed | tf_op | source)
XLA Modules:
  0.0 131.4 jit_solution(751655997715325517)
XLA Ops:
  1.8 3.0 %collective-permute-start.3 = (bf16[256,256]{1,0:T(8,128)(2,1)S(1)}, bf16[256,256]{1,0:T(8,128)(2,1)S(1)}, u32[]{:S(2)}, u32[]{:S(2)}) collective-permute-start(bf16[256,256]{1,0:T(8,128)(2,1)S(1)} %get-tuple-element.90), channel_id=1, source_target_pairs={{0,8},{8,0},{16,24},{24,16},{1,9},{9,1},{17,25},{25,17},{2,10},{10... | collective-permute-start | bytes 393224 | tf_op jit(solution)/shard_map/ppermute | solution.py:326
  4.8 1.5 %collective-permute-start.8 = (bf16[256,256]{1,0:T(8,128)(2,1)S(1)}, bf16[256,256]{1,0:T(8,128)(2,1)S(1)}, u32[]{:S(2)}, u32[]{:S(2)}) collective-permute-start(bf16[256,256]{1,0:T(8,128)(2,1)S(1)} %get-tuple-element.92), channel_id=1, source_target_pairs={{0,24},{8,16},{16,8},{24,0},{1,25},{9,17},{17,9},{25,1},{2,26},{10... | collective-permute-start | bytes 393224 | tf_op jit(solution)/shard_map/ppermute | solution.py:326
  6.3 2.4 %collective-permute-done.3 = bf16[256,256]{1,0:T(8,128)(2,1)S(1)} collective-permute-done((bf16[256,256]{1,0:T(8,128)(2,1)S(1)}, bf16[256,256]{1,0:T(8,128)(2,1)S(1)}, u32[]{:S(2)}, u32[]{:S(2)}) %collective-permute-start.3) | collective-permute-done | bytes 131104 | tf_op jit(solution)/shard_map/ppermute | solution.py:326
  9.6 1.3 %table.1 = s32[50]{0:T(128)S(1)} custom-call(s32[2]{0:T(128)S(1)} %pad_add_fusion.ids_ref, s32[2,20]{1,0:T(2,128)S(1)} %copy-done.3), custom_call_target="tpu_custom_call" | custom-call | flops 1 | bytes 1 | tf_op jit(solution)/shard_map/table/pallas_call | solution.py:112
  10.9 2.1 %collective-permute-start.4 = (bf16[2,256,256]{2,1,0:T(8,128)(2,1)S(1)}, bf16[2,256,256]{2,1,0:T(8,128)(2,1)S(1)}, u32[]{:S(2)}, u32[]{:S(2)}) collective-permute-start(bf16[2,256,256]{2,1,0:T(8,128)(2,1)S(1)} %pad_maximum_fusion.1.refs_0_), channel_id=1, source_target_pairs={{0,2},{1,3},{2,4},{3,5},{4,6},{5,7},{6,0},{7,1},{8,10},{9,11},{10,... | collective-permute-start | bytes 786440 | tf_op jit(solution)/shard_map/ppermute | solution.py:318
  13.8 1.6 %collective-permute-start.12 = (bf16[2,256,256]{2,1,0:T(8,128)(2,1)S(1)}, bf16[2,256,256]{2,1,0:T(8,128)(2,1)S(1)}, u32[]{:S(2)}, u32[]{:S(2)}) collective-permute-start(bf16[2,256,256]{2,1,0:T(8,128)(2,1)S(1)} %pad_maximum_fusion.2.refs_1_), channel_id=1, source_target_pairs={{0,2},{1,3},{2,4},{3,5},{4,6},{5,7},{6,0},{7,1},{8,10},{9,11},{10,... | collective-permute-start | bytes 786440 | tf_op jit(solution)/shard_map/ppermute | solution.py:318
  16.6 1.6 %collective-permute-start = (bf16[256,256]{1,0:T(8,128)(2,1)S(1)}, bf16[256,256]{1,0:T(8,128)(2,1)S(1)}, u32[]{:S(2)}, u32[]{:S(2)}) collective-permute-start(bf16[256,256]{1,0:T(8,128)(2,1)S(1)} %get-tuple-element.94), channel_id=1, source_target_pairs={{0,8},{8,0},{16,24},{24,16},{1,9},{9,1},{17,25},{25,17},{2,10},{10... | collective-permute-start | bytes 393224 | tf_op jit(solution)/shard_map/ppermute | solution.py:326
  20.1 4.1 %load.2 = (bf16[640,8192]{1,0:T(8,128)(2,1)S(1)}, bf16[2,256,256]{2,1,0:T(8,128)(2,1)}) custom-call(bf16[640,8192]{1,0:T(8,128)(2,1)} %w_ref.1, bf16[2,256,256]{2,1,0:T(8,128)(2,1)} %copy-done), custom_call_target="tpu_custom_call", output_to_operand_aliasing={{1}: (1, {})} | custom-call | bytes 10485760 | tf_op jit(solution)/shard_map/load/pallas_call | solution.py:57
  25.9 1.6 %collective-permute-start.6 = (bf16[2,256,256]{2,1,0:T(8,128)(2,1)S(1)}, bf16[2,256,256]{2,1,0:T(8,128)(2,1)S(1)}, u32[]{:S(2)}, u32[]{:S(2)}) collective-permute-start(bf16[2,256,256]{2,1,0:T(8,128)(2,1)S(1)} %collective-permute-done.4.refs_4_), channel_id=1, source_target_pairs={{0,2},{1,3},{2,4},{3,5},{4,6},{5,7},{6,0},{7,1},{8,10},{9,11},{10,... | collective-permute-start | bytes 786440 | tf_op jit(solution)/shard_map/ppermute | solution.py:318
  28.9 4.1 %load.3 = (bf16[32,256,640]{2,1,0:T(8,128)(2,1)S(1)}, bf16[2,256,256]{2,1,0:T(8,128)(2,1)S(1)}) custom-call(bf16[32,256,640]{2,1,0:T(8,128)(2,1)} %bitcast.17, bf16[2,256,256]{2,1,0:T(8,128)(2,1)S(1)} %collective-permute-done.9.through_ref), custom_call_target="tpu_custom_call", output_to_operand_aliasing={{1}: (1, {})} | custom-call | bytes 10485760 | tf_op jit(solution)/shard_map/load/pallas_call | solution.py:57
  32.9 4.0 %collective-permute-done.6.refs_0_ = bf16[2,256,256]{2,1,0:T(8,128)(2,1)S(1)} collective-permute-done((bf16[2,256,256]{2,1,0:T(8,128)(2,1)S(1)}, bf16[2,256,256]{2,1,0:T(8,128)(2,1)S(1)}, u32[]{:S(2)}, u32[]{:S(2)}) %collective-permute-start.6) | collective-permute-done | bytes 262176 | tf_op jit(solution)/shard_map/ppermute | solution.py:318
  37.0 5.6 %collective-permute-done.13.refs_1_ = bf16[2,256,256]{2,1,0:T(8,128)(2,1)S(1)} collective-permute-done((bf16[2,256,256]{2,1,0:T(8,128)(2,1)S(1)}, bf16[2,256,256]{2,1,0:T(8,128)(2,1)S(1)}, u32[]{:S(2)}, u32[]{:S(2)}) %collective-permute-start.13) | collective-permute-done | bytes 262176 | tf_op jit(solution)/shard_map/ppermute | solution.py:318
  42.6 5.6 %collective-permute-done.11.refs_4_ = bf16[2,256,256]{2,1,0:T(8,128)(2,1)S(1)} collective-permute-done((bf16[2,256,256]{2,1,0:T(8,128)(2,1)S(1)}, bf16[2,256,256]{2,1,0:T(8,128)(2,1)S(1)}, u32[]{:S(2)}, u32[]{:S(2)}) %collective-permute-start.11) | collective-permute-done | bytes 262176 | tf_op jit(solution)/shard_map/ppermute | solution.py:318
  48.2 3.0 %encode.2 = (f32[256,640]{1,0:T(8,128)S(1)}, bf16[256,1024]{1,0:T(8,128)(2,1)S(1)}) custom-call(s32[50]{0:T(128)S(1)} %table.1, bf16[2,256,256]{2,1,0:T(8,128)(2,1)S(1)} %pad_maximum_fusion.1.refs_0_, bf16[2,256,256]{2,1,0:T(8,128)(2,1)S(1)} %pad_maximum_fusion.2.refs_1_, bf16[2,256,256]{2,1,0:T(8,128)(2,1)S(1)} %copy-done.1, ...), custom_call_target="tpu_custom_call" | custom-call | flops 1342177280 | bytes 4194304 | tf_op jit(solution)/shard_map/encode/pallas_call | solution.py:31
  51.8 1.7 %collective-permute-start.16 = (bf16[4,256,256]{2,1,0:T(8,128)(2,1)S(1)}, bf16[4,256,256]{2,1,0:T(8,128)(2,1)S(1)}, u32[]{:S(2)}, u32[]{:S(2)}) collective-permute-start(bf16[4,256,256]{2,1,0:T(8,128)(2,1)S(1)} %pad_maximum_fusion.refs_0_), channel_id=1, source_target_pairs={{0,2},{1,3},{2,4},{3,5},{4,6},{5,7},{8,10},{9,11},{10,12},{11,13},... | collective-permute-start | bytes 1572872 | tf_op jit(solution)/shard_map/ppermute | solution.py:318
  53.5 1.3 collective-permute-start.17
  57.1 3.2 %encode.3 = (bf16[256,640]{1,0:T(8,128)(2,1)S(1)}, bf16[256,1024]{1,0:T(8,128)(2,1)S(1)}) custom-call(s32[50]{0:T(128)S(1)} %table.1, bf16[2,256,256]{2,1,0:T(8,128)(2,1)S(1)} %collective-permute-done.6.refs_0_, bf16[2,256,256]{2,1,0:T(8,128)(2,1)S(1)} %collective-permute-done.13.refs_1_, bf16[2,256,256]{2,1,0:T(8,128)(2,1)S(1)} %collective-permute-done.18.refs_2_, ...), custom_call_target="tpu_custom_call" | custom-call | flops 1 | bytes 1 | tf_op jit(solution)/shard_map/encode/pallas_call | solution.py:31
  60.3 4.0 %decode.1 = (bf16[128,1024]{1,0:T(8,128)(2,1)S(1)}, bf16[128,1024]{1,0:T(8,128)(2,1)S(1)}, bf16[256,1024]{1,0:T(8,128)(2,1)S(1)}, bf16[256,1024]{1,0:T(8,128)(2,...) custom-call(s32[50]{0:T(128)S(1)} %table.1, ...), custom_call_target="tpu_custom_call" | custom-call | flops 1 | bytes 1 | tf_op jit(solution)/shard_map/decode/pallas_call | solution.py:31
  64.9 2.3 %collective-permute-done.17.refs_4_ = bf16[4,256,256]{2,1,0:T(8,128)(2,1)S(1)} collective-permute-done((bf16[4,256,256]{2,1,0:T(8,128)(2,1)S(1)}, bf16[4,256,256]{2,1,0:T(8,128)(2,1)S(1)}, u32[]{:S(2)}, u32[]{:S(2)}) %collective-permute-start.17) | collective-permute-done | bytes 524320 | tf_op jit(solution)/shard_map/ppermute | solution.py:318
  67.9 1.3 collective-permute-start.23
  70.0 5.8 %collective-permute-start.31 = (bf16[256,1024]{1,0:T(8,128)(2,1)S(1)}, bf16[256,1024]{1,0:T(8,128)(2,1)S(1)}, u32[]{:S(2)}, u32[]{:S(2)}) collective-permute-start(bf16[256,1024]{1,0:T(8,128)(2,1)S(1)} %sum.1), channel_id=1, source_target_pairs={{0,2},{1,3},{6,4},{7,5},{8,10},{9,11},{14,12},{15,13},{16,18},{17,... | collective-permute-start | bytes 1572872 | tf_op jit(solution)/shard_map/ppermute | solution.py:318
  76.4 8.5 %collective-permute-done.23 = bf16[4,256,256]{2,1,0:T(8,128)(2,1)S(1)} collective-permute-done((bf16[4,256,256]{2,1,0:T(8,128)(2,1)S(1)}, bf16[4,256,256]{2,1,0:T(8,128)(2,1)S(1)}, u32[]{:S(2)}, u32[]{:S(2)}) %collective-permute-start.23) | collective-permute-done | bytes 524320 | tf_op jit(solution)/shard_map/ppermute | solution.py:318
  85.6 2.0 %collective-permute-done.31 = bf16[256,1024]{1,0:T(8,128)(2,1)S(1)} collective-permute-done((bf16[256,1024]{1,0:T(8,128)(2,1)S(1)}, bf16[256,1024]{1,0:T(8,128)(2,1)S(1)}, u32[]{:S(2)}, u32[]{:S(2)}) %collective-permute-start.31) | collective-permute-done | bytes 524320 | tf_op jit(solution)/shard_map/ppermute | solution.py:318
  89.2 4.6 %collective-permute-start.32 = (bf16[256,1024]{1,0:T(8,128)(2,1)S(1)}, bf16[256,1024]{1,0:T(8,128)(2,1)S(1)}, u32[]{:S(2)}, u32[]{:S(2)}) collective-permute-start(bf16[256,1024]{1,0:T(8,128)(2,1)S(1)} %add_convert_fusion), channel_id=1, source_target_pairs={{0,2},{1,3},{2,4},{3,5},{8,10},{9,11},{10,12},{11,13},{16,18},{17,... | collective-permute-start | bytes 1572872 | tf_op jit(solution)/shard_map/ppermute | solution.py:318
  94.8 8.3 %collective-permute-done.25.refs_2_ = bf16[4,256,256]{2,1,0:T(8,128)(2,1)S(1)} collective-permute-done((bf16[4,256,256]{2,1,0:T(8,128)(2,1)S(1)}, bf16[4,256,256]{2,1,0:T(8,128)(2,1)S(1)}, u32[]{:S(2)}, u32[]{:S(2)}) %collective-permute-start.25) | collective-permute-done | bytes 524320 | tf_op jit(solution)/shard_map/ppermute | solution.py:318
  103.4 3.6 %project.2 = (f32[256,640]{1,0:T(8,128)S(1)}, f32[256,1]{1,0:T(8,128)S(1)}) custom-call(s32[50]{0:T(128)S(1)} %table.1, bf16[4,256,256]{2,1,0:T(8,128)(2,1)S(1)} %pad_maximum_fusion.refs_0_, bf16[4,256,256]{2,1,0:T(8,128)(2,1)S(1)} %collective-permute-done.34.refs_1_, bf16[4,256,256]{2,1,0:T(8,128)(2,1)S(1)} %collective-permute-done.16.refs_2_, ...), custom_call_target="tpu_custom_call" | custom-call | flops 2013265920 | bytes 4194304 | tf_op jit(solution)/shard_map/project/pallas_call | solution.py:31
  108.0 6.7 %collective-permute-start.38 = (bf16[256,1024]{1,0:T(8,128)(2,1)S(1)}, bf16[256,1024]{1,0:T(8,128)(2,1)S(1)}, u32[]{:S(2)}, u32[]{:S(2)}) collective-permute-start(bf16[256,1024]{1,0:T(8,128)(2,1)S(1)} %get-tuple-element.84), channel_id=1, source_target_pairs={{0,2},{1,3},{2,4},{3,5},{4,6},{5,7},{8,10},{9,11},{10,12},{11,13},... | collective-permute-start | bytes 1572872 | tf_op jit(solution)/shard_map/ppermute | solution.py:318
  114.7 1.3 collective-permute-start.39
  116.0 3.9 %project.3 = (f32[256,640]{1,0:T(8,128)}, f32[8,256]{1,0:T(8,128)S(1)}) custom-call(s32[50]{0:T(128)S(1)} %table.1, bf16[4,256,256]{2,1,0:T(8,128)(2,1)S(1)} %add.47.refs_0_, bf16[4,256,256]{2,1,0:T(8,128)(2,1)S(1)} %collective-permute-done.24.refs_1_, bf16[4,256,256]{2,1,0:T(8,128)(2,1)S(1)} %collective-permute-done.25.refs_2_, ...), custom_call_target="tpu_custom_call" | custom-call | flops 1 | bytes 1 | tf_op jit(solution)/shard_map/project/pallas_call | solution.py:31
  121.0 1.5 %collective-permute-start.41 = (f32[1,256]{1,0:T(1,128)S(1)}, f32[1,256]{1,0:T(1,128)S(1)}, u32[]{:S(2)}, u32[]{:S(2)}) collective-permute-start(f32[1,256]{1,0:T(1,128)S(1)} %slice_add_fusion), channel_id=1, source_target_pairs={{0,2},{1,3},{2,0},{3,1},{4,6},{5,7},{6,4},{7,5},{8,10},{9,11},{10,... | collective-permute-start | bytes 3080 | tf_op jit(solution)/shard_map/ppermute | solution.py:318
  123.3 2.2 %collective-permute-start.43 = (f32[1,256]{1,0:T(1,128)S(1)}, f32[1,256]{1,0:T(1,128)S(1)}, u32[]{:S(2)}, u32[]{:S(2)}) collective-permute-start(f32[1,256]{1,0:T(1,128)S(1)} %slice_add_fusion), channel_id=1, source_target_pairs={{0,6},{1,7},{2,4},{3,5},{4,2},{5,3},{6,0},{7,1},{8,14},{9,15},{10,... | collective-permute-start | bytes 3080 | tf_op jit(solution)/shard_map/ppermute | solution.py:318
  125.4 4.1 %collective-permute-done.39 = bf16[256,1024]{1,0:T(8,128)(2,1)S(1)} collective-permute-done((bf16[256,1024]{1,0:T(8,128)(2,1)S(1)}, bf16[256,1024]{1,0:T(8,128)(2,1)S(1)}, u32[]{:S(2)}, u32[]{:S(2)}) %collective-permute-start.39) | collective-permute-done | bytes 524320 | tf_op jit(solution)/shard_map/ppermute | solution.py:318
  (90 shorter events, 22.7 us)
Async XLA Ops:
  4.8 8.2 %collective-permute-start.8 = (bf16[256,256]{1,0:T(8,128)(2,1)S(1)}, bf16[256,256]{1,0:T(8,128)(2,1)S(1)}, u32[]{:S(2)}, u32[]{:S(2)}) collective-permute-start(bf16[256,256]{1,0:T(8,128)(2,1)S(1)} %get-tuple-element.92), channel_id=1, source_target_pairs={{0,24},{8,16},{16,8},{24,0},{1,25},{9,17},{17,9},{25,1},{2,26},{10... | collective-permute-start | bytes 393224 | tf_op jit(solution)/shard_map/ppermute | solution.py:326
  8.7 10.7 %collective-permute-start.5 = (bf16[2,256,256]{2,1,0:T(8,128)(2,1)S(1)}, bf16[2,256,256]{2,1,0:T(8,128)(2,1)S(1)}, u32[]{:S(2)}, u32[]{:S(2)}) collective-permute-start(bf16[2,256,256]{2,1,0:T(8,128)(2,1)S(1)} %pad_maximum_fusion.1.refs_0_), channel_id=1, source_target_pairs={{0,1},{1,0},{2,3},{3,2},{4,5},{5,4},{6,7},{7,6},{8,9},{9,8},{10,11... | collective-permute-start | bytes 786440 | tf_op jit(solution)/shard_map/ppermute | solution.py:321
  10.9 13.3 %collective-permute-start.4 = (bf16[2,256,256]{2,1,0:T(8,128)(2,1)S(1)}, bf16[2,256,256]{2,1,0:T(8,128)(2,1)S(1)}, u32[]{:S(2)}, u32[]{:S(2)}) collective-permute-start(bf16[2,256,256]{2,1,0:T(8,128)(2,1)S(1)} %pad_maximum_fusion.1.refs_0_), channel_id=1, source_target_pairs={{0,2},{1,3},{2,4},{3,5},{4,6},{5,7},{6,0},{7,1},{8,10},{9,11},{10,... | collective-permute-start | bytes 786440 | tf_op jit(solution)/shard_map/ppermute | solution.py:318
  13.8 13.8 %collective-permute-start.12 = (bf16[2,256,256]{2,1,0:T(8,128)(2,1)S(1)}, bf16[2,256,256]{2,1,0:T(8,128)(2,1)S(1)}, u32[]{:S(2)}, u32[]{:S(2)}) collective-permute-start(bf16[2,256,256]{2,1,0:T(8,128)(2,1)S(1)} %pad_maximum_fusion.2.refs_1_), channel_id=1, source_target_pairs={{0,2},{1,3},{2,4},{3,5},{4,6},{5,7},{6,0},{7,1},{8,10},{9,11},{10,... | collective-permute-start | bytes 786440 | tf_op jit(solution)/shard_map/ppermute | solution.py:318
  18.1 7.8 %collective-permute-start.1 = (bf16[256,256]{1,0:T(8,128)(2,1)S(1)}, bf16[256,256]{1,0:T(8,128)(2,1)S(1)}, u32[]{:S(2)}, u32[]{:S(2)}) collective-permute-start(bf16[256,256]{1,0:T(8,128)(2,1)S(1)} %get-tuple-element.96), channel_id=1, source_target_pairs={{0,16},{8,24},{16,0},{24,8},{1,17},{9,25},{17,1},{25,9},{2,18},{10... | collective-permute-start | bytes 393224 | tf_op jit(solution)/shard_map/ppermute | solution.py:326
  19.4 8.1 %collective-permute-start.2 = (bf16[256,256]{1,0:T(8,128)(2,1)S(1)}, bf16[256,256]{1,0:T(8,128)(2,1)S(1)}, u32[]{:S(2)}, u32[]{:S(2)}) collective-permute-start(bf16[256,256]{1,0:T(8,128)(2,1)S(1)} %get-tuple-element.95), channel_id=1, source_target_pairs={{0,24},{8,16},{16,8},{24,0},{1,25},{9,17},{17,9},{25,1},{2,26},{10... | collective-permute-start | bytes 393224 | tf_op jit(solution)/shard_map/ppermute | solution.py:326
  25.9 11.0 %collective-permute-start.6 = (bf16[2,256,256]{2,1,0:T(8,128)(2,1)S(1)}, bf16[2,256,256]{2,1,0:T(8,128)(2,1)S(1)}, u32[]{:S(2)}, u32[]{:S(2)}) collective-permute-start(bf16[2,256,256]{2,1,0:T(8,128)(2,1)S(1)} %collective-permute-done.4.refs_4_), channel_id=1, source_target_pairs={{0,2},{1,3},{2,4},{3,5},{4,6},{5,7},{6,0},{7,1},{8,10},{9,11},{10,... | collective-permute-start | bytes 786440 | tf_op jit(solution)/shard_map/ppermute | solution.py:318
  27.6 14.9 %collective-permute-start.13 = (bf16[2,256,256]{2,1,0:T(8,128)(2,1)S(1)}, bf16[2,256,256]{2,1,0:T(8,128)(2,1)S(1)}, u32[]{:S(2)}, u32[]{:S(2)}) collective-permute-start(bf16[2,256,256]{2,1,0:T(8,128)(2,1)S(1)} %collective-permute-done.12.refs_5_), channel_id=1, source_target_pairs={{0,2},{1,3},{2,4},{3,5},{4,6},{5,7},{6,0},{7,1},{8,10},{9,11},{10,... | collective-permute-start | bytes 786440 | tf_op jit(solution)/shard_map/ppermute | solution.py:318
  36.9 11.2 %collective-permute-start.11 = (bf16[2,256,256]{2,1,0:T(8,128)(2,1)S(1)}, bf16[2,256,256]{2,1,0:T(8,128)(2,1)S(1)}, u32[]{:S(2)}, u32[]{:S(2)}) collective-permute-start(bf16[2,256,256]{2,1,0:T(8,128)(2,1)S(1)} %collective-permute-done.6.refs_0_), channel_id=1, source_target_pairs={{0,2},{1,3},{2,4},{3,5},{4,6},{5,7},{6,0},{7,1},{8,10},{9,11},{10,... | collective-permute-start | bytes 786440 | tf_op jit(solution)/shard_map/ppermute | solution.py:318
  36.9 11.2 %collective-permute-start.15 = (bf16[2,256,256]{2,1,0:T(8,128)(2,1)S(1)}, bf16[2,256,256]{2,1,0:T(8,128)(2,1)S(1)}, u32[]{:S(2)}, u32[]{:S(2)}) collective-permute-start(bf16[2,256,256]{2,1,0:T(8,128)(2,1)S(1)} %collective-permute-done.12.refs_5_), channel_id=1, source_target_pairs={{0,1},{1,0},{2,3},{3,2},{4,5},{5,4},{6,7},{7,6},{8,9},{9,8},{10,11... | collective-permute-start | bytes 786440 | tf_op jit(solution)/shard_map/ppermute | solution.py:321
  42.6 9.2 %collective-permute-start.14 = (bf16[2,256,256]{2,1,0:T(8,128)(2,1)S(1)}, bf16[2,256,256]{2,1,0:T(8,128)(2,1)S(1)}, u32[]{:S(2)}, u32[]{:S(2)}) collective-permute-start(bf16[2,256,256]{2,1,0:T(8,128)(2,1)S(1)} %collective-permute-done.13.refs_1_), channel_id=1, source_target_pairs={{0,2},{1,3},{2,4},{3,5},{4,6},{5,7},{6,0},{7,1},{8,10},{9,11},{10,... | collective-permute-start | bytes 786440 | tf_op jit(solution)/shard_map/ppermute | solution.py:318
  42.6 12.8 %collective-permute-start.18 = (bf16[2,256,256]{2,1,0:T(8,128)(2,1)S(1)}, bf16[2,256,256]{2,1,0:T(8,128)(2,1)S(1)}, u32[]{:S(2)}, u32[]{:S(2)}) collective-permute-start(bf16[2,256,256]{2,1,0:T(8,128)(2,1)S(1)} %collective-permute-done.6.refs_0_), channel_id=1, source_target_pairs={{0,1},{1,0},{2,3},{3,2},{4,5},{5,4},{6,7},{7,6},{8,9},{9,8},{10,11... | collective-permute-start | bytes 786440 | tf_op jit(solution)/shard_map/ppermute | solution.py:321
  51.8 13.1 %collective-permute-start.16 = (bf16[4,256,256]{2,1,0:T(8,128)(2,1)S(1)}, bf16[4,256,256]{2,1,0:T(8,128)(2,1)S(1)}, u32[]{:S(2)}, u32[]{:S(2)}) collective-permute-start(bf16[4,256,256]{2,1,0:T(8,128)(2,1)S(1)} %pad_maximum_fusion.refs_0_), channel_id=1, source_target_pairs={{0,2},{1,3},{2,4},{3,5},{4,6},{5,7},{8,10},{9,11},{10,12},{11,13},... | collective-permute-start | bytes 1572872 | tf_op jit(solution)/shard_map/ppermute | solution.py:318
  53.5 13.7 %collective-permute-start.17 = (bf16[4,256,256]{2,1,0:T(8,128)(2,1)S(1)}, bf16[4,256,256]{2,1,0:T(8,128)(2,1)S(1)}, u32[]{:S(2)}, u32[]{:S(2)}) collective-permute-start(bf16[4,256,256]{2,1,0:T(8,128)(2,1)S(1)} %pad_maximum_fusion.refs_0_), channel_id=1, source_target_pairs={{2,0},{3,1},{4,2},{5,3},{6,4},{7,5},{10,8},{11,9},{12,10},{13,11},... | collective-permute-start | bytes 1572872 | tf_op jit(solution)/shard_map/ppermute | solution.py:318
  67.2 8.9 %collective-permute-start.22 = (bf16[4,256,256]{2,1,0:T(8,128)(2,1)S(1)}, bf16[4,256,256]{2,1,0:T(8,128)(2,1)S(1)}, u32[]{:S(2)}, u32[]{:S(2)}) collective-permute-start(bf16[4,256,256]{2,1,0:T(8,128)(2,1)S(1)} %collective-permute-done.16.refs_2_), channel_id=1, source_target_pairs={{2,4},{3,5},{4,6},{5,7},{10,12},{11,13},{12,14},{13,15},{18,20},{1... | collective-permute-start | bytes 1572872 | tf_op jit(solution)/shard_map/ppermute | solution.py:318
  67.9 17.0 %collective-permute-start.23 = (bf16[4,256,256]{2,1,0:T(8,128)(2,1)S(1)}, bf16[4,256,256]{2,1,0:T(8,128)(2,1)S(1)}, u32[]{:S(2)}, u32[]{:S(2)}) collective-permute-start(bf16[4,256,256]{2,1,0:T(8,128)(2,1)S(1)} %collective-permute-done.17.refs_4_), channel_id=1, source_target_pairs={{2,0},{3,1},{4,2},{5,3},{10,8},{11,9},{12,10},{13,11},{18,16},{19,... | collective-permute-start | bytes 1572872 | tf_op jit(solution)/shard_map/ppermute | solution.py:318
  69.9 15.2 %collective-permute-start.30 = (bf16[256,1024]{1,0:T(8,128)(2,1)S(1)}, bf16[256,1024]{1,0:T(8,128)(2,1)S(1)}, u32[]{:S(2)}, u32[]{:S(2)}) collective-permute-start(bf16[256,1024]{1,0:T(8,128)(2,1)S(1)} %get-tuple-element.75), channel_id=1, source_target_pairs={{0,1},{1,0},{2,3},{3,2},{4,5},{5,4},{6,7},{7,6},{8,9},{9,8},{10,11... | collective-permute-start | bytes 1572872 | tf_op jit(solution)/shard_map/ppermute | solution.py:321
  70.0 17.6 %collective-permute-start.31 = (bf16[256,1024]{1,0:T(8,128)(2,1)S(1)}, bf16[256,1024]{1,0:T(8,128)(2,1)S(1)}, u32[]{:S(2)}, u32[]{:S(2)}) collective-permute-start(bf16[256,1024]{1,0:T(8,128)(2,1)S(1)} %sum.1), channel_id=1, source_target_pairs={{0,2},{1,3},{6,4},{7,5},{8,10},{9,11},{14,12},{15,13},{16,18},{17,... | collective-permute-start | bytes 1572872 | tf_op jit(solution)/shard_map/ppermute | solution.py:318
  75.8 13.3 %collective-permute-start.34 = (bf16[4,256,256]{2,1,0:T(8,128)(2,1)S(1)}, bf16[4,256,256]{2,1,0:T(8,128)(2,1)S(1)}, u32[]{:S(2)}, u32[]{:S(2)}) collective-permute-start(bf16[4,256,256]{2,1,0:T(8,128)(2,1)S(1)} %pad_maximum_fusion.refs_0_), channel_id=1, source_target_pairs={{0,1},{1,0},{2,3},{3,2},{4,5},{5,4},{6,7},{7,6},{8,9},{9,8},{10,11... | collective-permute-start | bytes 1572872 | tf_op jit(solution)/shard_map/ppermute | solution.py:321
  76.1 13.2 %collective-permute-start.37 = (bf16[256,1024]{1,0:T(8,128)(2,1)S(1)}, bf16[256,1024]{1,0:T(8,128)(2,1)S(1)}, u32[]{:S(2)}, u32[]{:S(2)}) collective-permute-start(bf16[256,1024]{1,0:T(8,128)(2,1)S(1)} %get-tuple-element.83), channel_id=1, source_target_pairs={{0,1},{1,0},{2,3},{3,2},{4,5},{5,4},{6,7},{7,6},{8,9},{9,8},{10,11... | collective-permute-start | bytes 1572872 | tf_op jit(solution)/shard_map/ppermute | solution.py:321
  84.9 9.0 %collective-permute-start.35 = (bf16[4,256,256]{2,1,0:T(8,128)(2,1)S(1)}, bf16[4,256,256]{2,1,0:T(8,128)(2,1)S(1)}, u32[]{:S(2)}, u32[]{:S(2)}) collective-permute-start(bf16[4,256,256]{2,1,0:T(8,128)(2,1)S(1)} %collective-permute-done.16.refs_2_), channel_id=1, source_target_pairs={{0,1},{1,0},{2,3},{3,2},{4,5},{5,4},{6,7},{7,6},{8,9},{9,8},{10,11... | collective-permute-start | bytes 1572872 | tf_op jit(solution)/shard_map/ppermute | solution.py:321
  85.0 9.5 %collective-permute-start.36 = (bf16[4,256,256]{2,1,0:T(8,128)(2,1)S(1)}, bf16[4,256,256]{2,1,0:T(8,128)(2,1)S(1)}, u32[]{:S(2)}, u32[]{:S(2)}) collective-permute-start(bf16[4,256,256]{2,1,0:T(8,128)(2,1)S(1)} %collective-permute-done.17.refs_4_), channel_id=1, source_target_pairs={{0,1},{1,0},{2,3},{3,2},{4,5},{5,4},{6,7},{7,6},{8,9},{9,8},{10,11... | collective-permute-start | bytes 1572872 | tf_op jit(solution)/shard_map/ppermute | solution.py:321
  87.6 15.5 %collective-permute-start.25 = (bf16[4,256,256]{2,1,0:T(8,128)(2,1)S(1)}, bf16[4,256,256]{2,1,0:T(8,128)(2,1)S(1)}, u32[]{:S(2)}, u32[]{:S(2)}) collective-permute-start(bf16[4,256,256]{2,1,0:T(8,128)(2,1)S(1)} %add.47.refs_0_), channel_id=1, source_target_pairs={{4,6},{5,7},{2,0},{3,1},{12,14},{13,15},{10,8},{11,9},{20,22},{21,... | collective-permute-start | bytes 1572872 | tf_op jit(solution)/shard_map/ppermute | solution.py:318
  89.1 17.9 %collective-permute-start.29 = (bf16[256,1024]{1,0:T(8,128)(2,1)S(1)}, bf16[256,1024]{1,0:T(8,128)(2,1)S(1)}, u32[]{:S(2)}, u32[]{:S(2)}) collective-permute-start(bf16[256,1024]{1,0:T(8,128)(2,1)S(1)} %get-tuple-element.73), channel_id=1, source_target_pairs={{0,1},{1,0},{2,3},{3,2},{4,5},{5,4},{6,7},{7,6},{8,9},{9,8},{10,11... | collective-permute-start | bytes 1572872 | tf_op jit(solution)/shard_map/ppermute | solution.py:321
  89.2 17.8 %collective-permute-start.32 = (bf16[256,1024]{1,0:T(8,128)(2,1)S(1)}, bf16[256,1024]{1,0:T(8,128)(2,1)S(1)}, u32[]{:S(2)}, u32[]{:S(2)}) collective-permute-start(bf16[256,1024]{1,0:T(8,128)(2,1)S(1)} %add_convert_fusion), channel_id=1, source_target_pairs={{0,2},{1,3},{2,4},{3,5},{8,10},{9,11},{10,12},{11,13},{16,18},{17,... | collective-permute-start | bytes 1572872 | tf_op jit(solution)/shard_map/ppermute | solution.py:318
  93.9 13.2 %collective-permute-start.33 = (bf16[256,1024]{1,0:T(8,128)(2,1)S(1)}, bf16[256,1024]{1,0:T(8,128)(2,1)S(1)}, u32[]{:S(2)}, u32[]{:S(2)}) collective-permute-start(bf16[256,1024]{1,0:T(8,128)(2,1)S(1)} %add_convert_fusion), channel_id=1, source_target_pairs={{4,2},{5,3},{6,4},{7,5},{12,10},{13,11},{14,12},{15,13},{20,18},{2... | collective-permute-start | bytes 1572872 | tf_op jit(solution)/shard_map/ppermute | solution.py:318
  94.6 21.4 %collective-permute-start.24 = (bf16[4,256,256]{2,1,0:T(8,128)(2,1)S(1)}, bf16[4,256,256]{2,1,0:T(8,128)(2,1)S(1)}, u32[]{:S(2)}, u32[]{:S(2)}) collective-permute-start(bf16[4,256,256]{2,1,0:T(8,128)(2,1)S(1)} %add.47.refs_0_), channel_id=1, source_target_pairs={{0,1},{1,0},{2,3},{3,2},{4,5},{5,4},{6,7},{7,6},{8,9},{9,8},{10,11... | collective-permute-start | bytes 1572872 | tf_op jit(solution)/shard_map/ppermute | solution.py:321
  103.1 12.9 %collective-permute-start.26 = (bf16[4,256,256]{2,1,0:T(8,128)(2,1)S(1)}, bf16[4,256,256]{2,1,0:T(8,128)(2,1)S(1)}, u32[]{:S(2)}, u32[]{:S(2)}) collective-permute-start(bf16[4,256,256]{2,1,0:T(8,128)(2,1)S(1)} %collective-permute-done.25.refs_2_), channel_id=1, source_target_pairs={{0,1},{1,0},{2,3},{3,2},{4,5},{5,4},{6,7},{7,6},{8,9},{9,8},{10,11... | collective-permute-start | bytes 1572872 | tf_op jit(solution)/shard_map/ppermute | solution.py:321
  108.0 17.5 %collective-permute-start.38 = (bf16[256,1024]{1,0:T(8,128)(2,1)S(1)}, bf16[256,1024]{1,0:T(8,128)(2,1)S(1)}, u32[]{:S(2)}, u32[]{:S(2)}) collective-permute-start(bf16[256,1024]{1,0:T(8,128)(2,1)S(1)} %get-tuple-element.84), channel_id=1, source_target_pairs={{0,2},{1,3},{2,4},{3,5},{4,6},{5,7},{8,10},{9,11},{10,12},{11,13},... | collective-permute-start | bytes 1572872 | tf_op jit(solution)/shard_map/ppermute | solution.py:318
  114.7 14.9 %collective-permute-start.39 = (bf16[256,1024]{1,0:T(8,128)(2,1)S(1)}, bf16[256,1024]{1,0:T(8,128)(2,1)S(1)}, u32[]{:S(2)}, u32[]{:S(2)}) collective-permute-start(bf16[256,1024]{1,0:T(8,128)(2,1)S(1)} %get-tuple-element.85), channel_id=1, source_target_pairs={{2,0},{3,1},{4,2},{5,3},{6,4},{7,5},{10,8},{11,9},{12,10},{13,11},... | collective-permute-start | bytes 1572872 | tf_op jit(solution)/shard_map/ppermute | solution.py:318
  121.0 9.7 %collective-permute-start.41 = (f32[1,256]{1,0:T(1,128)S(1)}, f32[1,256]{1,0:T(1,128)S(1)}, u32[]{:S(2)}, u32[]{:S(2)}) collective-permute-start(f32[1,256]{1,0:T(1,128)S(1)} %slice_add_fusion), channel_id=1, source_target_pairs={{0,2},{1,3},{2,0},{3,1},{4,6},{5,7},{6,4},{7,5},{8,10},{9,11},{10,... | collective-permute-start | bytes 3080 | tf_op jit(solution)/shard_map/ppermute | solution.py:318
  122.5 8.3 %collective-permute-start.42 = (f32[1,256]{1,0:T(1,128)S(1)}, f32[1,256]{1,0:T(1,128)S(1)}, u32[]{:S(2)}, u32[]{:S(2)}) collective-permute-start(f32[1,256]{1,0:T(1,128)S(1)} %slice_add_fusion), channel_id=1, source_target_pairs={{0,4},{1,5},{2,6},{3,7},{4,0},{5,1},{6,2},{7,3},{8,12},{9,13},{10,... | collective-permute-start | bytes 3080 | tf_op jit(solution)/shard_map/ppermute | solution.py:318
  (17 other events, 146.0 us)

commit v12 on v11

--- a/solution.py
+++ b/solution.py
@@ -341,9 +341,8 @@
         if k == 1:
             second = after(second, table)
         if k == 2:
-            second = after(second, shard_g)
             w_out, far_x[0][0] = load(w_dec, far_x[0][0], 44)
-            first = after(first, far_x[0][0])
+            second = after(second, shard_g, far_x[0][0])
         if k == 3:
             far_x[0][1] = after(far_x[0][1], far_x[1][0])
             w_in, far_x[0][1] = load(w_enc.reshape(n_tok * n_feat, width, feats), far_x[0][1], 36)

time: 132 us -> 132 us (level)
  waiting for transfers between devices: 48.1 us -> 45.1 us
  starting transfers between devices: 47.8 us -> 50.6 us
    ppermute x19, waiting for transfers between devices: 41 us -> 35.9 us  [send(): return lax.ppermute(array, 'feat', along(pairs))]
    ppermute x6, waiting for transfers between devices: 4.21 us -> 6.38 us  [exchange(): lax.ppermute(blocks[s], 'tok', [(a, a ^ s) for a in range(n_tok)])]
    ppermute x19, starting transfers between devices: 36.3 us -> 38.3 us  [send(): return lax.ppermute(array, 'feat', along(pairs))]
  transfers between devices with their start and end apart: 44 -> 44, of which waited for: 17 -> 16; matrix products, arithmetic and copies ran while one was open for 2% -> 2% of each run, Pallas kernels for 22% -> 22%
where the time goes in v12:
time: 132 us
  starting transfers between devices  50.6 us (38%)
  waiting for transfers between devices  45.1 us (34%)
  Pallas kernels  28.8 us (22%)
  local copies, waits for them, and re-layouts  3.67 us (3%)
  other arithmetic  2.65 us (2%)
    ppermute x19, starting transfers between devices, send(): return lax.ppermute(array, 'feat', along(pairs))  38.3 us
    ppermute x19, waiting for transfers between devices, send(): return lax.ppermute(array, 'feat', along(pairs))  35.9 us
    pallas_call x7, Pallas kernels, kernel_call(): pl.pallas_call(body, in_specs=[SMEM] + [VMEM] * (len(args) - 1), out_spec...  19.3 us
    ppermute x6, starting transfers between devices, exchange(): lax.ppermute(blocks[s], 'tok', [(a, a ^ s) for a in range(n_tok)])  8.91 us
    pallas_call x2, Pallas kernels, load(): pl.pallas_call(load_body, in_specs=[anywhere, anywhere], out_specs=[VMEM,...  8.17 us
    ppermute x6, waiting for transfers between devices, exchange(): lax.ppermute(blocks[s], 'tok', [(a, a ^ s) for a in range(n_tok)])  6.38 us
    ppermute x19, starting transfers between devices, cross(): return lax.ppermute(array, 'feat', [(a, a ^ 1) for a in range(n_feat)])  3.37 us
    ppermute x19, waiting for transfers between devices, cross(): return lax.ppermute(array, 'feat', [(a, a ^ 1) for a in range(n_feat)])  2.87 us
  transfers between devices with their start and end apart: 44, of which 16 were waited for; matrix products, arithmetic and copies ran while one was open for 2% of the time, Pallas kernels for 22%

profile of v12, /device:TPU:0, one launch (start us, length us, event | category | flops | bytes accessed | tf_op | source)
XLA Modules:
  0.0 131.8 jit_solution(16363598597549696027)
XLA Ops:
  1.8 3.0 %collective-permute-start.3 = (bf16[256,256]{1,0:T(8,128)(2,1)S(1)}, bf16[256,256]{1,0:T(8,128)(2,1)S(1)}, u32[]{:S(2)}, u32[]{:S(2)}) collective-permute-start(bf16[256,256]{1,0:T(8,128)(2,1)S(1)} %get-tuple-element.88), channel_id=1, source_target_pairs={{0,8},{8,0},{16,24},{24,16},{1,9},{9,1},{17,25},{25,17},{2,10},{10... | collective-permute-start | bytes 393224 | tf_op jit(solution)/shard_map/ppermute | solution.py:326
  6.0 3.0 %collective-permute-start.7 = (bf16[256,256]{1,0:T(8,128)(2,1)S(1)}, bf16[256,256]{1,0:T(8,128)(2,1)S(1)}, u32[]{:S(2)}, u32[]{:S(2)}) collective-permute-start(bf16[256,256]{1,0:T(8,128)(2,1)S(1)} %get-tuple-element.90), channel_id=1, source_target_pairs={{0,24},{8,16},{16,8},{24,0},{1,25},{9,17},{17,9},{25,1},{2,26},{10... | collective-permute-start | bytes 393224 | tf_op jit(solution)/shard_map/ppermute | solution.py:326
  9.5 1.6 %collective-permute-start.4 = (bf16[2,256,256]{2,1,0:T(8,128)(2,1)S(1)}, bf16[2,256,256]{2,1,0:T(8,128)(2,1)S(1)}, u32[]{:S(2)}, u32[]{:S(2)}) collective-permute-start(bf16[2,256,256]{2,1,0:T(8,128)(2,1)S(1)} %pad_maximum_fusion.1.refs_0_), channel_id=1, source_target_pairs={{0,2},{1,3},{2,4},{3,5},{4,6},{5,7},{6,0},{7,1},{8,10},{9,11},{10,... | collective-permute-start | bytes 786440 | tf_op jit(solution)/shard_map/ppermute | solution.py:318
  11.9 1.3 %table.1 = s32[50]{0:T(128)S(1)} custom-call(s32[2]{0:T(128)S(1)} %pad_add_fusion.ids_ref, s32[2,20]{1,0:T(2,128)S(1)} %copy-done.3), custom_call_target="tpu_custom_call" | custom-call | flops 1 | bytes 1 | tf_op jit(solution)/shard_map/table/pallas_call | solution.py:112
  13.3 1.9 %collective-permute-done.7 = bf16[256,256]{1,0:T(8,128)(2,1)S(1)} collective-permute-done((bf16[256,256]{1,0:T(8,128)(2,1)S(1)}, bf16[256,256]{1,0:T(8,128)(2,1)S(1)}, u32[]{:S(2)}, u32[]{:S(2)}) %collective-permute-start.7) | collective-permute-done | bytes 131104 | tf_op jit(solution)/shard_map/ppermute | solution.py:326
  16.2 1.6 %collective-permute-start.11 = (bf16[2,256,256]{2,1,0:T(8,128)(2,1)S(1)}, bf16[2,256,256]{2,1,0:T(8,128)(2,1)S(1)}, u32[]{:S(2)}, u32[]{:S(2)}) collective-permute-start(bf16[2,256,256]{2,1,0:T(8,128)(2,1)S(1)} %pad_maximum_fusion.2.refs_1_), channel_id=1, source_target_pairs={{0,2},{1,3},{2,4},{3,5},{4,6},{5,7},{6,0},{7,1},{8,10},{9,11},{10,... | collective-permute-start | bytes 786440 | tf_op jit(solution)/shard_map/ppermute | solution.py:318
  18.4 1.8 %collective-permute-start.2 = (bf16[256,256]{1,0:T(8,128)(2,1)S(1)}, bf16[256,256]{1,0:T(8,128)(2,1)S(1)}, u32[]{:S(2)}, u32[]{:S(2)}) collective-permute-start(bf16[256,256]{1,0:T(8,128)(2,1)S(1)} %get-tuple-element.93), channel_id=1, source_target_pairs={{0,24},{8,16},{16,8},{24,0},{1,25},{9,17},{17,9},{25,1},{2,26},{10... | collective-permute-start | bytes 393224 | tf_op jit(solution)/shard_map/ppermute | solution.py:326
  20.2 2.6 %collective-permute-done.1 = bf16[256,256]{1,0:T(8,128)(2,1)S(1)} collective-permute-done((bf16[256,256]{1,0:T(8,128)(2,1)S(1)}, bf16[256,256]{1,0:T(8,128)(2,1)S(1)}, u32[]{:S(2)}, u32[]{:S(2)}) %collective-permute-start.1) | collective-permute-done | bytes 131104 | tf_op jit(solution)/shard_map/ppermute | solution.py:326
  24.2 1.6 %collective-permute-start.5 = (bf16[2,256,256]{2,1,0:T(8,128)(2,1)S(1)}, bf16[2,256,256]{2,1,0:T(8,128)(2,1)S(1)}, u32[]{:S(2)}, u32[]{:S(2)}) collective-permute-start(bf16[2,256,256]{2,1,0:T(8,128)(2,1)S(1)} %collective-permute-done.4.refs_4_), channel_id=1, source_target_pairs={{0,2},{1,3},{2,4},{3,5},{4,6},{5,7},{6,0},{7,1},{8,10},{9,11},{10,... | collective-permute-start | bytes 786440 | tf_op jit(solution)/shard_map/ppermute | solution.py:318
  26.6 4.1 %load.3 = (bf16[640,8192]{1,0:T(8,128)(2,1)S(1)}, bf16[2,256,256]{2,1,0:T(8,128)(2,1)}) custom-call(bf16[640,8192]{1,0:T(8,128)(2,1)} %w_ref.1, bf16[2,256,256]{2,1,0:T(8,128)(2,1)} %copy-done), custom_call_target="tpu_custom_call", output_to_operand_aliasing={{1}: (1, {})} | custom-call | bytes 10485760 | tf_op jit(solution)/shard_map/load/pallas_call | solution.py:57
  30.7 1.6 %collective-permute-start.13 = (bf16[2,256,256]{2,1,0:T(8,128)(2,1)S(1)}, bf16[2,256,256]{2,1,0:T(8,128)(2,1)S(1)}, u32[]{:S(2)}, u32[]{:S(2)}) collective-permute-start(bf16[2,256,256]{2,1,0:T(8,128)(2,1)S(1)} %collective-permute-done.11.refs_5_), channel_id=1, source_target_pairs={{0,2},{1,3},{2,4},{3,5},{4,6},{5,7},{6,0},{7,1},{8,10},{9,11},{10,... | collective-permute-start | bytes 786440 | tf_op jit(solution)/shard_map/ppermute | solution.py:318
  32.3 4.1 %load.2 = (bf16[32,256,640]{2,1,0:T(8,128)(2,1)S(1)}, bf16[2,256,256]{2,1,0:T(8,128)(2,1)S(1)}) custom-call(bf16[32,256,640]{2,1,0:T(8,128)(2,1)} %bitcast.17, bf16[2,256,256]{2,1,0:T(8,128)(2,1)S(1)} %collective-permute-done.8.through_ref), custom_call_target="tpu_custom_call", output_to_operand_aliasing={{1}: (1, {})} | custom-call | bytes 10485760 | tf_op jit(solution)/shard_map/load/pallas_call | solution.py:57
  37.5 2.3 %collective-permute-done.13.refs_1_ = bf16[2,256,256]{2,1,0:T(8,128)(2,1)S(1)} collective-permute-done((bf16[2,256,256]{2,1,0:T(8,128)(2,1)S(1)}, bf16[2,256,256]{2,1,0:T(8,128)(2,1)S(1)}, u32[]{:S(2)}, u32[]{:S(2)}) %collective-permute-start.13) | collective-permute-done | bytes 262176 | tf_op jit(solution)/shard_map/ppermute | solution.py:318
  40.1 7.5 %collective-permute-done.10.refs_4_ = bf16[2,256,256]{2,1,0:T(8,128)(2,1)S(1)} collective-permute-done((bf16[2,256,256]{2,1,0:T(8,128)(2,1)S(1)}, bf16[2,256,256]{2,1,0:T(8,128)(2,1)S(1)}, u32[]{:S(2)}, u32[]{:S(2)}) %collective-permute-start.10) | collective-permute-done | bytes 262176 | tf_op jit(solution)/shard_map/ppermute | solution.py:318
  47.5 3.0 %encode.2 = (f32[256,640]{1,0:T(8,128)S(1)}, bf16[256,1024]{1,0:T(8,128)(2,1)S(1)}) custom-call(s32[50]{0:T(128)S(1)} %table.1, bf16[2,256,256]{2,1,0:T(8,128)(2,1)S(1)} %pad_maximum_fusion.1.refs_0_, bf16[2,256,256]{2,1,0:T(8,128)(2,1)S(1)} %pad_maximum_fusion.2.refs_1_, bf16[2,256,256]{2,1,0:T(8,128)(2,1)S(1)} %copy-done.1, ...), custom_call_target="tpu_custom_call" | custom-call | flops 1342177280 | bytes 4194304 | tf_op jit(solution)/shard_map/encode/pallas_call | solution.py:31
  50.9 1.8 %collective-permute-start.16 = (bf16[4,256,256]{2,1,0:T(8,128)(2,1)S(1)}, bf16[4,256,256]{2,1,0:T(8,128)(2,1)S(1)}, u32[]{:S(2)}, u32[]{:S(2)}) collective-permute-start(bf16[4,256,256]{2,1,0:T(8,128)(2,1)S(1)} %pad_maximum_fusion.refs_0_), channel_id=1, source_target_pairs={{0,2},{1,3},{2,4},{3,5},{4,6},{5,7},{8,10},{9,11},{10,12},{11,13},... | collective-permute-start | bytes 1572872 | tf_op jit(solution)/shard_map/ppermute | solution.py:318
  52.8 1.3 collective-permute-start.17
  56.4 3.2 %encode.3 = (bf16[256,640]{1,0:T(8,128)(2,1)S(1)}, bf16[256,1024]{1,0:T(8,128)(2,1)S(1)}) custom-call(s32[50]{0:T(128)S(1)} %table.1, bf16[2,256,256]{2,1,0:T(8,128)(2,1)S(1)} %collective-permute-done.5.refs_0_, bf16[2,256,256]{2,1,0:T(8,128)(2,1)S(1)} %collective-permute-done.13.refs_1_, bf16[2,256,256]{2,1,0:T(8,128)(2,1)S(1)} %collective-permute-done.18.refs_2_, ...), custom_call_target="tpu_custom_call" | custom-call | flops 1 | bytes 1 | tf_op jit(solution)/shard_map/encode/pallas_call | solution.py:31
  59.6 4.0 %decode.1 = (bf16[128,1024]{1,0:T(8,128)(2,1)S(1)}, bf16[128,1024]{1,0:T(8,128)(2,1)S(1)}, bf16[256,1024]{1,0:T(8,128)(2,1)S(1)}, bf16[256,1024]{1,0:T(8,128)(2,...) custom-call(s32[50]{0:T(128)S(1)} %table.1, ...), custom_call_target="tpu_custom_call" | custom-call | flops 1 | bytes 1 | tf_op jit(solution)/shard_map/decode/pallas_call | solution.py:31
  64.2 2.9 %collective-permute-done.17.refs_4_ = bf16[4,256,256]{2,1,0:T(8,128)(2,1)S(1)} collective-permute-done((bf16[4,256,256]{2,1,0:T(8,128)(2,1)S(1)}, bf16[4,256,256]{2,1,0:T(8,128)(2,1)S(1)}, u32[]{:S(2)}, u32[]{:S(2)}) %collective-permute-start.17) | collective-permute-done | bytes 524320 | tf_op jit(solution)/shard_map/ppermute | solution.py:318
  67.8 1.3 collective-permute-start.23
  69.8 6.4 %collective-permute-start.31 = (bf16[256,1024]{1,0:T(8,128)(2,1)S(1)}, bf16[256,1024]{1,0:T(8,128)(2,1)S(1)}, u32[]{:S(2)}, u32[]{:S(2)}) collective-permute-start(bf16[256,1024]{1,0:T(8,128)(2,1)S(1)} %sum.1), channel_id=1, source_target_pairs={{0,2},{1,3},{6,4},{7,5},{8,10},{9,11},{14,12},{15,13},{16,18},{17,... | collective-permute-start | bytes 1572872 | tf_op jit(solution)/shard_map/ppermute | solution.py:318
  76.8 7.5 %collective-permute-done.23 = bf16[4,256,256]{2,1,0:T(8,128)(2,1)S(1)} collective-permute-done((bf16[4,256,256]{2,1,0:T(8,128)(2,1)S(1)}, bf16[4,256,256]{2,1,0:T(8,128)(2,1)S(1)}, u32[]{:S(2)}, u32[]{:S(2)}) %collective-permute-start.23) | collective-permute-done | bytes 524320 | tf_op jit(solution)/shard_map/ppermute | solution.py:318
  85.0 3.0 %collective-permute-done.31 = bf16[256,1024]{1,0:T(8,128)(2,1)S(1)} collective-permute-done((bf16[256,1024]{1,0:T(8,128)(2,1)S(1)}, bf16[256,1024]{1,0:T(8,128)(2,1)S(1)}, u32[]{:S(2)}, u32[]{:S(2)}) %collective-permute-start.31) | collective-permute-done | bytes 524320 | tf_op jit(solution)/shard_map/ppermute | solution.py:318
  89.7 4.6 %collective-permute-start.32 = (bf16[256,1024]{1,0:T(8,128)(2,1)S(1)}, bf16[256,1024]{1,0:T(8,128)(2,1)S(1)}, u32[]{:S(2)}, u32[]{:S(2)}) collective-permute-start(bf16[256,1024]{1,0:T(8,128)(2,1)S(1)} %add_convert_fusion), channel_id=1, source_target_pairs={{0,2},{1,3},{2,4},{3,5},{8,10},{9,11},{10,12},{11,13},{16,18},{17,... | collective-permute-start | bytes 1572872 | tf_op jit(solution)/shard_map/ppermute | solution.py:318
  95.3 8.3 %collective-permute-done.25.refs_2_ = bf16[4,256,256]{2,1,0:T(8,128)(2,1)S(1)} collective-permute-done((bf16[4,256,256]{2,1,0:T(8,128)(2,1)S(1)}, bf16[4,256,256]{2,1,0:T(8,128)(2,1)S(1)}, u32[]{:S(2)}, u32[]{:S(2)}) %collective-permute-start.25) | collective-permute-done | bytes 524320 | tf_op jit(solution)/shard_map/ppermute | solution.py:318
  103.8 3.6 %project.2 = (f32[256,640]{1,0:T(8,128)S(1)}, f32[256,1]{1,0:T(8,128)S(1)}) custom-call(s32[50]{0:T(128)S(1)} %table.1, bf16[4,256,256]{2,1,0:T(8,128)(2,1)S(1)} %pad_maximum_fusion.refs_0_, bf16[4,256,256]{2,1,0:T(8,128)(2,1)S(1)} %collective-permute-done.34.refs_1_, bf16[4,256,256]{2,1,0:T(8,128)(2,1)S(1)} %collective-permute-done.16.refs_2_, ...), custom_call_target="tpu_custom_call" | custom-call | flops 2013265920 | bytes 4194304 | tf_op jit(solution)/shard_map/project/pallas_call | solution.py:31
  108.5 6.7 %collective-permute-start.38 = (bf16[256,1024]{1,0:T(8,128)(2,1)S(1)}, bf16[256,1024]{1,0:T(8,128)(2,1)S(1)}, u32[]{:S(2)}, u32[]{:S(2)}) collective-permute-start(bf16[256,1024]{1,0:T(8,128)(2,1)S(1)} %get-tuple-element.82), channel_id=1, source_target_pairs={{0,2},{1,3},{2,4},{3,5},{4,6},{5,7},{8,10},{9,11},{10,12},{11,13},... | collective-permute-start | bytes 1572872 | tf_op jit(solution)/shard_map/ppermute | solution.py:318
  116.5 3.9 %project.3 = (f32[256,640]{1,0:T(8,128)}, f32[8,256]{1,0:T(8,128)S(1)}) custom-call(s32[50]{0:T(128)S(1)} %table.1, bf16[4,256,256]{2,1,0:T(8,128)(2,1)S(1)} %add.47.refs_0_, bf16[4,256,256]{2,1,0:T(8,128)(2,1)S(1)} %collective-permute-done.24.refs_1_, bf16[4,256,256]{2,1,0:T(8,128)(2,1)S(1)} %collective-permute-done.25.refs_2_, ...), custom_call_target="tpu_custom_call" | custom-call | flops 1 | bytes 1 | tf_op jit(solution)/shard_map/project/pallas_call | solution.py:31
  121.5 1.5 %collective-permute-start.41 = (f32[1,256]{1,0:T(1,128)S(1)}, f32[1,256]{1,0:T(1,128)S(1)}, u32[]{:S(2)}, u32[]{:S(2)}) collective-permute-start(f32[1,256]{1,0:T(1,128)S(1)} %slice_add_fusion), channel_id=1, source_target_pairs={{0,2},{1,3},{2,0},{3,1},{4,6},{5,7},{6,4},{7,5},{8,10},{9,11},{10,... | collective-permute-start | bytes 3080 | tf_op jit(solution)/shard_map/ppermute | solution.py:318
  123.7 2.2 %collective-permute-start.43 = (f32[1,256]{1,0:T(1,128)S(1)}, f32[1,256]{1,0:T(1,128)S(1)}, u32[]{:S(2)}, u32[]{:S(2)}) collective-permute-start(f32[1,256]{1,0:T(1,128)S(1)} %slice_add_fusion), channel_id=1, source_target_pairs={{0,6},{1,7},{2,4},{3,5},{4,2},{5,3},{6,0},{7,1},{8,14},{9,15},{10,... | collective-permute-start | bytes 3080 | tf_op jit(solution)/shard_map/ppermute | solution.py:318
  125.9 4.1 %collective-permute-done.39 = bf16[256,1024]{1,0:T(8,128)(2,1)S(1)} collective-permute-done((bf16[256,1024]{1,0:T(8,128)(2,1)S(1)}, bf16[256,1024]{1,0:T(8,128)(2,1)S(1)}, u32[]{:S(2)}, u32[]{:S(2)}) %collective-permute-start.39) | collective-permute-done | bytes 524320 | tf_op jit(solution)/shard_map/ppermute | solution.py:318
  (90 shorter events, 23.5 us)
Async XLA Ops:
  5.9 12.4 %collective-permute-start = (bf16[256,256]{1,0:T(8,128)(2,1)S(1)}, bf16[256,256]{1,0:T(8,128)(2,1)S(1)}, u32[]{:S(2)}, u32[]{:S(2)}) collective-permute-start(bf16[256,256]{1,0:T(8,128)(2,1)S(1)} %get-tuple-element.92), channel_id=1, source_target_pairs={{0,8},{8,0},{16,24},{24,16},{1,9},{9,1},{17,25},{25,17},{2,10},{10... | collective-permute-start | bytes 393224 | tf_op jit(solution)/shard_map/ppermute | solution.py:326
  6.0 9.2 %collective-permute-start.7 = (bf16[256,256]{1,0:T(8,128)(2,1)S(1)}, bf16[256,256]{1,0:T(8,128)(2,1)S(1)}, u32[]{:S(2)}, u32[]{:S(2)}) collective-permute-start(bf16[256,256]{1,0:T(8,128)(2,1)S(1)} %get-tuple-element.90), channel_id=1, source_target_pairs={{0,24},{8,16},{16,8},{24,0},{1,25},{9,17},{17,9},{25,1},{2,26},{10... | collective-permute-start | bytes 393224 | tf_op jit(solution)/shard_map/ppermute | solution.py:326
  9.5 13.3 %collective-permute-start.4 = (bf16[2,256,256]{2,1,0:T(8,128)(2,1)S(1)}, bf16[2,256,256]{2,1,0:T(8,128)(2,1)S(1)}, u32[]{:S(2)}, u32[]{:S(2)}) collective-permute-start(bf16[2,256,256]{2,1,0:T(8,128)(2,1)S(1)} %pad_maximum_fusion.1.refs_0_), channel_id=1, source_target_pairs={{0,2},{1,3},{2,4},{3,5},{4,6},{5,7},{6,0},{7,1},{8,10},{9,11},{10,... | collective-permute-start | bytes 786440 | tf_op jit(solution)/shard_map/ppermute | solution.py:318
  13.2 12.6 %collective-permute-start.12 = (bf16[2,256,256]{2,1,0:T(8,128)(2,1)S(1)}, bf16[2,256,256]{2,1,0:T(8,128)(2,1)S(1)}, u32[]{:S(2)}, u32[]{:S(2)}) collective-permute-start(bf16[2,256,256]{2,1,0:T(8,128)(2,1)S(1)} %pad_maximum_fusion.1.refs_0_), channel_id=1, source_target_pairs={{0,1},{1,0},{2,3},{3,2},{4,5},{5,4},{6,7},{7,6},{8,9},{9,8},{10,11... | collective-permute-start | bytes 786440 | tf_op jit(solution)/shard_map/ppermute | solution.py:321
  16.2 14.5 %collective-permute-start.11 = (bf16[2,256,256]{2,1,0:T(8,128)(2,1)S(1)}, bf16[2,256,256]{2,1,0:T(8,128)(2,1)S(1)}, u32[]{:S(2)}, u32[]{:S(2)}) collective-permute-start(bf16[2,256,256]{2,1,0:T(8,128)(2,1)S(1)} %pad_maximum_fusion.2.refs_1_), channel_id=1, source_target_pairs={{0,2},{1,3},{2,4},{3,5},{4,6},{5,7},{6,0},{7,1},{8,10},{9,11},{10,... | collective-permute-start | bytes 786440 | tf_op jit(solution)/shard_map/ppermute | solution.py:318
  22.8 9.5 %collective-permute-start.8 = (bf16[2,256,256]{2,1,0:T(8,128)(2,1)S(1)}, bf16[2,256,256]{2,1,0:T(8,128)(2,1)S(1)}, u32[]{:S(2)}, u32[]{:S(2)}) collective-permute-start(bf16[2,256,256]{2,1,0:T(8,128)(2,1)S(1)} %pad_maximum_fusion.2.refs_1_), channel_id=1, source_target_pairs={{0,1},{1,0},{2,3},{3,2},{4,5},{5,4},{6,7},{7,6},{8,9},{9,8},{10,11... | collective-permute-start | bytes 786440 | tf_op jit(solution)/shard_map/ppermute | solution.py:321
  22.8 9.5 %collective-permute-start.9 = (bf16[2,256,256]{2,1,0:T(8,128)(2,1)S(1)}, bf16[2,256,256]{2,1,0:T(8,128)(2,1)S(1)}, u32[]{:S(2)}, u32[]{:S(2)}) collective-permute-start(bf16[2,256,256]{2,1,0:T(8,128)(2,1)S(1)} %collective-permute-done.4.refs_4_), channel_id=1, source_target_pairs={{0,1},{1,0},{2,3},{3,2},{4,5},{5,4},{6,7},{7,6},{8,9},{9,8},{10,11... | collective-permute-start | bytes 786440 | tf_op jit(solution)/shard_map/ppermute | solution.py:321
  24.2 12.2 %collective-permute-start.5 = (bf16[2,256,256]{2,1,0:T(8,128)(2,1)S(1)}, bf16[2,256,256]{2,1,0:T(8,128)(2,1)S(1)}, u32[]{:S(2)}, u32[]{:S(2)}) collective-permute-start(bf16[2,256,256]{2,1,0:T(8,128)(2,1)S(1)} %collective-permute-done.4.refs_4_), channel_id=1, source_target_pairs={{0,2},{1,3},{2,4},{3,5},{4,6},{5,7},{6,0},{7,1},{8,10},{9,11},{10,... | collective-permute-start | bytes 786440 | tf_op jit(solution)/shard_map/ppermute | solution.py:318
  30.7 9.0 %collective-permute-start.13 = (bf16[2,256,256]{2,1,0:T(8,128)(2,1)S(1)}, bf16[2,256,256]{2,1,0:T(8,128)(2,1)S(1)}, u32[]{:S(2)}, u32[]{:S(2)}) collective-permute-start(bf16[2,256,256]{2,1,0:T(8,128)(2,1)S(1)} %collective-permute-done.11.refs_5_), channel_id=1, source_target_pairs={{0,2},{1,3},{2,4},{3,5},{4,6},{5,7},{6,0},{7,1},{8,10},{9,11},{10,... | collective-permute-start | bytes 786440 | tf_op jit(solution)/shard_map/ppermute | solution.py:318
  36.5 11.1 %collective-permute-start.10 = (bf16[2,256,256]{2,1,0:T(8,128)(2,1)S(1)}, bf16[2,256,256]{2,1,0:T(8,128)(2,1)S(1)}, u32[]{:S(2)}, u32[]{:S(2)}) collective-permute-start(bf16[2,256,256]{2,1,0:T(8,128)(2,1)S(1)} %collective-permute-done.5.refs_0_), channel_id=1, source_target_pairs={{0,2},{1,3},{2,4},{3,5},{4,6},{5,7},{6,0},{7,1},{8,10},{9,11},{10,... | collective-permute-start | bytes 786440 | tf_op jit(solution)/shard_map/ppermute | solution.py:318
  37.5 10.1 %collective-permute-start.15 = (bf16[2,256,256]{2,1,0:T(8,128)(2,1)S(1)}, bf16[2,256,256]{2,1,0:T(8,128)(2,1)S(1)}, u32[]{:S(2)}, u32[]{:S(2)}) collective-permute-start(bf16[2,256,256]{2,1,0:T(8,128)(2,1)S(1)} %collective-permute-done.11.refs_5_), channel_id=1, source_target_pairs={{0,1},{1,0},{2,3},{3,2},{4,5},{5,4},{6,7},{7,6},{8,9},{9,8},{10,11... | collective-permute-start | bytes 786440 | tf_op jit(solution)/shard_map/ppermute | solution.py:321
  39.8 11.1 %collective-permute-start.14 = (bf16[2,256,256]{2,1,0:T(8,128)(2,1)S(1)}, bf16[2,256,256]{2,1,0:T(8,128)(2,1)S(1)}, u32[]{:S(2)}, u32[]{:S(2)}) collective-permute-start(bf16[2,256,256]{2,1,0:T(8,128)(2,1)S(1)} %collective-permute-done.13.refs_1_), channel_id=1, source_target_pairs={{0,2},{1,3},{2,4},{3,5},{4,6},{5,7},{6,0},{7,1},{8,10},{9,11},{10,... | collective-permute-start | bytes 786440 | tf_op jit(solution)/shard_map/ppermute | solution.py:318
  40.1 14.6 %collective-permute-start.19 = (bf16[2,256,256]{2,1,0:T(8,128)(2,1)S(1)}, bf16[2,256,256]{2,1,0:T(8,128)(2,1)S(1)}, u32[]{:S(2)}, u32[]{:S(2)}) collective-permute-start(bf16[2,256,256]{2,1,0:T(8,128)(2,1)S(1)} %collective-permute-done.13.refs_1_), channel_id=1, source_target_pairs={{0,1},{1,0},{2,3},{3,2},{4,5},{5,4},{6,7},{7,6},{8,9},{9,8},{10,11... | collective-permute-start | bytes 786440 | tf_op jit(solution)/shard_map/ppermute | solution.py:321
  50.9 13.3 %collective-permute-start.16 = (bf16[4,256,256]{2,1,0:T(8,128)(2,1)S(1)}, bf16[4,256,256]{2,1,0:T(8,128)(2,1)S(1)}, u32[]{:S(2)}, u32[]{:S(2)}) collective-permute-start(bf16[4,256,256]{2,1,0:T(8,128)(2,1)S(1)} %pad_maximum_fusion.refs_0_), channel_id=1, source_target_pairs={{0,2},{1,3},{2,4},{3,5},{4,6},{5,7},{8,10},{9,11},{10,12},{11,13},... | collective-permute-start | bytes 1572872 | tf_op jit(solution)/shard_map/ppermute | solution.py:318
  52.8 14.3 %collective-permute-start.17 = (bf16[4,256,256]{2,1,0:T(8,128)(2,1)S(1)}, bf16[4,256,256]{2,1,0:T(8,128)(2,1)S(1)}, u32[]{:S(2)}, u32[]{:S(2)}) collective-permute-start(bf16[4,256,256]{2,1,0:T(8,128)(2,1)S(1)} %pad_maximum_fusion.refs_0_), channel_id=1, source_target_pairs={{2,0},{3,1},{4,2},{5,3},{6,4},{7,5},{10,8},{11,9},{12,10},{13,11},... | collective-permute-start | bytes 1572872 | tf_op jit(solution)/shard_map/ppermute | solution.py:318
  67.1 9.5 %collective-permute-start.22 = (bf16[4,256,256]{2,1,0:T(8,128)(2,1)S(1)}, bf16[4,256,256]{2,1,0:T(8,128)(2,1)S(1)}, u32[]{:S(2)}, u32[]{:S(2)}) collective-permute-start(bf16[4,256,256]{2,1,0:T(8,128)(2,1)S(1)} %collective-permute-done.16.refs_2_), channel_id=1, source_target_pairs={{2,4},{3,5},{4,6},{5,7},{10,12},{11,13},{12,14},{13,15},{18,20},{1... | collective-permute-start | bytes 1572872 | tf_op jit(solution)/shard_map/ppermute | solution.py:318
  67.8 16.6 %collective-permute-start.23 = (bf16[4,256,256]{2,1,0:T(8,128)(2,1)S(1)}, bf16[4,256,256]{2,1,0:T(8,128)(2,1)S(1)}, u32[]{:S(2)}, u32[]{:S(2)}) collective-permute-start(bf16[4,256,256]{2,1,0:T(8,128)(2,1)S(1)} %collective-permute-done.17.refs_4_), channel_id=1, source_target_pairs={{2,0},{3,1},{4,2},{5,3},{10,8},{11,9},{12,10},{13,11},{18,16},{19,... | collective-permute-start | bytes 1572872 | tf_op jit(solution)/shard_map/ppermute | solution.py:318
  69.7 14.7 %collective-permute-start.30 = (bf16[256,1024]{1,0:T(8,128)(2,1)S(1)}, bf16[256,1024]{1,0:T(8,128)(2,1)S(1)}, u32[]{:S(2)}, u32[]{:S(2)}) collective-permute-start(bf16[256,1024]{1,0:T(8,128)(2,1)S(1)} %get-tuple-element.73), channel_id=1, source_target_pairs={{0,1},{1,0},{2,3},{3,2},{4,5},{5,4},{6,7},{7,6},{8,9},{9,8},{10,11... | collective-permute-start | bytes 1572872 | tf_op jit(solution)/shard_map/ppermute | solution.py:321
  69.8 18.2 %collective-permute-start.31 = (bf16[256,1024]{1,0:T(8,128)(2,1)S(1)}, bf16[256,1024]{1,0:T(8,128)(2,1)S(1)}, u32[]{:S(2)}, u32[]{:S(2)}) collective-permute-start(bf16[256,1024]{1,0:T(8,128)(2,1)S(1)} %sum.1), channel_id=1, source_target_pairs={{0,2},{1,3},{6,4},{7,5},{8,10},{9,11},{14,12},{15,13},{16,18},{17,... | collective-permute-start | bytes 1572872 | tf_op jit(solution)/shard_map/ppermute | solution.py:318
  76.3 13.3 %collective-permute-start.34 = (bf16[4,256,256]{2,1,0:T(8,128)(2,1)S(1)}, bf16[4,256,256]{2,1,0:T(8,128)(2,1)S(1)}, u32[]{:S(2)}, u32[]{:S(2)}) collective-permute-start(bf16[4,256,256]{2,1,0:T(8,128)(2,1)S(1)} %pad_maximum_fusion.refs_0_), channel_id=1, source_target_pairs={{0,1},{1,0},{2,3},{3,2},{4,5},{5,4},{6,7},{7,6},{8,9},{9,8},{10,11... | collective-permute-start | bytes 1572872 | tf_op jit(solution)/shard_map/ppermute | solution.py:321
  76.5 13.2 %collective-permute-start.37 = (bf16[256,1024]{1,0:T(8,128)(2,1)S(1)}, bf16[256,1024]{1,0:T(8,128)(2,1)S(1)}, u32[]{:S(2)}, u32[]{:S(2)}) collective-permute-start(bf16[256,1024]{1,0:T(8,128)(2,1)S(1)} %get-tuple-element.81), channel_id=1, source_target_pairs={{0,1},{1,0},{2,3},{3,2},{4,5},{5,4},{6,7},{7,6},{8,9},{9,8},{10,11... | collective-permute-start | bytes 1572872 | tf_op jit(solution)/shard_map/ppermute | solution.py:321
  84.3 10.0 %collective-permute-start.35 = (bf16[4,256,256]{2,1,0:T(8,128)(2,1)S(1)}, bf16[4,256,256]{2,1,0:T(8,128)(2,1)S(1)}, u32[]{:S(2)}, u32[]{:S(2)}) collective-permute-start(bf16[4,256,256]{2,1,0:T(8,128)(2,1)S(1)} %collective-permute-done.16.refs_2_), channel_id=1, source_target_pairs={{0,1},{1,0},{2,3},{3,2},{4,5},{5,4},{6,7},{7,6},{8,9},{9,8},{10,11... | collective-permute-start | bytes 1572872 | tf_op jit(solution)/shard_map/ppermute | solution.py:321
  84.5 10.6 %collective-permute-start.36 = (bf16[4,256,256]{2,1,0:T(8,128)(2,1)S(1)}, bf16[4,256,256]{2,1,0:T(8,128)(2,1)S(1)}, u32[]{:S(2)}, u32[]{:S(2)}) collective-permute-start(bf16[4,256,256]{2,1,0:T(8,128)(2,1)S(1)} %collective-permute-done.17.refs_4_), channel_id=1, source_target_pairs={{0,1},{1,0},{2,3},{3,2},{4,5},{5,4},{6,7},{7,6},{8,9},{9,8},{10,11... | collective-permute-start | bytes 1572872 | tf_op jit(solution)/shard_map/ppermute | solution.py:321
  88.0 15.5 %collective-permute-start.25 = (bf16[4,256,256]{2,1,0:T(8,128)(2,1)S(1)}, bf16[4,256,256]{2,1,0:T(8,128)(2,1)S(1)}, u32[]{:S(2)}, u32[]{:S(2)}) collective-permute-start(bf16[4,256,256]{2,1,0:T(8,128)(2,1)S(1)} %add.47.refs_0_), channel_id=1, source_target_pairs={{4,6},{5,7},{2,0},{3,1},{12,14},{13,15},{10,8},{11,9},{20,22},{21,... | collective-permute-start | bytes 1572872 | tf_op jit(solution)/shard_map/ppermute | solution.py:318
  89.6 17.9 %collective-permute-start.29 = (bf16[256,1024]{1,0:T(8,128)(2,1)S(1)}, bf16[256,1024]{1,0:T(8,128)(2,1)S(1)}, u32[]{:S(2)}, u32[]{:S(2)}) collective-permute-start(bf16[256,1024]{1,0:T(8,128)(2,1)S(1)} %get-tuple-element.71), channel_id=1, source_target_pairs={{0,1},{1,0},{2,3},{3,2},{4,5},{5,4},{6,7},{7,6},{8,9},{9,8},{10,11... | collective-permute-start | bytes 1572872 | tf_op jit(solution)/shard_map/ppermute | solution.py:321
  89.7 17.8 %collective-permute-start.32 = (bf16[256,1024]{1,0:T(8,128)(2,1)S(1)}, bf16[256,1024]{1,0:T(8,128)(2,1)S(1)}, u32[]{:S(2)}, u32[]{:S(2)}) collective-permute-start(bf16[256,1024]{1,0:T(8,128)(2,1)S(1)} %add_convert_fusion), channel_id=1, source_target_pairs={{0,2},{1,3},{2,4},{3,5},{8,10},{9,11},{10,12},{11,13},{16,18},{17,... | collective-permute-start | bytes 1572872 | tf_op jit(solution)/shard_map/ppermute | solution.py:318
  94.3 13.2 %collective-permute-start.33 = (bf16[256,1024]{1,0:T(8,128)(2,1)S(1)}, bf16[256,1024]{1,0:T(8,128)(2,1)S(1)}, u32[]{:S(2)}, u32[]{:S(2)}) collective-permute-start(bf16[256,1024]{1,0:T(8,128)(2,1)S(1)} %add_convert_fusion), channel_id=1, source_target_pairs={{4,2},{5,3},{6,4},{7,5},{12,10},{13,11},{14,12},{15,13},{20,18},{2... | collective-permute-start | bytes 1572872 | tf_op jit(solution)/shard_map/ppermute | solution.py:318
  95.0 21.4 %collective-permute-start.24 = (bf16[4,256,256]{2,1,0:T(8,128)(2,1)S(1)}, bf16[4,256,256]{2,1,0:T(8,128)(2,1)S(1)}, u32[]{:S(2)}, u32[]{:S(2)}) collective-permute-start(bf16[4,256,256]{2,1,0:T(8,128)(2,1)S(1)} %add.47.refs_0_), channel_id=1, source_target_pairs={{0,1},{1,0},{2,3},{3,2},{4,5},{5,4},{6,7},{7,6},{8,9},{9,8},{10,11... | collective-permute-start | bytes 1572872 | tf_op jit(solution)/shard_map/ppermute | solution.py:321
  103.6 12.9 %collective-permute-start.26 = (bf16[4,256,256]{2,1,0:T(8,128)(2,1)S(1)}, bf16[4,256,256]{2,1,0:T(8,128)(2,1)S(1)}, u32[]{:S(2)}, u32[]{:S(2)}) collective-permute-start(bf16[4,256,256]{2,1,0:T(8,128)(2,1)S(1)} %collective-permute-done.25.refs_2_), channel_id=1, source_target_pairs={{0,1},{1,0},{2,3},{3,2},{4,5},{5,4},{6,7},{7,6},{8,9},{9,8},{10,11... | collective-permute-start | bytes 1572872 | tf_op jit(solution)/shard_map/ppermute | solution.py:321
  108.5 17.5 %collective-permute-start.38 = (bf16[256,1024]{1,0:T(8,128)(2,1)S(1)}, bf16[256,1024]{1,0:T(8,128)(2,1)S(1)}, u32[]{:S(2)}, u32[]{:S(2)}) collective-permute-start(bf16[256,1024]{1,0:T(8,128)(2,1)S(1)} %get-tuple-element.82), channel_id=1, source_target_pairs={{0,2},{1,3},{2,4},{3,5},{4,6},{5,7},{8,10},{9,11},{10,12},{11,13},... | collective-permute-start | bytes 1572872 | tf_op jit(solution)/shard_map/ppermute | solution.py:318
  115.2 14.9 %collective-permute-start.39 = (bf16[256,1024]{1,0:T(8,128)(2,1)S(1)}, bf16[256,1024]{1,0:T(8,128)(2,1)S(1)}, u32[]{:S(2)}, u32[]{:S(2)}) collective-permute-start(bf16[256,1024]{1,0:T(8,128)(2,1)S(1)} %get-tuple-element.83), channel_id=1, source_target_pairs={{2,0},{3,1},{4,2},{5,3},{6,4},{7,5},{10,8},{11,9},{12,10},{13,11},... | collective-permute-start | bytes 1572872 | tf_op jit(solution)/shard_map/ppermute | solution.py:318
  121.5 9.7 %collective-permute-start.41 = (f32[1,256]{1,0:T(1,128)S(1)}, f32[1,256]{1,0:T(1,128)S(1)}, u32[]{:S(2)}, u32[]{:S(2)}) collective-permute-start(f32[1,256]{1,0:T(1,128)S(1)} %slice_add_fusion), channel_id=1, source_target_pairs={{0,2},{1,3},{2,0},{3,1},{4,6},{5,7},{6,4},{7,5},{8,10},{9,11},{10,... | collective-permute-start | bytes 3080 | tf_op jit(solution)/shard_map/ppermute | solution.py:318
  (17 other events, 135.1 us)

commit v13 on v11

--- a/solution.py
+++ b/solution.py
@@ -147,22 +147,28 @@
     )(table, array)
 
 
-def third_body(chips, table, *refs):
-    near_1, far_1, near_3, far_3, up_ref, down_ref = refs[:3] + (refs[3:-4],) + refs[-4:-2]
+def second_body(table, near_ref, far_ref, come_ref, *out_refs):
+    rows = out_refs[0].shape[0]
+    for h, out_ref in enumerate(out_refs):
+        part = slice(h * rows, (h + 1) * rows)
+        total = near_ref[part].astype(F32) + far_ref[part].astype(F32)
+        out_ref[...] = (total + come_ref[part].astype(F32)).astype(BF16)
+
+
+def third_body(chips, h, table, near_1, far_1, near_3, far_3, up_ref, down_ref, *targets):
     chip = table[3]
-    for target, come_ref, turn in ((refs[-2], up_ref, 1), (refs[-1], down_ref, chips - 2)):
+    rows = far_3.shape[0]
+    part = slice(h * rows, (h + 1) * rows)
+    for target, come_ref, turn in ((targets[0], up_ref, 1), (targets[1], down_ref, chips - 2)):
 
         @pl.when(chip == turn)
         def _():
-            rows = far_3[0].shape[0]
-            for h, far_ref in enumerate(far_3):
-                part = slice(h * rows, (h + 1) * rows)
-                total = near_3[part].astype(F32) + far_ref[...].astype(F32)
-                target[part] = (total + come_ref[part].astype(F32)).astype(BF16)
+            total = near_3[part].astype(F32) + far_3[...].astype(F32)
+            target[...] = (total + come_ref[...].astype(F32)).astype(BF16)
 
         @pl.when(chip != turn)
         def _():
-            total = near_1[...].astype(F32) + far_1[...].astype(F32)
+            total = near_1[part].astype(F32) + far_1[part].astype(F32)
             target[...] = (total + come_ref[...].astype(F32)).astype(BF16)
 
 
@@ -383,12 +389,13 @@
 
     come = send(start, [(0, 1), (3, 2)])
     up_2, down_2 = send(up_1, up_pairs[1:]), send(down_1, down_pairs[:-1])
-    going = (pair_sum(2) + come.astype(F32)).astype(BF16)
+    half = ((rows // 2, share), BF16)
+    going = kernel_call(second_body, [half] * 2, [table, *parts[2], come], "second")
     two_g = up_2 + down_2
     three_g = send(two_g, [(2, 3), (1, 0)])
 
-    up = send(going, up_pairs[:2])
-    down = send(going, down_pairs[1:])
+    up = [send(a, up_pairs[:2]) for a in going]
+    down = [send(a, down_pairs[1:]) for a in going]
 
     slots = [shard_g, cross(shard_g), up_1, cross(up_1), down_1, cross(down_1)]
     carry = project(
@@ -396,19 +403,21 @@
     )
     base = own_x.astype(F32) - b_row - pair_sum(0)
 
-    going_up, going_down = kernel_call(
-        functools.partial(third_body, chips),
-        [((rows, share), BF16)] * 2,
-        [table, *parts[1], near_3, *far_in, up, down],
-        "third",
-    )
-    going_up, going_down = after((going_up, going_down), carry, base)
-    up = send(going_up, up_pairs)
-    down = send(going_down, down_pairs)
+    last, come = [], []
+    for h in range(2):
+        sums = kernel_call(
+            functools.partial(third_body, chips, h),
+            [half] * 2,
+            [table, *parts[1], near_3, far_in[h], up[h], down[h]],
+            "third",
+        )
+        going_up, going_down = after(tuple(sums), carry, base)
+        last += [going_up, going_down]
+        come.append(send(going_up, up_pairs).astype(F32) + send(going_down, down_pairs).astype(F32))
 
     slots = [two_g, cross(two_g), three_g, cross(three_g)]
     feature_attr, attr = project(
-        table, SLOTS["proj_b"], slots, w_out, after(acts, going_up, going_down), own_x, b_row, carry, True, n_feat
+        table, SLOTS["proj_b"], slots, w_out, after(acts, *last), own_x, b_row, carry, True, n_feat
     )
     attr = attr[:1]
     attr = attr + cross(attr)
@@ -416,7 +425,7 @@
     for other in others:
         attr = attr + other
 
-    error = base - (up.astype(F32) + down.astype(F32))
+    error = base - jnp.concatenate(come)
     return feature_attr, error, attr.reshape(rows)
 
 

time: 132 us -> 140 us (1.061)
  starting transfers between devices: 47.8 us -> 61.1 us
  waiting for transfers between devices: 48.1 us -> 41.9 us
    ppermute x19 -> x23, starting transfers between devices: 36.3 us -> 49.2 us  [send(): return lax.ppermute(array, 'feat', along(pairs))]
    ppermute x19 -> x23, waiting for transfers between devices: 41 us -> 36.3 us  [send(): return lax.ppermute(array, 'feat', along(pairs))]
    ppermute x19, waiting for transfers between devices: 2.87 us -> 1.36 us  [cross(): return lax.ppermute(array, 'feat', [(a, a ^ 1) for a in range(n_feat)])]
    pallas_call x7 -> x9, Pallas kernels: 19.3 us -> 20.6 us  [kernel_call(): pl.pallas_call(body, in_specs=[SMEM] + [VMEM] * (len(args) - 1), out_spec...]
  transfers between devices with their start and end apart: 44 -> 48, of which waited for: 17 -> 18; matrix products, arithmetic and copies ran while one was open for 2% -> 2% of each run, Pallas kernels for 22% -> 22%
where the time goes in v13:
time: 140 us
  starting transfers between devices  61.1 us (44%)
  waiting for transfers between devices  41.9 us (30%)
  Pallas kernels  30.1 us (22%)
  local copies, waits for them, and re-layouts  2.97 us (2%)
  other arithmetic  2.41 us (2%)
    ppermute x23, starting transfers between devices, send(): return lax.ppermute(array, 'feat', along(pairs))  49.2 us
    ppermute x23, waiting for transfers between devices, send(): return lax.ppermute(array, 'feat', along(pairs))  36.3 us
    pallas_call x9, Pallas kernels, kernel_call(): pl.pallas_call(body, in_specs=[SMEM] + [VMEM] * (len(args) - 1), out_spec...  20.6 us
    pallas_call x2, Pallas kernels, load(): pl.pallas_call(load_body, in_specs=[anywhere, anywhere], out_specs=[VMEM,...  8.17 us
    ppermute x6, starting transfers between devices, exchange(): lax.ppermute(blocks[s], 'tok', [(a, a ^ s) for a in range(n_tok)])  8.1 us
    ppermute x6, waiting for transfers between devices, exchange(): lax.ppermute(blocks[s], 'tok', [(a, a ^ s) for a in range(n_tok)])  4.21 us
    ppermute x19, starting transfers between devices, cross(): return lax.ppermute(array, 'feat', [(a, a ^ 1) for a in range(n_feat)])  3.79 us
  transfers between devices with their start and end apart: 48, of which 18 were waited for; matrix products, arithmetic and copies ran while one was open for 2% of the time, Pallas kernels for 22%

profile of v13, /device:TPU:0, one launch (start us, length us, event | category | flops | bytes accessed | tf_op | source)
XLA Modules:
  0.0 139.6 jit_solution(4609301956047558214)
XLA Ops:
  1.8 3.0 %collective-permute-start.3 = (bf16[256,256]{1,0:T(8,128)(2,1)S(1)}, bf16[256,256]{1,0:T(8,128)(2,1)S(1)}, u32[]{:S(2)}, u32[]{:S(2)}) collective-permute-start(bf16[256,256]{1,0:T(8,128)(2,1)S(1)} %get-tuple-element.102), channel_id=1, source_target_pairs={{0,8},{8,0},{16,24},{24,16},{1,9},{9,1},{17,25},{25,17},{2,10},{10... | collective-permute-start | bytes 393224 | tf_op jit(solution)/shard_map/ppermute | solution.py:332
  4.8 1.5 %collective-permute-start.8 = (bf16[256,256]{1,0:T(8,128)(2,1)S(1)}, bf16[256,256]{1,0:T(8,128)(2,1)S(1)}, u32[]{:S(2)}, u32[]{:S(2)}) collective-permute-start(bf16[256,256]{1,0:T(8,128)(2,1)S(1)} %get-tuple-element.104), channel_id=1, source_target_pairs={{0,24},{8,16},{16,8},{24,0},{1,25},{9,17},{17,9},{25,1},{2,26},{10... | collective-permute-start | bytes 393224 | tf_op jit(solution)/shard_map/ppermute | solution.py:332
  6.3 2.4 %collective-permute-done.3 = bf16[256,256]{1,0:T(8,128)(2,1)S(1)} collective-permute-done((bf16[256,256]{1,0:T(8,128)(2,1)S(1)}, bf16[256,256]{1,0:T(8,128)(2,1)S(1)}, u32[]{:S(2)}, u32[]{:S(2)}) %collective-permute-start.3) | collective-permute-done | bytes 131104 | tf_op jit(solution)/shard_map/ppermute | solution.py:332
  9.6 1.3 table.1
  10.9 2.1 %collective-permute-start.4 = (bf16[2,256,256]{2,1,0:T(8,128)(2,1)S(1)}, bf16[2,256,256]{2,1,0:T(8,128)(2,1)S(1)}, u32[]{:S(2)}, u32[]{:S(2)}) collective-permute-start(bf16[2,256,256]{2,1,0:T(8,128)(2,1)S(1)} %pad_maximum_fusion.1.refs_0_), channel_id=1, source_target_pairs={{0,2},{1,3},{2,4},{3,5},{4,6},{5,7},{6,0},{7,1},{8,10},{9,11},{10,... | collective-permute-start | bytes 786440 | tf_op jit(solution)/shard_map/ppermute | solution.py:324
  13.8 1.6 %collective-permute-start.12 = (bf16[2,256,256]{2,1,0:T(8,128)(2,1)S(1)}, bf16[2,256,256]{2,1,0:T(8,128)(2,1)S(1)}, u32[]{:S(2)}, u32[]{:S(2)}) collective-permute-start(bf16[2,256,256]{2,1,0:T(8,128)(2,1)S(1)} %pad_maximum_fusion.2.refs_1_), channel_id=1, source_target_pairs={{0,2},{1,3},{2,4},{3,5},{4,6},{5,7},{6,0},{7,1},{8,10},{9,11},{10,... | collective-permute-start | bytes 786440 | tf_op jit(solution)/shard_map/ppermute | solution.py:324
  16.6 1.6 %collective-permute-start = (bf16[256,256]{1,0:T(8,128)(2,1)S(1)}, bf16[256,256]{1,0:T(8,128)(2,1)S(1)}, u32[]{:S(2)}, u32[]{:S(2)}) collective-permute-start(bf16[256,256]{1,0:T(8,128)(2,1)S(1)} %get-tuple-element.106), channel_id=1, source_target_pairs={{0,8},{8,0},{16,24},{24,16},{1,9},{9,1},{17,25},{25,17},{2,10},{10... | collective-permute-start | bytes 393224 | tf_op jit(solution)/shard_map/ppermute | solution.py:332
  20.1 4.1 %load.2 = (bf16[640,8192]{1,0:T(8,128)(2,1)S(1)}, bf16[2,256,256]{2,1,0:T(8,128)(2,1)}) custom-call(bf16[640,8192]{1,0:T(8,128)(2,1)} %w_ref.1, bf16[2,256,256]{2,1,0:T(8,128)(2,1)} %copy-done), custom_call_target="tpu_custom_call", output_to_operand_aliasing={{1}: (1, {})} | custom-call | bytes 10485760 | tf_op jit(solution)/shard_map/load/pallas_call | solution.py:57
  25.9 1.6 %collective-permute-start.6 = (bf16[2,256,256]{2,1,0:T(8,128)(2,1)S(1)}, bf16[2,256,256]{2,1,0:T(8,128)(2,1)S(1)}, u32[]{:S(2)}, u32[]{:S(2)}) collective-permute-start(bf16[2,256,256]{2,1,0:T(8,128)(2,1)S(1)} %collective-permute-done.4.refs_4_), channel_id=1, source_target_pairs={{0,2},{1,3},{2,4},{3,5},{4,6},{5,7},{6,0},{7,1},{8,10},{9,11},{10,... | collective-permute-start | bytes 786440 | tf_op jit(solution)/shard_map/ppermute | solution.py:324
  28.9 4.1 %load.3 = (bf16[32,256,640]{2,1,0:T(8,128)(2,1)S(1)}, bf16[2,256,256]{2,1,0:T(8,128)(2,1)S(1)}) custom-call(bf16[32,256,640]{2,1,0:T(8,128)(2,1)} %bitcast.17, bf16[2,256,256]{2,1,0:T(8,128)(2,1)S(1)} %collective-permute-done.9.through_ref), custom_call_target="tpu_custom_call", output_to_operand_aliasing={{1}: (1, {})} | custom-call | bytes 10485760 | tf_op jit(solution)/shard_map/load/pallas_call | solution.py:57
  32.9 4.0 %collective-permute-done.6.refs_0_ = bf16[2,256,256]{2,1,0:T(8,128)(2,1)S(1)} collective-permute-done((bf16[2,256,256]{2,1,0:T(8,128)(2,1)S(1)}, bf16[2,256,256]{2,1,0:T(8,128)(2,1)S(1)}, u32[]{:S(2)}, u32[]{:S(2)}) %collective-permute-start.6) | collective-permute-done | bytes 262176 | tf_op jit(solution)/shard_map/ppermute | solution.py:324
  37.0 5.6 %collective-permute-done.13.refs_1_ = bf16[2,256,256]{2,1,0:T(8,128)(2,1)S(1)} collective-permute-done((bf16[2,256,256]{2,1,0:T(8,128)(2,1)S(1)}, bf16[2,256,256]{2,1,0:T(8,128)(2,1)S(1)}, u32[]{:S(2)}, u32[]{:S(2)}) %collective-permute-start.13) | collective-permute-done | bytes 262176 | tf_op jit(solution)/shard_map/ppermute | solution.py:324
  43.2 5.0 %collective-permute-done.11.refs_4_ = bf16[2,256,256]{2,1,0:T(8,128)(2,1)S(1)} collective-permute-done((bf16[2,256,256]{2,1,0:T(8,128)(2,1)S(1)}, bf16[2,256,256]{2,1,0:T(8,128)(2,1)S(1)}, u32[]{:S(2)}, u32[]{:S(2)}) %collective-permute-start.11) | collective-permute-done | bytes 262176 | tf_op jit(solution)/shard_map/ppermute | solution.py:324
  48.2 3.0 %encode.2 = (f32[256,640]{1,0:T(8,128)S(1)}, bf16[256,1024]{1,0:T(8,128)(2,1)S(1)}) custom-call(s32[50]{0:T(128)S(1)} %table.1, bf16[2,256,256]{2,1,0:T(8,128)(2,1)S(1)} %pad_maximum_fusion.1.refs_0_, bf16[2,256,256]{2,1,0:T(8,128)(2,1)S(1)} %pad_maximum_fusion.2.refs_1_, bf16[2,256,256]{2,1,0:T(8,128)(2,1)S(1)} %copy-done.1, ...), custom_call_target="tpu_custom_call" | custom-call | flops 1342177280 | bytes 4194304 | tf_op jit(solution)/shard_map/encode/pallas_call | solution.py:31
  52.3 1.7 %collective-permute-start.16 = (bf16[4,256,256]{2,1,0:T(8,128)(2,1)S(1)}, bf16[4,256,256]{2,1,0:T(8,128)(2,1)S(1)}, u32[]{:S(2)}, u32[]{:S(2)}) collective-permute-start(bf16[4,256,256]{2,1,0:T(8,128)(2,1)S(1)} %pad_maximum_fusion.refs_0_), channel_id=1, source_target_pairs={{0,2},{1,3},{2,4},{3,5},{4,6},{5,7},{8,10},{9,11},{10,12},{11,13},... | collective-permute-start | bytes 1572872 | tf_op jit(solution)/shard_map/ppermute | solution.py:324
  54.0 1.3 collective-permute-start.17
  55.3 3.2 %encode.3 = (bf16[256,640]{1,0:T(8,128)(2,1)S(1)}, bf16[256,1024]{1,0:T(8,128)(2,1)S(1)}) custom-call(s32[50]{0:T(128)S(1)} %table.1, bf16[2,256,256]{2,1,0:T(8,128)(2,1)S(1)} %collective-permute-done.6.refs_0_, bf16[2,256,256]{2,1,0:T(8,128)(2,1)S(1)} %collective-permute-done.13.refs_1_, bf16[2,256,256]{2,1,0:T(8,128)(2,1)S(1)} %collective-permute-done.18.refs_2_, ...), custom_call_target="tpu_custom_call" | custom-call | flops 1 | bytes 1 | tf_op jit(solution)/shard_map/encode/pallas_call | solution.py:31
  58.5 4.0 %decode.1 = (bf16[128,1024]{1,0:T(8,128)(2,1)S(1)}, bf16[128,1024]{1,0:T(8,128)(2,1)S(1)}, bf16[256,1024]{1,0:T(8,128)(2,1)S(1)}, bf16[256,1024]{1,0:T(8,128)(2,...) custom-call(s32[50]{0:T(128)S(1)} %table.1, ...), custom_call_target="tpu_custom_call" | custom-call | flops 1 | bytes 1 | tf_op jit(solution)/shard_map/decode/pallas_call | solution.py:31
  65.4 4.1 %collective-permute-done.17.refs_4_ = bf16[4,256,256]{2,1,0:T(8,128)(2,1)S(1)} collective-permute-done((bf16[4,256,256]{2,1,0:T(8,128)(2,1)S(1)}, bf16[4,256,256]{2,1,0:T(8,128)(2,1)S(1)}, u32[]{:S(2)}, u32[]{:S(2)}) %collective-permute-start.17) | collective-permute-done | bytes 524320 | tf_op jit(solution)/shard_map/ppermute | solution.py:324
  71.4 5.6 %collective-permute-start.31 = (bf16[256,1024]{1,0:T(8,128)(2,1)S(1)}, bf16[256,1024]{1,0:T(8,128)(2,1)S(1)}, u32[]{:S(2)}, u32[]{:S(2)}) collective-permute-start(bf16[256,1024]{1,0:T(8,128)(2,1)S(1)} %sum.1), channel_id=1, source_target_pairs={{0,2},{1,3},{6,4},{7,5},{8,10},{9,11},{14,12},{15,13},{16,18},{17,... | collective-permute-start | bytes 1572872 | tf_op jit(solution)/shard_map/ppermute | solution.py:324
  77.8 8.0 %collective-permute-done.23 = bf16[4,256,256]{2,1,0:T(8,128)(2,1)S(1)} collective-permute-done((bf16[4,256,256]{2,1,0:T(8,128)(2,1)S(1)}, bf16[4,256,256]{2,1,0:T(8,128)(2,1)S(1)}, u32[]{:S(2)}, u32[]{:S(2)}) %collective-permute-start.23) | collective-permute-done | bytes 524320 | tf_op jit(solution)/shard_map/ppermute | solution.py:324
  89.0 4.6 %collective-permute-start.38 = (bf16[128,1024]{1,0:T(8,128)(2,1)S(1)}, bf16[128,1024]{1,0:T(8,128)(2,1)S(1)}, u32[]{:S(2)}, u32[]{:S(2)}) collective-permute-start(bf16[128,1024]{1,0:T(8,128)(2,1)S(1)} %get-tuple-element.85), channel_id=1, source_target_pairs={{0,2},{1,3},{2,4},{3,5},{8,10},{9,11},{10,12},{11,13},{16,18},{17,... | collective-permute-start | bytes 786440 | tf_op jit(solution)/shard_map/ppermute | solution.py:324
  93.6 3.7 %collective-permute-start.32 = (bf16[128,1024]{1,0:T(8,128)(2,1)S(1)}, bf16[128,1024]{1,0:T(8,128)(2,1)S(1)}, u32[]{:S(2)}, u32[]{:S(2)}) collective-permute-start(bf16[128,1024]{1,0:T(8,128)(2,1)S(1)} %get-tuple-element.82), channel_id=1, source_target_pairs={{0,2},{1,3},{2,4},{3,5},{8,10},{9,11},{10,12},{11,13},{16,18},{17,... | collective-permute-start | bytes 786440 | tf_op jit(solution)/shard_map/ppermute | solution.py:324
  97.3 3.6 %project.2 = (f32[256,640]{1,0:T(8,128)S(1)}, f32[256,1]{1,0:T(8,128)S(1)}) custom-call(s32[50]{0:T(128)S(1)} %table.1, bf16[4,256,256]{2,1,0:T(8,128)(2,1)S(1)} %pad_maximum_fusion.refs_0_, bf16[4,256,256]{2,1,0:T(8,128)(2,1)S(1)} %collective-permute-done.34.refs_1_, bf16[4,256,256]{2,1,0:T(8,128)(2,1)S(1)} %collective-permute-done.16.refs_2_, ...), custom_call_target="tpu_custom_call" | custom-call | flops 2013265920 | bytes 4194304 | tf_op jit(solution)/shard_map/project/pallas_call | solution.py:31
  102.6 1.5 %collective-permute-done.32.up_ref = bf16[128,1024]{1,0:T(8,128)(2,1)S(1)} collective-permute-done((bf16[128,1024]{1,0:T(8,128)(2,1)S(1)}, bf16[128,1024]{1,0:T(8,128)(2,1)S(1)}, u32[]{:S(2)}, u32[]{:S(2)}) %collective-permute-start.32) | collective-permute-done | bytes 262176 | tf_op jit(solution)/shard_map/ppermute | solution.py:324
  105.5 9.6 %collective-permute-start.40 = (bf16[128,1024]{1,0:T(8,128)(2,1)S(1)}, bf16[128,1024]{1,0:T(8,128)(2,1)S(1)}, u32[]{:S(2)}, u32[]{:S(2)}) collective-permute-start(bf16[128,1024]{1,0:T(8,128)(2,1)S(1)} %get-tuple-element.92), channel_id=1, source_target_pairs={{0,2},{1,3},{2,4},{3,5},{4,6},{5,7},{8,10},{9,11},{10,12},{11,13},... | collective-permute-start | bytes 786440 | tf_op jit(solution)/shard_map/ppermute | solution.py:324
  117.1 4.6 %collective-permute-start.42 = (bf16[128,1024]{1,0:T(8,128)(2,1)S(1)}, bf16[128,1024]{1,0:T(8,128)(2,1)S(1)}, u32[]{:S(2)}, u32[]{:S(2)}) collective-permute-start(bf16[128,1024]{1,0:T(8,128)(2,1)S(1)} %get-tuple-element.96), channel_id=1, source_target_pairs={{0,2},{1,3},{2,4},{3,5},{4,6},{5,7},{8,10},{9,11},{10,12},{11,13},... | collective-permute-start | bytes 786440 | tf_op jit(solution)/shard_map/ppermute | solution.py:324
  123.0 2.4 %collective-permute-done.41 = bf16[128,1024]{1,0:T(8,128)(2,1)S(1)} collective-permute-done((bf16[128,1024]{1,0:T(8,128)(2,1)S(1)}, bf16[128,1024]{1,0:T(8,128)(2,1)S(1)}, u32[]{:S(2)}, u32[]{:S(2)}) %collective-permute-start.41) | collective-permute-done | bytes 262176 | tf_op jit(solution)/shard_map/ppermute | solution.py:324
  125.5 3.9 %project.3 = (f32[256,640]{1,0:T(8,128)}, f32[8,256]{1,0:T(8,128)S(1)}) custom-call(s32[50]{0:T(128)S(1)} %table.1, bf16[4,256,256]{2,1,0:T(8,128)(2,1)S(1)} %add.44.refs_0_, bf16[4,256,256]{2,1,0:T(8,128)(2,1)S(1)} %collective-permute-done.24.refs_1_, bf16[4,256,256]{2,1,0:T(8,128)(2,1)S(1)} %collective-permute-done.25.refs_2_, ...), custom_call_target="tpu_custom_call" | custom-call | flops 1 | bytes 1 | tf_op jit(solution)/shard_map/project/pallas_call | solution.py:31
  129.4 2.4 %collective-permute-done.43 = bf16[128,1024]{1,0:T(8,128)(2,1)S(1)} collective-permute-done((bf16[128,1024]{1,0:T(8,128)(2,1)S(1)}, bf16[128,1024]{1,0:T(8,128)(2,1)S(1)}, u32[]{:S(2)}, u32[]{:S(2)}) %collective-permute-start.43) | collective-permute-done | bytes 262176 | tf_op jit(solution)/shard_map/ppermute | solution.py:324
  131.9 1.8 %collective-permute-start.45 = (f32[1,256]{1,0:T(1,128)S(1)}, f32[1,256]{1,0:T(1,128)S(1)}, u32[]{:S(2)}, u32[]{:S(2)}) collective-permute-start(f32[1,256]{1,0:T(1,128)S(1)} %slice_add_fusion), channel_id=1, source_target_pairs={{0,2},{1,3},{2,0},{3,1},{4,6},{5,7},{6,4},{7,5},{8,10},{9,11},{10,... | collective-permute-start | bytes 3080 | tf_op jit(solution)/shard_map/ppermute | solution.py:324
  133.7 2.6 %collective-permute-start.47 = (f32[1,256]{1,0:T(1,128)S(1)}, f32[1,256]{1,0:T(1,128)S(1)}, u32[]{:S(2)}, u32[]{:S(2)}) collective-permute-start(f32[1,256]{1,0:T(1,128)S(1)} %slice_add_fusion), channel_id=1, source_target_pairs={{0,6},{1,7},{2,4},{3,5},{4,2},{5,3},{6,0},{7,1},{8,14},{9,15},{10,... | collective-permute-start | bytes 3080 | tf_op jit(solution)/shard_map/ppermute | solution.py:324
  (101 shorter events, 29.1 us)
Async XLA Ops:
  4.8 8.2 %collective-permute-start.8 = (bf16[256,256]{1,0:T(8,128)(2,1)S(1)}, bf16[256,256]{1,0:T(8,128)(2,1)S(1)}, u32[]{:S(2)}, u32[]{:S(2)}) collective-permute-start(bf16[256,256]{1,0:T(8,128)(2,1)S(1)} %get-tuple-element.104), channel_id=1, source_target_pairs={{0,24},{8,16},{16,8},{24,0},{1,25},{9,17},{17,9},{25,1},{2,26},{10... | collective-permute-start | bytes 393224 | tf_op jit(solution)/shard_map/ppermute | solution.py:332
  8.7 10.7 %collective-permute-start.5 = (bf16[2,256,256]{2,1,0:T(8,128)(2,1)S(1)}, bf16[2,256,256]{2,1,0:T(8,128)(2,1)S(1)}, u32[]{:S(2)}, u32[]{:S(2)}) collective-permute-start(bf16[2,256,256]{2,1,0:T(8,128)(2,1)S(1)} %pad_maximum_fusion.1.refs_0_), channel_id=1, source_target_pairs={{0,1},{1,0},{2,3},{3,2},{4,5},{5,4},{6,7},{7,6},{8,9},{9,8},{10,11... | collective-permute-start | bytes 786440 | tf_op jit(solution)/shard_map/ppermute | solution.py:327
  10.9 13.3 %collective-permute-start.4 = (bf16[2,256,256]{2,1,0:T(8,128)(2,1)S(1)}, bf16[2,256,256]{2,1,0:T(8,128)(2,1)S(1)}, u32[]{:S(2)}, u32[]{:S(2)}) collective-permute-start(bf16[2,256,256]{2,1,0:T(8,128)(2,1)S(1)} %pad_maximum_fusion.1.refs_0_), channel_id=1, source_target_pairs={{0,2},{1,3},{2,4},{3,5},{4,6},{5,7},{6,0},{7,1},{8,10},{9,11},{10,... | collective-permute-start | bytes 786440 | tf_op jit(solution)/shard_map/ppermute | solution.py:324
  13.8 13.8 %collective-permute-start.12 = (bf16[2,256,256]{2,1,0:T(8,128)(2,1)S(1)}, bf16[2,256,256]{2,1,0:T(8,128)(2,1)S(1)}, u32[]{:S(2)}, u32[]{:S(2)}) collective-permute-start(bf16[2,256,256]{2,1,0:T(8,128)(2,1)S(1)} %pad_maximum_fusion.2.refs_1_), channel_id=1, source_target_pairs={{0,2},{1,3},{2,4},{3,5},{4,6},{5,7},{6,0},{7,1},{8,10},{9,11},{10,... | collective-permute-start | bytes 786440 | tf_op jit(solution)/shard_map/ppermute | solution.py:324
  25.9 11.0 %collective-permute-start.6 = (bf16[2,256,256]{2,1,0:T(8,128)(2,1)S(1)}, bf16[2,256,256]{2,1,0:T(8,128)(2,1)S(1)}, u32[]{:S(2)}, u32[]{:S(2)}) collective-permute-start(bf16[2,256,256]{2,1,0:T(8,128)(2,1)S(1)} %collective-permute-done.4.refs_4_), channel_id=1, source_target_pairs={{0,2},{1,3},{2,4},{3,5},{4,6},{5,7},{6,0},{7,1},{8,10},{9,11},{10,... | collective-permute-start | bytes 786440 | tf_op jit(solution)/shard_map/ppermute | solution.py:324
  27.6 14.9 %collective-permute-start.13 = (bf16[2,256,256]{2,1,0:T(8,128)(2,1)S(1)}, bf16[2,256,256]{2,1,0:T(8,128)(2,1)S(1)}, u32[]{:S(2)}, u32[]{:S(2)}) collective-permute-start(bf16[2,256,256]{2,1,0:T(8,128)(2,1)S(1)} %collective-permute-done.12.refs_5_), channel_id=1, source_target_pairs={{0,2},{1,3},{2,4},{3,5},{4,6},{5,7},{6,0},{7,1},{8,10},{9,11},{10,... | collective-permute-start | bytes 786440 | tf_op jit(solution)/shard_map/ppermute | solution.py:324
  36.9 11.2 %collective-permute-start.11 = (bf16[2,256,256]{2,1,0:T(8,128)(2,1)S(1)}, bf16[2,256,256]{2,1,0:T(8,128)(2,1)S(1)}, u32[]{:S(2)}, u32[]{:S(2)}) collective-permute-start(bf16[2,256,256]{2,1,0:T(8,128)(2,1)S(1)} %collective-permute-done.6.refs_0_), channel_id=1, source_target_pairs={{0,2},{1,3},{2,4},{3,5},{4,6},{5,7},{6,0},{7,1},{8,10},{9,11},{10,... | collective-permute-start | bytes 786440 | tf_op jit(solution)/shard_map/ppermute | solution.py:324
  36.9 11.2 %collective-permute-start.15 = (bf16[2,256,256]{2,1,0:T(8,128)(2,1)S(1)}, bf16[2,256,256]{2,1,0:T(8,128)(2,1)S(1)}, u32[]{:S(2)}, u32[]{:S(2)}) collective-permute-start(bf16[2,256,256]{2,1,0:T(8,128)(2,1)S(1)} %collective-permute-done.12.refs_5_), channel_id=1, source_target_pairs={{0,1},{1,0},{2,3},{3,2},{4,5},{5,4},{6,7},{7,6},{8,9},{9,8},{10,11... | collective-permute-start | bytes 786440 | tf_op jit(solution)/shard_map/ppermute | solution.py:327
  42.6 9.2 %collective-permute-start.14 = (bf16[2,256,256]{2,1,0:T(8,128)(2,1)S(1)}, bf16[2,256,256]{2,1,0:T(8,128)(2,1)S(1)}, u32[]{:S(2)}, u32[]{:S(2)}) collective-permute-start(bf16[2,256,256]{2,1,0:T(8,128)(2,1)S(1)} %collective-permute-done.13.refs_1_), channel_id=1, source_target_pairs={{0,2},{1,3},{2,4},{3,5},{4,6},{5,7},{6,0},{7,1},{8,10},{9,11},{10,... | collective-permute-start | bytes 786440 | tf_op jit(solution)/shard_map/ppermute | solution.py:324
  42.6 11.4 %collective-permute-start.18 = (bf16[2,256,256]{2,1,0:T(8,128)(2,1)S(1)}, bf16[2,256,256]{2,1,0:T(8,128)(2,1)S(1)}, u32[]{:S(2)}, u32[]{:S(2)}) collective-permute-start(bf16[2,256,256]{2,1,0:T(8,128)(2,1)S(1)} %collective-permute-done.6.refs_0_), channel_id=1, source_target_pairs={{0,1},{1,0},{2,3},{3,2},{4,5},{5,4},{6,7},{7,6},{8,9},{9,8},{10,11... | collective-permute-start | bytes 786440 | tf_op jit(solution)/shard_map/ppermute | solution.py:327
  42.7 12.7 %collective-permute-start.19 = (bf16[2,256,256]{2,1,0:T(8,128)(2,1)S(1)}, bf16[2,256,256]{2,1,0:T(8,128)(2,1)S(1)}, u32[]{:S(2)}, u32[]{:S(2)}) collective-permute-start(bf16[2,256,256]{2,1,0:T(8,128)(2,1)S(1)} %collective-permute-done.13.refs_1_), channel_id=1, source_target_pairs={{0,1},{1,0},{2,3},{3,2},{4,5},{5,4},{6,7},{7,6},{8,9},{9,8},{10,11... | collective-permute-start | bytes 786440 | tf_op jit(solution)/shard_map/ppermute | solution.py:327
  52.3 13.1 %collective-permute-start.16 = (bf16[4,256,256]{2,1,0:T(8,128)(2,1)S(1)}, bf16[4,256,256]{2,1,0:T(8,128)(2,1)S(1)}, u32[]{:S(2)}, u32[]{:S(2)}) collective-permute-start(bf16[4,256,256]{2,1,0:T(8,128)(2,1)S(1)} %pad_maximum_fusion.refs_0_), channel_id=1, source_target_pairs={{0,2},{1,3},{2,4},{3,5},{4,6},{5,7},{8,10},{9,11},{10,12},{11,13},... | collective-permute-start | bytes 1572872 | tf_op jit(solution)/shard_map/ppermute | solution.py:324
  54.0 15.4 %collective-permute-start.17 = (bf16[4,256,256]{2,1,0:T(8,128)(2,1)S(1)}, bf16[4,256,256]{2,1,0:T(8,128)(2,1)S(1)}, u32[]{:S(2)}, u32[]{:S(2)}) collective-permute-start(bf16[4,256,256]{2,1,0:T(8,128)(2,1)S(1)} %pad_maximum_fusion.refs_0_), channel_id=1, source_target_pairs={{2,0},{3,1},{4,2},{5,3},{6,4},{7,5},{10,8},{11,9},{12,10},{13,11},... | collective-permute-start | bytes 1572872 | tf_op jit(solution)/shard_map/ppermute | solution.py:324
  63.1 14.0 %collective-permute-start.34 = (bf16[4,256,256]{2,1,0:T(8,128)(2,1)S(1)}, bf16[4,256,256]{2,1,0:T(8,128)(2,1)S(1)}, u32[]{:S(2)}, u32[]{:S(2)}) collective-permute-start(bf16[4,256,256]{2,1,0:T(8,128)(2,1)S(1)} %pad_maximum_fusion.refs_0_), channel_id=1, source_target_pairs={{0,1},{1,0},{2,3},{3,2},{4,5},{5,4},{6,7},{7,6},{8,9},{9,8},{10,11... | collective-permute-start | bytes 1572872 | tf_op jit(solution)/shard_map/ppermute | solution.py:327
  65.2 12.0 %collective-permute-start.30 = (bf16[256,1024]{1,0:T(8,128)(2,1)S(1)}, bf16[256,1024]{1,0:T(8,128)(2,1)S(1)}, u32[]{:S(2)}, u32[]{:S(2)}) collective-permute-start(bf16[256,1024]{1,0:T(8,128)(2,1)S(1)} %get-tuple-element.81), channel_id=1, source_target_pairs={{0,1},{1,0},{2,3},{3,2},{4,5},{5,4},{6,7},{7,6},{8,9},{9,8},{10,11... | collective-permute-start | bytes 1572872 | tf_op jit(solution)/shard_map/ppermute | solution.py:327
  69.5 8.2 %collective-permute-start.22 = (bf16[4,256,256]{2,1,0:T(8,128)(2,1)S(1)}, bf16[4,256,256]{2,1,0:T(8,128)(2,1)S(1)}, u32[]{:S(2)}, u32[]{:S(2)}) collective-permute-start(bf16[4,256,256]{2,1,0:T(8,128)(2,1)S(1)} %collective-permute-done.16.refs_2_), channel_id=1, source_target_pairs={{2,4},{3,5},{4,6},{5,7},{10,12},{11,13},{12,14},{13,15},{18,20},{1... | collective-permute-start | bytes 1572872 | tf_op jit(solution)/shard_map/ppermute | solution.py:324
  70.1 15.6 %collective-permute-start.23 = (bf16[4,256,256]{2,1,0:T(8,128)(2,1)S(1)}, bf16[4,256,256]{2,1,0:T(8,128)(2,1)S(1)}, u32[]{:S(2)}, u32[]{:S(2)}) collective-permute-start(bf16[4,256,256]{2,1,0:T(8,128)(2,1)S(1)} %collective-permute-done.17.refs_4_), channel_id=1, source_target_pairs={{2,0},{3,1},{4,2},{5,3},{10,8},{11,9},{12,10},{13,11},{18,16},{19,... | collective-permute-start | bytes 1572872 | tf_op jit(solution)/shard_map/ppermute | solution.py:324
  71.4 15.5 %collective-permute-start.31 = (bf16[256,1024]{1,0:T(8,128)(2,1)S(1)}, bf16[256,1024]{1,0:T(8,128)(2,1)S(1)}, u32[]{:S(2)}, u32[]{:S(2)}) collective-permute-start(bf16[256,1024]{1,0:T(8,128)(2,1)S(1)} %sum.1), channel_id=1, source_target_pairs={{0,2},{1,3},{6,4},{7,5},{8,10},{9,11},{14,12},{15,13},{16,18},{17,... | collective-permute-start | bytes 1572872 | tf_op jit(solution)/shard_map/ppermute | solution.py:324
  77.1 11.9 %collective-permute-start.35 = (bf16[4,256,256]{2,1,0:T(8,128)(2,1)S(1)}, bf16[4,256,256]{2,1,0:T(8,128)(2,1)S(1)}, u32[]{:S(2)}, u32[]{:S(2)}) collective-permute-start(bf16[4,256,256]{2,1,0:T(8,128)(2,1)S(1)} %collective-permute-done.16.refs_2_), channel_id=1, source_target_pairs={{0,1},{1,0},{2,3},{3,2},{4,5},{5,4},{6,7},{7,6},{8,9},{9,8},{10,11... | collective-permute-start | bytes 1572872 | tf_op jit(solution)/shard_map/ppermute | solution.py:327
  77.2 16.4 %collective-permute-start.36 = (bf16[4,256,256]{2,1,0:T(8,128)(2,1)S(1)}, bf16[4,256,256]{2,1,0:T(8,128)(2,1)S(1)}, u32[]{:S(2)}, u32[]{:S(2)}) collective-permute-start(bf16[4,256,256]{2,1,0:T(8,128)(2,1)S(1)} %collective-permute-done.17.refs_4_), channel_id=1, source_target_pairs={{0,1},{1,0},{2,3},{3,2},{4,5},{5,4},{6,7},{7,6},{8,9},{9,8},{10,11... | collective-permute-start | bytes 1572872 | tf_op jit(solution)/shard_map/ppermute | solution.py:327
  77.7 23.2 %collective-permute-start.37 = (bf16[256,1024]{1,0:T(8,128)(2,1)S(1)}, bf16[256,1024]{1,0:T(8,128)(2,1)S(1)}, u32[]{:S(2)}, u32[]{:S(2)}) collective-permute-start(bf16[256,1024]{1,0:T(8,128)(2,1)S(1)} %get-tuple-element.91), channel_id=1, source_target_pairs={{0,1},{1,0},{2,3},{3,2},{4,5},{5,4},{6,7},{7,6},{8,9},{9,8},{10,11... | collective-permute-start | bytes 1572872 | tf_op jit(solution)/shard_map/ppermute | solution.py:327
  85.8 16.1 %collective-permute-start.29 = (bf16[256,1024]{1,0:T(8,128)(2,1)S(1)}, bf16[256,1024]{1,0:T(8,128)(2,1)S(1)}, u32[]{:S(2)}, u32[]{:S(2)}) collective-permute-start(bf16[256,1024]{1,0:T(8,128)(2,1)S(1)} %get-tuple-element.79), channel_id=1, source_target_pairs={{0,1},{1,0},{2,3},{3,2},{4,5},{5,4},{6,7},{7,6},{8,9},{9,8},{10,11... | collective-permute-start | bytes 1572872 | tf_op jit(solution)/shard_map/ppermute | solution.py:327
  87.0 17.9 %collective-permute-start.25 = (bf16[4,256,256]{2,1,0:T(8,128)(2,1)S(1)}, bf16[4,256,256]{2,1,0:T(8,128)(2,1)S(1)}, u32[]{:S(2)}, u32[]{:S(2)}) collective-permute-start(bf16[4,256,256]{2,1,0:T(8,128)(2,1)S(1)} %add.44.refs_0_), channel_id=1, source_target_pairs={{4,6},{5,7},{2,0},{3,1},{12,14},{13,15},{10,8},{11,9},{20,22},{21,... | collective-permute-start | bytes 1572872 | tf_op jit(solution)/shard_map/ppermute | solution.py:324
  89.0 26.0 %collective-permute-start.38 = (bf16[128,1024]{1,0:T(8,128)(2,1)S(1)}, bf16[128,1024]{1,0:T(8,128)(2,1)S(1)}, u32[]{:S(2)}, u32[]{:S(2)}) collective-permute-start(bf16[128,1024]{1,0:T(8,128)(2,1)S(1)} %get-tuple-element.85), channel_id=1, source_target_pairs={{0,2},{1,3},{2,4},{3,5},{8,10},{9,11},{10,12},{11,13},{16,18},{17,... | collective-permute-start | bytes 786440 | tf_op jit(solution)/shard_map/ppermute | solution.py:324
  93.6 10.5 %collective-permute-start.32 = (bf16[128,1024]{1,0:T(8,128)(2,1)S(1)}, bf16[128,1024]{1,0:T(8,128)(2,1)S(1)}, u32[]{:S(2)}, u32[]{:S(2)}) collective-permute-start(bf16[128,1024]{1,0:T(8,128)(2,1)S(1)} %get-tuple-element.82), channel_id=1, source_target_pairs={{0,2},{1,3},{2,4},{3,5},{8,10},{9,11},{10,12},{11,13},{16,18},{17,... | collective-permute-start | bytes 786440 | tf_op jit(solution)/shard_map/ppermute | solution.py:324
  101.9 14.5 %collective-permute-start.39 = (bf16[128,1024]{1,0:T(8,128)(2,1)S(1)}, bf16[128,1024]{1,0:T(8,128)(2,1)S(1)}, u32[]{:S(2)}, u32[]{:S(2)}) collective-permute-start(bf16[128,1024]{1,0:T(8,128)(2,1)S(1)} %get-tuple-element.85), channel_id=1, source_target_pairs={{4,2},{5,3},{6,4},{7,5},{12,10},{13,11},{14,12},{15,13},{20,18},{2... | collective-permute-start | bytes 786440 | tf_op jit(solution)/shard_map/ppermute | solution.py:324
  104.1 21.3 %collective-permute-start.24 = (bf16[4,256,256]{2,1,0:T(8,128)(2,1)S(1)}, bf16[4,256,256]{2,1,0:T(8,128)(2,1)S(1)}, u32[]{:S(2)}, u32[]{:S(2)}) collective-permute-start(bf16[4,256,256]{2,1,0:T(8,128)(2,1)S(1)} %add.44.refs_0_), channel_id=1, source_target_pairs={{0,1},{1,0},{2,3},{3,2},{4,5},{5,4},{6,7},{7,6},{8,9},{9,8},{10,11... | collective-permute-start | bytes 1572872 | tf_op jit(solution)/shard_map/ppermute | solution.py:327
  104.9 20.5 %collective-permute-start.26 = (bf16[4,256,256]{2,1,0:T(8,128)(2,1)S(1)}, bf16[4,256,256]{2,1,0:T(8,128)(2,1)S(1)}, u32[]{:S(2)}, u32[]{:S(2)}) collective-permute-start(bf16[4,256,256]{2,1,0:T(8,128)(2,1)S(1)} %collective-permute-done.25.refs_2_), channel_id=1, source_target_pairs={{0,1},{1,0},{2,3},{3,2},{4,5},{5,4},{6,7},{7,6},{8,9},{9,8},{10,11... | collective-permute-start | bytes 1572872 | tf_op jit(solution)/shard_map/ppermute | solution.py:327
  105.5 16.2 %collective-permute-start.40 = (bf16[128,1024]{1,0:T(8,128)(2,1)S(1)}, bf16[128,1024]{1,0:T(8,128)(2,1)S(1)}, u32[]{:S(2)}, u32[]{:S(2)}) collective-permute-start(bf16[128,1024]{1,0:T(8,128)(2,1)S(1)} %get-tuple-element.92), channel_id=1, source_target_pairs={{0,2},{1,3},{2,4},{3,5},{4,6},{5,7},{8,10},{9,11},{10,12},{11,13},... | collective-permute-start | bytes 786440 | tf_op jit(solution)/shard_map/ppermute | solution.py:324
  115.1 10.3 %collective-permute-start.41 = (bf16[128,1024]{1,0:T(8,128)(2,1)S(1)}, bf16[128,1024]{1,0:T(8,128)(2,1)S(1)}, u32[]{:S(2)}, u32[]{:S(2)}) collective-permute-start(bf16[128,1024]{1,0:T(8,128)(2,1)S(1)} %get-tuple-element.93), channel_id=1, source_target_pairs={{2,0},{3,1},{4,2},{5,3},{6,4},{7,5},{10,8},{11,9},{12,10},{13,11},... | collective-permute-start | bytes 786440 | tf_op jit(solution)/shard_map/ppermute | solution.py:324
  117.1 12.2 %collective-permute-start.42 = (bf16[128,1024]{1,0:T(8,128)(2,1)S(1)}, bf16[128,1024]{1,0:T(8,128)(2,1)S(1)}, u32[]{:S(2)}, u32[]{:S(2)}) collective-permute-start(bf16[128,1024]{1,0:T(8,128)(2,1)S(1)} %get-tuple-element.96), channel_id=1, source_target_pairs={{0,2},{1,3},{2,4},{3,5},{4,6},{5,7},{8,10},{9,11},{10,12},{11,13},... | collective-permute-start | bytes 786440 | tf_op jit(solution)/shard_map/ppermute | solution.py:324
  121.7 10.1 %collective-permute-start.43 = (bf16[128,1024]{1,0:T(8,128)(2,1)S(1)}, bf16[128,1024]{1,0:T(8,128)(2,1)S(1)}, u32[]{:S(2)}, u32[]{:S(2)}) collective-permute-start(bf16[128,1024]{1,0:T(8,128)(2,1)S(1)} %get-tuple-element.97), channel_id=1, source_target_pairs={{2,0},{3,1},{4,2},{5,3},{6,4},{7,5},{10,8},{11,9},{12,10},{13,11},... | collective-permute-start | bytes 786440 | tf_op jit(solution)/shard_map/ppermute | solution.py:324
  (21 other events, 166.1 us)

commit v14 on v9

--- a/solution.py
+++ b/solution.py
@@ -352,7 +352,7 @@
         near_x.append([send(first, ring), send(second, ring)])
     slots = [near_x[0], far_x[0], near_x[1], far_x[1]]
     carry = encode(
-        table, SLOTS["enc_a"], slots, w_in, bias, None, X_STREAMS, False, n_feat
+        after(table, near_x[3][0]), SLOTS["enc_a"], slots, w_in, bias, None, X_STREAMS, False, n_feat
     )
     far_x.append([cross(after(near_x[3][0], shard_g)), cross(after(near_x[3][1], carry))])
 

time: 132 us -> 130 us (0.985)
  starting transfers between devices: 52.2 us -> 46 us
  waiting for transfers between devices: 43 us -> 47.4 us
    ppermute x19, starting transfers between devices: 38.5 us -> 33.7 us  [send(): return lax.ppermute(array, 'feat', along(pairs))]
    ppermute x6, waiting for transfers between devices: 3.32 us -> 5.98 us  [exchange(): lax.ppermute(blocks[s], 'tok', [(a, a ^ s) for a in range(n_tok)])]
    ppermute x19, waiting for transfers between devices: 36.9 us -> 38.6 us  [send(): return lax.ppermute(array, 'feat', along(pairs))]
  transfers between devices with their start and end apart: 44 -> 44, of which waited for: 16 -> 20; matrix products, arithmetic and copies ran while one was open for 2% -> 2% of each run, Pallas kernels for 23% -> 23%
where the time goes in v14:
time: 130 us
  waiting for transfers between devices  47.4 us (36%)
  starting transfers between devices  46 us (35%)
  Pallas kernels  30 us (23%)
  other arithmetic  2.61 us (2%)
  local copies, waits for them, and re-layouts  2.55 us (2%)
    ppermute x19, waiting for transfers between devices, send(): return lax.ppermute(array, 'feat', along(pairs))  38.6 us
    ppermute x19, starting transfers between devices, send(): return lax.ppermute(array, 'feat', along(pairs))  33.7 us
    pallas_call x7, Pallas kernels, kernel_call(): pl.pallas_call(body, in_specs=[SMEM] + [VMEM] * (len(args) - 1), out_spec...  19.3 us
    ppermute x6, starting transfers between devices, exchange(): lax.ppermute(blocks[s], 'tok', [(a, a ^ s) for a in range(n_tok)])  9.36 us
    pallas_call x2, Pallas kernels, load(): pl.pallas_call(load_body, in_specs=[anywhere, anywhere], out_specs=[VMEM,...  8.17 us
    ppermute x6, waiting for transfers between devices, exchange(): lax.ppermute(blocks[s], 'tok', [(a, a ^ s) for a in range(n_tok)])  5.98 us
    ppermute x19, waiting for transfers between devices, cross(): return lax.ppermute(array, 'feat', [(a, a ^ 1) for a in range(n_feat)])  2.87 us
    ppermute x19, starting transfers between devices, cross(): return lax.ppermute(array, 'feat', [(a, a ^ 1) for a in range(n_feat)])  2.86 us
  transfers between devices with their start and end apart: 44, of which 20 were waited for; matrix products, arithmetic and copies ran while one was open for 2% of the time, Pallas kernels for 23%

profile of v14, /device:TPU:0, one launch (start us, length us, event | category | flops | bytes accessed | tf_op | source)
XLA Modules:
  0.0 129.6 jit_solution(5901563650546245718)
XLA Ops:
  1.8 3.0 %collective-permute-start = (bf16[256,256]{1,0:T(8,128)(2,1)S(1)}, bf16[256,256]{1,0:T(8,128)(2,1)S(1)}, u32[]{:S(2)}, u32[]{:S(2)}) collective-permute-start(bf16[256,256]{1,0:T(8,128)(2,1)S(1)} %get-tuple-element.100), channel_id=1, source_target_pairs={{0,8},{8,0},{16,24},{24,16},{1,9},{9,1},{17,25},{25,17},{2,10},{10... | collective-permute-start | bytes 393224 | tf_op jit(solution)/shard_map/ppermute | solution.py:326
  4.8 1.5 %collective-permute-start.4 = (bf16[256,256]{1,0:T(8,128)(2,1)S(1)}, bf16[256,256]{1,0:T(8,128)(2,1)S(1)}, u32[]{:S(2)}, u32[]{:S(2)}) collective-permute-start(bf16[256,256]{1,0:T(8,128)(2,1)S(1)} %get-tuple-element.99), channel_id=1, source_target_pairs={{0,16},{8,24},{16,0},{24,8},{1,17},{9,25},{17,1},{25,9},{2,18},{10... | collective-permute-start | bytes 393224 | tf_op jit(solution)/shard_map/ppermute | solution.py:326
  7.1 1.3 %table.1 = s32[50]{0:T(128)S(1)} custom-call(s32[2]{0:T(128)S(1)} %pad_add_fusion.ids_ref, s32[2,20]{1,0:T(2,128)S(1)} %copy-done.4), custom_call_target="tpu_custom_call" | custom-call | flops 1 | bytes 1 | tf_op jit(solution)/shard_map/table/pallas_call | solution.py:112
  8.8 1.9 %collective-permute-start.1 = (bf16[2,256,256]{2,1,0:T(8,128)(2,1)S(1)}, bf16[2,256,256]{2,1,0:T(8,128)(2,1)S(1)}, u32[]{:S(2)}, u32[]{:S(2)}) collective-permute-start(bf16[2,256,256]{2,1,0:T(8,128)(2,1)S(1)} %pad_maximum_fusion.1.refs_0_), channel_id=1, source_target_pairs={{0,2},{1,3},{2,4},{3,5},{4,6},{5,7},{6,0},{7,1},{8,10},{9,11},{10,... | collective-permute-start | bytes 786440 | tf_op jit(solution)/shard_map/ppermute | solution.py:318
  10.7 1.9 %collective-permute-done.4 = bf16[256,256]{1,0:T(8,128)(2,1)S(1)} collective-permute-done((bf16[256,256]{1,0:T(8,128)(2,1)S(1)}, bf16[256,256]{1,0:T(8,128)(2,1)S(1)}, u32[]{:S(2)}, u32[]{:S(2)}) %collective-permute-start.4) | collective-permute-done | bytes 131104 | tf_op jit(solution)/shard_map/ppermute | solution.py:326
  12.6 1.6 %collective-permute-start.12 = (bf16[2,256,256]{2,1,0:T(8,128)(2,1)S(1)}, bf16[2,256,256]{2,1,0:T(8,128)(2,1)S(1)}, u32[]{:S(2)}, u32[]{:S(2)}) collective-permute-start(bf16[2,256,256]{2,1,0:T(8,128)(2,1)S(1)} %pad_maximum_fusion.2.refs_1_), channel_id=1, source_target_pairs={{0,2},{1,3},{2,4},{3,5},{4,6},{5,7},{6,0},{7,1},{8,10},{9,11},{10,... | collective-permute-start | bytes 786440 | tf_op jit(solution)/shard_map/ppermute | solution.py:318
  15.0 4.1 %load.2 = (bf16[640,8192]{1,0:T(8,128)(2,1)S(1)}, bf16[2,256,256]{2,1,0:T(8,128)(2,1)}) custom-call(bf16[640,8192]{1,0:T(8,128)(2,1)} %w_ref.1, bf16[2,256,256]{2,1,0:T(8,128)(2,1)} %copy-done), custom_call_target="tpu_custom_call", output_to_operand_aliasing={{1}: (1, {})} | custom-call | bytes 10485760 | tf_op jit(solution)/shard_map/load/pallas_call | solution.py:57
  19.9 1.4 %collective-permute-start.3 = (bf16[2,256,256]{2,1,0:T(8,128)(2,1)S(1)}, bf16[2,256,256]{2,1,0:T(8,128)(2,1)S(1)}, u32[]{:S(2)}, u32[]{:S(2)}) collective-permute-start(bf16[2,256,256]{2,1,0:T(8,128)(2,1)S(1)} %collective-permute-done.1.refs_4_), channel_id=1, source_target_pairs={{0,2},{1,3},{2,4},{3,5},{4,6},{5,7},{6,0},{7,1},{8,10},{9,11},{10,... | collective-permute-start | bytes 786440 | tf_op jit(solution)/shard_map/ppermute | solution.py:318
  21.2 4.2 %collective-permute-done.12.refs_5_ = bf16[2,256,256]{2,1,0:T(8,128)(2,1)S(1)} collective-permute-done((bf16[2,256,256]{2,1,0:T(8,128)(2,1)S(1)}, bf16[2,256,256]{2,1,0:T(8,128)(2,1)S(1)}, u32[]{:S(2)}, u32[]{:S(2)}) %collective-permute-start.12) | collective-permute-done | bytes 262176 | tf_op jit(solution)/shard_map/ppermute | solution.py:318
  25.5 4.1 %load.3 = (bf16[32,256,640]{2,1,0:T(8,128)(2,1)S(1)}, bf16[2,256,256]{2,1,0:T(8,128)(2,1)S(1)}) custom-call(bf16[32,256,640]{2,1,0:T(8,128)(2,1)} %bitcast.17, bf16[2,256,256]{2,1,0:T(8,128)(2,1)S(1)} %collective-permute-done.6.through_ref), custom_call_target="tpu_custom_call", output_to_operand_aliasing={{1}: (1, {})} | custom-call | bytes 10485760 | tf_op jit(solution)/shard_map/load/pallas_call | solution.py:57
  29.6 1.5 %collective-permute-done.3.refs_0_ = bf16[2,256,256]{2,1,0:T(8,128)(2,1)S(1)} collective-permute-done((bf16[2,256,256]{2,1,0:T(8,128)(2,1)S(1)}, bf16[2,256,256]{2,1,0:T(8,128)(2,1)S(1)}, u32[]{:S(2)}, u32[]{:S(2)}) %collective-permute-start.3) | collective-permute-done | bytes 262176 | tf_op jit(solution)/shard_map/ppermute | solution.py:318
  32.4 3.3 %collective-permute-start.10 = (bf16[256,256]{1,0:T(8,128)(2,1)S(1)}, bf16[256,256]{1,0:T(8,128)(2,1)S(1)}, u32[]{:S(2)}, u32[]{:S(2)}) collective-permute-start(bf16[256,256]{1,0:T(8,128)(2,1)S(1)} %get-tuple-element.60), channel_id=1, source_target_pairs={{0,24},{8,16},{16,8},{24,0},{1,25},{9,17},{17,9},{25,1},{2,26},{10... | collective-permute-start | bytes 393224 | tf_op jit(solution)/shard_map/ppermute | solution.py:326
  36.5 1.5 %collective-permute-start.9 = (bf16[256,256]{1,0:T(8,128)(2,1)S(1)}, bf16[256,256]{1,0:T(8,128)(2,1)S(1)}, u32[]{:S(2)}, u32[]{:S(2)}) collective-permute-start(bf16[256,256]{1,0:T(8,128)(2,1)S(1)} %get-tuple-element.59), channel_id=1, source_target_pairs={{0,16},{8,24},{16,0},{24,8},{1,17},{9,25},{17,1},{25,9},{2,18},{10... | collective-permute-start | bytes 393224 | tf_op jit(solution)/shard_map/ppermute | solution.py:326
  38.0 1.6 %collective-permute-done.10 = bf16[256,256]{1,0:T(8,128)(2,1)S(1)} collective-permute-done((bf16[256,256]{1,0:T(8,128)(2,1)S(1)}, bf16[256,256]{1,0:T(8,128)(2,1)S(1)}, u32[]{:S(2)}, u32[]{:S(2)}) %collective-permute-start.10) | collective-permute-done | bytes 131104 | tf_op jit(solution)/shard_map/ppermute | solution.py:326
  39.6 2.0 %collective-permute-done.8 = bf16[256,256]{1,0:T(8,128)(2,1)S(1)} collective-permute-done((bf16[256,256]{1,0:T(8,128)(2,1)S(1)}, bf16[256,256]{1,0:T(8,128)(2,1)S(1)}, u32[]{:S(2)}, u32[]{:S(2)}) %collective-permute-start.8) | collective-permute-done | bytes 131104 | tf_op jit(solution)/shard_map/ppermute | solution.py:326
  41.9 4.8 %collective-permute-done.11.refs_4_ = bf16[2,256,256]{2,1,0:T(8,128)(2,1)S(1)} collective-permute-done((bf16[2,256,256]{2,1,0:T(8,128)(2,1)S(1)}, bf16[2,256,256]{2,1,0:T(8,128)(2,1)S(1)}, u32[]{:S(2)}, u32[]{:S(2)}) %collective-permute-start.11) | collective-permute-done | bytes 262176 | tf_op jit(solution)/shard_map/ppermute | solution.py:318
  46.7 3.0 %encode.2 = (f32[256,640]{1,0:T(8,128)S(1)}, bf16[256,1024]{1,0:T(8,128)(2,1)S(1)}) custom-call(s32[50]{0:T(128)S(1)} %table.1, bf16[2,256,256]{2,1,0:T(8,128)(2,1)S(1)} %pad_maximum_fusion.1.refs_0_, bf16[2,256,256]{2,1,0:T(8,128)(2,1)S(1)} %pad_maximum_fusion.2.refs_1_, bf16[2,256,256]{2,1,0:T(8,128)(2,1)S(1)} %copy-done.1, ...), custom_call_target="tpu_custom_call" | custom-call | flops 1342177280 | bytes 4194304 | tf_op jit(solution)/shard_map/encode/pallas_call | solution.py:31
  50.6 1.3 %collective-permute-start.16 = (bf16[4,256,256]{2,1,0:T(8,128)(2,1)S(1)}, bf16[4,256,256]{2,1,0:T(8,128)(2,1)S(1)}, u32[]{:S(2)}, u32[]{:S(2)}) collective-permute-start(bf16[4,256,256]{2,1,0:T(8,128)(2,1)S(1)} %pad_maximum_fusion.refs_0_), channel_id=1, source_target_pairs={{0,2},{1,3},{2,4},{3,5},{4,6},{5,7},{8,10},{9,11},{10,12},{11,13},... | collective-permute-start | bytes 1572872 | tf_op jit(solution)/shard_map/ppermute | solution.py:318
  55.6 3.2 %encode.3 = (bf16[256,640]{1,0:T(8,128)(2,1)S(1)}, bf16[256,1024]{1,0:T(8,128)(2,1)S(1)}) custom-call(s32[50]{0:T(128)S(1)} %table.1, bf16[2,256,256]{2,1,0:T(8,128)(2,1)S(1)} %collective-permute-done.3.refs_0_, bf16[2,256,256]{2,1,0:T(8,128)(2,1)S(1)} %collective-permute-done.13.refs_1_, bf16[2,256,256]{2,1,0:T(8,128)(2,1)S(1)} %collective-permute-done.18.refs_2_, ...), custom_call_target="tpu_custom_call" | custom-call | flops 1 | bytes 1 | tf_op jit(solution)/shard_map/encode/pallas_call | solution.py:31
  58.7 4.0 %decode.1 = (bf16[128,1024]{1,0:T(8,128)(2,1)S(1)}, bf16[128,1024]{1,0:T(8,128)(2,1)S(1)}, bf16[256,1024]{1,0:T(8,128)(2,1)S(1)}, bf16[256,1024]{1,0:T(8,128)(2,...) custom-call(s32[50]{0:T(128)S(1)} %table.1, ...), custom_call_target="tpu_custom_call" | custom-call | flops 1 | bytes 1 | tf_op jit(solution)/shard_map/decode/pallas_call | solution.py:31
  63.3 2.7 %collective-permute-done.17.refs_4_ = bf16[4,256,256]{2,1,0:T(8,128)(2,1)S(1)} collective-permute-done((bf16[4,256,256]{2,1,0:T(8,128)(2,1)S(1)}, bf16[4,256,256]{2,1,0:T(8,128)(2,1)S(1)}, u32[]{:S(2)}, u32[]{:S(2)}) %collective-permute-start.17) | collective-permute-done | bytes 524320 | tf_op jit(solution)/shard_map/ppermute | solution.py:318
  68.8 5.3 %collective-permute-start.31 = (bf16[256,1024]{1,0:T(8,128)(2,1)S(1)}, bf16[256,1024]{1,0:T(8,128)(2,1)S(1)}, u32[]{:S(2)}, u32[]{:S(2)}) collective-permute-start(bf16[256,1024]{1,0:T(8,128)(2,1)S(1)} %sum.1), channel_id=1, source_target_pairs={{0,2},{1,3},{6,4},{7,5},{8,10},{9,11},{14,12},{15,13},{16,18},{17,... | collective-permute-start | bytes 1572872 | tf_op jit(solution)/shard_map/ppermute | solution.py:318
  74.7 7.0 %collective-permute-done.23 = bf16[4,256,256]{2,1,0:T(8,128)(2,1)S(1)} collective-permute-done((bf16[4,256,256]{2,1,0:T(8,128)(2,1)S(1)}, bf16[4,256,256]{2,1,0:T(8,128)(2,1)S(1)}, u32[]{:S(2)}, u32[]{:S(2)}) %collective-permute-start.23) | collective-permute-done | bytes 524320 | tf_op jit(solution)/shard_map/ppermute | solution.py:318
  82.4 3.5 %collective-permute-done.31 = bf16[256,1024]{1,0:T(8,128)(2,1)S(1)} collective-permute-done((bf16[256,1024]{1,0:T(8,128)(2,1)S(1)}, bf16[256,1024]{1,0:T(8,128)(2,1)S(1)}, u32[]{:S(2)}, u32[]{:S(2)}) %collective-permute-start.31) | collective-permute-done | bytes 524320 | tf_op jit(solution)/shard_map/ppermute | solution.py:318
  87.5 4.6 %collective-permute-start.32 = (bf16[256,1024]{1,0:T(8,128)(2,1)S(1)}, bf16[256,1024]{1,0:T(8,128)(2,1)S(1)}, u32[]{:S(2)}, u32[]{:S(2)}) collective-permute-start(bf16[256,1024]{1,0:T(8,128)(2,1)S(1)} %add_convert_fusion), channel_id=1, source_target_pairs={{0,2},{1,3},{2,4},{3,5},{8,10},{9,11},{10,12},{11,13},{16,18},{17,... | collective-permute-start | bytes 1572872 | tf_op jit(solution)/shard_map/ppermute | solution.py:318
  93.2 8.3 %collective-permute-done.25.refs_2_ = bf16[4,256,256]{2,1,0:T(8,128)(2,1)S(1)} collective-permute-done((bf16[4,256,256]{2,1,0:T(8,128)(2,1)S(1)}, bf16[4,256,256]{2,1,0:T(8,128)(2,1)S(1)}, u32[]{:S(2)}, u32[]{:S(2)}) %collective-permute-start.25) | collective-permute-done | bytes 524320 | tf_op jit(solution)/shard_map/ppermute | solution.py:318
  101.7 3.6 %project.2 = (f32[256,640]{1,0:T(8,128)S(1)}, f32[256,1]{1,0:T(8,128)S(1)}) custom-call(s32[50]{0:T(128)S(1)} %table.1, bf16[4,256,256]{2,1,0:T(8,128)(2,1)S(1)} %pad_maximum_fusion.refs_0_, bf16[4,256,256]{2,1,0:T(8,128)(2,1)S(1)} %collective-permute-done.34.refs_1_, bf16[4,256,256]{2,1,0:T(8,128)(2,1)S(1)} %collective-permute-done.16.refs_2_, ...), custom_call_target="tpu_custom_call" | custom-call | flops 2013265920 | bytes 4194304 | tf_op jit(solution)/shard_map/project/pallas_call | solution.py:31
  106.3 6.7 %collective-permute-start.38 = (bf16[256,1024]{1,0:T(8,128)(2,1)S(1)}, bf16[256,1024]{1,0:T(8,128)(2,1)S(1)}, u32[]{:S(2)}, u32[]{:S(2)}) collective-permute-start(bf16[256,1024]{1,0:T(8,128)(2,1)S(1)} %get-tuple-element.94), channel_id=1, source_target_pairs={{0,2},{1,3},{2,4},{3,5},{4,6},{5,7},{8,10},{9,11},{10,12},{11,13},... | collective-permute-start | bytes 1572872 | tf_op jit(solution)/shard_map/ppermute | solution.py:318
  114.3 3.9 %project.3 = (f32[256,640]{1,0:T(8,128)}, f32[8,256]{1,0:T(8,128)S(1)}) custom-call(s32[50]{0:T(128)S(1)} %table.1, bf16[4,256,256]{2,1,0:T(8,128)(2,1)S(1)} %add.43.refs_0_, bf16[4,256,256]{2,1,0:T(8,128)(2,1)S(1)} %collective-permute-done.24.refs_1_, bf16[4,256,256]{2,1,0:T(8,128)(2,1)S(1)} %collective-permute-done.25.refs_2_, ...), custom_call_target="tpu_custom_call" | custom-call | flops 1 | bytes 1 | tf_op jit(solution)/shard_map/project/pallas_call | solution.py:31
  119.4 1.5 %collective-permute-start.41 = (f32[1,256]{1,0:T(1,128)S(1)}, f32[1,256]{1,0:T(1,128)S(1)}, u32[]{:S(2)}, u32[]{:S(2)}) collective-permute-start(f32[1,256]{1,0:T(1,128)S(1)} %slice_add_fusion), channel_id=1, source_target_pairs={{0,2},{1,3},{2,0},{3,1},{4,6},{5,7},{6,4},{7,5},{8,10},{9,11},{10,... | collective-permute-start | bytes 3080 | tf_op jit(solution)/shard_map/ppermute | solution.py:318
  121.6 2.2 %collective-permute-start.43 = (f32[1,256]{1,0:T(1,128)S(1)}, f32[1,256]{1,0:T(1,128)S(1)}, u32[]{:S(2)}, u32[]{:S(2)}) collective-permute-start(f32[1,256]{1,0:T(1,128)S(1)} %slice_add_fusion), channel_id=1, source_target_pairs={{0,6},{1,7},{2,4},{3,5},{4,2},{5,3},{6,0},{7,1},{8,14},{9,15},{10,... | collective-permute-start | bytes 3080 | tf_op jit(solution)/shard_map/ppermute | solution.py:318
  123.8 4.1 %collective-permute-done.39 = bf16[256,1024]{1,0:T(8,128)(2,1)S(1)} collective-permute-done((bf16[256,1024]{1,0:T(8,128)(2,1)S(1)}, bf16[256,1024]{1,0:T(8,128)(2,1)S(1)}, u32[]{:S(2)}, u32[]{:S(2)}) %collective-permute-start.39) | collective-permute-done | bytes 524320 | tf_op jit(solution)/shard_map/ppermute | solution.py:318
  (92 shorter events, 24.0 us)
Async XLA Ops:
  4.8 7.8 %collective-permute-start.4 = (bf16[256,256]{1,0:T(8,128)(2,1)S(1)}, bf16[256,256]{1,0:T(8,128)(2,1)S(1)}, u32[]{:S(2)}, u32[]{:S(2)}) collective-permute-start(bf16[256,256]{1,0:T(8,128)(2,1)S(1)} %get-tuple-element.99), channel_id=1, source_target_pairs={{0,16},{8,24},{16,0},{24,8},{1,17},{9,25},{17,1},{25,9},{2,18},{10... | collective-permute-start | bytes 393224 | tf_op jit(solution)/shard_map/ppermute | solution.py:326
  8.8 11.0 %collective-permute-start.1 = (bf16[2,256,256]{2,1,0:T(8,128)(2,1)S(1)}, bf16[2,256,256]{2,1,0:T(8,128)(2,1)S(1)}, u32[]{:S(2)}, u32[]{:S(2)}) collective-permute-start(bf16[2,256,256]{2,1,0:T(8,128)(2,1)S(1)} %pad_maximum_fusion.1.refs_0_), channel_id=1, source_target_pairs={{0,2},{1,3},{2,4},{3,5},{4,6},{5,7},{6,0},{7,1},{8,10},{9,11},{10,... | collective-permute-start | bytes 786440 | tf_op jit(solution)/shard_map/ppermute | solution.py:318
  12.6 12.8 %collective-permute-start.12 = (bf16[2,256,256]{2,1,0:T(8,128)(2,1)S(1)}, bf16[2,256,256]{2,1,0:T(8,128)(2,1)S(1)}, u32[]{:S(2)}, u32[]{:S(2)}) collective-permute-start(bf16[2,256,256]{2,1,0:T(8,128)(2,1)S(1)} %pad_maximum_fusion.2.refs_1_), channel_id=1, source_target_pairs={{0,2},{1,3},{2,4},{3,5},{4,6},{5,7},{6,0},{7,1},{8,10},{9,11},{10,... | collective-permute-start | bytes 786440 | tf_op jit(solution)/shard_map/ppermute | solution.py:318
  14.3 11.2 %collective-permute-start.6 = (bf16[2,256,256]{2,1,0:T(8,128)(2,1)S(1)}, bf16[2,256,256]{2,1,0:T(8,128)(2,1)S(1)}, u32[]{:S(2)}, u32[]{:S(2)}) collective-permute-start(bf16[2,256,256]{2,1,0:T(8,128)(2,1)S(1)} %pad_maximum_fusion.2.refs_1_), channel_id=1, source_target_pairs={{0,1},{1,0},{2,3},{3,2},{4,5},{5,4},{6,7},{7,6},{8,9},{9,8},{10,11... | collective-permute-start | bytes 786440 | tf_op jit(solution)/shard_map/ppermute | solution.py:321
  19.9 11.2 %collective-permute-start.3 = (bf16[2,256,256]{2,1,0:T(8,128)(2,1)S(1)}, bf16[2,256,256]{2,1,0:T(8,128)(2,1)S(1)}, u32[]{:S(2)}, u32[]{:S(2)}) collective-permute-start(bf16[2,256,256]{2,1,0:T(8,128)(2,1)S(1)} %collective-permute-done.1.refs_4_), channel_id=1, source_target_pairs={{0,2},{1,3},{2,4},{3,5},{4,6},{5,7},{6,0},{7,1},{8,10},{9,11},{10,... | collective-permute-start | bytes 786440 | tf_op jit(solution)/shard_map/ppermute | solution.py:318
  25.5 11.0 %collective-permute-start.13 = (bf16[2,256,256]{2,1,0:T(8,128)(2,1)S(1)}, bf16[2,256,256]{2,1,0:T(8,128)(2,1)S(1)}, u32[]{:S(2)}, u32[]{:S(2)}) collective-permute-start(bf16[2,256,256]{2,1,0:T(8,128)(2,1)S(1)} %collective-permute-done.12.refs_5_), channel_id=1, source_target_pairs={{0,2},{1,3},{2,4},{3,5},{4,6},{5,7},{6,0},{7,1},{8,10},{9,11},{10,... | collective-permute-start | bytes 786440 | tf_op jit(solution)/shard_map/ppermute | solution.py:318
  32.4 7.2 %collective-permute-start.10 = (bf16[256,256]{1,0:T(8,128)(2,1)S(1)}, bf16[256,256]{1,0:T(8,128)(2,1)S(1)}, u32[]{:S(2)}, u32[]{:S(2)}) collective-permute-start(bf16[256,256]{1,0:T(8,128)(2,1)S(1)} %get-tuple-element.60), channel_id=1, source_target_pairs={{0,24},{8,16},{16,8},{24,0},{1,25},{9,17},{17,9},{25,1},{2,26},{10... | collective-permute-start | bytes 393224 | tf_op jit(solution)/shard_map/ppermute | solution.py:326
  35.7 11.0 %collective-permute-start.11 = (bf16[2,256,256]{2,1,0:T(8,128)(2,1)S(1)}, bf16[2,256,256]{2,1,0:T(8,128)(2,1)S(1)}, u32[]{:S(2)}, u32[]{:S(2)}) collective-permute-start(bf16[2,256,256]{2,1,0:T(8,128)(2,1)S(1)} %collective-permute-done.3.refs_0_), channel_id=1, source_target_pairs={{0,2},{1,3},{2,4},{3,5},{4,6},{5,7},{6,0},{7,1},{8,10},{9,11},{10,... | collective-permute-start | bytes 786440 | tf_op jit(solution)/shard_map/ppermute | solution.py:318
  35.7 11.0 %collective-permute-start.15 = (bf16[2,256,256]{2,1,0:T(8,128)(2,1)S(1)}, bf16[2,256,256]{2,1,0:T(8,128)(2,1)S(1)}, u32[]{:S(2)}, u32[]{:S(2)}) collective-permute-start(bf16[2,256,256]{2,1,0:T(8,128)(2,1)S(1)} %collective-permute-done.12.refs_5_), channel_id=1, source_target_pairs={{0,1},{1,0},{2,3},{3,2},{4,5},{5,4},{6,7},{7,6},{8,9},{9,8},{10,11... | collective-permute-start | bytes 786440 | tf_op jit(solution)/shard_map/ppermute | solution.py:321
  39.6 11.0 %collective-permute-start.14 = (bf16[2,256,256]{2,1,0:T(8,128)(2,1)S(1)}, bf16[2,256,256]{2,1,0:T(8,128)(2,1)S(1)}, u32[]{:S(2)}, u32[]{:S(2)}) collective-permute-start(bf16[2,256,256]{2,1,0:T(8,128)(2,1)S(1)} %collective-permute-done.13.refs_1_), channel_id=1, source_target_pairs={{0,2},{1,3},{2,4},{3,5},{4,6},{5,7},{6,0},{7,1},{8,10},{9,11},{10,... | collective-permute-start | bytes 786440 | tf_op jit(solution)/shard_map/ppermute | solution.py:318
  41.6 12.2 %collective-permute-start.18 = (bf16[2,256,256]{2,1,0:T(8,128)(2,1)S(1)}, bf16[2,256,256]{2,1,0:T(8,128)(2,1)S(1)}, u32[]{:S(2)}, u32[]{:S(2)}) collective-permute-start(bf16[2,256,256]{2,1,0:T(8,128)(2,1)S(1)} %collective-permute-done.3.refs_0_), channel_id=1, source_target_pairs={{0,1},{1,0},{2,3},{3,2},{4,5},{5,4},{6,7},{7,6},{8,9},{9,8},{10,11... | collective-permute-start | bytes 786440 | tf_op jit(solution)/shard_map/ppermute | solution.py:321
  50.6 12.7 %collective-permute-start.16 = (bf16[4,256,256]{2,1,0:T(8,128)(2,1)S(1)}, bf16[4,256,256]{2,1,0:T(8,128)(2,1)S(1)}, u32[]{:S(2)}, u32[]{:S(2)}) collective-permute-start(bf16[4,256,256]{2,1,0:T(8,128)(2,1)S(1)} %pad_maximum_fusion.refs_0_), channel_id=1, source_target_pairs={{0,2},{1,3},{2,4},{3,5},{4,6},{5,7},{8,10},{9,11},{10,12},{11,13},... | collective-permute-start | bytes 1572872 | tf_op jit(solution)/shard_map/ppermute | solution.py:318
  51.9 14.1 %collective-permute-start.17 = (bf16[4,256,256]{2,1,0:T(8,128)(2,1)S(1)}, bf16[4,256,256]{2,1,0:T(8,128)(2,1)S(1)}, u32[]{:S(2)}, u32[]{:S(2)}) collective-permute-start(bf16[4,256,256]{2,1,0:T(8,128)(2,1)S(1)} %pad_maximum_fusion.refs_0_), channel_id=1, source_target_pairs={{2,0},{3,1},{4,2},{5,3},{6,4},{7,5},{10,8},{11,9},{12,10},{13,11},... | collective-permute-start | bytes 1572872 | tf_op jit(solution)/shard_map/ppermute | solution.py:318
  66.0 8.4 %collective-permute-start.22 = (bf16[4,256,256]{2,1,0:T(8,128)(2,1)S(1)}, bf16[4,256,256]{2,1,0:T(8,128)(2,1)S(1)}, u32[]{:S(2)}, u32[]{:S(2)}) collective-permute-start(bf16[4,256,256]{2,1,0:T(8,128)(2,1)S(1)} %collective-permute-done.16.refs_2_), channel_id=1, source_target_pairs={{2,4},{3,5},{4,6},{5,7},{10,12},{11,13},{12,14},{13,15},{18,20},{1... | collective-permute-start | bytes 1572872 | tf_op jit(solution)/shard_map/ppermute | solution.py:318
  66.7 15.0 %collective-permute-start.23 = (bf16[4,256,256]{2,1,0:T(8,128)(2,1)S(1)}, bf16[4,256,256]{2,1,0:T(8,128)(2,1)S(1)}, u32[]{:S(2)}, u32[]{:S(2)}) collective-permute-start(bf16[4,256,256]{2,1,0:T(8,128)(2,1)S(1)} %collective-permute-done.17.refs_4_), channel_id=1, source_target_pairs={{2,0},{3,1},{4,2},{5,3},{10,8},{11,9},{12,10},{13,11},{18,16},{19,... | collective-permute-start | bytes 1572872 | tf_op jit(solution)/shard_map/ppermute | solution.py:318
  68.7 13.1 %collective-permute-start.30 = (bf16[256,1024]{1,0:T(8,128)(2,1)S(1)}, bf16[256,1024]{1,0:T(8,128)(2,1)S(1)}, u32[]{:S(2)}, u32[]{:S(2)}) collective-permute-start(bf16[256,1024]{1,0:T(8,128)(2,1)S(1)} %get-tuple-element.85), channel_id=1, source_target_pairs={{0,1},{1,0},{2,3},{3,2},{4,5},{5,4},{6,7},{7,6},{8,9},{9,8},{10,11... | collective-permute-start | bytes 1572872 | tf_op jit(solution)/shard_map/ppermute | solution.py:321
  68.8 17.1 %collective-permute-start.31 = (bf16[256,1024]{1,0:T(8,128)(2,1)S(1)}, bf16[256,1024]{1,0:T(8,128)(2,1)S(1)}, u32[]{:S(2)}, u32[]{:S(2)}) collective-permute-start(bf16[256,1024]{1,0:T(8,128)(2,1)S(1)} %sum.1), channel_id=1, source_target_pairs={{0,2},{1,3},{6,4},{7,5},{8,10},{9,11},{14,12},{15,13},{16,18},{17,... | collective-permute-start | bytes 1572872 | tf_op jit(solution)/shard_map/ppermute | solution.py:318
  74.1 13.3 %collective-permute-start.34 = (bf16[4,256,256]{2,1,0:T(8,128)(2,1)S(1)}, bf16[4,256,256]{2,1,0:T(8,128)(2,1)S(1)}, u32[]{:S(2)}, u32[]{:S(2)}) collective-permute-start(bf16[4,256,256]{2,1,0:T(8,128)(2,1)S(1)} %pad_maximum_fusion.refs_0_), channel_id=1, source_target_pairs={{0,1},{1,0},{2,3},{3,2},{4,5},{5,4},{6,7},{7,6},{8,9},{9,8},{10,11... | collective-permute-start | bytes 1572872 | tf_op jit(solution)/shard_map/ppermute | solution.py:321
  74.4 13.2 %collective-permute-start.37 = (bf16[256,1024]{1,0:T(8,128)(2,1)S(1)}, bf16[256,1024]{1,0:T(8,128)(2,1)S(1)}, u32[]{:S(2)}, u32[]{:S(2)}) collective-permute-start(bf16[256,1024]{1,0:T(8,128)(2,1)S(1)} %get-tuple-element.93), channel_id=1, source_target_pairs={{0,1},{1,0},{2,3},{3,2},{4,5},{5,4},{6,7},{7,6},{8,9},{9,8},{10,11... | collective-permute-start | bytes 1572872 | tf_op jit(solution)/shard_map/ppermute | solution.py:321
  81.7 10.5 %collective-permute-start.35 = (bf16[4,256,256]{2,1,0:T(8,128)(2,1)S(1)}, bf16[4,256,256]{2,1,0:T(8,128)(2,1)S(1)}, u32[]{:S(2)}, u32[]{:S(2)}) collective-permute-start(bf16[4,256,256]{2,1,0:T(8,128)(2,1)S(1)} %collective-permute-done.16.refs_2_), channel_id=1, source_target_pairs={{0,1},{1,0},{2,3},{3,2},{4,5},{5,4},{6,7},{7,6},{8,9},{9,8},{10,11... | collective-permute-start | bytes 1572872 | tf_op jit(solution)/shard_map/ppermute | solution.py:321
  81.8 11.1 %collective-permute-start.36 = (bf16[4,256,256]{2,1,0:T(8,128)(2,1)S(1)}, bf16[4,256,256]{2,1,0:T(8,128)(2,1)S(1)}, u32[]{:S(2)}, u32[]{:S(2)}) collective-permute-start(bf16[4,256,256]{2,1,0:T(8,128)(2,1)S(1)} %collective-permute-done.17.refs_4_), channel_id=1, source_target_pairs={{0,1},{1,0},{2,3},{3,2},{4,5},{5,4},{6,7},{7,6},{8,9},{9,8},{10,11... | collective-permute-start | bytes 1572872 | tf_op jit(solution)/shard_map/ppermute | solution.py:321
  85.9 15.5 %collective-permute-start.25 = (bf16[4,256,256]{2,1,0:T(8,128)(2,1)S(1)}, bf16[4,256,256]{2,1,0:T(8,128)(2,1)S(1)}, u32[]{:S(2)}, u32[]{:S(2)}) collective-permute-start(bf16[4,256,256]{2,1,0:T(8,128)(2,1)S(1)} %add.43.refs_0_), channel_id=1, source_target_pairs={{4,6},{5,7},{2,0},{3,1},{12,14},{13,15},{10,8},{11,9},{20,22},{21,... | collective-permute-start | bytes 1572872 | tf_op jit(solution)/shard_map/ppermute | solution.py:318
  87.5 17.9 %collective-permute-start.29 = (bf16[256,1024]{1,0:T(8,128)(2,1)S(1)}, bf16[256,1024]{1,0:T(8,128)(2,1)S(1)}, u32[]{:S(2)}, u32[]{:S(2)}) collective-permute-start(bf16[256,1024]{1,0:T(8,128)(2,1)S(1)} %get-tuple-element.83), channel_id=1, source_target_pairs={{0,1},{1,0},{2,3},{3,2},{4,5},{5,4},{6,7},{7,6},{8,9},{9,8},{10,11... | collective-permute-start | bytes 1572872 | tf_op jit(solution)/shard_map/ppermute | solution.py:321
  87.5 17.8 %collective-permute-start.32 = (bf16[256,1024]{1,0:T(8,128)(2,1)S(1)}, bf16[256,1024]{1,0:T(8,128)(2,1)S(1)}, u32[]{:S(2)}, u32[]{:S(2)}) collective-permute-start(bf16[256,1024]{1,0:T(8,128)(2,1)S(1)} %add_convert_fusion), channel_id=1, source_target_pairs={{0,2},{1,3},{2,4},{3,5},{8,10},{9,11},{10,12},{11,13},{16,18},{17,... | collective-permute-start | bytes 1572872 | tf_op jit(solution)/shard_map/ppermute | solution.py:318
  92.2 13.2 %collective-permute-start.33 = (bf16[256,1024]{1,0:T(8,128)(2,1)S(1)}, bf16[256,1024]{1,0:T(8,128)(2,1)S(1)}, u32[]{:S(2)}, u32[]{:S(2)}) collective-permute-start(bf16[256,1024]{1,0:T(8,128)(2,1)S(1)} %add_convert_fusion), channel_id=1, source_target_pairs={{4,2},{5,3},{6,4},{7,5},{12,10},{13,11},{14,12},{15,13},{20,18},{2... | collective-permute-start | bytes 1572872 | tf_op jit(solution)/shard_map/ppermute | solution.py:318
  92.9 21.4 %collective-permute-start.24 = (bf16[4,256,256]{2,1,0:T(8,128)(2,1)S(1)}, bf16[4,256,256]{2,1,0:T(8,128)(2,1)S(1)}, u32[]{:S(2)}, u32[]{:S(2)}) collective-permute-start(bf16[4,256,256]{2,1,0:T(8,128)(2,1)S(1)} %add.43.refs_0_), channel_id=1, source_target_pairs={{0,1},{1,0},{2,3},{3,2},{4,5},{5,4},{6,7},{7,6},{8,9},{9,8},{10,11... | collective-permute-start | bytes 1572872 | tf_op jit(solution)/shard_map/ppermute | solution.py:321
  101.4 12.9 %collective-permute-start.26 = (bf16[4,256,256]{2,1,0:T(8,128)(2,1)S(1)}, bf16[4,256,256]{2,1,0:T(8,128)(2,1)S(1)}, u32[]{:S(2)}, u32[]{:S(2)}) collective-permute-start(bf16[4,256,256]{2,1,0:T(8,128)(2,1)S(1)} %collective-permute-done.25.refs_2_), channel_id=1, source_target_pairs={{0,1},{1,0},{2,3},{3,2},{4,5},{5,4},{6,7},{7,6},{8,9},{9,8},{10,11... | collective-permute-start | bytes 1572872 | tf_op jit(solution)/shard_map/ppermute | solution.py:321
  106.3 17.4 %collective-permute-start.38 = (bf16[256,1024]{1,0:T(8,128)(2,1)S(1)}, bf16[256,1024]{1,0:T(8,128)(2,1)S(1)}, u32[]{:S(2)}, u32[]{:S(2)}) collective-permute-start(bf16[256,1024]{1,0:T(8,128)(2,1)S(1)} %get-tuple-element.94), channel_id=1, source_target_pairs={{0,2},{1,3},{2,4},{3,5},{4,6},{5,7},{8,10},{9,11},{10,12},{11,13},... | collective-permute-start | bytes 1572872 | tf_op jit(solution)/shard_map/ppermute | solution.py:318
  113.0 14.9 %collective-permute-start.39 = (bf16[256,1024]{1,0:T(8,128)(2,1)S(1)}, bf16[256,1024]{1,0:T(8,128)(2,1)S(1)}, u32[]{:S(2)}, u32[]{:S(2)}) collective-permute-start(bf16[256,1024]{1,0:T(8,128)(2,1)S(1)} %get-tuple-element.95), channel_id=1, source_target_pairs={{2,0},{3,1},{4,2},{5,3},{6,4},{7,5},{10,8},{11,9},{12,10},{13,11},... | collective-permute-start | bytes 1572872 | tf_op jit(solution)/shard_map/ppermute | solution.py:318
  119.4 9.7 %collective-permute-start.41 = (f32[1,256]{1,0:T(1,128)S(1)}, f32[1,256]{1,0:T(1,128)S(1)}, u32[]{:S(2)}, u32[]{:S(2)}) collective-permute-start(f32[1,256]{1,0:T(1,128)S(1)} %slice_add_fusion), channel_id=1, source_target_pairs={{0,2},{1,3},{2,0},{3,1},{4,6},{5,7},{6,4},{7,5},{8,10},{9,11},{10,... | collective-permute-start | bytes 3080 | tf_op jit(solution)/shard_map/ppermute | solution.py:318
  120.8 8.2 %collective-permute-start.42 = (f32[1,256]{1,0:T(1,128)S(1)}, f32[1,256]{1,0:T(1,128)S(1)}, u32[]{:S(2)}, u32[]{:S(2)}) collective-permute-start(f32[1,256]{1,0:T(1,128)S(1)} %slice_add_fusion), channel_id=1, source_target_pairs={{0,4},{1,5},{2,6},{3,7},{4,0},{5,1},{6,2},{7,3},{8,12},{9,13},{10,... | collective-permute-start | bytes 3080 | tf_op jit(solution)/shard_map/ppermute | solution.py:318
  121.6 7.5 %collective-permute-start.43 = (f32[1,256]{1,0:T(1,128)S(1)}, f32[1,256]{1,0:T(1,128)S(1)}, u32[]{:S(2)}, u32[]{:S(2)}) collective-permute-start(f32[1,256]{1,0:T(1,128)S(1)} %slice_add_fusion), channel_id=1, source_target_pairs={{0,6},{1,7},{2,4},{3,5},{4,2},{5,3},{6,0},{7,1},{8,14},{9,15},{10,... | collective-permute-start | bytes 3080 | tf_op jit(solution)/shard_map/ppermute | solution.py:318
  (18 other events, 169.5 us)
